TPU v7x, 32 devices: a whole 2x2x4 slice. The times are simulated.
32 devices in a mesh: tiles: 16 (over z, x, core), dp: 2 (over y).
Axes of the slice: x: 2, y: 2, z: 4, core: 2. Of those that a mesh axis runs over, the one named last changes fastest.
Arguments:
- fields: bfloat16 [2, 48, 16, 16, 256], P('dp', 'tiles'), may hold values from -6 to 6
- grad_out: bfloat16 [2, 48, 16, 16, 256], P('dp', 'tiles'), may hold values from -6 to 6
- block_count: int32 [16], P('tiles'), may hold values from 1 to 3, as said below
- ocean: int32 [48], P('tiles'), may hold values from 0 to 1, as said below
- kernel: bfloat16 [7, 7, 256], replicated, may hold values from -0.875 to 0.875
- ln_gain: float32 [256], replicated, may hold values from 0.1 to 1.9
- w_in: bfloat16 [256, 1024], replicated, may hold values from -0.375 to 0.375
- w_out: bfloat16 [1024, 256], replicated, may hold values from -0.1875 to 0.1875
- layer_scale: float32 [256], replicated, may hold values from 0.3 to 1.5
Outputs:
- state_next: bfloat16 [2, 48, 16, 16, 256], P('dp', 'tiles')
- grad_fields: bfloat16 [2, 48, 16, 16, 256], P('dp', 'tiles')
- grad_kernel: float32 [7, 7, 256], replicated
- grad_gain: float32 [256], replicated
- grad_w_in: float32 [256, 1024], replicated
- grad_w_out: float32 [1024, 256], replicated
- grad_scale: float32 [256], replicated
Inputs may be any that keep to these rules, and one draw needn't show every extreme that they name: Index i of tiles owns block_count[i] consecutive cycle tiles in its first slots, in the cycle order of the first step; index i and index i + H (i < H, H half the number of entries) own equally many; some index owns 3 and some index owns one. 1 marks an ocean tile; the first and the last cycle tile that each index of tiles owns are ocean.
All inputs are finite; a program needn't handle non-finite values.
Results may differ from a plain program's by a relative error of at most 0.0066.
Values may be sent and summed in bfloat16 or wider, within the bound.
No kernel may reach another device: no remote copies, remote signals or barrier semaphores. Data moves between devices by JAX's collectives and lax.ppermute only.
A program may use at most 64 MiB of HBM per device.

v0:
```python
import functools

import jax
import jax.numpy as jnp
from jax import lax
from jax.experimental import pallas as pl
from jax.experimental.pallas import tpu as pltpu
from jax.sharding import Mesh, PartitionSpec as P

KSIZE = 7
HALF = KSIZE // 2
TILE = 16
EPS = 1e-06
TILES = ("chips", "core")
F32 = jnp.float32
BF16 = jnp.bfloat16
LANES = 128
LEFT = 8
GELU_C = 0.7978845608028654
GELU_A = 0.044715


def dot(lhs, rhs, lhs_dim, rhs_dim):
    return lax.dot_general(
        lhs, rhs, (((lhs_dim,), (rhs_dim,)), ((), ())), preferred_element_type=F32
    )


def cycle_rank():
    count = lax.axis_size(TILES)
    here = lax.axis_index("chips") * lax.axis_size("core") + lax.axis_index("core")
    return jnp.where(here < count // 2, here, count - 1 + count // 2 - here)


def is_even():
    return lax.rem(cycle_rank(), 2) == 0


class Fetch:
    def __init__(self, sems, *pairs):
        self.copies = [
            pltpu.make_async_copy(source, target, sems.at[at]) for at, (source, target) in enumerate(pairs)
        ]
        for copy in self.copies:
            copy.start()

    def wait(self, *which):
        for at in which:
            self.copies[at].wait()


def slot_flag(count_ref, ocean_ref, slot):
    live = jnp.logical_and(slot < count_ref[0], ocean_ref[slot] > 0)
    return jnp.where(live, 1.0, 0.0).astype(F32)


class Shape:
    def __init__(self, slots, channels, hidden):
        self.slots = slots
        self.channels = channels
        self.hidden = hidden
        self.parts = channels // LANES
        self.columns = slots * TILE
        self.pitch = self.columns + 2 * LEFT
        self.cells = slots * TILE * TILE
        self.edge_rows = HALF * TILE
        self.early = 12

    def lanes(self, part):
        return slice(part * LANES, (part + 1) * LANES)


def edge_planes(shape, source, start, stride):
    return [
        jnp.concatenate(
            [source[part, pl.ds(start + col, TILE, stride=stride), :] for part in range(shape.parts)], axis=1
        )
        for col in range(HALF)
    ]


def send_edges(shape, left, right, first, second):
    even = is_even()
    for col in range(HALF):
        rows = pl.ds(col * TILE, TILE)
        first[rows, :] = jnp.where(even, right[col], left[col]).astype(BF16)
        second[rows, :] = jnp.where(even, left[col], right[col]).astype(BF16)


def flip_matrix(shape, used):
    to = lax.broadcasted_iota(jnp.int32, (shape.pitch, shape.pitch), 0)
    frm = lax.broadcasted_iota(jnp.int32, (shape.pitch, shape.pitch), 1)
    return jnp.where(to + frm == used + 2 * LEFT - 1, 1.0, 0.0).astype(BF16)


def prep_kernel(shape, count_hbm, ocean_hbm, fields_hbm, first, second, count, ocean, fields, work, sems):
    fetch = Fetch(sems, (fields_hbm, fields), (count_hbm, count), (ocean_hbm, ocean))
    fetch.wait(0, 1, 2)
    owned = count[0]
    per_slot = TILE * TILE
    for slot in range(shape.slots):
        flag = slot_flag(count, ocean, slot)
        cells = fields[pl.ds(slot * per_slot, per_slot), :].astype(F32) * flag
        for part in range(shape.parts):
            work[part, pl.ds(slot * per_slot, per_slot), :] = cells[:, shape.lanes(part)]
    left = edge_planes(shape, work, 0, TILE)
    right = edge_planes(shape, work, (owned - 1) * per_slot + TILE - HALF, TILE)
    send_edges(shape, left, right, first, second)


def cotangent_kernel(
    shape, count_hbm, ocean_hbm, tangent_hbm, scale_hbm, w_out_hbm,
    dproj, dproj_t, dact,
    count, ocean, tangent, scale, w_out, sems,
):
    fetch = Fetch(
        sems, (tangent_hbm, tangent), (count_hbm, count), (ocean_hbm, ocean), (scale_hbm, scale), (w_out_hbm, w_out)
    )
    fetch.wait(0, 1, 2, 3)
    per_slot = TILE * TILE
    for slot in range(shape.slots):
        rows = pl.ds(slot * per_slot, per_slot)
        flag = slot_flag(count, ocean, slot)
        scaled = (tangent[rows, :].astype(F32) * (scale[...] * flag)).astype(BF16)
        dproj[rows, :] = scaled
        dproj_t[:, slot * per_slot : (slot + 1) * per_slot] = scaled.T
    fetch.wait(4)
    for slot in range(shape.slots):
        rows = pl.ds(slot * per_slot, per_slot)
        for h in range(shape.hidden // shape.channels):
            cols = slice(h * shape.channels, (h + 1) * shape.channels)
            dact[rows, cols] = dot(dproj[rows, :], w_out[cols, :], 1, 1)


def band_kernel(shape, count_hbm, ocean_hbm, fields_hbm, first, second, band, fold, count, ocean, fields, sems):
    fetch = Fetch(sems, (fields_hbm, fields), (count_hbm, count), (ocean_hbm, ocean))
    even = is_even()
    blank = jnp.zeros((LEFT, LANES), F32)
    per_slot = TILE * TILE
    for part in range(shape.parts):
        band[part, pl.ds(0, HALF * shape.pitch), :] = jnp.zeros((HALF * shape.pitch, LANES), F32)
        for row in range(TILE):
            base = (row + HALF) * shape.pitch
            band[part, pl.ds(base, LEFT), :] = blank
            band[part, pl.ds(base + LEFT + shape.columns, LEFT), :] = blank
    fetch.wait(0, 1, 2)
    used = count[0] * TILE
    flags = [slot_flag(count, ocean, slot) for slot in range(shape.slots)]
    top = HALF * shape.pitch
    for part in range(shape.parts):
        for row in range(TILE):
            base = (row + HALF) * shape.pitch
            for slot in range(shape.slots):
                cells = fields[pl.ds(slot * per_slot + row * TILE, TILE), shape.lanes(part)]
                band[part, pl.ds(base + LEFT + slot * TILE, TILE), :] = cells.astype(F32) * flags[slot]
        for col in range(HALF):
            rows = pl.ds(col * TILE, TILE)
            one = first[rows, shape.lanes(part)].astype(F32)
            two = second[rows, shape.lanes(part)].astype(F32)
            west = jnp.where(even, two, one)
            east = jnp.where(even, one, two)
            band[part, pl.ds(top + LEFT - HALF + col, TILE, stride=shape.pitch), :] = west
            band[part, pl.ds(top + LEFT + used + col, TILE, stride=shape.pitch), :] = east
    turn_rows(shape, used, band, (HALF + TILE - 1, HALF + TILE - 2, HALF + TILE - 3), fold)


def turn_rows(shape, used, source, rows, fold):
    flip = flip_matrix(shape, used)
    for k, row in enumerate(rows):
        at = pl.ds(row * shape.pitch, shape.pitch)
        cells = jnp.concatenate([source[part, at, :] for part in range(shape.parts)], axis=1)
        turned = dot(flip, cells.astype(BF16), 1, 0)
        fold[pl.ds(k * shape.pitch, shape.pitch), :] = turned.astype(BF16)


def put_fold(shape, fold, padded, first_row):
    for part in range(shape.parts):
        rows = pl.ds(first_row * shape.pitch, HALF * shape.pitch)
        padded[part, rows, :] = fold[:, shape.lanes(part)].astype(F32)


def spread_taps(shape, kernel, taps):
    for part in range(shape.parts):
        for tap in range(KSIZE * KSIZE):
            row = kernel[pl.ds(tap, 1), shape.lanes(part)].astype(F32)
            taps[part, tap] = jnp.broadcast_to(row, (8, LANES))


def convolve(shape, rows, padded, taps, convolved):
    run = shape.columns // 8
    pair = 2
    origin = LEFT - HALF

    def two_rows(step, carry):
        row = step * pair
        for part in range(shape.parts):
            sums = [[None] * run for _ in range(pair)]
            for above in range(KSIZE + pair - 1):
                base = (row + above) * shape.pitch + origin
                loaded = [
                    padded[part, pl.ds(base + at, 8, stride=run), :]
                    for at in range(run + KSIZE - 1)
                ]
                for which in range(pair):
                    tap_row = above - which
                    if not 0 <= tap_row < KSIZE:
                        continue
                    for shift in range(KSIZE):
                        weight = taps[part, tap_row * KSIZE + shift]
                        for at in range(run):
                            term = weight * loaded[at + shift]
                            old = sums[which][at]
                            sums[which][at] = term if old is None else old + term
            for which in range(pair):
                for at in range(run):
                    start = (row + which) * shape.columns + at
                    convolved[part, pl.ds(start, 8, stride=run), :] = sums[which][at]
        return carry

    lax.fori_loop(0, rows // pair, two_rows, 0)


def normalise(shape, rows, first_row, convolved, gain, normed, yhat, inverse):
    def one_row(row, carry):
        for slot in range(shape.slots):
            start = pl.multiple_of(row * shape.columns + slot * TILE, TILE)
            at = slot * TILE * TILE + (first_row + row) * TILE
            out = pl.ds(pl.multiple_of(at, TILE), TILE)
            parts = [convolved[part, pl.ds(start, TILE), :] for part in range(shape.parts)]
            mean = jnp.sum(sum(parts), axis=-1, keepdims=True) * (1.0 / shape.channels)
            parts = [value - mean for value in parts]
            square = jnp.sum(sum(value * value for value in parts), axis=-1, keepdims=True)
            scale = lax.rsqrt(square * (1.0 / shape.channels) + EPS)
            inverse[out, :] = jnp.broadcast_to(scale, (TILE, LANES))
            for part in range(shape.parts):
                value = parts[part] * scale
                yhat[out, shape.lanes(part)] = value
                normed[out, shape.lanes(part)] = (value * gain[:, shape.lanes(part)]).astype(BF16)
        return carry

    lax.fori_loop(0, rows, one_row, 0, unroll=2)


def early_kernel(
    shape, taps_hbm, gain_hbm, band,
    normed, yhat, inverse,
    kernel, gain, taps, convolved, sems,
):
    fetch = Fetch(sems, (taps_hbm, kernel), (gain_hbm, gain))
    fetch.wait(0, 1)
    spread_taps(shape, kernel, taps)
    convolve(shape, shape.early, band, taps, convolved)
    normalise(shape, shape.early, 0, convolved, gain, normed, yhat, inverse)


def late_kernel(
    shape, taps_hbm, gain_hbm, w_in_hbm, band, fold, normed_in, yhat_in, inverse_in, dproj_t, dact,
    keep, give, activated, dpreact, yhat, inverse,
    kernel, gain, w_in, taps, padded, convolved, normed, normed_t, sems,
):
    fetch = Fetch(sems, (taps_hbm, kernel), (gain_hbm, gain), (w_in_hbm, w_in))
    late = TILE - shape.early
    kept = late + HALF
    for part in range(shape.parts):
        rows = pl.ds(shape.early * shape.pitch, kept * shape.pitch)
        padded[part, pl.ds(0, kept * shape.pitch), :] = band[part, rows, :]
    put_fold(shape, fold, padded, kept)
    done = shape.early * TILE
    for slot in range(shape.slots):
        rows = pl.ds(slot * TILE * TILE, done)
        normed[rows, :] = normed_in[rows, :]
        yhat[rows, :] = yhat_in[rows, :]
        inverse[rows, :] = inverse_in[rows, :]
    fetch.wait(0, 1)
    spread_taps(shape, kernel, taps)
    convolve(shape, late, padded, taps, convolved)
    normalise(shape, late, shape.early, convolved, gain, normed, yhat, inverse)
    per_slot = TILE * TILE
    for slot in range(shape.slots):
        normed_t[:, slot * per_slot : (slot + 1) * per_slot] = normed[pl.ds(slot * per_slot, per_slot), :].T
    fetch.wait(2)
    keeps_in = lax.axis_index("core") == 0
    block = shape.channels
    for h in range(shape.hidden // block):
        cols = slice(h * block, (h + 1) * block)
        for slot in range(shape.slots):
            rows = pl.ds(slot * per_slot, per_slot)
            pre = dot(normed[rows, :], w_in[:, cols], 1, 0)
            square = pre * pre
            inner = pre * (GELU_C + (GELU_C * GELU_A) * square)
            gate = 0.5 + 0.5 * jnp.tanh(inner)
            activated[rows, cols] = (pre * gate).astype(BF16)
            slope = pre * (2.0 * GELU_C + (6.0 * GELU_C * GELU_A) * square)
            grown = gate + slope * (gate - gate * gate)
            dpreact[rows, cols] = (dact[rows, cols] * grown).astype(BF16)
        rows = slice(h * block, (h + 1) * block)
        of_in = dot(normed_t[...], dpreact[:, cols], 1, 0)
        of_out = dot(dproj_t[...], activated[:, cols], 1, 0)
        keep[rows, :] = jnp.where(keeps_in, of_in, of_out)
        give[rows, :] = jnp.where(keeps_in, of_out, of_in).astype(BF16)


def fold_sum(value):
    return jnp.sum(value.reshape(-1, 8, value.shape[-1]), axis=0)


def norm_grad_kernel(shape, w_in_hbm, gain_hbm, dpreact, yhat, inverse, conv_grad, gain_part, w_in, gain, sems):
    fetch = Fetch(sems, (w_in_hbm, w_in), (gain_hbm, gain))
    fetch.wait(0, 1)
    chunk = TILE * TILE
    total = jnp.zeros((8, shape.channels), F32)
    for slot in range(shape.slots):
        rows = pl.ds(slot * chunk, chunk)
        dnormed = dot(dpreact[rows, :], w_in[...], 1, 1)
        unit = yhat[rows, :]
        total += fold_sum(dnormed * unit)
        dhat = dnormed * gain[...]
        mean = jnp.sum(dhat, axis=-1, keepdims=True) * (1.0 / shape.channels)
        along = jnp.sum(dhat * unit, axis=-1, keepdims=True) * (1.0 / shape.channels)
        scale = jnp.concatenate([inverse[rows, :]] * shape.parts, axis=1)
        conv_grad[rows, :] = (scale * (dhat - mean - unit * along)).astype(BF16)
    gain_part[...] = total


def state_kernel(
    shape, count_hbm, ocean_hbm, fields_hbm, tangent_hbm, w_out_hbm, scale_hbm, activated,
    state, scale_part,
    count, ocean, fields, tangent, w_out, scale, sems,
):
    fetch = Fetch(
        sems, (w_out_hbm, w_out), (fields_hbm, fields), (tangent_hbm, tangent),
        (scale_hbm, scale), (count_hbm, count), (ocean_hbm, ocean),
    )
    fetch.wait(0, 1, 2, 3, 4, 5)
    chunk = TILE * TILE
    total = jnp.zeros((8, shape.channels), F32)
    for slot in range(shape.slots):
        rows = pl.ds(slot * chunk, chunk)
        flag = slot_flag(count, ocean, slot)
        projected = dot(activated[rows, :], w_out[...], 1, 0)
        kept = fields[rows, :].astype(F32) + scale[...] * projected
        state[rows, :] = (flag * kept).astype(BF16)
        total += fold_sum(flag * tangent[rows, :].astype(F32) * projected)
    scale_part[...] = total


def place_grad(shape, conv_grad, spaced):
    blank = jnp.zeros((LEFT, LANES), F32)
    for part in range(shape.parts):
        for row in range(TILE):
            base = row * shape.pitch
            spaced[part, pl.ds(base, LEFT), :] = blank
            spaced[part, pl.ds(base + LEFT + shape.columns, LEFT), :] = blank
            for slot in range(shape.slots):
                cells = conv_grad[pl.ds(slot * TILE * TILE + row * TILE, TILE), shape.lanes(part)]
                spaced[part, pl.ds(base + LEFT + slot * TILE, TILE), :] = cells.astype(F32)


def taps_kernel(shape, band, fold, conv_grad, gain_part, scale_part, small, padded, spaced):
    taps = KSIZE * KSIZE
    small[...] = jnp.zeros_like(small)
    small[pl.ds(taps, 1), :] = jnp.sum(gain_part[...], axis=0, keepdims=True)
    small[pl.ds(taps + 1, 1), :] = jnp.sum(scale_part[...], axis=0, keepdims=True)
    place_grad(shape, conv_grad, spaced)
    kept = TILE + HALF
    for part in range(shape.parts):
        padded[part, pl.ds(0, kept * shape.pitch), :] = band[part]
    put_fold(shape, fold, padded, kept)
    run = shape.columns // 8
    origin = LEFT - HALF
    for part in range(shape.parts):
        for above in range(KSIZE):

            def one_row(row, sums, part=part, above=above):
                base = (row + above) * shape.pitch + origin
                loaded = [
                    padded[part, pl.ds(base + at, 8, stride=run), :] for at in range(run + KSIZE - 1)
                ]
                grads = [
                    spaced[part, pl.ds(row * shape.pitch + LEFT + at, 8, stride=run), :] for at in range(run)
                ]
                sums = list(sums)
                for shift in range(KSIZE):
                    for at in range(run):
                        sums[shift] = sums[shift] + grads[at] * loaded[at + shift]
                return tuple(sums)

            blank = tuple(jnp.zeros((8, LANES), F32) for _ in range(KSIZE))
            sums = lax.fori_loop(0, TILE, one_row, blank, unroll=2)
            for shift in range(KSIZE):
                small[pl.ds(above * KSIZE + shift, 1), shape.lanes(part)] = jnp.sum(
                    sums[shift], axis=0, keepdims=True
                )


def back_kernel(shape, count_hbm, taps_hbm, conv_grad, core_grad, fold, count, kernel, spaced, taps, sems):
    fetch = Fetch(sems, (count_hbm, count), (taps_hbm, kernel))
    place_grad(shape, conv_grad, spaced)
    blank = jnp.zeros((LEFT, LANES), F32)
    for part in range(shape.parts):
        for row in range(TILE + HALF):
            core_grad[part, pl.ds(row * shape.pitch, LEFT), :] = blank
            core_grad[part, pl.ds((row + 1) * shape.pitch - LEFT, LEFT), :] = blank
    fetch.wait(0, 1)
    spread_taps(shape, kernel, taps)
    run = -(-(shape.columns + 2 * HALF) // 8)

    def one_row(row, tap_rows):
        for part in range(shape.parts):
            sums = [None] * run
            for above in tap_rows:
                base = (row - above) * shape.pitch + LEFT
                loaded = [
                    spaced[part, pl.ds(base + at - KSIZE + 1, 8, stride=run), :]
                    for at in range(run + KSIZE - 1)
                ]
                for shift in range(KSIZE):
                    weight = taps[part, above * KSIZE + shift]
                    for at in range(run):
                        term = weight * loaded[at - shift + KSIZE - 1]
                        sums[at] = term if sums[at] is None else sums[at] + term
            start = (row - HALF) * shape.pitch + LEFT - HALF
            for at in range(run):
                core_grad[part, pl.ds(start + at, 8, stride=run), :] = sums[at]

    inner = (KSIZE - 1, TILE - 1)
    for row in range(HALF, TILE + 2 * HALF):
        if not inner[0] <= row <= inner[1]:
            low = max(0, row - TILE + 1)
            one_row(row, range(low, min(KSIZE - 1, row) + 1))

    def inner_row(step, carry):
        one_row(step, range(KSIZE))
        return carry

    lax.fori_loop(inner[0], inner[1] + 1, inner_row, 0)
    turn_rows(shape, count[0] * TILE, core_grad, (TILE, TILE + 1, TILE + 2), fold)


def rims_kernel(shape, count_hbm, core_grad, fold, folded, first, second, count, sems):
    fetch = Fetch(sems, (count_hbm, count))
    for part in range(shape.parts):
        folded[part] = core_grad[part, pl.ds(0, TILE * shape.pitch), :]
        for k in range(HALF):
            rows = pl.ds((TILE - 1 - k) * shape.pitch, shape.pitch)
            returned = fold[pl.ds(k * shape.pitch, shape.pitch), shape.lanes(part)]
            folded[part, rows, :] += returned.astype(F32)
    fetch.wait(0)
    west = edge_planes(shape, folded, LEFT - HALF, shape.pitch)
    east = edge_planes(shape, folded, LEFT + count[0] * TILE, shape.pitch)
    send_edges(shape, west, east, first, second)


def final_kernel(
    shape, count_hbm, ocean_hbm, tangent_hbm, folded, first, second,
    grad_fields,
    count, ocean, tangent, work, sems,
):
    fetch = Fetch(sems, (tangent_hbm, tangent), (count_hbm, count), (ocean_hbm, ocean))
    even = is_even()
    work[...] = folded[...]
    fetch.wait(0, 1, 2)
    used = count[0] * TILE
    for part in range(shape.parts):
        for col in range(HALF):
            planes = pl.ds(col * TILE, TILE)
            one = first[planes, shape.lanes(part)].astype(F32)
            two = second[planes, shape.lanes(part)].astype(F32)
            to_tail = jnp.where(even, one, two)
            to_head = jnp.where(even, two, one)
            head = pl.ds(LEFT + col, TILE, stride=shape.pitch)
            work[part, head, :] = work[part, head, :] + to_head
            tail = pl.ds(LEFT + used - HALF + col, TILE, stride=shape.pitch)
            work[part, tail, :] = work[part, tail, :] + to_tail
        for slot in range(shape.slots):
            flag = slot_flag(count, ocean, slot)
            for row in range(TILE):
                rows = pl.ds(slot * TILE * TILE + row * TILE, TILE)
                cells = work[part, pl.ds(row * shape.pitch + LEFT + slot * TILE, TILE), :]
                total = tangent[rows, shape.lanes(part)].astype(F32) + cells
                grad_fields[rows, shape.lanes(part)] = (flag * total).astype(BF16)


def unpack_kernel(norm, own, other, small, w_in, w_out, kernel_sum, gain_sum, scale_sum):
    is_first = lax.axis_index("core") == 0
    channels = own.shape[-1]
    for h in range(w_out.shape[0] // channels):
        rows = slice(h * channels, (h + 1) * channels)
        mine = own[rows, :].astype(F32) * norm
        theirs = other[rows, :].astype(F32) * norm
        w_in[:, rows] = jnp.where(is_first, mine, theirs)
        w_out[rows, :] = jnp.where(is_first, theirs, mine).T
    for above in range(KSIZE):
        kernel_sum[above] = small[pl.ds(above * KSIZE, KSIZE), :] * norm
    gain_sum[...] = small[pl.ds(KSIZE * KSIZE, 1), :] * norm
    scale_sum[...] = small[pl.ds(KSIZE * KSIZE + 1, 1), :] * norm


def pairs_of(kind):
    count = lax.axis_size(TILES)
    half = count // 2
    place = [rank if rank < half else count - 1 + half - rank for rank in range(count)]
    partner = {
        "first": lambda rank: rank ^ 1,
        "second": lambda rank: ((rank + 1) ^ 1) - 1,
        "fold": lambda rank: count - 1 - rank,
    }[kind]
    return [(place[rank], place[partner(rank) % count]) for rank in range(count)]


def swap(block, kind):
    return lax.ppermute(block, TILES, pairs_of(kind))


def core_swap(block):
    return lax.ppermute(block, "core", [(0, 1), (1, 0)])


def stages():
    chip_bits = lax.axis_size("chips").bit_length() - 1
    rest = list(range(2, chip_bits))
    return list(zip([0, -1, 1] + rest, [1, 0, -1] + rest))


def bit_swap(block, stage):
    chips, cores, samples = (lax.axis_size(axis) for axis in ("chips", "core", "dp"))
    pairs = []
    for chip in range(chips):
        for core in range(cores):
            for sample in range(samples):
                bit = stage[core]
                to = (chip, sample ^ 1) if bit < 0 else (chip ^ (1 << bit), sample)
                pairs.append(
                    ((chip * cores + core) * samples + sample, (to[0] * cores + core) * samples + to[1])
                )
    return lax.ppermute(block, ("chips", "core", "dp"), pairs)


def bit_here(stage):
    bits = [
        lax.axis_index("dp") if bit < 0 else lax.axis_index("chips") >> bit & 1 for bit in stage
    ]
    return jnp.where(lax.axis_index("core") == 0, bits[0], bits[1])


def halved(keep, give):
    mine = keep + core_swap(give).astype(F32)
    for stage in stages():
        bit = bit_here(stage)
        halves = mine.reshape(2, -1, mine.shape[-1])
        send = lax.dynamic_index_in_dim(halves, 1 - bit, 0, keepdims=False).astype(BF16)
        mine = lax.dynamic_index_in_dim(halves, bit, 0, keepdims=False) + bit_swap(send, stage).astype(F32)
    return mine.astype(BF16)


def doubled(mine, small):
    for stage in reversed(stages()):
        rows = mine.shape[0]
        rounded = small.astype(BF16)
        came = bit_swap(jnp.concatenate([mine, rounded]), stage)
        first = bit_here(stage) == 0
        other = came[:rows]
        mine = jnp.concatenate([jnp.where(first, mine, other), jnp.where(first, other, mine)])
        small = lax.reduce_precision(small, 8, 7) + came[rows:].astype(F32)
    rows = mine.shape[0]
    high = lax.reduce_precision(small, 8, 7)
    low = lax.reduce_precision(small - high, 8, 7)
    came = core_swap(jnp.concatenate([mine, high.astype(BF16), low.astype(BF16)]))
    extra = came[rows:].astype(F32).reshape(2, -1, small.shape[-1])
    small = (high + low) + (extra[0] + extra[1])
    return mine, came[:rows], small


def call(kernel, outs, scratch, hbm, vmem, copies=0, micros=1.0):
    in_specs = [pl.BlockSpec(memory_space=pl.ANY)] * len(hbm)
    in_specs += [pl.BlockSpec(memory_space=pltpu.VMEM)] * len(vmem)
    shapes = [pltpu.SMEM(*one) if one[1] == jnp.int32 else pltpu.VMEM(*one) for one in scratch]
    if copies:
        shapes.append(pltpu.SemaphoreType.DMA((copies,)))
    return pl.pallas_call(
        kernel,
        out_shape=[jax.ShapeDtypeStruct(*out) for out in outs],
        in_specs=in_specs,
        out_specs=[pl.BlockSpec(memory_space=pltpu.VMEM)] * len(outs),
        scratch_shapes=shapes,
        cost_estimate=pl.CostEstimate(flops=int(micros * 1e9), bytes_accessed=0, transcendentals=0),
        compiler_params=pltpu.CompilerParams(vmem_limit_bytes=24 * 1024 * 1024),
    )(*hbm, *vmem)


def shards(fields, grad_out, block_count, ocean, kernel, ln_gain, w_in, w_out, layer_scale):
    samples, slots, tile_rows, tile_cols, channels = fields.shape
    hidden = w_in.shape[1]
    shape = Shape(slots, channels, hidden)
    cells, parts, pitch = shape.cells, shape.parts, shape.pitch
    grid = fields.shape
    fields = fields.reshape(cells, channels)
    tangent = grad_out.reshape(cells, channels)
    taps_in = kernel.reshape(KSIZE * KSIZE, channels)
    gain = ln_gain.reshape(1, channels)
    scale = layer_scale.reshape(1, channels)

    def bind(body):
        return functools.partial(body, shape)

    def strip(rows):
        return ((parts, rows * pitch, LANES), F32)

    edge = ((shape.edge_rows, channels), BF16)
    turned = ((HALF * pitch, channels), BF16)
    whole = ((cells, channels), BF16)
    whole_f = ((cells, channels), F32)
    wide = ((cells, hidden), BF16)
    narrow = ((cells, LANES), F32)
    row = ((1, channels), F32)
    eight = ((8, channels), F32)
    taps = ((parts, KSIZE * KSIZE, 8, LANES), F32)
    taps_raw = (taps_in.shape, BF16)
    count_s = (block_count.shape, jnp.int32)
    ocean_s = (ocean.shape, jnp.int32)
    w_in_s = (w_in.shape, BF16)
    w_out_s = (w_out.shape, BF16)
    flat = ((channels, cells), BF16)
    late = TILE - shape.early

    first, second = call(
        bind(prep_kernel), [edge, edge], [count_s, ocean_s, whole, ((parts, cells, LANES), F32)],
        [block_count, ocean, fields], [], 3, 1.5,
    )
    first, second = swap(first, "first"), swap(second, "second")
    dproj, dproj_t, dact = call(
        bind(cotangent_kernel), [whole, flat, ((cells, hidden), F32)],
        [count_s, ocean_s, whole, row, w_out_s],
        [block_count, ocean, tangent, scale, w_out], [], 5, 2.5,
    )
    band, fold = call(
        bind(band_kernel), [strip(TILE + HALF), turned], [count_s, ocean_s, whole],
        [block_count, ocean, fields], [first, second], 3, 1.0,
    )
    fold = swap(fold, "fold")
    normed, yhat, inverse = call(
        bind(early_kernel), [whole, whole_f, narrow],
        [taps_raw, row, taps, ((parts, shape.early * shape.columns, LANES), F32)],
        [taps_in, gain], [band], 2, 4.0,
    )
    keep, give, activated, dpreact, yhat, inverse = call(
        bind(late_kernel),
        [((hidden, channels), F32), ((hidden, channels), BF16), wide, wide, whole_f, narrow],
        [
            taps_raw, row, w_in_s, taps, strip(late + 2 * HALF),
            ((parts, late * shape.columns, LANES), F32), whole, flat,
        ],
        [taps_in, gain, w_in], [band, fold, normed, yhat, inverse, dproj_t, dact], 3, 6.0,
    )
    conv_grad, gain_part = call(
        bind(norm_grad_kernel), [whole, eight], [w_in_s, row], [w_in, gain], [dpreact, yhat, inverse], 2, 1.5,
    )
    mine = halved(keep, give)
    core_grad, fold_back = call(
        bind(back_kernel), [strip(TILE + HALF), turned],
        [count_s, taps_raw, strip(TILE), taps],
        [block_count, taps_in], [conv_grad], 2, 4.0,
    )
    fold_back = swap(fold_back, "fold")
    state, scale_part = call(
        bind(state_kernel), [whole, eight], [count_s, ocean_s, whole, whole, w_out_s, row],
        [block_count, ocean, fields, tangent, w_out, scale], [activated], 6, 1.5,
    )
    small_rows = -(-(KSIZE * KSIZE + 2) // 16) * 16
    (small,) = call(
        bind(taps_kernel), [((small_rows, channels), F32)], [strip(TILE + 2 * HALF), strip(TILE)],
        [], [band, fold, conv_grad, gain_part, scale_part], 0, 3.5,
    )
    folded, first, second = call(
        bind(rims_kernel), [strip(TILE), edge, edge], [count_s], [block_count], [core_grad, fold_back], 1, 1.0,
    )
    first, second = swap(first, "first"), swap(second, "second")
    (grad_fields,) = call(
        bind(final_kernel), [whole], [count_s, ocean_s, whole, strip(TILE)],
        [block_count, ocean, tangent], [folded, first, second], 3, 1.5,
    )
    own, other, small = doubled(mine, small)
    total = samples * lax.axis_size("dp") * slots * lax.axis_size(TILES) * tile_rows * tile_cols
    w_in_sum, w_out_sum, kernel_sum, gain_sum, scale_sum = call(
        functools.partial(unpack_kernel, total ** (-0.5)),
        [((channels, hidden), F32), ((hidden, channels), F32), (kernel.shape, F32), row, row],
        [], [], [own, other, small], 0, 1.5,
    )
    return (
        state.reshape(grid),
        grad_fields.reshape(grid),
        kernel_sum,
        gain_sum.reshape(ln_gain.shape),
        w_in_sum,
        w_out_sum,
        scale_sum.reshape(layer_scale.shape),
    )


def solution(mesh):
    cores = Mesh(mesh.devices.reshape(-1, 2, mesh.devices.shape[1]), ("chips", "core", "dp"))
    banded = P("dp", TILES, None, None, None)
    placed = (banded, banded, P(TILES), P(TILES), P(), P(), P(), P(), P())
    return jax.shard_map(
        shards,
        mesh=cores,
        in_specs=placed,
        out_specs=(banded, banded, P(), P(), P(), P(), P()),
        check_vma=False,
    )
```

profile of v0, /device:TPU:0, one launch (start us, length us, event | category | flops | bytes accessed | tf_op | source)
XLA Modules:
  0.0 100.1 jit_solution(5814097826475802723)
XLA Ops:
  1.3 1.0 copy-done.2
  2.3 0.7 copy-done.7
  2.9 0.9 shard_map.144
  3.8 0.5 collective-permute-start
  4.3 3.7 %collective-permute-start.1 = (bf16[48,256]{1,0:T(8,128)(2,1)S(1)}, bf16[48,256]{1,0:T(8,128)(2,1)S(1)}, u32[]{:S(2)}, u32[]{:S(2)}) collective-permute-start(bf16[48,256]{1,0:T(8,128)(2,1)S(1)} %get-tuple-element.37), channel_id=1, source_target_pairs={{0,16},{2,4},{4,2},{6,8},{8,6},{10,12},{12,10},{14,30},{30,14},{28... | collective-permute-start | bytes 73736 | tf_op jit(solution)/shard_map/ppermute | solution.py:512
  8.0 1.7 %shard_map.147 = (bf16[768,256]{1,0:T(8,128)(2,1)}, bf16[256,768]{1,0:T(8,128)(2,1)S(1)}, f32[768,1024]{1,0:T(8,128)S(1)}) custom-call(s32[1]{0:T(128)S(6)} %copy.16.count_hbm, s32[3]{0:T(128)S(1)} %copy-done.7, bf16[768,256]{1,0:T(8,128)(2,1)S(1)} %bitcast.33, f32[1,256]{1,0:T(1,128)S(1)} %bitcast.36, bf16[1024,256]{1,0:T(8,128)(2,1)S(1)} %copy-done), custom_call_target="tpu_custom_call" | custom-call | flops 2500000000 | tf_op jit(solution)/shard_map/pallas_call | solution.py:580
  9.8 1.6 %copy-done.19 = f32[768,1024]{1,0:T(8,128)} copy-done((f32[768,1024]{1,0:T(8,128)}, f32[768,1024]{1,0:T(8,128)S(1)}, u32[]{:S(2)}) %copy-start.19) | copy-done | bytes 3145752
  11.4 0.7 copy-done.21
  12.2 1.1 %shard_map.145 = (f32[2,1216,128]{2,1,0:T(8,128)S(1)}, bf16[192,256]{1,0:T(8,128)(2,1)S(1)}) custom-call(s32[1]{0:T(128)S(6)} %copy.16.count_hbm, s32[3]{0:T(128)S(1)} %copy-done.8, bf16[768,256]{1,0:T(8,128)(2,1)S(1)} %bitcast.31, bf16[48,256]{1,0:T(8,128)(2,1)S(1)} %collective-permute-done.first, bf16[48,256]{1,0:T(8,128)(2,1)S(1)} %collective-permute-done.1.second), custom_call_target="tpu_custom_call" | custom-call | flops 1000000000 | tf_op jit(solution)/shard_map/pallas_call | solution.py:580
  13.3 0.6 collective-permute-start.2
  13.9 3.5 %shard_map.146 = (bf16[768,256]{1,0:T(8,128)(2,1)S(1)}, f32[768,256]{1,0:T(8,128)S(1)}, f32[768,128]{1,0:T(8,128)S(1)}) custom-call(bf16[49,256]{1,0:T(8,128)(2,1)S(1)} %reshape.65.taps_hbm, f32[1,256]{1,0:T(1,128)S(1)} %bitcast.38, f32[2,1216,128]{2,1,0:T(8,128)S(1)} %get-tuple-element.38.band), custom_call_target="tpu_custom_call" | custom-call | flops 4000000000 | tf_op jit(solution)/shard_map/pallas_call | solution.py:580
  17.4 2.7 %collective-permute-done.2.fold = bf16[192,256]{1,0:T(8,128)(2,1)S(1)} collective-permute-done((bf16[192,256]{1,0:T(8,128)(2,1)S(1)}, bf16[192,256]{1,0:T(8,128)(2,1)S(1)}, u32[]{:S(2)}, u32[]{:S(2)}) %collective-permute-start.2) | collective-permute-done | bytes 98336 | tf_op jit(solution)/shard_map/ppermute | solution.py:512
  20.1 4.6 %shard_map.148 = (f32[1024,256]{1,0:T(8,128)S(1)}, bf16[1024,256]{1,0:T(8,128)(2,1)S(1)}, bf16[768,1024]{1,0:T(8,128)(2,1)S(1)}, bf16[768,1024]{1,0:T(8,128)(2,1...) custom-call(bf16[49,256]{1,0:T(8,128)(2,1)S(1)} %reshape.65.taps_hbm, f32[1,256]{1,0:T(1,128)S(1)} %bitcast.39, ...), custom_call_target="tpu_custom_call" | custom-call | flops 6000000000 | tf_op jit(solution)/shard_map/pallas_call | solution.py:580
  24.7 1.2 %copy-done.9 = bf16[768,1024]{1,0:T(8,128)(2,1)} copy-done((bf16[768,1024]{1,0:T(8,128)(2,1)}, bf16[768,1024]{1,0:T(8,128)(2,1)S(1)}, u32[]{:S(2)}) %copy-start.9) | copy-done | bytes 1572888
  25.9 1.1 %copy-done.11 = bf16[768,1024]{1,0:T(8,128)(2,1)} copy-done((bf16[768,1024]{1,0:T(8,128)(2,1)}, bf16[768,1024]{1,0:T(8,128)(2,1)S(1)}, u32[]{:S(2)}) %copy-start.11) | copy-done | bytes 1572888
  27.0 0.9 copy-done.13
  27.9 0.7 copy-done.17
  28.6 2.0 %collective-permute-done.6 = bf16[1024,256]{1,0:T(8,128)(2,1)} collective-permute-done((bf16[1024,256]{1,0:T(8,128)(2,1)S(1)}, bf16[1024,256]{1,0:T(8,128)(2,1)}, u32[]{:S(2)}, u32[]{:S(2)}) %collective-permute-start.6) | collective-permute-done | bytes 524320 | tf_op jit(solution)/shard_map/ppermute | solution.py:516
  30.7 1.2 %convert_add_fusion = f32[1024,256]{1,0:T(8,128)S(1)} fusion(f32[1024,256]{1,0:T(8,128)S(1)} %get-tuple-element.56, bf16[1024,256]{1,0:T(8,128)(2,1)} %collective-permute-done.6), kind=kLoop, calls=%fused_computation | loop fusion | flops 524288 | bytes 2621440 | tf_op jit(solution)/shard_map/add | solution.py:547
  31.9 1.0 copy-done.23
  32.9 0.8 collective-permute-start.7
  33.7 5.6 %collective-permute-done.7 = bf16[512,256]{1,0:T(8,128)(2,1)S(1)} collective-permute-done((bf16[512,256]{1,0:T(8,128)(2,1)S(1)}, bf16[512,256]{1,0:T(8,128)(2,1)S(1)}, u32[]{:S(2)}, u32[]{:S(2)}) %collective-permute-start.7) | collective-permute-done | bytes 262176 | tf_op jit(solution)/shard_map/ppermute | solution.py:536
  39.3 1.1 %bitcast_add_fusion = f32[512,256]{1,0:T(8,128)S(1)} fusion(bf16[512,256]{1,0:T(8,128)(2,1)S(1)} %collective-permute-done.7, f32[2,512,256]{2,1,0:T(8,128)} %bitcast.42, s32[]{:T(128)S(6)} %select_n.98), kind=kLoop, calls=%fused_computation.3 | loop fusion | flops 262144 | bytes 1310724 | tf_op jit(solution)/shard_map/add | solution.py:552
  40.5 1.6 %collective-permute-start.8 = (bf16[256,256]{1,0:T(8,128)(2,1)S(1)}, bf16[256,256]{1,0:T(8,128)(2,1)S(1)}, u32[]{:S(2)}, u32[]{:S(2)}) collective-permute-start(bf16[256,256]{1,0:T(8,128)(2,1)S(1)} %fusion.1), channel_id=1, source_target_pairs={{0,1},{1,0},{2,6},{3,7},{4,5},{5,4},{6,2},{7,3},{8,9},{9,8},{10,14... | collective-permute-start | bytes 393224 | tf_op jit(solution)/shard_map/ppermute | solution.py:536
  42.0 1.4 %copy-done.12 = bf16[768,1024]{1,0:T(8,128)(2,1)S(1)} copy-done((bf16[768,1024]{1,0:T(8,128)(2,1)S(1)}, bf16[768,1024]{1,0:T(8,128)(2,1)}, u32[]{:S(2)}) %copy-start.12) | copy-done | bytes 1572888
  43.5 2.4 %shard_map.149 = (bf16[768,256]{1,0:T(8,128)(2,1)}, f32[8,256]{1,0:T(8,128)S(1)}) custom-call(s32[1]{0:T(128)S(6)} %copy.16.count_hbm, s32[3]{0:T(128)S(1)} %copy-done.8, bf16[768,256]{1,0:T(8,128)(2,1)S(1)} %bitcast.32, bf16[768,256]{1,0:T(8,128)(2,1)S(1)} %bitcast.34, bf16[1024,256]{1,0:T(8,128)(2,1)S(1)} %copy-done, f32[1,256]{1,0:T(1,128)S(1)} %bitcast.37, ...), custom_call_target="tpu_custom_call" | custom-call | flops 1500000000 | tf_op jit(solution)/shard_map/pallas_call | solution.py:580
  45.9 0.6 collective-permute-start.9
  46.6 0.9 shard_map.150
  47.5 2.8 %collective-permute-done.9 = bf16[128,256]{1,0:T(8,128)(2,1)S(1)} collective-permute-done((bf16[128,256]{1,0:T(8,128)(2,1)S(1)}, bf16[128,256]{1,0:T(8,128)(2,1)S(1)}, u32[]{:S(2)}, u32[]{:S(2)}) %collective-permute-start.9) | collective-permute-done | bytes 65568 | tf_op jit(solution)/shard_map/ppermute | solution.py:536
  50.3 2.1 %collective-permute-start.10 = (bf16[64,256]{1,0:T(8,128)(2,1)S(1)}, bf16[64,256]{1,0:T(8,128)(2,1)S(1)}, u32[]{:S(2)}, u32[]{:S(2)}) collective-permute-start(bf16[64,256]{1,0:T(8,128)(2,1)S(1)} %fusion.9), channel_id=1, source_target_pairs={{0,16},{1,17},{2,18},{3,19},{4,20},{5,21},{6,22},{7,23},{8,24},{9,... | collective-permute-start | bytes 98312 | tf_op jit(solution)/shard_map/ppermute | solution.py:536
  52.4 3.6 %shard_map.154 = f32[64,256]{1,0:T(8,128)S(1)} custom-call(f32[2,1216,128]{2,1,0:T(8,128)S(1)} %copy-done.16, bf16[192,256]{1,0:T(8,128)(2,1)S(1)} %collective-permute-done.2.fold, bf16[768,256]{1,0:T(8,128)(2,1)S(1)} %get-tuple-element.50.conv_grad, f32[8,256]{1,0:T(8,128)S(1)} %get-tuple-element.58.gain_part, f32[8,256]{1,0:T(8,128)S(1)} %get-tuple-element.59.scale_part), custom_call_target="tpu_custom_call" | custom-call | flops 3500000000 | tf_op jit(solution)/shard_map/pallas_call | solution.py:580
  56.0 1.3 %collective-permute-start.11 = (bf16[128,256]{1,0:T(8,128)(2,1)S(1)}, bf16[128,256]{1,0:T(8,128)(2,1)S(1)}, u32[]{:S(2)}, u32[]{:S(2)}) collective-permute-start(bf16[128,256]{1,0:T(8,128)(2,1)S(1)} %pad_maximum_fusion.7), channel_id=1, source_target_pairs={{0,16},{1,17},{2,18},{3,19},{4,20},{5,21},{6,22},{7,23},{8,24},{9,... | collective-permute-start | bytes 196616 | tf_op jit(solution)/shard_map/ppermute | solution.py:536
  57.3 3.9 %collective-permute-done.11 = bf16[128,256]{1,0:T(8,128)(2,1)S(1)} collective-permute-done((bf16[128,256]{1,0:T(8,128)(2,1)S(1)}, bf16[128,256]{1,0:T(8,128)(2,1)S(1)}, u32[]{:S(2)}, u32[]{:S(2)}) %collective-permute-start.11) | collective-permute-done | bytes 65568 | tf_op jit(solution)/shard_map/ppermute | solution.py:536
  61.3 2.0 %collective-permute-start.12 = (bf16[192,256]{1,0:T(8,128)(2,1)S(1)}, bf16[192,256]{1,0:T(8,128)(2,1)S(1)}, u32[]{:S(2)}, u32[]{:S(2)}) collective-permute-start(bf16[192,256]{1,0:T(8,128)(2,1)S(1)} %pad_maximum_fusion.6), channel_id=1, source_target_pairs={{0,8},{1,9},{2,3},{3,2},{4,12},{5,13},{6,7},{7,6},{8,0},{9,1},{10,... | collective-permute-start | bytes 294920 | tf_op jit(solution)/shard_map/ppermute | solution.py:536
  63.3 2.7 %collective-permute-done.12 = bf16[192,256]{1,0:T(8,128)(2,1)S(1)} collective-permute-done((bf16[192,256]{1,0:T(8,128)(2,1)S(1)}, bf16[192,256]{1,0:T(8,128)(2,1)S(1)}, u32[]{:S(2)}, u32[]{:S(2)}) %collective-permute-start.12) | collective-permute-done | bytes 98336 | tf_op jit(solution)/shard_map/ppermute | solution.py:536
  66.1 1.0 %collective-permute-start.13 = (bf16[320,256]{1,0:T(8,128)(2,1)S(1)}, bf16[320,256]{1,0:T(8,128)(2,1)S(1)}, u32[]{:S(2)}, u32[]{:S(2)}) collective-permute-start(bf16[320,256]{1,0:T(8,128)(2,1)S(1)} %pad_maximum_fusion.4), channel_id=1, source_target_pairs={{0,1},{1,0},{2,6},{3,7},{4,5},{5,4},{6,2},{7,3},{8,9},{9,8},{10,14... | collective-permute-start | bytes 491528 | tf_op jit(solution)/shard_map/ppermute | solution.py:536
  67.1 4.3 %collective-permute-done.13 = bf16[320,256]{1,0:T(8,128)(2,1)S(1)} collective-permute-done((bf16[320,256]{1,0:T(8,128)(2,1)S(1)}, bf16[320,256]{1,0:T(8,128)(2,1)S(1)}, u32[]{:S(2)}, u32[]{:S(2)}) %collective-permute-start.13) | collective-permute-done | bytes 163872 | tf_op jit(solution)/shard_map/ppermute | solution.py:536
  71.6 0.7 collective-permute-start.14
  72.2 6.1 %collective-permute-done.14 = bf16[576,256]{1,0:T(8,128)(2,1)S(1)} collective-permute-done((bf16[576,256]{1,0:T(8,128)(2,1)S(1)}, bf16[576,256]{1,0:T(8,128)(2,1)S(1)}, u32[]{:S(2)}, u32[]{:S(2)}) %collective-permute-start.14) | collective-permute-done | bytes 294944 | tf_op jit(solution)/shard_map/ppermute | solution.py:536
  78.7 4.1 %shard_map.151 = (f32[2,1216,128]{2,1,0:T(8,128)S(1)}, bf16[192,256]{1,0:T(8,128)(2,1)S(1)}) custom-call(s32[1]{0:T(128)S(6)} %copy.16.count_hbm, bf16[49,256]{1,0:T(8,128)(2,1)S(1)} %reshape.65.taps_hbm, bf16[768,256]{1,0:T(8,128)(2,1)S(1)} %get-tuple-element.50.conv_grad), custom_call_target="tpu_custom_call" | custom-call | flops 4000000000 | tf_op jit(solution)/shard_map/pallas_call | solution.py:580
  82.7 2.2 %collective-permute-start.3 = (bf16[192,256]{1,0:T(8,128)(2,1)S(1)}, bf16[192,256]{1,0:T(8,128)(2,1)S(1)}, u32[]{:S(2)}, u32[]{:S(2)}) collective-permute-start(bf16[192,256]{1,0:T(8,128)(2,1)S(1)} %get-tuple-element.52), channel_id=1, source_target_pairs={{0,16},{2,18},{4,20},{6,22},{8,24},{10,26},{12,28},{14,30},{30,14}... | collective-permute-start | bytes 294920 | tf_op jit(solution)/shard_map/ppermute | solution.py:512
  84.9 6.1 %collective-permute-done.3.fold = bf16[192,256]{1,0:T(8,128)(2,1)S(1)} collective-permute-done((bf16[192,256]{1,0:T(8,128)(2,1)S(1)}, bf16[192,256]{1,0:T(8,128)(2,1)S(1)}, u32[]{:S(2)}, u32[]{:S(2)}) %collective-permute-start.3) | collective-permute-done | bytes 98336 | tf_op jit(solution)/shard_map/ppermute | solution.py:512
  91.0 0.6 shard_map.152
  91.7 0.2 collective-permute-start.5
  91.9 1.0 collective-permute-done.4.first
  92.9 3.6 %collective-permute-done.5.second = bf16[48,256]{1,0:T(8,128)(2,1)S(1)} collective-permute-done((bf16[48,256]{1,0:T(8,128)(2,1)S(1)}, bf16[48,256]{1,0:T(8,128)(2,1)S(1)}, u32[]{:S(2)}, u32[]{:S(2)}) %collective-permute-start.5) | collective-permute-done | bytes 24608 | tf_op jit(solution)/shard_map/ppermute | solution.py:512
  96.5 1.8 %shard_map.153 = bf16[768,256]{1,0:T(8,128)(2,1)} custom-call(s32[1]{0:T(128)S(6)} %copy.16.count_hbm, s32[3]{0:T(128)S(1)} %copy-done.8, bf16[768,256]{1,0:T(8,128)(2,1)S(1)} %bitcast.35, f32[2,1024,128]{2,1,0:T(8,128)S(1)} %get-tuple-element.53.folded, bf16[48,256]{1,0:T(8,128)(2,1)S(1)} %collective-permute-done.4.first, ...), custom_call_target="tpu_custom_call" | custom-call | flops 1500000000 | tf_op jit(solution)/shard_map/pallas_call | solution.py:580
  98.5 1.6 %shard_map.155 = (f32[256,1024]{1,0:T(8,128)}, f32[1024,256]{1,0:T(8,128)}, f32[7,7,256]{2,1,0:T(8,128)}, f32[1,256]{1,0:T(1,128)}, f32[1,256]{1,0:T(1,128)}) custom-call(bf16[1024,256]{1,0:T(8,128)(2,1)S(1)} %pad_maximum_fusion.1.own, bf16[1024,256]{1,0:T(8,128)(2,1)S(1)} %slice.58.other, f32[64,256]{1,0:T(8,128)S(1)} %fusion.4.small), custom_call_target="tpu_custom_call" | custom-call | flops 1500000000 | tf_op jit(solution)/shard_map/pallas_call | solution.py:580
  (75 shorter events, 0.9 us)
Async XLA Ops:
  1.3 1.0 copy-start.2
  2.3 0.7 copy-start.7
  2.9 5.1 %copy-start = (bf16[1024,256]{1,0:T(8,128)(2,1)S(1)}, bf16[1024,256]{1,0:T(8,128)(2,1)}, u32[]{:S(2)}) copy-start(bf16[1024,256]{1,0:T(8,128)(2,1)} %w_out_hbm.3) | copy-start | bytes 1572868
  2.9 5.1 %copy-start.4 = (bf16[1,3,16,16,256]{4,3,2,1,0:T(8,128)(2,1)S(1)}, bf16[1,3,16,16,256]{4,3,2,1,0:T(8,128)(2,1)}, u32[]{:S(2)}) copy-start(bf16[1,3,16,16,256]{4,3,2,1,0:T(8,128)(2,1)} %param.10) | copy-start | bytes 1179652
  2.9 5.1 %copy-start.5 = (f32[256]{0:T(256)S(1)}, f32[256]{0:T(256)}, u32[]{:S(2)}) copy-start(f32[256]{0:T(256)} %param.17) | copy-start | bytes 3076
  3.8 8.4 %collective-permute-start = (bf16[48,256]{1,0:T(8,128)(2,1)S(1)}, bf16[48,256]{1,0:T(8,128)(2,1)S(1)}, u32[]{:S(2)}, u32[]{:S(2)}) collective-permute-start(bf16[48,256]{1,0:T(8,128)(2,1)S(1)} %get-tuple-element.36), channel_id=1, source_target_pairs={{0,2},{2,0},{4,6},{6,4},{8,10},{10,8},{12,14},{14,12},{30,28},{28,... | collective-permute-start | bytes 73736 | tf_op jit(solution)/shard_map/ppermute | solution.py:512
  4.3 7.9 %collective-permute-start.1 = (bf16[48,256]{1,0:T(8,128)(2,1)S(1)}, bf16[48,256]{1,0:T(8,128)(2,1)S(1)}, u32[]{:S(2)}, u32[]{:S(2)}) collective-permute-start(bf16[48,256]{1,0:T(8,128)(2,1)S(1)} %get-tuple-element.37), channel_id=1, source_target_pairs={{0,16},{2,4},{4,2},{6,8},{8,6},{10,12},{12,10},{14,30},{30,14},{28... | collective-permute-start | bytes 73736 | tf_op jit(solution)/shard_map/ppermute | solution.py:512
  8.0 4.1 %copy-start.24 = (bf16[7,7,256]{2,1,0:T(8,128)(2,1)S(1)}, bf16[7,7,256]{2,1,0:T(8,128)(2,1)}, u32[]{:S(2)}) copy-start(bf16[7,7,256]{2,1,0:T(8,128)(2,1)} %param.13) | copy-start | bytes 75268
  8.0 4.2 %copy-start.3 = (bf16[1,3,16,16,256]{4,3,2,1,0:T(8,128)(2,1)S(1)}, bf16[1,3,16,16,256]{4,3,2,1,0:T(8,128)(2,1)}, u32[]{:S(2)}) copy-start(bf16[1,3,16,16,256]{4,3,2,1,0:T(8,128)(2,1)} %param.9) | copy-start | bytes 1179652
  8.0 4.2 %copy-start.8 = (s32[3]{0:T(128)S(1)}, s32[3]{0:T(128)}, u32[]{:S(2)}) copy-start(s32[3]{0:T(128)} %ocean_hbm.9) | copy-start | bytes 40
  9.7 1.6 %copy-start.19 = (f32[768,1024]{1,0:T(8,128)}, f32[768,1024]{1,0:T(8,128)S(1)}, u32[]{:S(2)}) copy-start(f32[768,1024]{1,0:T(8,128)S(1)} %get-tuple-element.44.dact) | copy-start | bytes 9437188
  11.4 0.7 copy-start.21
  12.1 1.7 %copy-start.6 = (f32[256]{0:T(256)S(1)}, f32[256]{0:T(256)}, u32[]{:S(2)}) copy-start(f32[256]{0:T(256)} %param.14) | copy-start | bytes 3076
  13.3 6.8 %copy-start.15 = (f32[2,1216,128]{2,1,0:T(8,128)}, f32[2,1216,128]{2,1,0:T(8,128)S(1)}, u32[]{:S(2)}) copy-start(f32[2,1216,128]{2,1,0:T(8,128)S(1)} %get-tuple-element.38.band) | copy-start | bytes 3735556
  13.3 6.8 %collective-permute-start.2 = (bf16[192,256]{1,0:T(8,128)(2,1)S(1)}, bf16[192,256]{1,0:T(8,128)(2,1)S(1)}, u32[]{:S(2)}, u32[]{:S(2)}) collective-permute-start(bf16[192,256]{1,0:T(8,128)(2,1)S(1)} %get-tuple-element.39), channel_id=1, source_target_pairs={{0,16},{2,18},{4,20},{6,22},{8,24},{10,26},{12,28},{14,30},{30,14}... | collective-permute-start | bytes 294920 | tf_op jit(solution)/shard_map/ppermute | solution.py:512
  13.9 6.2 %copy-start.1 = (bf16[256,1024]{1,0:T(8,128)(2,1)S(1)}, bf16[256,1024]{1,0:T(8,128)(2,1)}, u32[]{:S(2)}) copy-start(bf16[256,1024]{1,0:T(8,128)(2,1)} %w_in_hbm.3) | copy-start | bytes 1572868
  13.9 6.2 %copy-start.20 = (f32[768,1024]{1,0:T(8,128)S(1)}, f32[768,1024]{1,0:T(8,128)}, u32[]{:S(2)}) copy-start(f32[768,1024]{1,0:T(8,128)} %copy-done.19) | copy-start | bytes 9437188
  13.9 6.2 %copy-start.22 = (bf16[256,768]{1,0:T(8,128)(2,1)S(1)}, bf16[256,768]{1,0:T(8,128)(2,1)}, u32[]{:S(2)}) copy-start(bf16[256,768]{1,0:T(8,128)(2,1)} %copy-done.21) | copy-start | bytes 1179652
  24.7 1.2 %copy-start.9 = (bf16[768,1024]{1,0:T(8,128)(2,1)}, bf16[768,1024]{1,0:T(8,128)(2,1)S(1)}, u32[]{:S(2)}) copy-start(bf16[768,1024]{1,0:T(8,128)(2,1)S(1)} %get-tuple-element.47.dpreact) | copy-start | bytes 4718596
  25.9 1.1 %copy-start.11 = (bf16[768,1024]{1,0:T(8,128)(2,1)}, bf16[768,1024]{1,0:T(8,128)(2,1)S(1)}, u32[]{:S(2)}) copy-start(bf16[768,1024]{1,0:T(8,128)(2,1)S(1)} %get-tuple-element.45.activated) | copy-start | bytes 4718596
  27.0 0.9 copy-start.13
  27.9 0.7 copy-start.17
  28.6 2.0 %collective-permute-start.6 = (bf16[1024,256]{1,0:T(8,128)(2,1)S(1)}, bf16[1024,256]{1,0:T(8,128)(2,1)}, u32[]{:S(2)}, u32[]{:S(2)}) collective-permute-start(bf16[1024,256]{1,0:T(8,128)(2,1)S(1)} %get-tuple-element.57), channel_id=1, source_target_pairs={{0,2},{2,0},{1,3},{3,1},{4,6},{6,4},{5,7},{7,5},{8,10},{10,8},{9,1... | collective-permute-start | bytes 1572872 | tf_op jit(solution)/shard_map/ppermute | solution.py:516
  31.9 1.0 copy-start.23
  32.9 6.4 %collective-permute-start.7 = (bf16[512,256]{1,0:T(8,128)(2,1)S(1)}, bf16[512,256]{1,0:T(8,128)(2,1)S(1)}, u32[]{:S(2)}, u32[]{:S(2)}) collective-permute-start(bf16[512,256]{1,0:T(8,128)(2,1)S(1)} %fusion), channel_id=1, source_target_pairs={{0,4},{1,5},{2,10},{3,11},{4,0},{5,1},{6,14},{7,15},{8,12},{9,13},... | collective-permute-start | bytes 786440 | tf_op jit(solution)/shard_map/ppermute | solution.py:536
  40.5 5.4 %collective-permute-start.8 = (bf16[256,256]{1,0:T(8,128)(2,1)S(1)}, bf16[256,256]{1,0:T(8,128)(2,1)S(1)}, u32[]{:S(2)}, u32[]{:S(2)}) collective-permute-start(bf16[256,256]{1,0:T(8,128)(2,1)S(1)} %fusion.1), channel_id=1, source_target_pairs={{0,1},{1,0},{2,6},{3,7},{4,5},{5,4},{6,2},{7,3},{8,9},{9,8},{10,14... | collective-permute-start | bytes 393224 | tf_op jit(solution)/shard_map/ppermute | solution.py:536
  42.0 1.4 %copy-start.12 = (bf16[768,1024]{1,0:T(8,128)(2,1)S(1)}, bf16[768,1024]{1,0:T(8,128)(2,1)}, u32[]{:S(2)}) copy-start(bf16[768,1024]{1,0:T(8,128)(2,1)} %copy-done.11) | copy-start | bytes 4718596
  43.4 3.1 %copy-start.10 = (bf16[768,1024]{1,0:T(8,128)(2,1)S(1)}, bf16[768,1024]{1,0:T(8,128)(2,1)}, u32[]{:S(2)}) copy-start(bf16[768,1024]{1,0:T(8,128)(2,1)} %copy-done.9) | copy-start | bytes 4718596
  43.4 3.1 %copy-start.14 = (f32[768,256]{1,0:T(8,128)S(1)}, f32[768,256]{1,0:T(8,128)}, u32[]{:S(2)}) copy-start(f32[768,256]{1,0:T(8,128)} %copy-done.13) | copy-start | bytes 2359300
  43.4 3.1 %copy-start.18 = (f32[768,128]{1,0:T(8,128)S(1)}, f32[768,128]{1,0:T(8,128)}, u32[]{:S(2)}) copy-start(f32[768,128]{1,0:T(8,128)} %copy-done.17) | copy-start | bytes 1179652
  45.9 4.3 %collective-permute-start.9 = (bf16[128,256]{1,0:T(8,128)(2,1)S(1)}, bf16[128,256]{1,0:T(8,128)(2,1)S(1)}, u32[]{:S(2)}, u32[]{:S(2)}) collective-permute-start(bf16[128,256]{1,0:T(8,128)(2,1)S(1)} %fusion.5), channel_id=1, source_target_pairs={{0,8},{1,9},{2,3},{3,2},{4,12},{5,13},{6,7},{7,6},{8,0},{9,1},{10,... | collective-permute-start | bytes 196616 | tf_op jit(solution)/shard_map/ppermute | solution.py:536
  46.6 5.9 %copy-start.16 = (f32[2,1216,128]{2,1,0:T(8,128)S(1)}, f32[2,1216,128]{2,1,0:T(8,128)}, u32[]{:S(2)}) copy-start(f32[2,1216,128]{2,1,0:T(8,128)} %copy-done.15) | copy-start | bytes 3735556
  50.3 5.7 %collective-permute-start.10 = (bf16[64,256]{1,0:T(8,128)(2,1)S(1)}, bf16[64,256]{1,0:T(8,128)(2,1)S(1)}, u32[]{:S(2)}, u32[]{:S(2)}) collective-permute-start(bf16[64,256]{1,0:T(8,128)(2,1)S(1)} %fusion.9), channel_id=1, source_target_pairs={{0,16},{1,17},{2,18},{3,19},{4,20},{5,21},{6,22},{7,23},{8,24},{9,... | collective-permute-start | bytes 98312 | tf_op jit(solution)/shard_map/ppermute | solution.py:536
  56.0 5.2 %collective-permute-start.11 = (bf16[128,256]{1,0:T(8,128)(2,1)S(1)}, bf16[128,256]{1,0:T(8,128)(2,1)S(1)}, u32[]{:S(2)}, u32[]{:S(2)}) collective-permute-start(bf16[128,256]{1,0:T(8,128)(2,1)S(1)} %pad_maximum_fusion.7), channel_id=1, source_target_pairs={{0,16},{1,17},{2,18},{3,19},{4,20},{5,21},{6,22},{7,23},{8,24},{9,... | collective-permute-start | bytes 196616 | tf_op jit(solution)/shard_map/ppermute | solution.py:536
  61.3 4.7 %collective-permute-start.12 = (bf16[192,256]{1,0:T(8,128)(2,1)S(1)}, bf16[192,256]{1,0:T(8,128)(2,1)S(1)}, u32[]{:S(2)}, u32[]{:S(2)}) collective-permute-start(bf16[192,256]{1,0:T(8,128)(2,1)S(1)} %pad_maximum_fusion.6), channel_id=1, source_target_pairs={{0,8},{1,9},{2,3},{3,2},{4,12},{5,13},{6,7},{7,6},{8,0},{9,1},{10,... | collective-permute-start | bytes 294920 | tf_op jit(solution)/shard_map/ppermute | solution.py:536
  66.1 5.4 %collective-permute-start.13 = (bf16[320,256]{1,0:T(8,128)(2,1)S(1)}, bf16[320,256]{1,0:T(8,128)(2,1)S(1)}, u32[]{:S(2)}, u32[]{:S(2)}) collective-permute-start(bf16[320,256]{1,0:T(8,128)(2,1)S(1)} %pad_maximum_fusion.4), channel_id=1, source_target_pairs={{0,1},{1,0},{2,6},{3,7},{4,5},{5,4},{6,2},{7,3},{8,9},{9,8},{10,14... | collective-permute-start | bytes 491528 | tf_op jit(solution)/shard_map/ppermute | solution.py:536
  71.6 6.8 %collective-permute-start.14 = (bf16[576,256]{1,0:T(8,128)(2,1)S(1)}, bf16[576,256]{1,0:T(8,128)(2,1)S(1)}, u32[]{:S(2)}, u32[]{:S(2)}) collective-permute-start(bf16[576,256]{1,0:T(8,128)(2,1)S(1)} %pad_maximum_fusion.2), channel_id=1, source_target_pairs={{0,4},{1,5},{2,10},{3,11},{4,0},{5,1},{6,14},{7,15},{8,12},{9,13},... | collective-permute-start | bytes 884744 | tf_op jit(solution)/shard_map/ppermute | solution.py:536
  78.6 19.8 %collective-permute-start.15 = (bf16[1152,256]{1,0:T(8,128)(2,1)S(1)}, bf16[1152,256]{1,0:T(8,128)(2,1)S(1)}, u32[]{:S(2)}, u32[]{:S(2)}) collective-permute-start(bf16[1152,256]{1,0:T(8,128)(2,1)S(1)} %pad_maximum_fusion), channel_id=1, source_target_pairs={{0,2},{2,0},{1,3},{3,1},{4,6},{6,4},{5,7},{7,5},{8,10},{10,8},{9,1... | collective-permute-start | bytes 1769480 | tf_op jit(solution)/shard_map/ppermute | solution.py:516
  82.7 8.3 %collective-permute-start.3 = (bf16[192,256]{1,0:T(8,128)(2,1)S(1)}, bf16[192,256]{1,0:T(8,128)(2,1)S(1)}, u32[]{:S(2)}, u32[]{:S(2)}) collective-permute-start(bf16[192,256]{1,0:T(8,128)(2,1)S(1)} %get-tuple-element.52), channel_id=1, source_target_pairs={{0,16},{2,18},{4,20},{6,22},{8,24},{10,26},{12,28},{14,30},{30,14}... | collective-permute-start | bytes 294920 | tf_op jit(solution)/shard_map/ppermute | solution.py:512
  91.6 1.3 %collective-permute-start.4 = (bf16[48,256]{1,0:T(8,128)(2,1)S(1)}, bf16[48,256]{1,0:T(8,128)(2,1)S(1)}, u32[]{:S(2)}, u32[]{:S(2)}) collective-permute-start(bf16[48,256]{1,0:T(8,128)(2,1)S(1)} %get-tuple-element.54), channel_id=1, source_target_pairs={{0,2},{2,0},{4,6},{6,4},{8,10},{10,8},{12,14},{14,12},{30,28},{28,... | collective-permute-start | bytes 73736 | tf_op jit(solution)/shard_map/ppermute | solution.py:512
  91.7 4.8 %collective-permute-start.5 = (bf16[48,256]{1,0:T(8,128)(2,1)S(1)}, bf16[48,256]{1,0:T(8,128)(2,1)S(1)}, u32[]{:S(2)}, u32[]{:S(2)}) collective-permute-start(bf16[48,256]{1,0:T(8,128)(2,1)S(1)} %get-tuple-element.55), channel_id=1, source_target_pairs={{0,16},{2,4},{4,2},{6,8},{8,6},{10,12},{12,10},{14,30},{30,14},{28... | collective-permute-start | bytes 73736 | tf_op jit(solution)/shard_map/ppermute | solution.py:512
where the time goes:
time: 100 us
  waiting for transfers between devices  41 us (41%)
  Pallas kernels  26.7 us (27%)
  starting transfers between devices  17.3 us (17%)
  local copies, waits for them, and re-layouts  10.5 us (10%)
  other arithmetic  2.81 us (3%)
  between operations  1.74 us (2%)
    pallas_call x12, Pallas kernels, call(): pl.pallas_call(kernel, out_shape=[jax.ShapeDtypeStruct(*out) for out in o...  26.7 us
    ppermute x8, waiting for transfers between devices, bit_swap(): return lax.ppermute(block, ('chips', 'core', 'dp'), pairs)  25.6 us
    ppermute x6, waiting for transfers between devices, swap(): return lax.ppermute(block, TILES, pairs_of(kind))  13.3 us
    unnamed x50, local copies, waits for them, and re-layouts  10.4 us
    ppermute x8, starting transfers between devices, bit_swap(): return lax.ppermute(block, ('chips', 'core', 'dp'), pairs)  10 us
    ppermute x6, starting transfers between devices, swap(): return lax.ppermute(block, TILES, pairs_of(kind))  7.21 us
    ppermute x2, waiting for transfers between devices, core_swap(): return lax.ppermute(block, 'core', [(0, 1), (1, 0)])  2.04 us
  transfers between devices with their start and end apart: 16, of which 11 were waited for; matrix products, arithmetic and copies ran while one was open for 0% of the time, Pallas kernels for 19%

commit v1 on v0

--- a/solution.py
+++ b/solution.py
@@ -93,30 +93,21 @@
     return jnp.where(to + frm == used + 2 * LEFT - 1, 1.0, 0.0).astype(BF16)
 
 
-def prep_kernel(shape, count_hbm, ocean_hbm, fields_hbm, first, second, count, ocean, fields, work, sems):
-    fetch = Fetch(sems, (fields_hbm, fields), (count_hbm, count), (ocean_hbm, ocean))
-    fetch.wait(0, 1, 2)
-    owned = count[0]
-    per_slot = TILE * TILE
-    for slot in range(shape.slots):
-        flag = slot_flag(count, ocean, slot)
-        cells = fields[pl.ds(slot * per_slot, per_slot), :].astype(F32) * flag
-        for part in range(shape.parts):
-            work[part, pl.ds(slot * per_slot, per_slot), :] = cells[:, shape.lanes(part)]
+def prep_kernel(shape, count_hbm, fields, first, second, count, work, sems):
+    fetch = Fetch(sems, (count_hbm, count))
+    for part in range(shape.parts):
+        work[part] = fields[:, shape.lanes(part)].astype(F32)
     left = edge_planes(shape, work, 0, TILE)
-    right = edge_planes(shape, work, (owned - 1) * per_slot + TILE - HALF, TILE)
+    fetch.wait(0)
+    right = edge_planes(shape, work, (count[0] - 1) * TILE * TILE + TILE - HALF, TILE)
     send_edges(shape, left, right, first, second)
 
 
 def cotangent_kernel(
-    shape, count_hbm, ocean_hbm, tangent_hbm, scale_hbm, w_out_hbm,
-    dproj, dproj_t, dact,
-    count, ocean, tangent, scale, w_out, sems,
+    shape, count_hbm, ocean_hbm, tangent, scale, dproj, dproj_t, count, ocean, sems
 ):
-    fetch = Fetch(
-        sems, (tangent_hbm, tangent), (count_hbm, count), (ocean_hbm, ocean), (scale_hbm, scale), (w_out_hbm, w_out)
-    )
-    fetch.wait(0, 1, 2, 3)
+    fetch = Fetch(sems, (count_hbm, count), (ocean_hbm, ocean))
+    fetch.wait(0, 1)
     per_slot = TILE * TILE
     for slot in range(shape.slots):
         rows = pl.ds(slot * per_slot, per_slot)
@@ -124,16 +115,10 @@
         scaled = (tangent[rows, :].astype(F32) * (scale[...] * flag)).astype(BF16)
         dproj[rows, :] = scaled
         dproj_t[:, slot * per_slot : (slot + 1) * per_slot] = scaled.T
-    fetch.wait(4)
-    for slot in range(shape.slots):
-        rows = pl.ds(slot * per_slot, per_slot)
-        for h in range(shape.hidden // shape.channels):
-            cols = slice(h * shape.channels, (h + 1) * shape.channels)
-            dact[rows, cols] = dot(dproj[rows, :], w_out[cols, :], 1, 1)
-
-
-def band_kernel(shape, count_hbm, ocean_hbm, fields_hbm, first, second, band, fold, count, ocean, fields, sems):
-    fetch = Fetch(sems, (fields_hbm, fields), (count_hbm, count), (ocean_hbm, ocean))
+
+
+def band_kernel(shape, count_hbm, ocean_hbm, fields, first, second, band, fold, count, ocean, sems):
+    fetch = Fetch(sems, (count_hbm, count), (ocean_hbm, ocean))
     even = is_even()
     blank = jnp.zeros((LEFT, LANES), F32)
     per_slot = TILE * TILE
@@ -143,7 +128,7 @@
             base = (row + HALF) * shape.pitch
             band[part, pl.ds(base, LEFT), :] = blank
             band[part, pl.ds(base + LEFT + shape.columns, LEFT), :] = blank
-    fetch.wait(0, 1, 2)
+    fetch.wait(0, 1)
     used = count[0] * TILE
     flags = [slot_flag(count, ocean, slot) for slot in range(shape.slots)]
     top = HALF * shape.pitch
@@ -180,10 +165,12 @@
 
 
 def spread_taps(shape, kernel, taps):
-    for part in range(shape.parts):
-        for tap in range(KSIZE * KSIZE):
-            row = kernel[pl.ds(tap, 1), shape.lanes(part)].astype(F32)
-            taps[part, tap] = jnp.broadcast_to(row, (8, LANES))
+    for above in range(KSIZE):
+        rows = kernel[above].astype(F32)
+        for part in range(shape.parts):
+            for shift in range(KSIZE):
+                row = rows[shift : shift + 1, shape.lanes(part)]
+                taps[part, above * KSIZE + shift] = jnp.broadcast_to(row, (8, LANES))
 
 
 def convolve(shape, rows, padded, taps, convolved):
@@ -242,23 +229,26 @@
 
 
 def early_kernel(
-    shape, taps_hbm, gain_hbm, band,
-    normed, yhat, inverse,
-    kernel, gain, taps, convolved, sems,
+    shape, kernel, gain, w_out, band, dproj,
+    normed, yhat, inverse, dact,
+    taps, convolved,
 ):
-    fetch = Fetch(sems, (taps_hbm, kernel), (gain_hbm, gain))
-    fetch.wait(0, 1)
     spread_taps(shape, kernel, taps)
     convolve(shape, shape.early, band, taps, convolved)
     normalise(shape, shape.early, 0, convolved, gain, normed, yhat, inverse)
+    per_slot = TILE * TILE
+    for slot in range(shape.slots):
+        rows = pl.ds(slot * per_slot, per_slot)
+        for h in range(shape.hidden // shape.channels):
+            cols = slice(h * shape.channels, (h + 1) * shape.channels)
+            dact[rows, cols] = dot(dproj[rows, :], w_out[cols, :], 1, 1)
 
 
 def late_kernel(
-    shape, taps_hbm, gain_hbm, w_in_hbm, band, fold, normed_in, yhat_in, inverse_in, dproj_t, dact,
+    shape, kernel, gain, w_in, band, fold, normed_in, yhat_in, inverse_in, dproj_t, dact,
     keep, give, activated, dpreact, yhat, inverse,
-    kernel, gain, w_in, taps, padded, convolved, normed, normed_t, sems,
+    taps, padded, convolved, normed, normed_t,
 ):
-    fetch = Fetch(sems, (taps_hbm, kernel), (gain_hbm, gain), (w_in_hbm, w_in))
     late = TILE - shape.early
     kept = late + HALF
     for part in range(shape.parts):
@@ -271,14 +261,12 @@
         normed[rows, :] = normed_in[rows, :]
         yhat[rows, :] = yhat_in[rows, :]
         inverse[rows, :] = inverse_in[rows, :]
-    fetch.wait(0, 1)
     spread_taps(shape, kernel, taps)
     convolve(shape, late, padded, taps, convolved)
     normalise(shape, late, shape.early, convolved, gain, normed, yhat, inverse)
     per_slot = TILE * TILE
     for slot in range(shape.slots):
         normed_t[:, slot * per_slot : (slot + 1) * per_slot] = normed[pl.ds(slot * per_slot, per_slot), :].T
-    fetch.wait(2)
     keeps_in = lax.axis_index("core") == 0
     block = shape.channels
     for h in range(shape.hidden // block):
@@ -304,9 +292,7 @@
     return jnp.sum(value.reshape(-1, 8, value.shape[-1]), axis=0)
 
 
-def norm_grad_kernel(shape, w_in_hbm, gain_hbm, dpreact, yhat, inverse, conv_grad, gain_part, w_in, gain, sems):
-    fetch = Fetch(sems, (w_in_hbm, w_in), (gain_hbm, gain))
-    fetch.wait(0, 1)
+def norm_grad_kernel(shape, w_in, gain, dpreact, yhat, inverse, conv_grad, gain_part):
     chunk = TILE * TILE
     total = jnp.zeros((8, shape.channels), F32)
     for slot in range(shape.slots):
@@ -323,15 +309,12 @@
 
 
 def state_kernel(
-    shape, count_hbm, ocean_hbm, fields_hbm, tangent_hbm, w_out_hbm, scale_hbm, activated,
+    shape, count_hbm, ocean_hbm, fields, tangent, w_out, scale, activated,
     state, scale_part,
-    count, ocean, fields, tangent, w_out, scale, sems,
+    count, ocean, sems,
 ):
-    fetch = Fetch(
-        sems, (w_out_hbm, w_out), (fields_hbm, fields), (tangent_hbm, tangent),
-        (scale_hbm, scale), (count_hbm, count), (ocean_hbm, ocean),
-    )
-    fetch.wait(0, 1, 2, 3, 4, 5)
+    fetch = Fetch(sems, (count_hbm, count), (ocean_hbm, ocean))
+    fetch.wait(0, 1)
     chunk = TILE * TILE
     total = jnp.zeros((8, shape.channels), F32)
     for slot in range(shape.slots):
@@ -393,15 +376,15 @@
                 )
 
 
-def back_kernel(shape, count_hbm, taps_hbm, conv_grad, core_grad, fold, count, kernel, spaced, taps, sems):
-    fetch = Fetch(sems, (count_hbm, count), (taps_hbm, kernel))
+def back_kernel(shape, count_hbm, kernel, conv_grad, core_grad, fold, count, spaced, taps, sems):
+    fetch = Fetch(sems, (count_hbm, count))
     place_grad(shape, conv_grad, spaced)
     blank = jnp.zeros((LEFT, LANES), F32)
     for part in range(shape.parts):
         for row in range(TILE + HALF):
             core_grad[part, pl.ds(row * shape.pitch, LEFT), :] = blank
             core_grad[part, pl.ds((row + 1) * shape.pitch - LEFT, LEFT), :] = blank
-    fetch.wait(0, 1)
+    fetch.wait(0)
     spread_taps(shape, kernel, taps)
     run = -(-(shape.columns + 2 * HALF) // 8)
 
@@ -452,14 +435,15 @@
 
 
 def final_kernel(
-    shape, count_hbm, ocean_hbm, tangent_hbm, folded, first, second,
-    grad_fields,
-    count, ocean, tangent, work, sems,
+    shape, count_hbm, ocean_hbm, tangent, folded, first, second,
+    grad_fields, done,
+    count, ocean, work, sems,
 ):
-    fetch = Fetch(sems, (tangent_hbm, tangent), (count_hbm, count), (ocean_hbm, ocean))
+    fetch = Fetch(sems, (count_hbm, count), (ocean_hbm, ocean))
     even = is_even()
+    done[...] = jnp.zeros_like(done)
     work[...] = folded[...]
-    fetch.wait(0, 1, 2)
+    fetch.wait(0, 1)
     used = count[0] * TILE
     for part in range(shape.parts):
         for col in range(HALF):
@@ -481,19 +465,24 @@
                 grad_fields[rows, shape.lanes(part)] = (flag * total).astype(BF16)
 
 
-def unpack_kernel(norm, own, other, small, w_in, w_out, kernel_sum, gain_sum, scale_sum):
+def unpack_kernel(norm, own, came, w_in, w_out, kernel_sum, gain_sum, scale_sum):
     is_first = lax.axis_index("core") == 0
     channels = own.shape[-1]
-    for h in range(w_out.shape[0] // channels):
+    hidden = w_out.shape[0]
+    for h in range(hidden // channels):
         rows = slice(h * channels, (h + 1) * channels)
         mine = own[rows, :].astype(F32) * norm
-        theirs = other[rows, :].astype(F32) * norm
+        theirs = came[rows, :].astype(F32) * norm
         w_in[:, rows] = jnp.where(is_first, mine, theirs)
         w_out[rows, :] = jnp.where(is_first, theirs, mine).T
+    extra = (own.shape[0] - hidden) // 2
+    high, low = pl.ds(hidden, extra), pl.ds(hidden + extra, extra)
+    small = own[high, :].astype(F32) + own[low, :].astype(F32)
+    small = (small + (came[high, :].astype(F32) + came[low, :].astype(F32))) * norm
     for above in range(KSIZE):
-        kernel_sum[above] = small[pl.ds(above * KSIZE, KSIZE), :] * norm
-    gain_sum[...] = small[pl.ds(KSIZE * KSIZE, 1), :] * norm
-    scale_sum[...] = small[pl.ds(KSIZE * KSIZE + 1, 1), :] * norm
+        kernel_sum[above] = small[above * KSIZE : (above + 1) * KSIZE, :]
+    gain_sum[...] = small[KSIZE * KSIZE : KSIZE * KSIZE + 1, :]
+    scale_sum[...] = small[KSIZE * KSIZE + 1 : KSIZE * KSIZE + 2, :]
 
 
 def pairs_of(kind):
@@ -543,49 +532,74 @@
     return jnp.where(lax.axis_index("core") == 0, bits[0], bits[1])
 
 
-def halved(keep, give):
-    mine = keep + core_swap(give).astype(F32)
-    for stage in stages():
+def half_rows(bit, rows):
+    return pl.ds(pl.multiple_of(bit * rows, rows), rows)
+
+
+def join_kernel(stage, keep, came, mine, send):
+    rows = send.shape[0]
+    mine[...] = keep[...] + came[...].astype(F32)
+    send[...] = mine[half_rows(1 - bit_here(stage), rows), :].astype(BF16)
+
+
+def halve_kernel(stage, following, whole, came, mine, send):
+    rows = mine.shape[0]
+    mine[...] = whole[half_rows(bit_here(stage), rows), :] + came[...].astype(F32)
+    send[...] = mine[half_rows(1 - bit_here(following), rows // 2), :].astype(BF16)
+
+
+def turn_kernel(stage, whole, came, small, payload):
+    rows = came.shape[0]
+    share = whole[half_rows(bit_here(stage), rows), :] + came[...].astype(F32)
+    payload[pl.ds(0, rows), :] = share.astype(BF16)
+    payload[pl.ds(rows, small.shape[0]), :] = small[...].astype(BF16)
+
+
+def double_kernel(stage, extra, own, came, payload):
+    rows = own.shape[0] - extra
+    bit = bit_here(stage)
+    payload[half_rows(bit, rows), :] = own[pl.ds(0, rows), :]
+    payload[half_rows(1 - bit, rows), :] = came[pl.ds(0, rows), :]
+    total = own[pl.ds(rows, extra), :].astype(F32) + came[pl.ds(rows, extra), :].astype(F32)
+    high = total.astype(BF16)
+    payload[pl.ds(2 * rows, extra), :] = high
+    if payload.shape[0] > 2 * rows + extra:
+        payload[pl.ds(2 * rows + extra, extra), :] = (total - high.astype(F32)).astype(BF16)
+
+
+def halved(mine, send, order):
+    for at, stage in enumerate(order[:-1]):
+        came = bit_swap(send, stage)
+        rows = came.shape[0]
         bit = bit_here(stage)
-        halves = mine.reshape(2, -1, mine.shape[-1])
+        mine = lax.dynamic_index_in_dim(mine.reshape(2, rows, -1), bit, 0, keepdims=False) + came.astype(F32)
+        bit = bit_here(order[at + 1])
+        halves = mine.reshape(2, rows // 2, -1)
         send = lax.dynamic_index_in_dim(halves, 1 - bit, 0, keepdims=False).astype(BF16)
-        mine = lax.dynamic_index_in_dim(halves, bit, 0, keepdims=False) + bit_swap(send, stage).astype(F32)
-    return mine.astype(BF16)
-
-
-def doubled(mine, small):
-    for stage in reversed(stages()):
-        rows = mine.shape[0]
-        rounded = small.astype(BF16)
-        came = bit_swap(jnp.concatenate([mine, rounded]), stage)
-        first = bit_here(stage) == 0
-        other = came[:rows]
-        mine = jnp.concatenate([jnp.where(first, mine, other), jnp.where(first, other, mine)])
-        small = lax.reduce_precision(small, 8, 7) + came[rows:].astype(F32)
-    rows = mine.shape[0]
-    high = lax.reduce_precision(small, 8, 7)
-    low = lax.reduce_precision(small - high, 8, 7)
-    came = core_swap(jnp.concatenate([mine, high.astype(BF16), low.astype(BF16)]))
-    extra = came[rows:].astype(F32).reshape(2, -1, small.shape[-1])
-    small = (high + low) + (extra[0] + extra[1])
-    return mine, came[:rows], small
-
-
-def call(kernel, outs, scratch, hbm, vmem, copies=0, micros=1.0):
+    return mine, send
+
+
+def call(kernel, outs, scratch, hbm, vmem, copies=0, micros=1.0, after=(), limit=20):
     in_specs = [pl.BlockSpec(memory_space=pl.ANY)] * len(hbm)
     in_specs += [pl.BlockSpec(memory_space=pltpu.VMEM)] * len(vmem)
+    in_specs += [pl.BlockSpec(memory_space=pl.ANY)] * len(after)
     shapes = [pltpu.SMEM(*one) if one[1] == jnp.int32 else pltpu.VMEM(*one) for one in scratch]
     if copies:
         shapes.append(pltpu.SemaphoreType.DMA((copies,)))
+    taken = len(hbm) + len(vmem)
+
+    def body(*refs):
+        kernel(*refs[:taken], *refs[taken + len(after) :])
+
     return pl.pallas_call(
-        kernel,
+        body,
         out_shape=[jax.ShapeDtypeStruct(*out) for out in outs],
         in_specs=in_specs,
         out_specs=[pl.BlockSpec(memory_space=pltpu.VMEM)] * len(outs),
         scratch_shapes=shapes,
         cost_estimate=pl.CostEstimate(flops=int(micros * 1e9), bytes_accessed=0, transcendentals=0),
-        compiler_params=pltpu.CompilerParams(vmem_limit_bytes=24 * 1024 * 1024),
-    )(*hbm, *vmem)
+        compiler_params=pltpu.CompilerParams(vmem_limit_bytes=limit * 1024 * 1024),
+    )(*hbm, *vmem, *after)
 
 
 def shards(fields, grad_out, block_count, ocean, kernel, ln_gain, w_in, w_out, layer_scale):
@@ -596,7 +610,7 @@
     grid = fields.shape
     fields = fields.reshape(cells, channels)
     tangent = grad_out.reshape(cells, channels)
-    taps_in = kernel.reshape(KSIZE * KSIZE, channels)
+    taps_in = kernel
     gain = ln_gain.reshape(1, channels)
     scale = layer_scale.reshape(1, channels)
 
@@ -615,76 +629,125 @@
     row = ((1, channels), F32)
     eight = ((8, channels), F32)
     taps = ((parts, KSIZE * KSIZE, 8, LANES), F32)
-    taps_raw = (taps_in.shape, BF16)
     count_s = (block_count.shape, jnp.int32)
     ocean_s = (ocean.shape, jnp.int32)
-    w_in_s = (w_in.shape, BF16)
-    w_out_s = (w_out.shape, BF16)
     flat = ((channels, cells), BF16)
     late = TILE - shape.early
 
     first, second = call(
-        bind(prep_kernel), [edge, edge], [count_s, ocean_s, whole, ((parts, cells, LANES), F32)],
-        [block_count, ocean, fields], [], 3, 1.5,
+        bind(prep_kernel), [edge, edge], [count_s, ((parts, cells, LANES), F32)],
+        [block_count], [fields], 1, 1.0,
+    )
+    dproj, dproj_t = call(
+        bind(cotangent_kernel), [whole, flat], [count_s, ocean_s],
+        [block_count, ocean], [tangent, scale], 2, 1.0, after=[first],
     )
     first, second = swap(first, "first"), swap(second, "second")
-    dproj, dproj_t, dact = call(
-        bind(cotangent_kernel), [whole, flat, ((cells, hidden), F32)],
-        [count_s, ocean_s, whole, row, w_out_s],
-        [block_count, ocean, tangent, scale, w_out], [], 5, 2.5,
-    )
     band, fold = call(
-        bind(band_kernel), [strip(TILE + HALF), turned], [count_s, ocean_s, whole],
-        [block_count, ocean, fields], [first, second], 3, 1.0,
+        bind(band_kernel), [strip(TILE + HALF), turned], [count_s, ocean_s],
+        [block_count, ocean], [fields, first, second], 2, 1.0, after=[dproj],
     )
     fold = swap(fold, "fold")
-    normed, yhat, inverse = call(
-        bind(early_kernel), [whole, whole_f, narrow],
-        [taps_raw, row, taps, ((parts, shape.early * shape.columns, LANES), F32)],
-        [taps_in, gain], [band], 2, 4.0,
+    normed, yhat, inverse, dact = call(
+        bind(early_kernel), [whole, whole_f, narrow, ((cells, hidden), F32)],
+        [taps, ((parts, shape.early * shape.columns, LANES), F32)],
+        [], [taps_in, gain, w_out, band, dproj], 0, 4.5,
     )
     keep, give, activated, dpreact, yhat, inverse = call(
         bind(late_kernel),
         [((hidden, channels), F32), ((hidden, channels), BF16), wide, wide, whole_f, narrow],
         [
-            taps_raw, row, w_in_s, taps, strip(late + 2 * HALF),
-            ((parts, late * shape.columns, LANES), F32), whole, flat,
+            taps, strip(late + 2 * HALF), ((parts, late * shape.columns, LANES), F32), whole, flat,
         ],
-        [taps_in, gain, w_in], [band, fold, normed, yhat, inverse, dproj_t, dact], 3, 6.0,
-    )
+        [], [taps_in, gain, w_in, band, fold, normed, yhat, inverse, dproj_t, dact], 0, 5.0,
+    )
+
+    order = stages()
+    rows = hidden // 2
+
+    def half_step(at, rows):
+        return functools.partial(halve_kernel, order[at], order[at + 1]), [
+            ((rows, channels), F32), ((rows // 2, channels), BF16),
+        ]
+
+    came = core_swap(give)
     conv_grad, gain_part = call(
-        bind(norm_grad_kernel), [whole, eight], [w_in_s, row], [w_in, gain], [dpreact, yhat, inverse], 2, 1.5,
-    )
-    mine = halved(keep, give)
+        bind(norm_grad_kernel), [whole, eight], [], [], [w_in, gain, dpreact, yhat, inverse], 0, 1.0,
+    )
+    mine, send = call(
+        functools.partial(join_kernel, order[0]),
+        [((hidden, channels), F32), ((rows, channels), BF16)], [], [], [keep, came], after=[conv_grad], micros=0.3,
+    )
+    came = bit_swap(send, order[0])
     core_grad, fold_back = call(
-        bind(back_kernel), [strip(TILE + HALF), turned],
-        [count_s, taps_raw, strip(TILE), taps],
-        [block_count, taps_in], [conv_grad], 2, 4.0,
-    )
+        bind(back_kernel), [strip(TILE + HALF), turned], [count_s, strip(TILE), taps],
+        [block_count], [taps_in, conv_grad], 1, 4.0, after=[send],
+    )
+    body, outs = half_step(0, rows)
+    mine, send = call(body, outs, [], [], [mine, came], after=[fold_back], micros=0.3)
+    came = bit_swap(send, order[1])
     fold_back = swap(fold_back, "fold")
     state, scale_part = call(
-        bind(state_kernel), [whole, eight], [count_s, ocean_s, whole, whole, w_out_s, row],
-        [block_count, ocean, fields, tangent, w_out, scale], [activated], 6, 1.5,
-    )
+        bind(state_kernel), [whole, eight], [count_s, ocean_s],
+        [block_count, ocean], [fields, tangent, w_out, scale, activated], 2, 1.5, after=[send],
+    )
+    rows //= 2
+    body, outs = half_step(1, rows)
+    mine, send = call(body, outs, [], [], [mine, came], after=[scale_part], micros=0.3)
+    came = bit_swap(send, order[2])
     small_rows = -(-(KSIZE * KSIZE + 2) // 16) * 16
     (small,) = call(
         bind(taps_kernel), [((small_rows, channels), F32)], [strip(TILE + 2 * HALF), strip(TILE)],
-        [], [band, fold, conv_grad, gain_part, scale_part], 0, 3.5,
-    )
+        [], [band, fold, conv_grad, gain_part, scale_part], 0, 3.5, after=[send],
+    )
+    rows //= 2
+    body, outs = half_step(2, rows)
+    mine, send = call(body, outs, [], [], [mine, came], after=[small], micros=0.3)
+    mine, send = halved(mine, send, order[3:])
+    came = bit_swap(send, order[-1])
     folded, first, second = call(
         bind(rims_kernel), [strip(TILE), edge, edge], [count_s], [block_count], [core_grad, fold_back], 1, 1.0,
-    )
+        after=[send],
+    )
+    rows = came.shape[0]
+    if rows % 16 == 0:
+        (payload,) = call(
+            functools.partial(turn_kernel, order[-1]), [((rows + small_rows, channels), BF16)],
+            [], [], [mine, came, small], after=[first], micros=0.3,
+        )
+    else:
+        bit = bit_here(order[-1])
+        share = lax.dynamic_index_in_dim(mine.reshape(2, rows, channels), bit, 0, keepdims=False)
+        payload = jnp.concatenate([share + came.astype(F32), small]).astype(BF16)
+    came = bit_swap(payload, order[-1])
     first, second = swap(first, "first"), swap(second, "second")
-    (grad_fields,) = call(
-        bind(final_kernel), [whole], [count_s, ocean_s, whole, strip(TILE)],
-        [block_count, ocean, tangent], [folded, first, second], 3, 1.5,
-    )
-    own, other, small = doubled(mine, small)
+    grad_fields, done = call(
+        bind(final_kernel), [whole, ((8, LANES), F32)], [count_s, ocean_s, strip(TILE)],
+        [block_count, ocean], [tangent, folded, first, second], 2, 1.5, after=[payload],
+    )
+    after = [done]
+    for at in reversed(range(len(order))):
+        copies = 2 if at == 0 else 1
+        if rows % 16 == 0:
+            (payload,) = call(
+                functools.partial(double_kernel, order[at], small_rows),
+                [((2 * rows + copies * small_rows, channels), BF16)],
+                [], [], [payload, came], after=after, micros=0.3,
+            )
+        else:
+            first = bit_here(order[at]) == 0
+            low, high = payload[:rows], came[:rows]
+            small = payload[rows:].astype(F32) + came[rows:].astype(F32)
+            joined = [jnp.where(first, low, high), jnp.where(first, high, low), small.astype(BF16)]
+            payload = jnp.concatenate(joined)
+        after = []
+        rows *= 2
+        came = bit_swap(payload, order[at - 1]) if at else core_swap(payload)
     total = samples * lax.axis_size("dp") * slots * lax.axis_size(TILES) * tile_rows * tile_cols
     w_in_sum, w_out_sum, kernel_sum, gain_sum, scale_sum = call(
         functools.partial(unpack_kernel, total ** (-0.5)),
         [((channels, hidden), F32), ((hidden, channels), F32), (kernel.shape, F32), row, row],
-        [], [], [own, other, small], 0, 1.5,
+        [], [], [payload, came], 0, 1.5,
     )
     return (
         state.reshape(grid),

time: 100 us -> 73.5 us (0.73)
  waiting for transfers between devices: 41 us -> 27 us
  local copies, waits for them, and re-layouts: 10.5 us -> 1.03 us
  other arithmetic: 2.81 us -> 0 us
  Pallas kernels: 26.7 us -> 25.2 us
  starting transfers between devices: 17.3 us -> 18.6 us
    ppermute x6, waiting for transfers between devices: 13.3 us -> 1.95 us  [swap(): return lax.ppermute(block, TILES, pairs_of(kind))]
    unnamed x50 -> x18, local copies, waits for them, and re-layouts: 10.4 us -> 1.03 us
    ppermute x8, waiting for transfers between devices: 25.6 us -> 21.9 us  [bit_swap(): return lax.ppermute(block, ('chips', 'core', 'dp'), pairs)]
    ppermute x6, starting transfers between devices: 7.21 us -> 10.3 us  [swap(): return lax.ppermute(block, TILES, pairs_of(kind))]
    add x5 -> x0, other arithmetic: 2.37 us -> none  [the longest x1 1.21 us: halved(): mine = keep + core_swap(give).astype(F32)]
    ppermute x8, starting transfers between devices: 10 us -> 8.15 us  [bit_swap(): return lax.ppermute(block, ('chips', 'core', 'dp'), pairs)]
    pallas_call x12 -> x21, Pallas kernels: 26.7 us -> 25.2 us  [call(): pl.pallas_call(body, out_shape=[jax.ShapeDtypeStruct(*out) for out in out...]
    ppermute x2, waiting for transfers between devices: 2.04 us -> 3.11 us  [core_swap(): return lax.ppermute(block, 'core', [(0, 1), (1, 0)])]
  transfers between devices with their start and end apart: 16 -> 16, of which waited for: 11 -> 12; matrix products, arithmetic and copies ran while one was open for 0% -> 0% of each run, Pallas kernels for 19% -> 24%
where the time goes in v1:
time: 73.5 us; the launch traced here: 73.4 us
  waiting for transfers between devices  27 us (37%)
  Pallas kernels  25.2 us (34%)
  starting transfers between devices  18.6 us (25%)
  between operations  1.51 us (2%)
  local copies, waits for them, and re-layouts  1.03 us (1%)
    pallas_call x21, Pallas kernels, call(): pl.pallas_call(body, out_shape=[jax.ShapeDtypeStruct(*out) for out in out...  25.2 us
    ppermute x8, waiting for transfers between devices, bit_swap(): return lax.ppermute(block, ('chips', 'core', 'dp'), pairs)  21.9 us
    ppermute x6, starting transfers between devices, swap(): return lax.ppermute(block, TILES, pairs_of(kind))  10.3 us
    ppermute x8, starting transfers between devices, bit_swap(): return lax.ppermute(block, ('chips', 'core', 'dp'), pairs)  8.15 us
    ppermute x2, waiting for transfers between devices, core_swap(): return lax.ppermute(block, 'core', [(0, 1), (1, 0)])  3.11 us
    ppermute x6, waiting for transfers between devices, swap(): return lax.ppermute(block, TILES, pairs_of(kind))  1.95 us
  transfers between devices with their start and end apart: 16, of which 12 were waited for; matrix products, arithmetic and copies ran while one was open for 0% of the time, Pallas kernels for 24%

profile of v1, /device:TPU:0, one launch (start us, length us, event | category | flops | bytes accessed | tf_op | source)
XLA Modules:
  0.0 73.4 jit_solution(17071760830196923041)
XLA Ops:
  1.3 0.0 copy-start.2
  1.3 1.0 %copy-done.2 = bf16[1,3,16,16,256]{4,3,2,1,0:T(8,128)(2,1)S(1)} copy-done((bf16[1,3,16,16,256]{4,3,2,1,0:T(8,128)(2,1)S(1)}, bf16[1,3,16,16,256]{4,3,2,1,0:T(8,128)(2,1)}, u32[]{:S(2)}) %copy-start.2) | copy-done | bytes 393240
  2.3 0.6 shard_map.144
  2.9 4.1 %collective-permute-start.1 = (bf16[48,256]{1,0:T(8,128)(2,1)S(1)}, bf16[48,256]{1,0:T(8,128)(2,1)S(1)}, u32[]{:S(2)}, u32[]{:S(2)}) collective-permute-start(bf16[48,256]{1,0:T(8,128)(2,1)S(1)} %get-tuple-element.48), channel_id=1, source_target_pairs={{0,16},{2,4},{4,2},{6,8},{8,6},{10,12},{12,10},{14,30},{30,14},{28... | collective-permute-start | bytes 73736 | tf_op jit(solution)/shard_map/ppermute | solution.py:501
  7.0 0.0 collective-permute-start
  7.0 0.0 copy-start.3
  7.0 0.7 %shard_map.145 = (bf16[768,256]{1,0:T(8,128)(2,1)S(1)}, bf16[256,768]{1,0:T(8,128)(2,1)S(1)}) custom-call(s32[1]{0:T(128)S(6)} %copy.16.refs_0_, s32[3]{0:T(128)S(1)} %copy-done.8, bf16[768,256]{1,0:T(8,128)(2,1)S(1)} %bitcast.11, f32[1,256]{1,0:T(1,128)S(1)} %bitcast.17, bf16[48,256]{1,0:T(8,128)(2,1)S(1)} %get-tuple-element.47.refs_4_), custom_call_target="tpu_custom_call" | custom-call | flops 1000000000 | tf_op jit(solution)/shard_map/pallas_call | solution.py:594
  7.8 1.1 %collective-permute-done.1.refs_4_ = bf16[48,256]{1,0:T(8,128)(2,1)S(1)} collective-permute-done((bf16[48,256]{1,0:T(8,128)(2,1)S(1)}, bf16[48,256]{1,0:T(8,128)(2,1)S(1)}, u32[]{:S(2)}, u32[]{:S(2)}) %collective-permute-start.1) | collective-permute-done | bytes 24608 | tf_op jit(solution)/shard_map/ppermute | solution.py:501
  8.8 0.0 collective-permute-done.refs_3_
  8.9 0.0 copy-start.5
  8.9 0.0 copy-start.6
  8.9 0.9 %shard_map.146 = (f32[2,1216,128]{2,1,0:T(8,128)S(1)}, bf16[192,256]{1,0:T(8,128)(2,1)S(1)}) custom-call(s32[1]{0:T(128)S(6)} %copy.16.refs_0_, s32[3]{0:T(128)S(1)} %copy-done.8, bf16[768,256]{1,0:T(8,128)(2,1)S(1)} %bitcast.9, bf16[48,256]{1,0:T(8,128)(2,1)S(1)} %collective-permute-done.refs_3_, bf16[48,256]{1,0:T(8,128)(2,1)S(1)} %collective-permute-done.1.refs_4_, ...), custom_call_target="tpu_custom_call" | custom-call | flops 1000000000 | tf_op jit(solution)/shard_map/pallas_call | solution.py:594
  9.8 2.9 %collective-permute-start.2 = (bf16[192,256]{1,0:T(8,128)(2,1)S(1)}, bf16[192,256]{1,0:T(8,128)(2,1)S(1)}, u32[]{:S(2)}, u32[]{:S(2)}) collective-permute-start(bf16[192,256]{1,0:T(8,128)(2,1)S(1)} %get-tuple-element.51), channel_id=1, source_target_pairs={{0,16},{2,18},{4,20},{6,22},{8,24},{10,26},{12,28},{14,30},{30,14}... | collective-permute-start | bytes 294920 | tf_op jit(solution)/shard_map/ppermute | solution.py:501
  12.7 4.1 %shard_map.147 = (bf16[768,256]{1,0:T(8,128)(2,1)S(1)}, f32[768,256]{1,0:T(8,128)S(1)}, f32[768,128]{1,0:T(8,128)S(1)}, f32[768,1024]{1,0:T(8,128)S(1)}) custom-call(bf16[7,7,256]{2,1,0:T(8,128)(2,1)S(1)} %copy-done.5, f32[1,256]{1,0:T(1,128)S(1)} %bitcast.14, bf16[1024,256]{1,0:T(8,128)(2,1)S(1)} %copy-done.1, ...), custom_call_target="tpu_custom_call" | custom-call | flops 4499999744 | tf_op jit(solution)/shard_map/pallas_call | solution.py:594
  16.8 0.4 collective-permute-done.2.refs_4_.refs_1_
  17.2 4.4 %shard_map.148 = (f32[1024,256]{1,0:T(8,128)S(1)}, bf16[1024,256]{1,0:T(8,128)(2,1)S(1)}, bf16[768,1024]{1,0:T(8,128)(2,1)S(1)}, bf16[768,1024]{1,0:T(8,128)(2,1...) custom-call(bf16[7,7,256]{2,1,0:T(8,128)(2,1)S(1)} %copy-done.5, f32[1,256]{1,0:T(1,128)S(1)} %bitcast.15, ...), custom_call_target="tpu_custom_call" | custom-call | flops 5000000000 | tf_op jit(solution)/shard_map/pallas_call | solution.py:594
  21.5 0.1 collective-permute-start.3
  21.6 0.8 %shard_map.149 = (bf16[768,256]{1,0:T(8,128)(2,1)S(1)}, f32[8,256]{1,0:T(8,128)S(1)}) custom-call(bf16[256,1024]{1,0:T(8,128)(2,1)S(1)} %copy-done, f32[1,256]{1,0:T(1,128)S(1)} %bitcast.16, bf16[768,1024]{1,0:T(8,128)(2,1)S(1)} %get-tuple-element.60.refs_2_, f32[768,256]{1,0:T(8,128)S(1)} %get-tuple-element.61.refs_3_, f32[768,128]{1,0:T(8,128)S(1)} %get-tuple-element.62.refs_4_), custom_call_target="tpu_custom_call" | custom-call | flops 1000000000 | tf_op jit(solution)/shard_map/pallas_call | solution.py:594
  22.4 1.1 %collective-permute-done.3.refs_1_ = bf16[1024,256]{1,0:T(8,128)(2,1)S(1)} collective-permute-done((bf16[1024,256]{1,0:T(8,128)(2,1)S(1)}, bf16[1024,256]{1,0:T(8,128)(2,1)S(1)}, u32[]{:S(2)}, u32[]{:S(2)}) %collective-permute-start.3) | collective-permute-done | bytes 524320 | tf_op jit(solution)/shard_map/ppermute | solution.py:505
  23.5 0.2 shard_map.150
  23.7 1.5 %collective-permute-start.4 = (bf16[512,256]{1,0:T(8,128)(2,1)S(1)}, bf16[512,256]{1,0:T(8,128)(2,1)S(1)}, u32[]{:S(2)}, u32[]{:S(2)}) collective-permute-start(bf16[512,256]{1,0:T(8,128)(2,1)S(1)} %get-tuple-element.65.refs_3_), channel_id=1, source_target_pairs={{0,4},{1,5},{2,10},{3,11},{4,0},{5,1},{6,14},{7,15},{8,12},{9,13},... | collective-permute-start | bytes 786440 | tf_op jit(solution)/shard_map/ppermute | solution.py:525
  25.1 4.1 %shard_map.151 = (f32[2,1216,128]{2,1,0:T(8,128)S(1)}, bf16[192,256]{1,0:T(8,128)(2,1)S(1)}) custom-call(s32[1]{0:T(128)S(6)} %copy.16.refs_0_, bf16[7,7,256]{2,1,0:T(8,128)(2,1)S(1)} %copy-done.5, bf16[768,256]{1,0:T(8,128)(2,1)S(1)} %get-tuple-element.63.refs_2_, bf16[512,256]{1,0:T(8,128)(2,1)S(1)} %get-tuple-element.65.refs_3_), custom_call_target="tpu_custom_call" | custom-call | flops 4000000000 | tf_op jit(solution)/shard_map/pallas_call | solution.py:594
  29.2 0.6 collective-permute-start.5
  29.9 0.2 collective-permute-done.4.refs_1_
  30.1 0.1 shard_map.152
  30.2 1.6 %collective-permute-start.6 = (bf16[256,256]{1,0:T(8,128)(2,1)S(1)}, bf16[256,256]{1,0:T(8,128)(2,1)S(1)}, u32[]{:S(2)}, u32[]{:S(2)}) collective-permute-start(bf16[256,256]{1,0:T(8,128)(2,1)S(1)} %get-tuple-element.67.refs_7_), channel_id=1, source_target_pairs={{0,1},{1,0},{2,6},{3,7},{4,5},{5,4},{6,2},{7,3},{8,9},{9,8},{10,14... | collective-permute-start | bytes 393224 | tf_op jit(solution)/shard_map/ppermute | solution.py:525
  31.8 2.0 %shard_map.153 = (bf16[768,256]{1,0:T(8,128)(2,1)}, f32[8,256]{1,0:T(8,128)S(1)}) custom-call(s32[1]{0:T(128)S(6)} %copy.16.refs_0_, s32[3]{0:T(128)S(1)} %copy-done.8, bf16[768,256]{1,0:T(8,128)(2,1)S(1)} %bitcast.10, bf16[768,256]{1,0:T(8,128)(2,1)S(1)} %bitcast.12, bf16[1024,256]{1,0:T(8,128)(2,1)S(1)} %copy-done.1, f32[1,256]{1,0:T(1,128)S(1)} %bitcast.18, ...), custom_call_target="tpu_custom_call" | custom-call | flops 1500000000 | tf_op jit(solution)/shard_map/pallas_call | solution.py:594
  33.7 1.5 %collective-permute-done.6.refs_1_ = bf16[256,256]{1,0:T(8,128)(2,1)S(1)} collective-permute-done((bf16[256,256]{1,0:T(8,128)(2,1)S(1)}, bf16[256,256]{1,0:T(8,128)(2,1)S(1)}, u32[]{:S(2)}, u32[]{:S(2)}) %collective-permute-start.6) | collective-permute-done | bytes 131104 | tf_op jit(solution)/shard_map/ppermute | solution.py:525
  35.3 2.8 %collective-permute-start.7 = (bf16[128,256]{1,0:T(8,128)(2,1)S(1)}, bf16[128,256]{1,0:T(8,128)(2,1)S(1)}, u32[]{:S(2)}, u32[]{:S(2)}) collective-permute-start(bf16[128,256]{1,0:T(8,128)(2,1)S(1)} %get-tuple-element.73.refs_5_), channel_id=1, source_target_pairs={{0,8},{1,9},{2,3},{3,2},{4,12},{5,13},{6,7},{7,6},{8,0},{9,1},{10,... | collective-permute-start | bytes 196616 | tf_op jit(solution)/shard_map/ppermute | solution.py:525
  38.1 3.5 %shard_map.155.refs_2_ = f32[64,256]{1,0:T(8,128)S(1)} custom-call(f32[2,1216,128]{2,1,0:T(8,128)S(1)} %get-tuple-element.50.refs_3_.refs_0_, bf16[192,256]{1,0:T(8,128)(2,1)S(1)} %collective-permute-done.2.refs_4_.refs_1_, bf16[768,256]{1,0:T(8,128)(2,1)S(1)} %get-tuple-element.63.refs_2_, f32[8,256]{1,0:T(8,128)S(1)} %get-tuple-element.74.refs_3_, ...), custom_call_target="tpu_custom_call" | custom-call | flops 3500000000 | tf_op jit(solution)/shard_map/pallas_call | solution.py:594
  41.7 0.4 collective-permute-start.10
  42.1 0.6 shard_map.157
  42.7 2.7 %collective-permute-start.9 = (bf16[48,256]{1,0:T(8,128)(2,1)S(1)}, bf16[48,256]{1,0:T(8,128)(2,1)S(1)}, u32[]{:S(2)}, u32[]{:S(2)}) collective-permute-start(bf16[48,256]{1,0:T(8,128)(2,1)S(1)} %get-tuple-element.78), channel_id=1, source_target_pairs={{0,16},{2,4},{4,2},{6,8},{8,6},{10,12},{12,10},{14,30},{30,14},{28... | collective-permute-start | bytes 73736 | tf_op jit(solution)/shard_map/ppermute | solution.py:501
  45.4 1.5 %collective-permute-done.10.refs_1_ = bf16[64,256]{1,0:T(8,128)(2,1)S(1)} collective-permute-done((bf16[64,256]{1,0:T(8,128)(2,1)S(1)}, bf16[64,256]{1,0:T(8,128)(2,1)S(1)}, u32[]{:S(2)}, u32[]{:S(2)}) %collective-permute-start.10) | collective-permute-done | bytes 32800 | tf_op jit(solution)/shard_map/ppermute | solution.py:525
  47.0 0.1 collective-permute-start.11
  47.0 0.5 collective-permute-done.9.refs_5_
  47.5 1.6 %shard_map.159 = (bf16[768,256]{1,0:T(8,128)(2,1)}, f32[8,128]{1,0:T(8,128)S(1)}) custom-call(s32[1]{0:T(128)S(6)} %copy.16.refs_0_, s32[3]{0:T(128)S(1)} %copy-done.8, bf16[768,256]{1,0:T(8,128)(2,1)S(1)} %bitcast.13, f32[2,1024,128]{2,1,0:T(8,128)S(1)} %get-tuple-element.76.refs_3_, bf16[48,256]{1,0:T(8,128)(2,1)S(1)} %collective-permute-done.8.refs_4_, ...), custom_call_target="tpu_custom_call" | custom-call | flops 1500000000 | tf_op jit(solution)/shard_map/pallas_call | solution.py:594
  49.1 3.6 %collective-permute-done.11.refs_1_ = bf16[128,256]{1,0:T(8,128)(2,1)S(1)} collective-permute-done((bf16[128,256]{1,0:T(8,128)(2,1)S(1)}, bf16[128,256]{1,0:T(8,128)(2,1)S(1)}, u32[]{:S(2)}, u32[]{:S(2)}) %collective-permute-start.11) | collective-permute-done | bytes 65568 | tf_op jit(solution)/shard_map/ppermute | solution.py:525
  52.8 0.1 collective-permute-start.12
  52.9 4.6 %collective-permute-done.12.refs_1_ = bf16[192,256]{1,0:T(8,128)(2,1)S(1)} collective-permute-done((bf16[192,256]{1,0:T(8,128)(2,1)S(1)}, bf16[192,256]{1,0:T(8,128)(2,1)S(1)}, u32[]{:S(2)}, u32[]{:S(2)}) %collective-permute-start.12) | collective-permute-done | bytes 98336 | tf_op jit(solution)/shard_map/ppermute | solution.py:525
  57.5 1.4 %collective-permute-start.13 = (bf16[320,256]{1,0:T(8,128)(2,1)S(1)}, bf16[320,256]{1,0:T(8,128)(2,1)S(1)}, u32[]{:S(2)}, u32[]{:S(2)}) collective-permute-start(bf16[320,256]{1,0:T(8,128)(2,1)S(1)} %shard_map.161.refs_0_), channel_id=1, source_target_pairs={{0,1},{1,0},{2,6},{3,7},{4,5},{5,4},{6,2},{7,3},{8,9},{9,8},{10,14... | collective-permute-start | bytes 491528 | tf_op jit(solution)/shard_map/ppermute | solution.py:525
  58.9 4.0 %collective-permute-done.13.refs_1_ = bf16[320,256]{1,0:T(8,128)(2,1)S(1)} collective-permute-done((bf16[320,256]{1,0:T(8,128)(2,1)S(1)}, bf16[320,256]{1,0:T(8,128)(2,1)S(1)}, u32[]{:S(2)}, u32[]{:S(2)}) %collective-permute-start.13) | collective-permute-done | bytes 163872 | tf_op jit(solution)/shard_map/ppermute | solution.py:525
  62.9 0.3 collective-permute-start.14
  63.2 6.5 %collective-permute-done.14.refs_1_ = bf16[576,256]{1,0:T(8,128)(2,1)S(1)} collective-permute-done((bf16[576,256]{1,0:T(8,128)(2,1)S(1)}, bf16[576,256]{1,0:T(8,128)(2,1)S(1)}, u32[]{:S(2)}, u32[]{:S(2)}) %collective-permute-start.14) | collective-permute-done | bytes 294944 | tf_op jit(solution)/shard_map/ppermute | solution.py:525
  69.7 0.1 shard_map.163.refs_0_
  69.8 0.1 collective-permute-start.15
  69.8 2.0 %collective-permute-done.15.refs_1_ = bf16[1152,256]{1,0:T(8,128)(2,1)S(1)} collective-permute-done((bf16[1152,256]{1,0:T(8,128)(2,1)S(1)}, bf16[1152,256]{1,0:T(8,128)(2,1)S(1)}, u32[]{:S(2)}, u32[]{:S(2)}) %collective-permute-start.15) | collective-permute-done | bytes 589856 | tf_op jit(solution)/shard_map/ppermute | solution.py:505
  71.8 1.5 %shard_map.164 = (f32[256,1024]{1,0:T(8,128)}, f32[1024,256]{1,0:T(8,128)}, f32[7,7,256]{2,1,0:T(8,128)}, f32[1,256]{1,0:T(1,128)}, f32[1,256]{1,0:T(1,128)}) custom-call(bf16[1152,256]{1,0:T(8,128)(2,1)S(1)} %shard_map.163.refs_0_, bf16[1152,256]{1,0:T(8,128)(2,1)S(1)} %collective-permute-done.15.refs_1_), custom_call_target="tpu_custom_call" | custom-call | flops 1500000000 | tf_op jit(solution)/shard_map/pallas_call | solution.py:594
  (23 shorter events, 0.2 us)
Async XLA Ops:
  1.3 1.0 %copy-start.2 = (bf16[1,3,16,16,256]{4,3,2,1,0:T(8,128)(2,1)S(1)}, bf16[1,3,16,16,256]{4,3,2,1,0:T(8,128)(2,1)}, u32[]{:S(2)}) copy-start(bf16[1,3,16,16,256]{4,3,2,1,0:T(8,128)(2,1)} %param.9) | copy-start | bytes 1179652
  2.3 4.7 %copy-start.4 = (bf16[1,3,16,16,256]{4,3,2,1,0:T(8,128)(2,1)S(1)}, bf16[1,3,16,16,256]{4,3,2,1,0:T(8,128)(2,1)}, u32[]{:S(2)}) copy-start(bf16[1,3,16,16,256]{4,3,2,1,0:T(8,128)(2,1)} %param.10) | copy-start | bytes 1179652
  2.3 4.7 %copy-start.7 = (f32[256]{0:T(256)S(1)}, f32[256]{0:T(256)}, u32[]{:S(2)}) copy-start(f32[256]{0:T(256)} %param.17) | copy-start | bytes 3076
  2.3 4.7 %copy-start.8 = (s32[3]{0:T(128)S(1)}, s32[3]{0:T(128)}, u32[]{:S(2)}) copy-start(s32[3]{0:T(128)} %refs_1_.9) | copy-start | bytes 40
  2.9 6.0 %collective-permute-start.1 = (bf16[48,256]{1,0:T(8,128)(2,1)S(1)}, bf16[48,256]{1,0:T(8,128)(2,1)S(1)}, u32[]{:S(2)}, u32[]{:S(2)}) collective-permute-start(bf16[48,256]{1,0:T(8,128)(2,1)S(1)} %get-tuple-element.48), channel_id=1, source_target_pairs={{0,16},{2,4},{4,2},{6,8},{8,6},{10,12},{12,10},{14,30},{30,14},{28... | collective-permute-start | bytes 73736 | tf_op jit(solution)/shard_map/ppermute | solution.py:501
  7.0 1.9 %collective-permute-start = (bf16[48,256]{1,0:T(8,128)(2,1)S(1)}, bf16[48,256]{1,0:T(8,128)(2,1)S(1)}, u32[]{:S(2)}, u32[]{:S(2)}) collective-permute-start(bf16[48,256]{1,0:T(8,128)(2,1)S(1)} %get-tuple-element.47.refs_4_), channel_id=1, source_target_pairs={{0,2},{2,0},{4,6},{6,4},{8,10},{10,8},{12,14},{14,12},{30,28},{28,... | collective-permute-start | bytes 73736 | tf_op jit(solution)/shard_map/ppermute | solution.py:501
  7.0 1.9 %copy-start.3 = (bf16[1,3,16,16,256]{4,3,2,1,0:T(8,128)(2,1)S(1)}, bf16[1,3,16,16,256]{4,3,2,1,0:T(8,128)(2,1)}, u32[]{:S(2)}) copy-start(bf16[1,3,16,16,256]{4,3,2,1,0:T(8,128)(2,1)} %param.9) | copy-start | bytes 1179652
  8.8 3.9 %copy-start.1 = (bf16[1024,256]{1,0:T(8,128)(2,1)S(1)}, bf16[1024,256]{1,0:T(8,128)(2,1)}, u32[]{:S(2)}) copy-start(bf16[1024,256]{1,0:T(8,128)(2,1)} %refs_4_.1) | copy-start | bytes 1572868
  8.9 3.9 %copy-start.5 = (bf16[7,7,256]{2,1,0:T(8,128)(2,1)S(1)}, bf16[7,7,256]{2,1,0:T(8,128)(2,1)}, u32[]{:S(2)}) copy-start(bf16[7,7,256]{2,1,0:T(8,128)(2,1)} %refs_1_.7) | copy-start | bytes 75268
  8.9 3.8 %copy-start.6 = (f32[256]{0:T(256)S(1)}, f32[256]{0:T(256)}, u32[]{:S(2)}) copy-start(f32[256]{0:T(256)} %param.14) | copy-start | bytes 3076
  9.8 7.4 %collective-permute-start.2 = (bf16[192,256]{1,0:T(8,128)(2,1)S(1)}, bf16[192,256]{1,0:T(8,128)(2,1)S(1)}, u32[]{:S(2)}, u32[]{:S(2)}) collective-permute-start(bf16[192,256]{1,0:T(8,128)(2,1)S(1)} %get-tuple-element.51), channel_id=1, source_target_pairs={{0,16},{2,18},{4,20},{6,22},{8,24},{10,26},{12,28},{14,30},{30,14}... | collective-permute-start | bytes 294920 | tf_op jit(solution)/shard_map/ppermute | solution.py:501
  12.7 4.5 %copy-start = (bf16[256,1024]{1,0:T(8,128)(2,1)S(1)}, bf16[256,1024]{1,0:T(8,128)(2,1)}, u32[]{:S(2)}) copy-start(bf16[256,1024]{1,0:T(8,128)(2,1)} %refs_0_.12) | copy-start | bytes 1572868
  21.5 2.0 %collective-permute-start.3 = (bf16[1024,256]{1,0:T(8,128)(2,1)S(1)}, bf16[1024,256]{1,0:T(8,128)(2,1)S(1)}, u32[]{:S(2)}, u32[]{:S(2)}) collective-permute-start(bf16[1024,256]{1,0:T(8,128)(2,1)S(1)} %get-tuple-element.59), channel_id=1, source_target_pairs={{0,2},{2,0},{1,3},{3,1},{4,6},{6,4},{5,7},{7,5},{8,10},{10,8},{9,1... | collective-permute-start | bytes 1572872 | tf_op jit(solution)/shard_map/ppermute | solution.py:505
  23.7 6.4 %collective-permute-start.4 = (bf16[512,256]{1,0:T(8,128)(2,1)S(1)}, bf16[512,256]{1,0:T(8,128)(2,1)S(1)}, u32[]{:S(2)}, u32[]{:S(2)}) collective-permute-start(bf16[512,256]{1,0:T(8,128)(2,1)S(1)} %get-tuple-element.65.refs_3_), channel_id=1, source_target_pairs={{0,4},{1,5},{2,10},{3,11},{4,0},{5,1},{6,14},{7,15},{8,12},{9,13},... | collective-permute-start | bytes 786440 | tf_op jit(solution)/shard_map/ppermute | solution.py:525
  29.2 12.9 %collective-permute-start.5 = (bf16[192,256]{1,0:T(8,128)(2,1)S(1)}, bf16[192,256]{1,0:T(8,128)(2,1)S(1)}, u32[]{:S(2)}, u32[]{:S(2)}) collective-permute-start(bf16[192,256]{1,0:T(8,128)(2,1)S(1)} %get-tuple-element.66.refs_2_), channel_id=1, source_target_pairs={{0,16},{2,18},{4,20},{6,22},{8,24},{10,26},{12,28},{14,30},{30,14}... | collective-permute-start | bytes 294920 | tf_op jit(solution)/shard_map/ppermute | solution.py:501
  30.2 5.0 %collective-permute-start.6 = (bf16[256,256]{1,0:T(8,128)(2,1)S(1)}, bf16[256,256]{1,0:T(8,128)(2,1)S(1)}, u32[]{:S(2)}, u32[]{:S(2)}) collective-permute-start(bf16[256,256]{1,0:T(8,128)(2,1)S(1)} %get-tuple-element.67.refs_7_), channel_id=1, source_target_pairs={{0,1},{1,0},{2,6},{3,7},{4,5},{5,4},{6,2},{7,3},{8,9},{9,8},{10,14... | collective-permute-start | bytes 393224 | tf_op jit(solution)/shard_map/ppermute | solution.py:525
  35.3 6.4 %collective-permute-start.7 = (bf16[128,256]{1,0:T(8,128)(2,1)S(1)}, bf16[128,256]{1,0:T(8,128)(2,1)S(1)}, u32[]{:S(2)}, u32[]{:S(2)}) collective-permute-start(bf16[128,256]{1,0:T(8,128)(2,1)S(1)} %get-tuple-element.73.refs_5_), channel_id=1, source_target_pairs={{0,8},{1,9},{2,3},{3,2},{4,12},{5,13},{6,7},{7,6},{8,0},{9,1},{10,... | collective-permute-start | bytes 196616 | tf_op jit(solution)/shard_map/ppermute | solution.py:525
  41.7 5.2 %collective-permute-start.10 = (bf16[64,256]{1,0:T(8,128)(2,1)S(1)}, bf16[64,256]{1,0:T(8,128)(2,1)S(1)}, u32[]{:S(2)}, u32[]{:S(2)}) collective-permute-start(bf16[64,256]{1,0:T(8,128)(2,1)S(1)} %get-tuple-element.75.refs_3_), channel_id=1, source_target_pairs={{0,16},{1,17},{2,18},{3,19},{4,20},{5,21},{6,22},{7,23},{8,24},{9,... | collective-permute-start | bytes 98312 | tf_op jit(solution)/shard_map/ppermute | solution.py:525
  42.7 4.8 %collective-permute-start.9 = (bf16[48,256]{1,0:T(8,128)(2,1)S(1)}, bf16[48,256]{1,0:T(8,128)(2,1)S(1)}, u32[]{:S(2)}, u32[]{:S(2)}) collective-permute-start(bf16[48,256]{1,0:T(8,128)(2,1)S(1)} %get-tuple-element.78), channel_id=1, source_target_pairs={{0,16},{2,4},{4,2},{6,8},{8,6},{10,12},{12,10},{14,30},{30,14},{28... | collective-permute-start | bytes 73736 | tf_op jit(solution)/shard_map/ppermute | solution.py:501
  45.4 2.1 %collective-permute-start.8 = (bf16[48,256]{1,0:T(8,128)(2,1)S(1)}, bf16[48,256]{1,0:T(8,128)(2,1)S(1)}, u32[]{:S(2)}, u32[]{:S(2)}) collective-permute-start(bf16[48,256]{1,0:T(8,128)(2,1)S(1)} %get-tuple-element.77.refs_3_), channel_id=1, source_target_pairs={{0,2},{2,0},{4,6},{6,4},{8,10},{10,8},{12,14},{14,12},{30,28},{28,... | collective-permute-start | bytes 73736 | tf_op jit(solution)/shard_map/ppermute | solution.py:501
  47.0 5.8 %collective-permute-start.11 = (bf16[128,256]{1,0:T(8,128)(2,1)S(1)}, bf16[128,256]{1,0:T(8,128)(2,1)S(1)}, u32[]{:S(2)}, u32[]{:S(2)}) collective-permute-start(bf16[128,256]{1,0:T(8,128)(2,1)S(1)} %shard_map.158.refs_6_.refs_0_), channel_id=1, source_target_pairs={{0,16},{1,17},{2,18},{3,19},{4,20},{5,21},{6,22},{7,23},{8,24},{9,... | collective-permute-start | bytes 196616 | tf_op jit(solution)/shard_map/ppermute | solution.py:525
  52.8 4.7 %collective-permute-start.12 = (bf16[192,256]{1,0:T(8,128)(2,1)S(1)}, bf16[192,256]{1,0:T(8,128)(2,1)S(1)}, u32[]{:S(2)}, u32[]{:S(2)}) collective-permute-start(bf16[192,256]{1,0:T(8,128)(2,1)S(1)} %shard_map.160.refs_0_), channel_id=1, source_target_pairs={{0,8},{1,9},{2,3},{3,2},{4,12},{5,13},{6,7},{7,6},{8,0},{9,1},{10,... | collective-permute-start | bytes 294920 | tf_op jit(solution)/shard_map/ppermute | solution.py:525
  57.5 5.4 %collective-permute-start.13 = (bf16[320,256]{1,0:T(8,128)(2,1)S(1)}, bf16[320,256]{1,0:T(8,128)(2,1)S(1)}, u32[]{:S(2)}, u32[]{:S(2)}) collective-permute-start(bf16[320,256]{1,0:T(8,128)(2,1)S(1)} %shard_map.161.refs_0_), channel_id=1, source_target_pairs={{0,1},{1,0},{2,6},{3,7},{4,5},{5,4},{6,2},{7,3},{8,9},{9,8},{10,14... | collective-permute-start | bytes 491528 | tf_op jit(solution)/shard_map/ppermute | solution.py:525
  62.9 6.8 %collective-permute-start.14 = (bf16[576,256]{1,0:T(8,128)(2,1)S(1)}, bf16[576,256]{1,0:T(8,128)(2,1)S(1)}, u32[]{:S(2)}, u32[]{:S(2)}) collective-permute-start(bf16[576,256]{1,0:T(8,128)(2,1)S(1)} %shard_map.162.refs_0_), channel_id=1, source_target_pairs={{0,4},{1,5},{2,10},{3,11},{4,0},{5,1},{6,14},{7,15},{8,12},{9,13},... | collective-permute-start | bytes 884744 | tf_op jit(solution)/shard_map/ppermute | solution.py:525
  69.8 2.1 %collective-permute-start.15 = (bf16[1152,256]{1,0:T(8,128)(2,1)S(1)}, bf16[1152,256]{1,0:T(8,128)(2,1)S(1)}, u32[]{:S(2)}, u32[]{:S(2)}) collective-permute-start(bf16[1152,256]{1,0:T(8,128)(2,1)S(1)} %shard_map.163.refs_0_), channel_id=1, source_target_pairs={{0,2},{2,0},{1,3},{3,1},{4,6},{6,4},{5,7},{7,5},{8,10},{10,8},{9,1... | collective-permute-start | bytes 1769480 | tf_op jit(solution)/shard_map/ppermute | solution.py:505

commit v2 on v1

--- a/solution.py
+++ b/solution.py
@@ -87,10 +87,10 @@
         second[rows, :] = jnp.where(even, left[col], right[col]).astype(BF16)
 
 
-def flip_matrix(shape, used):
-    to = lax.broadcasted_iota(jnp.int32, (shape.pitch, shape.pitch), 0)
-    frm = lax.broadcasted_iota(jnp.int32, (shape.pitch, shape.pitch), 1)
-    return jnp.where(to + frm == used + 2 * LEFT - 1, 1.0, 0.0).astype(BF16)
+def flip_matrix(size, last):
+    to = lax.broadcasted_iota(jnp.int32, (size, size), 0)
+    frm = lax.broadcasted_iota(jnp.int32, (size, size), 1)
+    return jnp.where(to + frm == last, 1.0, 0.0).astype(BF16)
 
 
 def prep_kernel(shape, count_hbm, fields, first, second, count, work, sems):
@@ -103,21 +103,23 @@
     send_edges(shape, left, right, first, second)
 
 
-def cotangent_kernel(
-    shape, count_hbm, ocean_hbm, tangent, scale, dproj, dproj_t, count, ocean, sems
-):
+def top_kernel(shape, count_hbm, ocean_hbm, fields, fold, count, ocean, sems):
     fetch = Fetch(sems, (count_hbm, count), (ocean_hbm, ocean))
     fetch.wait(0, 1)
-    per_slot = TILE * TILE
-    for slot in range(shape.slots):
-        rows = pl.ds(slot * per_slot, per_slot)
-        flag = slot_flag(count, ocean, slot)
-        scaled = (tangent[rows, :].astype(F32) * (scale[...] * flag)).astype(BF16)
-        dproj[rows, :] = scaled
-        dproj_t[:, slot * per_slot : (slot + 1) * per_slot] = scaled.T
-
-
-def band_kernel(shape, count_hbm, ocean_hbm, fields, first, second, band, fold, count, ocean, sems):
+    flip = flip_matrix(shape.columns, count[0] * TILE - 1)
+    for k in range(HALF):
+        cells = jnp.concatenate(
+            [
+                fields[pl.ds(slot * TILE * TILE + (TILE - 1 - k) * TILE, TILE), :].astype(F32)
+                * slot_flag(count, ocean, slot)
+                for slot in range(shape.slots)
+            ]
+        )
+        turned = dot(flip, cells.astype(BF16), 1, 0)
+        fold[pl.ds(k * shape.columns, shape.columns), :] = turned.astype(BF16)
+
+
+def band_kernel(shape, count_hbm, ocean_hbm, fields, first, second, band, rims, count, ocean, sems):
     fetch = Fetch(sems, (count_hbm, count), (ocean_hbm, ocean))
     even = is_even()
     blank = jnp.zeros((LEFT, LANES), F32)
@@ -146,11 +148,16 @@
             east = jnp.where(even, one, two)
             band[part, pl.ds(top + LEFT - HALF + col, TILE, stride=shape.pitch), :] = west
             band[part, pl.ds(top + LEFT + used + col, TILE, stride=shape.pitch), :] = east
-    turn_rows(shape, used, band, (HALF + TILE - 1, HALF + TILE - 2, HALF + TILE - 3), fold)
+    for k in range(HALF):
+        base = (HALF + TILE - 1 - k) * shape.pitch
+        east = pl.multiple_of(base + LEFT + used, LEFT)
+        for part in range(shape.parts):
+            ends = jnp.concatenate([band[part, pl.ds(base, LEFT), :], band[part, pl.ds(east, LEFT), :]])
+            rims[pl.ds(k * 2 * LEFT, 2 * LEFT), shape.lanes(part)] = ends.astype(BF16)
 
 
 def turn_rows(shape, used, source, rows, fold):
-    flip = flip_matrix(shape, used)
+    flip = flip_matrix(shape.pitch, used + 2 * LEFT - 1)
     for k, row in enumerate(rows):
         at = pl.ds(row * shape.pitch, shape.pitch)
         cells = jnp.concatenate([source[part, at, :] for part in range(shape.parts)], axis=1)
@@ -158,10 +165,21 @@
         fold[pl.ds(k * shape.pitch, shape.pitch), :] = turned.astype(BF16)
 
 
-def put_fold(shape, fold, padded, first_row):
-    for part in range(shape.parts):
-        rows = pl.ds(first_row * shape.pitch, HALF * shape.pitch)
-        padded[part, rows, :] = fold[:, shape.lanes(part)].astype(F32)
+def put_fold(shape, used, fold, rims, parts, padded, first_row, work):
+    blank = jnp.zeros((LEFT, LANES), F32)
+    for at, part in enumerate(parts):
+        work[at] = rims[:, shape.lanes(part)].astype(F32)
+        for k in range(HALF):
+            base = (first_row + k) * shape.pitch
+            padded[at, pl.ds(base, LEFT), :] = blank
+            padded[at, pl.ds(base + LEFT + shape.columns, LEFT), :] = blank
+            cells = fold[pl.ds(k * shape.columns, shape.columns), shape.lanes(part)]
+            padded[at, pl.ds(base + LEFT, shape.columns), :] = cells.astype(F32)
+            for col in range(HALF):
+                west = work[at, pl.ds(k * 2 * LEFT + LEFT - 1 - col, 1), :]
+                east = work[at, pl.ds(k * 2 * LEFT + LEFT + col, 1), :]
+                padded[at, pl.ds(base + LEFT - 1 - col, 1), :] = east
+                padded[at, pl.ds(base + LEFT + used + col, 1), :] = west
 
 
 def spread_taps(shape, kernel, taps):
@@ -229,32 +247,38 @@
 
 
 def early_kernel(
-    shape, kernel, gain, w_out, band, dproj,
-    normed, yhat, inverse, dact,
-    taps, convolved,
+    shape, count_hbm, ocean_hbm, kernel, gain, w_out, scale, tangent, band,
+    normed, yhat, inverse, dproj_t, dact,
+    count, ocean, taps, convolved, dproj, sems,
 ):
+    fetch = Fetch(sems, (count_hbm, count), (ocean_hbm, ocean))
     spread_taps(shape, kernel, taps)
     convolve(shape, shape.early, band, taps, convolved)
     normalise(shape, shape.early, 0, convolved, gain, normed, yhat, inverse)
+    fetch.wait(0, 1)
     per_slot = TILE * TILE
     for slot in range(shape.slots):
         rows = pl.ds(slot * per_slot, per_slot)
+        flag = slot_flag(count, ocean, slot)
+        scaled = (tangent[rows, :].astype(F32) * (scale[...] * flag)).astype(BF16)
+        dproj[rows, :] = scaled
+        dproj_t[:, slot * per_slot : (slot + 1) * per_slot] = scaled.T
         for h in range(shape.hidden // shape.channels):
             cols = slice(h * shape.channels, (h + 1) * shape.channels)
             dact[rows, cols] = dot(dproj[rows, :], w_out[cols, :], 1, 1)
 
 
 def late_kernel(
-    shape, kernel, gain, w_in, band, fold, normed_in, yhat_in, inverse_in, dproj_t, dact,
+    shape, count_hbm, kernel, gain, w_in, band, fold, rims, normed_in, yhat_in, inverse_in, dproj_t, dact,
     keep, give, activated, dpreact, yhat, inverse,
-    taps, padded, convolved, normed, normed_t,
+    count, taps, padded, convolved, normed, normed_t, work, sems,
 ):
+    fetch = Fetch(sems, (count_hbm, count))
     late = TILE - shape.early
     kept = late + HALF
     for part in range(shape.parts):
         rows = pl.ds(shape.early * shape.pitch, kept * shape.pitch)
         padded[part, pl.ds(0, kept * shape.pitch), :] = band[part, rows, :]
-    put_fold(shape, fold, padded, kept)
     done = shape.early * TILE
     for slot in range(shape.slots):
         rows = pl.ds(slot * TILE * TILE, done)
@@ -262,6 +286,8 @@
         yhat[rows, :] = yhat_in[rows, :]
         inverse[rows, :] = inverse_in[rows, :]
     spread_taps(shape, kernel, taps)
+    fetch.wait(0)
+    put_fold(shape, count[0] * TILE, fold, rims, range(shape.parts), padded, kept, work)
     convolve(shape, late, padded, taps, convolved)
     normalise(shape, late, shape.early, convolved, gain, normed, yhat, inverse)
     per_slot = TILE * TILE
@@ -327,58 +353,56 @@
     scale_part[...] = total
 
 
-def place_grad(shape, conv_grad, spaced):
+def place_grad(shape, conv_grad, parts, spaced):
     blank = jnp.zeros((LEFT, LANES), F32)
-    for part in range(shape.parts):
+    for at, part in enumerate(parts):
         for row in range(TILE):
             base = row * shape.pitch
-            spaced[part, pl.ds(base, LEFT), :] = blank
-            spaced[part, pl.ds(base + LEFT + shape.columns, LEFT), :] = blank
+            spaced[at, pl.ds(base, LEFT), :] = blank
+            spaced[at, pl.ds(base + LEFT + shape.columns, LEFT), :] = blank
             for slot in range(shape.slots):
                 cells = conv_grad[pl.ds(slot * TILE * TILE + row * TILE, TILE), shape.lanes(part)]
-                spaced[part, pl.ds(base + LEFT + slot * TILE, TILE), :] = cells.astype(F32)
-
-
-def taps_kernel(shape, band, fold, conv_grad, gain_part, scale_part, small, padded, spaced):
+                spaced[at, pl.ds(base + LEFT + slot * TILE, TILE), :] = cells.astype(F32)
+
+
+def taps_kernel(
+    shape, part, count_hbm, band, fold, rims, conv_grad, gain_part, scale_part, small, count, padded, spaced, work, sems
+):
+    fetch = Fetch(sems, (count_hbm, count))
     taps = KSIZE * KSIZE
+    lanes = shape.lanes(part)
     small[...] = jnp.zeros_like(small)
-    small[pl.ds(taps, 1), :] = jnp.sum(gain_part[...], axis=0, keepdims=True)
-    small[pl.ds(taps + 1, 1), :] = jnp.sum(scale_part[...], axis=0, keepdims=True)
-    place_grad(shape, conv_grad, spaced)
+    small[pl.ds(taps, 1), :] = jnp.sum(gain_part[:, lanes], axis=0, keepdims=True)
+    small[pl.ds(taps + 1, 1), :] = jnp.sum(scale_part[:, lanes], axis=0, keepdims=True)
+    place_grad(shape, conv_grad, [part], spaced)
     kept = TILE + HALF
-    for part in range(shape.parts):
-        padded[part, pl.ds(0, kept * shape.pitch), :] = band[part]
-    put_fold(shape, fold, padded, kept)
+    padded[0, pl.ds(0, kept * shape.pitch), :] = band[part]
+    fetch.wait(0)
+    put_fold(shape, count[0] * TILE, fold, rims, [part], padded, kept, work)
     run = shape.columns // 8
     origin = LEFT - HALF
-    for part in range(shape.parts):
-        for above in range(KSIZE):
-
-            def one_row(row, sums, part=part, above=above):
-                base = (row + above) * shape.pitch + origin
-                loaded = [
-                    padded[part, pl.ds(base + at, 8, stride=run), :] for at in range(run + KSIZE - 1)
-                ]
-                grads = [
-                    spaced[part, pl.ds(row * shape.pitch + LEFT + at, 8, stride=run), :] for at in range(run)
-                ]
-                sums = list(sums)
-                for shift in range(KSIZE):
-                    for at in range(run):
-                        sums[shift] = sums[shift] + grads[at] * loaded[at + shift]
-                return tuple(sums)
-
-            blank = tuple(jnp.zeros((8, LANES), F32) for _ in range(KSIZE))
-            sums = lax.fori_loop(0, TILE, one_row, blank, unroll=2)
+    for above in range(KSIZE):
+
+        def one_row(row, sums, above=above):
+            base = (row + above) * shape.pitch + origin
+            loaded = [padded[0, pl.ds(base + at, 8, stride=run), :] for at in range(run + KSIZE - 1)]
+            start = row * shape.pitch + LEFT
+            grads = [spaced[0, pl.ds(start + at, 8, stride=run), :] for at in range(run)]
+            sums = list(sums)
             for shift in range(KSIZE):
-                small[pl.ds(above * KSIZE + shift, 1), shape.lanes(part)] = jnp.sum(
-                    sums[shift], axis=0, keepdims=True
-                )
+                for at in range(run):
+                    sums[shift] = sums[shift] + grads[at] * loaded[at + shift]
+            return tuple(sums)
+
+        blank = tuple(jnp.zeros((8, LANES), F32) for _ in range(KSIZE))
+        sums = lax.fori_loop(0, TILE, one_row, blank, unroll=2)
+        for shift in range(KSIZE):
+            small[pl.ds(above * KSIZE + shift, 1), :] = jnp.sum(sums[shift], axis=0, keepdims=True)
 
 
 def back_kernel(shape, count_hbm, kernel, conv_grad, core_grad, fold, count, spaced, taps, sems):
     fetch = Fetch(sems, (count_hbm, count))
-    place_grad(shape, conv_grad, spaced)
+    place_grad(shape, conv_grad, range(shape.parts), spaced)
     blank = jnp.zeros((LEFT, LANES), F32)
     for part in range(shape.parts):
         for row in range(TILE + HALF):
@@ -548,11 +572,17 @@
     send[...] = mine[half_rows(1 - bit_here(following), rows // 2), :].astype(BF16)
 
 
-def turn_kernel(stage, whole, came, small, payload):
+def turn_kernel(stage, whole, came, *refs):
+    small, payload = refs[:-1], refs[-1]
     rows = came.shape[0]
     share = whole[half_rows(bit_here(stage), rows), :] + came[...].astype(F32)
     payload[pl.ds(0, rows), :] = share.astype(BF16)
-    payload[pl.ds(rows, small.shape[0]), :] = small[...].astype(BF16)
+    for part, ref in enumerate(small):
+        payload[pl.ds(rows, ref.shape[0]), part * LANES : (part + 1) * LANES] = ref[...].astype(BF16)
+
+
+def add_kernel(own, came, payload):
+    payload[...] = (own[...].astype(F32) + came[...].astype(F32)).astype(BF16)
 
 
 def double_kernel(stage, extra, own, came, payload):
@@ -632,34 +662,38 @@
     count_s = (block_count.shape, jnp.int32)
     ocean_s = (ocean.shape, jnp.int32)
     flat = ((channels, cells), BF16)
+    ends = ((HALF * 2 * LEFT, channels), BF16)
+    ends_f = ((parts, HALF * 2 * LEFT, LANES), F32)
     late = TILE - shape.early
 
     first, second = call(
         bind(prep_kernel), [edge, edge], [count_s, ((parts, cells, LANES), F32)],
         [block_count], [fields], 1, 1.0,
     )
-    dproj, dproj_t = call(
-        bind(cotangent_kernel), [whole, flat], [count_s, ocean_s],
-        [block_count, ocean], [tangent, scale], 2, 1.0, after=[first],
+    (fold,) = call(
+        bind(top_kernel), [((HALF * shape.columns, channels), BF16)], [count_s, ocean_s],
+        [block_count, ocean], [fields], 2, 0.5, after=[first],
     )
     first, second = swap(first, "first"), swap(second, "second")
-    band, fold = call(
-        bind(band_kernel), [strip(TILE + HALF), turned], [count_s, ocean_s],
-        [block_count, ocean], [fields, first, second], 2, 1.0, after=[dproj],
-    )
-    fold = swap(fold, "fold")
-    normed, yhat, inverse, dact = call(
-        bind(early_kernel), [whole, whole_f, narrow, ((cells, hidden), F32)],
-        [taps, ((parts, shape.early * shape.columns, LANES), F32)],
-        [], [taps_in, gain, w_out, band, dproj], 0, 4.5,
+    band, rims = call(
+        bind(band_kernel), [strip(TILE + HALF), ends], [count_s, ocean_s],
+        [block_count, ocean], [fields, first, second], 2, 1.0, after=[fold],
+    )
+    fold, rims = swap(fold, "fold"), swap(rims, "fold")
+    normed, yhat, inverse, dproj_t, dact = call(
+        bind(early_kernel), [whole, whole_f, narrow, flat, ((cells, hidden), F32)],
+        [count_s, ocean_s, taps, ((parts, shape.early * shape.columns, LANES), F32), whole],
+        [block_count, ocean], [taps_in, gain, w_out, scale, tangent, band], 2, 5.0,
     )
     keep, give, activated, dpreact, yhat, inverse = call(
         bind(late_kernel),
         [((hidden, channels), F32), ((hidden, channels), BF16), wide, wide, whole_f, narrow],
         [
-            taps, strip(late + 2 * HALF), ((parts, late * shape.columns, LANES), F32), whole, flat,
+            count_s, taps, strip(late + 2 * HALF), ((parts, late * shape.columns, LANES), F32), whole, flat,
+            ends_f,
         ],
-        [], [taps_in, gain, w_in, band, fold, normed, yhat, inverse, dproj_t, dact], 0, 5.0,
+        [block_count],
+        [taps_in, gain, w_in, band, fold, rims, normed, yhat, inverse, dproj_t, dact], 1, 5.0,
     )
 
     order = stages()
@@ -670,6 +704,15 @@
             ((rows, channels), F32), ((rows // 2, channels), BF16),
         ]
 
+    def taps_part(part, after):
+        (small,) = call(
+            functools.partial(taps_kernel, shape, part), [((small_rows, LANES), F32)],
+            [count_s, ((1, (TILE + 2 * HALF) * pitch, LANES), F32), ((1, TILE * pitch, LANES), F32), ends_f],
+            [block_count], [band, fold, rims, conv_grad, gain_part, scale_part], 1, 1.8, after=after,
+        )
+        return small
+
+    small_rows = -(-(KSIZE * KSIZE + 2) // 16) * 16
     came = core_swap(give)
     conv_grad, gain_part = call(
         bind(norm_grad_kernel), [whole, eight], [], [], [w_in, gain, dpreact, yhat, inverse], 0, 1.0,
@@ -679,54 +722,42 @@
         [((hidden, channels), F32), ((rows, channels), BF16)], [], [], [keep, came], after=[conv_grad], micros=0.3,
     )
     came = bit_swap(send, order[0])
-    core_grad, fold_back = call(
-        bind(back_kernel), [strip(TILE + HALF), turned], [count_s, strip(TILE), taps],
-        [block_count], [taps_in, conv_grad], 1, 4.0, after=[send],
-    )
-    body, outs = half_step(0, rows)
-    mine, send = call(body, outs, [], [], [mine, came], after=[fold_back], micros=0.3)
-    came = bit_swap(send, order[1])
-    fold_back = swap(fold_back, "fold")
     state, scale_part = call(
         bind(state_kernel), [whole, eight], [count_s, ocean_s],
         [block_count, ocean], [fields, tangent, w_out, scale, activated], 2, 1.5, after=[send],
     )
+    small = [taps_part(0, [send])]
+    body, outs = half_step(0, rows)
+    mine, send = call(body, outs, [], [], [mine, came], after=small, micros=0.3)
+    came = bit_swap(send, order[1])
+    small += [taps_part(part, [send]) for part in range(1, parts)]
     rows //= 2
     body, outs = half_step(1, rows)
-    mine, send = call(body, outs, [], [], [mine, came], after=[scale_part], micros=0.3)
-    came = bit_swap(send, order[2])
-    small_rows = -(-(KSIZE * KSIZE + 2) // 16) * 16
-    (small,) = call(
-        bind(taps_kernel), [((small_rows, channels), F32)], [strip(TILE + 2 * HALF), strip(TILE)],
-        [], [band, fold, conv_grad, gain_part, scale_part], 0, 3.5, after=[send],
-    )
-    rows //= 2
-    body, outs = half_step(2, rows)
-    mine, send = call(body, outs, [], [], [mine, came], after=[small], micros=0.3)
-    mine, send = halved(mine, send, order[3:])
-    came = bit_swap(send, order[-1])
-    folded, first, second = call(
-        bind(rims_kernel), [strip(TILE), edge, edge], [count_s], [block_count], [core_grad, fold_back], 1, 1.0,
-        after=[send],
-    )
+    mine, send = call(body, outs, [], [], [mine, came], after=small[1:], micros=0.3)
+    mine, send = halved(mine, send, order[2:-1])
+    came = bit_swap(send, order[-2])
     rows = came.shape[0]
     if rows % 16 == 0:
         (payload,) = call(
-            functools.partial(turn_kernel, order[-1]), [((rows + small_rows, channels), BF16)],
-            [], [], [mine, came, small], after=[first], micros=0.3,
+            functools.partial(turn_kernel, order[-2]), [((rows + small_rows, channels), BF16)],
+            [], [], [mine, came, *small], micros=0.3,
         )
     else:
-        bit = bit_here(order[-1])
+        bit = bit_here(order[-2])
         share = lax.dynamic_index_in_dim(mine.reshape(2, rows, channels), bit, 0, keepdims=False)
-        payload = jnp.concatenate([share + came.astype(F32), small]).astype(BF16)
+        payload = jnp.concatenate([share + came.astype(F32), jnp.concatenate(small, axis=1)]).astype(BF16)
     came = bit_swap(payload, order[-1])
-    first, second = swap(first, "first"), swap(second, "second")
-    grad_fields, done = call(
-        bind(final_kernel), [whole, ((8, LANES), F32)], [count_s, ocean_s, strip(TILE)],
-        [block_count, ocean], [tangent, folded, first, second], 2, 1.5, after=[payload],
-    )
-    after = [done]
-    for at in reversed(range(len(order))):
+    core_grad, fold_back = call(
+        bind(back_kernel), [strip(TILE + HALF), turned], [count_s, strip(TILE), taps],
+        [block_count], [taps_in, conv_grad], 1, 4.0, after=[payload],
+    )
+    (payload,) = call(
+        add_kernel, [(payload.shape, BF16)], [], [], [payload, came], after=[fold_back], micros=0.3,
+    )
+    fold_back = swap(fold_back, "fold")
+    came = bit_swap(payload, order[-2])
+    after = []
+    for at in reversed(range(len(order) - 1)):
         copies = 2 if at == 0 else 1
         if rows % 16 == 0:
             (payload,) = call(
@@ -737,12 +768,25 @@
         else:
             first = bit_here(order[at]) == 0
             low, high = payload[:rows], came[:rows]
-            small = payload[rows:].astype(F32) + came[rows:].astype(F32)
-            joined = [jnp.where(first, low, high), jnp.where(first, high, low), small.astype(BF16)]
+            both = payload[rows:].astype(F32) + came[rows:].astype(F32)
+            joined = [jnp.where(first, low, high), jnp.where(first, high, low), both.astype(BF16)]
             payload = jnp.concatenate(joined)
         after = []
         rows *= 2
         came = bit_swap(payload, order[at - 1]) if at else core_swap(payload)
+        if at == 2:
+            folded, first, second = call(
+                bind(rims_kernel), [strip(TILE), edge, edge], [count_s], [block_count], [core_grad, fold_back], 1, 1.0,
+                after=[payload],
+            )
+            after = [folded]
+            first, second = swap(first, "first"), swap(second, "second")
+        if at == 1:
+            grad_fields, done = call(
+                bind(final_kernel), [whole, ((8, LANES), F32)], [count_s, ocean_s, strip(TILE)],
+                [block_count, ocean], [tangent, folded, first, second], 2, 1.5, after=[payload],
+            )
+            after = [done]
     total = samples * lax.axis_size("dp") * slots * lax.axis_size(TILES) * tile_rows * tile_cols
     w_in_sum, w_out_sum, kernel_sum, gain_sum, scale_sum = call(
         functools.partial(unpack_kernel, total ** (-0.5)),

time: 73.5 us -> 67.6 us (0.920)
  waiting for transfers between devices: 27 us -> 18.2 us
  Pallas kernels: 25.2 us -> 26.6 us
  starting transfers between devices: 18.6 us -> 20 us
    ppermute x8 -> x7, waiting for transfers between devices: 21.9 us -> 10.3 us  [bit_swap(): return lax.ppermute(block, ('chips', 'core', 'dp'), pairs)]
    ppermute x6 -> x7, waiting for transfers between devices: 1.95 us -> 5.19 us  [swap(): return lax.ppermute(block, TILES, pairs_of(kind))]
    ppermute x2, starting transfers between devices: 0.14 us -> 1.57 us  [core_swap(): return lax.ppermute(block, 'core', [(0, 1), (1, 0)])]
    pallas_call x21, Pallas kernels: 25.2 us -> 26.6 us  [call(): pl.pallas_call(body, out_shape=[jax.ShapeDtypeStruct(*out) for out in out...]
    ppermute x8 -> x7, starting transfers between devices: 8.15 us -> 7.41 us  [bit_swap(): return lax.ppermute(block, ('chips', 'core', 'dp'), pairs)]
    ppermute x6 -> x7, starting transfers between devices: 10.3 us -> 11.1 us  [swap(): return lax.ppermute(block, TILES, pairs_of(kind))]
  transfers between devices with their start and end apart: 16 -> 16, of which waited for: 12 -> 10; matrix products, arithmetic and copies ran while one was open for 0% -> 0% of each run, Pallas kernels for 24% -> 29%
where the time goes in v2:
time: 67.6 us; the launch traced here: 67.4 us
  Pallas kernels  26.6 us (39%)
  starting transfers between devices  20 us (30%)
  waiting for transfers between devices  18.2 us (27%)
  between operations  1.55 us (2%)
  local copies, waits for them, and re-layouts  1.04 us (2%)
    pallas_call x21, Pallas kernels, call(): pl.pallas_call(body, out_shape=[jax.ShapeDtypeStruct(*out) for out in out...  26.6 us
    ppermute x7, starting transfers between devices, swap(): return lax.ppermute(block, TILES, pairs_of(kind))  11.1 us
    ppermute x7, waiting for transfers between devices, bit_swap(): return lax.ppermute(block, ('chips', 'core', 'dp'), pairs)  10.3 us
    ppermute x7, starting transfers between devices, bit_swap(): return lax.ppermute(block, ('chips', 'core', 'dp'), pairs)  7.41 us
    ppermute x7, waiting for transfers between devices, swap(): return lax.ppermute(block, TILES, pairs_of(kind))  5.19 us
    ppermute x2, waiting for transfers between devices, core_swap(): return lax.ppermute(block, 'core', [(0, 1), (1, 0)])  2.73 us
    ppermute x2, starting transfers between devices, core_swap(): return lax.ppermute(block, 'core', [(0, 1), (1, 0)])  1.57 us
  transfers between devices with their start and end apart: 16, of which 10 were waited for; matrix products, arithmetic and copies ran while one was open for 0% of the time, Pallas kernels for 29%

profile of v2, /device:TPU:0, one launch (start us, length us, event | category | flops | bytes accessed | tf_op | source)
XLA Modules:
  0.0 67.4 jit_solution(2305664112542405413)
XLA Ops:
  1.3 0.0 copy-start.2
  1.3 1.0 %copy-done.2 = bf16[1,3,16,16,256]{4,3,2,1,0:T(8,128)(2,1)S(1)} copy-done((bf16[1,3,16,16,256]{4,3,2,1,0:T(8,128)(2,1)S(1)}, bf16[1,3,16,16,256]{4,3,2,1,0:T(8,128)(2,1)}, u32[]{:S(2)}) %copy-start.2) | copy-done | bytes 393240
  2.3 0.6 shard_map.144
  2.9 4.1 %collective-permute-start.1 = (bf16[48,256]{1,0:T(8,128)(2,1)S(1)}, bf16[48,256]{1,0:T(8,128)(2,1)S(1)}, u32[]{:S(2)}, u32[]{:S(2)}) collective-permute-start(bf16[48,256]{1,0:T(8,128)(2,1)S(1)} %get-tuple-element.45), channel_id=1, source_target_pairs={{0,16},{2,4},{4,2},{6,8},{8,6},{10,12},{12,10},{14,30},{30,14},{28... | collective-permute-start | bytes 73736 | tf_op jit(solution)/shard_map/ppermute | solution.py:525
  7.0 0.7 %shard_map.145.refs_5_ = bf16[144,256]{1,0:T(8,128)(2,1)S(1)} custom-call(s32[1]{0:T(128)S(6)} %copy.16.refs_0_, s32[3]{0:T(128)S(1)} %copy-done.8, bf16[768,256]{1,0:T(8,128)(2,1)S(1)} %bitcast.9, bf16[48,256]{1,0:T(8,128)(2,1)S(1)} %get-tuple-element.44.refs_3_), custom_call_target="tpu_custom_call" | custom-call | flops 500000000 | tf_op jit(solution)/shard_map/pallas_call | solution.py:624
  7.7 0.0 copy-start.1
  7.7 0.0 copy-start.4
  7.7 0.0 copy-start.5
  7.7 0.0 copy-start.6
  7.8 0.0 copy-start.7
  7.8 1.7 %collective-permute-start.2 = (bf16[144,256]{1,0:T(8,128)(2,1)S(1)}, bf16[144,256]{1,0:T(8,128)(2,1)S(1)}, u32[]{:S(2)}, u32[]{:S(2)}) collective-permute-start(bf16[144,256]{1,0:T(8,128)(2,1)S(1)} %shard_map.145.refs_5_), channel_id=1, source_target_pairs={{0,16},{2,18},{4,20},{6,22},{8,24},{10,26},{12,28},{14,30},{30,14}... | collective-permute-start | bytes 221192 | tf_op jit(solution)/shard_map/ppermute | solution.py:525
  9.4 0.7 %shard_map.146 = (f32[2,1216,128]{2,1,0:T(8,128)S(1)}, bf16[48,256]{1,0:T(8,128)(2,1)S(1)}) custom-call(s32[1]{0:T(128)S(6)} %copy.16.refs_0_, s32[3]{0:T(128)S(1)} %copy-done.8, bf16[768,256]{1,0:T(8,128)(2,1)S(1)} %bitcast.10, bf16[48,256]{1,0:T(8,128)(2,1)S(1)} %collective-permute-done.refs_3_, bf16[48,256]{1,0:T(8,128)(2,1)S(1)} %collective-permute-done.1.refs_4_, ...), custom_call_target="tpu_custom_call" | custom-call | flops 1000000000 | tf_op jit(solution)/shard_map/pallas_call | solution.py:624
  10.2 2.3 %collective-permute-start.3 = (bf16[48,256]{1,0:T(8,128)(2,1)S(1)}, bf16[48,256]{1,0:T(8,128)(2,1)S(1)}, u32[]{:S(2)}, u32[]{:S(2)}) collective-permute-start(bf16[48,256]{1,0:T(8,128)(2,1)S(1)} %get-tuple-element.47), channel_id=1, source_target_pairs={{0,16},{2,18},{4,20},{6,22},{8,24},{10,26},{12,28},{14,30},{30,14}... | collective-permute-start | bytes 73736 | tf_op jit(solution)/shard_map/ppermute | solution.py:525
  12.5 0.0 copy-start
  12.6 4.2 %shard_map.147 = (bf16[768,256]{1,0:T(8,128)(2,1)S(1)}, f32[768,256]{1,0:T(8,128)S(1)}, f32[768,128]{1,0:T(8,128)S(1)}, bf16[256,768]{1,0:T(8,128)(2,1)S(1)}, f32[768,1024]{1,0:T(8,128)S(1)}) custom-call(s32[1]{0:T(128)S(6)} %copy.16.refs_0_, s32[3]{0:T(128)S(1)} %copy-done.8, bf16[7,7,256]{2,1,0:T(8,128)(2,1)S(1)} %copy-done.5, f32[1,256]{1,0:T(1,128)S(1)} %bitcast.15, ...), custom_call_target="tpu_custom_call" | custom-call | flops 5000000000 | tf_op jit(solution)/shard_map/pallas_call | solution.py:624
  16.7 4.8 %shard_map.148 = (f32[1024,256]{1,0:T(8,128)S(1)}, bf16[1024,256]{1,0:T(8,128)(2,1)S(1)}, bf16[768,1024]{1,0:T(8,128)(2,1)S(1)}, bf16[768,1024]{1,0:T(8,128)(2,1...) custom-call(s32[1]{0:T(128)S(6)} %copy.16.refs_0_, bf16[7,7,256]{2,1,0:T(8,128)(2,1)S(1)} %copy-done.5, ...), custom_call_target="tpu_custom_call" | custom-call | flops 5000000000 | tf_op jit(solution)/shard_map/pallas_call | solution.py:624
  21.6 0.1 collective-permute-start.4
  21.6 0.8 %shard_map.149 = (bf16[768,256]{1,0:T(8,128)(2,1)S(1)}, f32[8,256]{1,0:T(8,128)S(1)}) custom-call(bf16[256,1024]{1,0:T(8,128)(2,1)S(1)} %copy-done, f32[1,256]{1,0:T(1,128)S(1)} %bitcast.17, bf16[768,1024]{1,0:T(8,128)(2,1)S(1)} %get-tuple-element.56.refs_2_, f32[768,256]{1,0:T(8,128)S(1)} %get-tuple-element.57.refs_3_, f32[768,128]{1,0:T(8,128)S(1)} %get-tuple-element.58.refs_4_), custom_call_target="tpu_custom_call" | custom-call | flops 1000000000 | tf_op jit(solution)/shard_map/pallas_call | solution.py:624
  22.4 1.1 %collective-permute-done.4.refs_1_ = bf16[1024,256]{1,0:T(8,128)(2,1)S(1)} collective-permute-done((bf16[1024,256]{1,0:T(8,128)(2,1)S(1)}, bf16[1024,256]{1,0:T(8,128)(2,1)S(1)}, u32[]{:S(2)}, u32[]{:S(2)}) %collective-permute-start.4) | collective-permute-done | bytes 524320 | tf_op jit(solution)/shard_map/ppermute | solution.py:529
  23.5 0.2 shard_map.150
  23.7 0.2 collective-permute-start.5
  23.9 2.0 %shard_map.151 = (bf16[768,256]{1,0:T(8,128)(2,1)}, f32[8,256]{1,0:T(8,128)S(1)}) custom-call(s32[1]{0:T(128)S(6)} %copy.16.refs_0_, s32[3]{0:T(128)S(1)} %copy-done.8, bf16[768,256]{1,0:T(8,128)(2,1)S(1)} %bitcast.11, bf16[768,256]{1,0:T(8,128)(2,1)S(1)} %bitcast.13, bf16[1024,256]{1,0:T(8,128)(2,1)S(1)} %copy-done.1, f32[1,256]{1,0:T(1,128)S(1)} %bitcast.19, ...), custom_call_target="tpu_custom_call" | custom-call | flops 1500000000 | tf_op jit(solution)/shard_map/pallas_call | solution.py:624
  25.8 2.3 %shard_map.152.refs_2_ = f32[64,128]{1,0:T(8,128)S(1)} custom-call(s32[1]{0:T(128)S(6)} %copy.16.refs_0_, f32[2,1216,128]{2,1,0:T(8,128)S(1)} %get-tuple-element.46.refs_7_.refs_4_.refs_1_, bf16[144,256]{1,0:T(8,128)(2,1)S(1)} %collective-permute-done.2.refs_5_.refs_2_, bf16[48,256]{1,0:T(8,128)(2,1)S(1)} %collective-permute-done.3.refs_6_.refs_3_, ...), custom_call_target="tpu_custom_call" | custom-call | flops 1800000000 | tf_op jit(solution)/shard_map/pallas_call | solution.py:624
  28.1 2.0 %collective-permute-done.5.refs_1_ = bf16[512,256]{1,0:T(8,128)(2,1)S(1)} collective-permute-done((bf16[512,256]{1,0:T(8,128)(2,1)S(1)}, bf16[512,256]{1,0:T(8,128)(2,1)S(1)}, u32[]{:S(2)}, u32[]{:S(2)}) %collective-permute-start.5) | collective-permute-done | bytes 262176 | tf_op jit(solution)/shard_map/ppermute | solution.py:549
  30.1 0.1 shard_map.153
  30.2 1.6 %collective-permute-start.6 = (bf16[256,256]{1,0:T(8,128)(2,1)S(1)}, bf16[256,256]{1,0:T(8,128)(2,1)S(1)}, u32[]{:S(2)}, u32[]{:S(2)}) collective-permute-start(bf16[256,256]{1,0:T(8,128)(2,1)S(1)} %get-tuple-element.66.refs_7_), channel_id=1, source_target_pairs={{0,1},{1,0},{2,6},{3,7},{4,5},{5,4},{6,2},{7,3},{8,9},{9,8},{10,14... | collective-permute-start | bytes 393224 | tf_op jit(solution)/shard_map/ppermute | solution.py:549
  31.8 2.3 %shard_map.154.refs_2_.refs_3_ = f32[64,128]{1,0:T(8,128)S(1)} custom-call(s32[1]{0:T(128)S(6)} %copy.16.refs_0_, f32[2,1216,128]{2,1,0:T(8,128)S(1)} %get-tuple-element.46.refs_7_.refs_4_.refs_1_, bf16[144,256]{1,0:T(8,128)(2,1)S(1)} %collective-permute-done.2.refs_5_.refs_2_, bf16[48,256]{1,0:T(8,128)(2,1)S(1)} %collective-permute-done.3.refs_6_.refs_3_, ...), custom_call_target="tpu_custom_call" | custom-call | flops 1800000000 | tf_op jit(solution)/shard_map/pallas_call | solution.py:624
  34.1 1.2 %collective-permute-done.6.refs_1_ = bf16[256,256]{1,0:T(8,128)(2,1)S(1)} collective-permute-done((bf16[256,256]{1,0:T(8,128)(2,1)S(1)}, bf16[256,256]{1,0:T(8,128)(2,1)S(1)}, u32[]{:S(2)}, u32[]{:S(2)}) %collective-permute-start.6) | collective-permute-done | bytes 131104 | tf_op jit(solution)/shard_map/ppermute | solution.py:549
  35.3 1.1 %collective-permute-start.7 = (bf16[128,256]{1,0:T(8,128)(2,1)S(1)}, bf16[128,256]{1,0:T(8,128)(2,1)S(1)}, u32[]{:S(2)}, u32[]{:S(2)}) collective-permute-start(bf16[128,256]{1,0:T(8,128)(2,1)S(1)} %get-tuple-element.68), channel_id=1, source_target_pairs={{0,8},{1,9},{2,3},{3,2},{4,12},{5,13},{6,7},{7,6},{8,0},{9,1},{10,... | collective-permute-start | bytes 196616 | tf_op jit(solution)/shard_map/ppermute | solution.py:549
  36.4 3.3 %collective-permute-done.7.refs_1_ = bf16[128,256]{1,0:T(8,128)(2,1)S(1)} collective-permute-done((bf16[128,256]{1,0:T(8,128)(2,1)S(1)}, bf16[128,256]{1,0:T(8,128)(2,1)S(1)}, u32[]{:S(2)}, u32[]{:S(2)}) %collective-permute-start.7) | collective-permute-done | bytes 65568 | tf_op jit(solution)/shard_map/ppermute | solution.py:549
  39.6 0.7 %collective-permute-start.9 = (bf16[192,256]{1,0:T(8,128)(2,1)S(1)}, bf16[192,256]{1,0:T(8,128)(2,1)S(1)}, u32[]{:S(2)}, u32[]{:S(2)}) collective-permute-start(bf16[192,256]{1,0:T(8,128)(2,1)S(1)} %shard_map.156.refs_3_.refs_0_), channel_id=1, source_target_pairs={{0,16},{1,17},{2,18},{3,19},{4,20},{5,21},{6,22},{7,23},{8,24},{9,... | collective-permute-start | bytes 294920 | tf_op jit(solution)/shard_map/ppermute | solution.py:549
  40.4 4.1 %shard_map.157 = (f32[2,1216,128]{2,1,0:T(8,128)S(1)}, bf16[192,256]{1,0:T(8,128)(2,1)S(1)}) custom-call(s32[1]{0:T(128)S(6)} %copy.16.refs_0_, bf16[7,7,256]{2,1,0:T(8,128)(2,1)S(1)} %copy-done.5, bf16[768,256]{1,0:T(8,128)(2,1)S(1)} %get-tuple-element.59.refs_2_.refs_4_, bf16[192,256]{1,0:T(8,128)(2,1)S(1)} %shard_map.156.refs_3_.refs_0_), custom_call_target="tpu_custom_call" | custom-call | flops 4000000000 | tf_op jit(solution)/shard_map/pallas_call | solution.py:624
  44.5 0.8 %collective-permute-done.9.refs_1_ = bf16[192,256]{1,0:T(8,128)(2,1)S(1)} collective-permute-done((bf16[192,256]{1,0:T(8,128)(2,1)S(1)}, bf16[192,256]{1,0:T(8,128)(2,1)S(1)}, u32[]{:S(2)}, u32[]{:S(2)}) %collective-permute-start.9) | collective-permute-done | bytes 98336 | tf_op jit(solution)/shard_map/ppermute | solution.py:549
  45.2 1.7 %collective-permute-start.10 = (bf16[192,256]{1,0:T(8,128)(2,1)S(1)}, bf16[192,256]{1,0:T(8,128)(2,1)S(1)}, u32[]{:S(2)}, u32[]{:S(2)}) collective-permute-start(bf16[192,256]{1,0:T(8,128)(2,1)S(1)} %shard_map.158.refs_0_), channel_id=1, source_target_pairs={{0,8},{1,9},{2,3},{3,2},{4,12},{5,13},{6,7},{7,6},{8,0},{9,1},{10,... | collective-permute-start | bytes 294920 | tf_op jit(solution)/shard_map/ppermute | solution.py:549
  47.0 1.6 %collective-permute-start.8 = (bf16[192,256]{1,0:T(8,128)(2,1)S(1)}, bf16[192,256]{1,0:T(8,128)(2,1)S(1)}, u32[]{:S(2)}, u32[]{:S(2)}) collective-permute-start(bf16[192,256]{1,0:T(8,128)(2,1)S(1)} %get-tuple-element.70.refs_2_), channel_id=1, source_target_pairs={{0,16},{2,18},{4,20},{6,22},{8,24},{10,26},{12,28},{14,30},{30,14}... | collective-permute-start | bytes 294920 | tf_op jit(solution)/shard_map/ppermute | solution.py:525
  48.5 1.6 %collective-permute-done.10.refs_1_ = bf16[192,256]{1,0:T(8,128)(2,1)S(1)} collective-permute-done((bf16[192,256]{1,0:T(8,128)(2,1)S(1)}, bf16[192,256]{1,0:T(8,128)(2,1)S(1)}, u32[]{:S(2)}, u32[]{:S(2)}) %collective-permute-start.10) | collective-permute-done | bytes 98336 | tf_op jit(solution)/shard_map/ppermute | solution.py:549
  50.1 1.4 %collective-permute-start.13 = (bf16[320,256]{1,0:T(8,128)(2,1)S(1)}, bf16[320,256]{1,0:T(8,128)(2,1)S(1)}, u32[]{:S(2)}, u32[]{:S(2)}) collective-permute-start(bf16[320,256]{1,0:T(8,128)(2,1)S(1)} %shard_map.159.refs_3_.refs_0_), channel_id=1, source_target_pairs={{0,1},{1,0},{2,6},{3,7},{4,5},{5,4},{6,2},{7,3},{8,9},{9,8},{10,14... | collective-permute-start | bytes 491528 | tf_op jit(solution)/shard_map/ppermute | solution.py:549
  51.5 1.8 %collective-permute-done.8.refs_2_ = bf16[192,256]{1,0:T(8,128)(2,1)S(1)} collective-permute-done((bf16[192,256]{1,0:T(8,128)(2,1)S(1)}, bf16[192,256]{1,0:T(8,128)(2,1)S(1)}, u32[]{:S(2)}, u32[]{:S(2)}) %collective-permute-start.8) | collective-permute-done | bytes 98336 | tf_op jit(solution)/shard_map/ppermute | solution.py:525
  53.4 0.6 shard_map.160
  54.0 1.5 %collective-permute-done.13.refs_1_ = bf16[320,256]{1,0:T(8,128)(2,1)S(1)} collective-permute-done((bf16[320,256]{1,0:T(8,128)(2,1)S(1)}, bf16[320,256]{1,0:T(8,128)(2,1)S(1)}, u32[]{:S(2)}, u32[]{:S(2)}) %collective-permute-start.13) | collective-permute-done | bytes 163872 | tf_op jit(solution)/shard_map/ppermute | solution.py:549
  55.5 0.7 %collective-permute-start.14 = (bf16[576,256]{1,0:T(8,128)(2,1)S(1)}, bf16[576,256]{1,0:T(8,128)(2,1)S(1)}, u32[]{:S(2)}, u32[]{:S(2)}) collective-permute-start(bf16[576,256]{1,0:T(8,128)(2,1)S(1)} %shard_map.161.refs_6_.refs_0_), channel_id=1, source_target_pairs={{0,4},{1,5},{2,10},{3,11},{4,0},{5,1},{6,14},{7,15},{8,12},{9,13},... | collective-permute-start | bytes 884744 | tf_op jit(solution)/shard_map/ppermute | solution.py:549
  56.3 1.4 %collective-permute-start.12 = (bf16[48,256]{1,0:T(8,128)(2,1)S(1)}, bf16[48,256]{1,0:T(8,128)(2,1)S(1)}, u32[]{:S(2)}, u32[]{:S(2)}) collective-permute-start(bf16[48,256]{1,0:T(8,128)(2,1)S(1)} %get-tuple-element.73), channel_id=1, source_target_pairs={{0,16},{2,4},{4,2},{6,8},{8,6},{10,12},{12,10},{14,30},{30,14},{28... | collective-permute-start | bytes 73736 | tf_op jit(solution)/shard_map/ppermute | solution.py:525
  57.7 3.3 %collective-permute-done.12.refs_5_ = bf16[48,256]{1,0:T(8,128)(2,1)S(1)} collective-permute-done((bf16[48,256]{1,0:T(8,128)(2,1)S(1)}, bf16[48,256]{1,0:T(8,128)(2,1)S(1)}, u32[]{:S(2)}, u32[]{:S(2)}) %collective-permute-start.12) | collective-permute-done | bytes 24608 | tf_op jit(solution)/shard_map/ppermute | solution.py:525
  61.0 1.6 %shard_map.162 = (bf16[768,256]{1,0:T(8,128)(2,1)}, f32[8,128]{1,0:T(8,128)S(1)}) custom-call(s32[1]{0:T(128)S(6)} %copy.16.refs_0_, s32[3]{0:T(128)S(1)} %copy-done.8, bf16[768,256]{1,0:T(8,128)(2,1)S(1)} %bitcast.14, f32[2,1024,128]{2,1,0:T(8,128)S(1)} %get-tuple-element.71.refs_2_.refs_3_, bf16[48,256]{1,0:T(8,128)(2,1)S(1)} %collective-permute-done.11.refs_4_, ...), custom_call_target="tpu_custom_call" | custom-call | flops 1500000000 | tf_op jit(solution)/shard_map/pallas_call | solution.py:624
  62.6 0.1 shard_map.163.refs_0_
  62.7 1.5 %collective-permute-start.15 = (bf16[1152,256]{1,0:T(8,128)(2,1)S(1)}, bf16[1152,256]{1,0:T(8,128)(2,1)S(1)}, u32[]{:S(2)}, u32[]{:S(2)}) collective-permute-start(bf16[1152,256]{1,0:T(8,128)(2,1)S(1)} %shard_map.163.refs_0_), channel_id=1, source_target_pairs={{0,2},{2,0},{1,3},{3,1},{4,6},{6,4},{5,7},{7,5},{8,10},{10,8},{9,1... | collective-permute-start | bytes 1769480 | tf_op jit(solution)/shard_map/ppermute | solution.py:529
  64.2 1.6 %collective-permute-done.15.refs_1_ = bf16[1152,256]{1,0:T(8,128)(2,1)S(1)} collective-permute-done((bf16[1152,256]{1,0:T(8,128)(2,1)S(1)}, bf16[1152,256]{1,0:T(8,128)(2,1)S(1)}, u32[]{:S(2)}, u32[]{:S(2)}) %collective-permute-start.15) | collective-permute-done | bytes 589856 | tf_op jit(solution)/shard_map/ppermute | solution.py:529
  65.8 1.5 %shard_map.164 = (f32[256,1024]{1,0:T(8,128)}, f32[1024,256]{1,0:T(8,128)}, f32[7,7,256]{2,1,0:T(8,128)}, f32[1,256]{1,0:T(1,128)}, f32[1,256]{1,0:T(1,128)}) custom-call(bf16[1152,256]{1,0:T(8,128)(2,1)S(1)} %shard_map.163.refs_0_, bf16[1152,256]{1,0:T(8,128)(2,1)S(1)} %collective-permute-done.15.refs_1_), custom_call_target="tpu_custom_call" | custom-call | flops 1500000000 | tf_op jit(solution)/shard_map/pallas_call | solution.py:624
  (23 shorter events, 0.2 us)
Async XLA Ops:
  1.3 1.0 %copy-start.2 = (bf16[1,3,16,16,256]{4,3,2,1,0:T(8,128)(2,1)S(1)}, bf16[1,3,16,16,256]{4,3,2,1,0:T(8,128)(2,1)}, u32[]{:S(2)}) copy-start(bf16[1,3,16,16,256]{4,3,2,1,0:T(8,128)(2,1)} %param.9) | copy-start | bytes 1179652
  2.3 4.7 %copy-start.8 = (s32[3]{0:T(128)S(1)}, s32[3]{0:T(128)}, u32[]{:S(2)}) copy-start(s32[3]{0:T(128)} %refs_1_.13) | copy-start | bytes 40
  2.9 6.6 %collective-permute-start.1 = (bf16[48,256]{1,0:T(8,128)(2,1)S(1)}, bf16[48,256]{1,0:T(8,128)(2,1)S(1)}, u32[]{:S(2)}, u32[]{:S(2)}) collective-permute-start(bf16[48,256]{1,0:T(8,128)(2,1)S(1)} %get-tuple-element.45), channel_id=1, source_target_pairs={{0,16},{2,4},{4,2},{6,8},{8,6},{10,12},{12,10},{14,30},{30,14},{28... | collective-permute-start | bytes 73736 | tf_op jit(solution)/shard_map/ppermute | solution.py:525
  7.0 2.5 %collective-permute-start = (bf16[48,256]{1,0:T(8,128)(2,1)S(1)}, bf16[48,256]{1,0:T(8,128)(2,1)S(1)}, u32[]{:S(2)}, u32[]{:S(2)}) collective-permute-start(bf16[48,256]{1,0:T(8,128)(2,1)S(1)} %get-tuple-element.44.refs_3_), channel_id=1, source_target_pairs={{0,2},{2,0},{4,6},{6,4},{8,10},{10,8},{12,14},{14,12},{30,28},{28,... | collective-permute-start | bytes 73736 | tf_op jit(solution)/shard_map/ppermute | solution.py:525
  7.7 4.8 %copy-start.1 = (bf16[1024,256]{1,0:T(8,128)(2,1)S(1)}, bf16[1024,256]{1,0:T(8,128)(2,1)}, u32[]{:S(2)}) copy-start(bf16[1024,256]{1,0:T(8,128)(2,1)} %refs_4_.3) | copy-start | bytes 1572868
  7.7 4.8 %copy-start.4 = (bf16[1,3,16,16,256]{4,3,2,1,0:T(8,128)(2,1)S(1)}, bf16[1,3,16,16,256]{4,3,2,1,0:T(8,128)(2,1)}, u32[]{:S(2)}) copy-start(bf16[1,3,16,16,256]{4,3,2,1,0:T(8,128)(2,1)} %param.10) | copy-start | bytes 1179652
  7.7 4.8 %copy-start.5 = (bf16[7,7,256]{2,1,0:T(8,128)(2,1)S(1)}, bf16[7,7,256]{2,1,0:T(8,128)(2,1)}, u32[]{:S(2)}) copy-start(bf16[7,7,256]{2,1,0:T(8,128)(2,1)} %refs_1_.12) | copy-start | bytes 75268
  7.7 4.8 %copy-start.6 = (f32[256]{0:T(256)S(1)}, f32[256]{0:T(256)}, u32[]{:S(2)}) copy-start(f32[256]{0:T(256)} %param.14) | copy-start | bytes 3076
  7.8 4.8 %copy-start.7 = (f32[256]{0:T(256)S(1)}, f32[256]{0:T(256)}, u32[]{:S(2)}) copy-start(f32[256]{0:T(256)} %param.17) | copy-start | bytes 3076
  7.8 9.0 %collective-permute-start.2 = (bf16[144,256]{1,0:T(8,128)(2,1)S(1)}, bf16[144,256]{1,0:T(8,128)(2,1)S(1)}, u32[]{:S(2)}, u32[]{:S(2)}) collective-permute-start(bf16[144,256]{1,0:T(8,128)(2,1)S(1)} %shard_map.145.refs_5_), channel_id=1, source_target_pairs={{0,16},{2,18},{4,20},{6,22},{8,24},{10,26},{12,28},{14,30},{30,14}... | collective-permute-start | bytes 221192 | tf_op jit(solution)/shard_map/ppermute | solution.py:525
  10.2 6.5 %collective-permute-start.3 = (bf16[48,256]{1,0:T(8,128)(2,1)S(1)}, bf16[48,256]{1,0:T(8,128)(2,1)S(1)}, u32[]{:S(2)}, u32[]{:S(2)}) collective-permute-start(bf16[48,256]{1,0:T(8,128)(2,1)S(1)} %get-tuple-element.47), channel_id=1, source_target_pairs={{0,16},{2,18},{4,20},{6,22},{8,24},{10,26},{12,28},{14,30},{30,14}... | collective-permute-start | bytes 73736 | tf_op jit(solution)/shard_map/ppermute | solution.py:525
  12.5 4.2 %copy-start = (bf16[256,1024]{1,0:T(8,128)(2,1)S(1)}, bf16[256,1024]{1,0:T(8,128)(2,1)}, u32[]{:S(2)}) copy-start(bf16[256,1024]{1,0:T(8,128)(2,1)} %refs_0_.12) | copy-start | bytes 1572868
  21.6 2.0 %collective-permute-start.4 = (bf16[1024,256]{1,0:T(8,128)(2,1)S(1)}, bf16[1024,256]{1,0:T(8,128)(2,1)S(1)}, u32[]{:S(2)}, u32[]{:S(2)}) collective-permute-start(bf16[1024,256]{1,0:T(8,128)(2,1)S(1)} %get-tuple-element.55), channel_id=1, source_target_pairs={{0,2},{2,0},{1,3},{3,1},{4,6},{6,4},{5,7},{7,5},{8,10},{10,8},{9,1... | collective-permute-start | bytes 1572872 | tf_op jit(solution)/shard_map/ppermute | solution.py:529
  22.4 1.4 %copy-start.3 = (bf16[1,3,16,16,256]{4,3,2,1,0:T(8,128)(2,1)S(1)}, bf16[1,3,16,16,256]{4,3,2,1,0:T(8,128)(2,1)}, u32[]{:S(2)}) copy-start(bf16[1,3,16,16,256]{4,3,2,1,0:T(8,128)(2,1)} %param.9) | copy-start | bytes 1179652
  23.7 6.4 %collective-permute-start.5 = (bf16[512,256]{1,0:T(8,128)(2,1)S(1)}, bf16[512,256]{1,0:T(8,128)(2,1)S(1)}, u32[]{:S(2)}, u32[]{:S(2)}) collective-permute-start(bf16[512,256]{1,0:T(8,128)(2,1)S(1)} %get-tuple-element.60.refs_7_), channel_id=1, source_target_pairs={{0,4},{1,5},{2,10},{3,11},{4,0},{5,1},{6,14},{7,15},{8,12},{9,13},... | collective-permute-start | bytes 786440 | tf_op jit(solution)/shard_map/ppermute | solution.py:549
  30.2 5.0 %collective-permute-start.6 = (bf16[256,256]{1,0:T(8,128)(2,1)S(1)}, bf16[256,256]{1,0:T(8,128)(2,1)S(1)}, u32[]{:S(2)}, u32[]{:S(2)}) collective-permute-start(bf16[256,256]{1,0:T(8,128)(2,1)S(1)} %get-tuple-element.66.refs_7_), channel_id=1, source_target_pairs={{0,1},{1,0},{2,6},{3,7},{4,5},{5,4},{6,2},{7,3},{8,9},{9,8},{10,14... | collective-permute-start | bytes 393224 | tf_op jit(solution)/shard_map/ppermute | solution.py:549
  35.3 4.3 %collective-permute-start.7 = (bf16[128,256]{1,0:T(8,128)(2,1)S(1)}, bf16[128,256]{1,0:T(8,128)(2,1)S(1)}, u32[]{:S(2)}, u32[]{:S(2)}) collective-permute-start(bf16[128,256]{1,0:T(8,128)(2,1)S(1)} %get-tuple-element.68), channel_id=1, source_target_pairs={{0,8},{1,9},{2,3},{3,2},{4,12},{5,13},{6,7},{7,6},{8,0},{9,1},{10,... | collective-permute-start | bytes 196616 | tf_op jit(solution)/shard_map/ppermute | solution.py:549
  39.6 5.6 %collective-permute-start.9 = (bf16[192,256]{1,0:T(8,128)(2,1)S(1)}, bf16[192,256]{1,0:T(8,128)(2,1)S(1)}, u32[]{:S(2)}, u32[]{:S(2)}) collective-permute-start(bf16[192,256]{1,0:T(8,128)(2,1)S(1)} %shard_map.156.refs_3_.refs_0_), channel_id=1, source_target_pairs={{0,16},{1,17},{2,18},{3,19},{4,20},{5,21},{6,22},{7,23},{8,24},{9,... | collective-permute-start | bytes 294920 | tf_op jit(solution)/shard_map/ppermute | solution.py:549
  45.2 4.8 %collective-permute-start.10 = (bf16[192,256]{1,0:T(8,128)(2,1)S(1)}, bf16[192,256]{1,0:T(8,128)(2,1)S(1)}, u32[]{:S(2)}, u32[]{:S(2)}) collective-permute-start(bf16[192,256]{1,0:T(8,128)(2,1)S(1)} %shard_map.158.refs_0_), channel_id=1, source_target_pairs={{0,8},{1,9},{2,3},{3,2},{4,12},{5,13},{6,7},{7,6},{8,0},{9,1},{10,... | collective-permute-start | bytes 294920 | tf_op jit(solution)/shard_map/ppermute | solution.py:549
  47.0 6.4 %collective-permute-start.8 = (bf16[192,256]{1,0:T(8,128)(2,1)S(1)}, bf16[192,256]{1,0:T(8,128)(2,1)S(1)}, u32[]{:S(2)}, u32[]{:S(2)}) collective-permute-start(bf16[192,256]{1,0:T(8,128)(2,1)S(1)} %get-tuple-element.70.refs_2_), channel_id=1, source_target_pairs={{0,16},{2,18},{4,20},{6,22},{8,24},{10,26},{12,28},{14,30},{30,14}... | collective-permute-start | bytes 294920 | tf_op jit(solution)/shard_map/ppermute | solution.py:525
  50.1 5.4 %collective-permute-start.13 = (bf16[320,256]{1,0:T(8,128)(2,1)S(1)}, bf16[320,256]{1,0:T(8,128)(2,1)S(1)}, u32[]{:S(2)}, u32[]{:S(2)}) collective-permute-start(bf16[320,256]{1,0:T(8,128)(2,1)S(1)} %shard_map.159.refs_3_.refs_0_), channel_id=1, source_target_pairs={{0,1},{1,0},{2,6},{3,7},{4,5},{5,4},{6,2},{7,3},{8,9},{9,8},{10,14... | collective-permute-start | bytes 491528 | tf_op jit(solution)/shard_map/ppermute | solution.py:549
  55.5 7.1 %collective-permute-start.14 = (bf16[576,256]{1,0:T(8,128)(2,1)S(1)}, bf16[576,256]{1,0:T(8,128)(2,1)S(1)}, u32[]{:S(2)}, u32[]{:S(2)}) collective-permute-start(bf16[576,256]{1,0:T(8,128)(2,1)S(1)} %shard_map.161.refs_6_.refs_0_), channel_id=1, source_target_pairs={{0,4},{1,5},{2,10},{3,11},{4,0},{5,1},{6,14},{7,15},{8,12},{9,13},... | collective-permute-start | bytes 884744 | tf_op jit(solution)/shard_map/ppermute | solution.py:549
  56.3 1.4 %collective-permute-start.11 = (bf16[48,256]{1,0:T(8,128)(2,1)S(1)}, bf16[48,256]{1,0:T(8,128)(2,1)S(1)}, u32[]{:S(2)}, u32[]{:S(2)}) collective-permute-start(bf16[48,256]{1,0:T(8,128)(2,1)S(1)} %get-tuple-element.72), channel_id=1, source_target_pairs={{0,2},{2,0},{4,6},{6,4},{8,10},{10,8},{12,14},{14,12},{30,28},{28,... | collective-permute-start | bytes 73736 | tf_op jit(solution)/shard_map/ppermute | solution.py:525
  56.3 4.7 %collective-permute-start.12 = (bf16[48,256]{1,0:T(8,128)(2,1)S(1)}, bf16[48,256]{1,0:T(8,128)(2,1)S(1)}, u32[]{:S(2)}, u32[]{:S(2)}) collective-permute-start(bf16[48,256]{1,0:T(8,128)(2,1)S(1)} %get-tuple-element.73), channel_id=1, source_target_pairs={{0,16},{2,4},{4,2},{6,8},{8,6},{10,12},{12,10},{14,30},{30,14},{28... | collective-permute-start | bytes 73736 | tf_op jit(solution)/shard_map/ppermute | solution.py:525
  62.7 3.1 %collective-permute-start.15 = (bf16[1152,256]{1,0:T(8,128)(2,1)S(1)}, bf16[1152,256]{1,0:T(8,128)(2,1)S(1)}, u32[]{:S(2)}, u32[]{:S(2)}) collective-permute-start(bf16[1152,256]{1,0:T(8,128)(2,1)S(1)} %shard_map.163.refs_0_), channel_id=1, source_target_pairs={{0,2},{2,0},{1,3},{3,1},{4,6},{6,4},{5,7},{7,5},{8,10},{10,8},{9,1... | collective-permute-start | bytes 1769480 | tf_op jit(solution)/shard_map/ppermute | solution.py:529

commit v3 on v2

--- a/solution.py
+++ b/solution.py
@@ -156,15 +156,6 @@
             rims[pl.ds(k * 2 * LEFT, 2 * LEFT), shape.lanes(part)] = ends.astype(BF16)
 
 
-def turn_rows(shape, used, source, rows, fold):
-    flip = flip_matrix(shape.pitch, used + 2 * LEFT - 1)
-    for k, row in enumerate(rows):
-        at = pl.ds(row * shape.pitch, shape.pitch)
-        cells = jnp.concatenate([source[part, at, :] for part in range(shape.parts)], axis=1)
-        turned = dot(flip, cells.astype(BF16), 1, 0)
-        fold[pl.ds(k * shape.pitch, shape.pitch), :] = turned.astype(BF16)
-
-
 def put_fold(shape, used, fold, rims, parts, padded, first_row, work):
     blank = jnp.zeros((LEFT, LANES), F32)
     for at, part in enumerate(parts):
@@ -182,13 +173,13 @@
                 padded[at, pl.ds(base + LEFT + used + col, 1), :] = west
 
 
-def spread_taps(shape, kernel, taps):
+def spread_taps(shape, kernel, parts, taps):
     for above in range(KSIZE):
         rows = kernel[above].astype(F32)
-        for part in range(shape.parts):
+        for at, part in enumerate(parts):
             for shift in range(KSIZE):
                 row = rows[shift : shift + 1, shape.lanes(part)]
-                taps[part, above * KSIZE + shift] = jnp.broadcast_to(row, (8, LANES))
+                taps[at, above * KSIZE + shift] = jnp.broadcast_to(row, (8, LANES))
 
 
 def convolve(shape, rows, padded, taps, convolved):
@@ -252,7 +243,7 @@
     count, ocean, taps, convolved, dproj, sems,
 ):
     fetch = Fetch(sems, (count_hbm, count), (ocean_hbm, ocean))
-    spread_taps(shape, kernel, taps)
+    spread_taps(shape, kernel, range(shape.parts), taps)
     convolve(shape, shape.early, band, taps, convolved)
     normalise(shape, shape.early, 0, convolved, gain, normed, yhat, inverse)
     fetch.wait(0, 1)
@@ -270,8 +261,8 @@
 
 def late_kernel(
     shape, count_hbm, kernel, gain, w_in, band, fold, rims, normed_in, yhat_in, inverse_in, dproj_t, dact,
-    keep, give, activated, dpreact, yhat, inverse,
-    count, taps, padded, convolved, normed, normed_t, work, sems,
+    keep, give, activated, dpreact, yhat, inverse, padded,
+    count, taps, convolved, normed, normed_t, work, sems,
 ):
     fetch = Fetch(sems, (count_hbm, count))
     late = TILE - shape.early
@@ -285,7 +276,7 @@
         normed[rows, :] = normed_in[rows, :]
         yhat[rows, :] = yhat_in[rows, :]
         inverse[rows, :] = inverse_in[rows, :]
-    spread_taps(shape, kernel, taps)
+    spread_taps(shape, kernel, range(shape.parts), taps)
     fetch.wait(0)
     put_fold(shape, count[0] * TILE, fold, rims, range(shape.parts), padded, kept, work)
     convolve(shape, late, padded, taps, convolved)
@@ -365,20 +356,11 @@
                 spaced[at, pl.ds(base + LEFT + slot * TILE, TILE), :] = cells.astype(F32)
 
 
-def taps_kernel(
-    shape, part, count_hbm, band, fold, rims, conv_grad, gain_part, scale_part, small, count, padded, spaced, work, sems
-):
-    fetch = Fetch(sems, (count_hbm, count))
-    taps = KSIZE * KSIZE
-    lanes = shape.lanes(part)
-    small[...] = jnp.zeros_like(small)
-    small[pl.ds(taps, 1), :] = jnp.sum(gain_part[:, lanes], axis=0, keepdims=True)
-    small[pl.ds(taps + 1, 1), :] = jnp.sum(scale_part[:, lanes], axis=0, keepdims=True)
+def taps_kernel(shape, part, band, top, conv_grad, small, padded, spaced):
     place_grad(shape, conv_grad, [part], spaced)
-    kept = TILE + HALF
-    padded[0, pl.ds(0, kept * shape.pitch), :] = band[part]
-    fetch.wait(0)
-    put_fold(shape, count[0] * TILE, fold, rims, [part], padded, kept, work)
+    kept = shape.early * shape.pitch
+    padded[0, pl.ds(0, kept), :] = band[part, pl.ds(0, kept), :]
+    padded[0, pl.ds(kept, top.shape[1]), :] = top[part]
     run = shape.columns // 8
     origin = LEFT - HALF
     for above in range(KSIZE):
@@ -400,35 +382,37 @@
             small[pl.ds(above * KSIZE + shift, 1), :] = jnp.sum(sums[shift], axis=0, keepdims=True)
 
 
-def back_kernel(shape, count_hbm, kernel, conv_grad, core_grad, fold, count, spaced, taps, sems):
+def back_kernel(shape, part, count_hbm, kernel, conv_grad, *refs):
+    before = refs[:part]
+    turns = part == shape.parts - 1
+    core_grad, *refs = refs[part:]
+    if turns:
+        fold, *refs = refs
+    count, spaced, taps, sems = refs
     fetch = Fetch(sems, (count_hbm, count))
-    place_grad(shape, conv_grad, range(shape.parts), spaced)
+    place_grad(shape, conv_grad, [part], spaced)
     blank = jnp.zeros((LEFT, LANES), F32)
-    for part in range(shape.parts):
-        for row in range(TILE + HALF):
-            core_grad[part, pl.ds(row * shape.pitch, LEFT), :] = blank
-            core_grad[part, pl.ds((row + 1) * shape.pitch - LEFT, LEFT), :] = blank
-    fetch.wait(0)
-    spread_taps(shape, kernel, taps)
+    for row in range(TILE + HALF):
+        core_grad[pl.ds(row * shape.pitch, LEFT), :] = blank
+        core_grad[pl.ds((row + 1) * shape.pitch - LEFT, LEFT), :] = blank
+    spread_taps(shape, kernel, [part], taps)
     run = -(-(shape.columns + 2 * HALF) // 8)
 
     def one_row(row, tap_rows):
-        for part in range(shape.parts):
-            sums = [None] * run
-            for above in tap_rows:
-                base = (row - above) * shape.pitch + LEFT
-                loaded = [
-                    spaced[part, pl.ds(base + at - KSIZE + 1, 8, stride=run), :]
-                    for at in range(run + KSIZE - 1)
-                ]
-                for shift in range(KSIZE):
-                    weight = taps[part, above * KSIZE + shift]
-                    for at in range(run):
-                        term = weight * loaded[at - shift + KSIZE - 1]
-                        sums[at] = term if sums[at] is None else sums[at] + term
-            start = (row - HALF) * shape.pitch + LEFT - HALF
-            for at in range(run):
-                core_grad[part, pl.ds(start + at, 8, stride=run), :] = sums[at]
+        sums = [None] * run
+        for above in tap_rows:
+            base = (row - above) * shape.pitch + LEFT
+            loaded = [
+                spaced[0, pl.ds(base + at - KSIZE + 1, 8, stride=run), :] for at in range(run + KSIZE - 1)
+            ]
+            for shift in range(KSIZE):
+                weight = taps[0, above * KSIZE + shift]
+                for at in range(run):
+                    term = weight * loaded[at - shift + KSIZE - 1]
+                    sums[at] = term if sums[at] is None else sums[at] + term
+        start = (row - HALF) * shape.pitch + LEFT - HALF
+        for at in range(run):
+            core_grad[pl.ds(start + at, 8, stride=run), :] = sums[at]
 
     inner = (KSIZE - 1, TILE - 1)
     for row in range(HALF, TILE + 2 * HALF):
@@ -441,13 +425,22 @@
         return carry
 
     lax.fori_loop(inner[0], inner[1] + 1, inner_row, 0)
-    turn_rows(shape, count[0] * TILE, core_grad, (TILE, TILE + 1, TILE + 2), fold)
-
-
-def rims_kernel(shape, count_hbm, core_grad, fold, folded, first, second, count, sems):
+    fetch.wait(0)
+    if turns:
+        flip = flip_matrix(shape.pitch, count[0] * TILE + 2 * LEFT - 1)
+        for k in range(HALF):
+            at = pl.ds((TILE + k) * shape.pitch, shape.pitch)
+            cells = jnp.concatenate([one[at, :] for one in (*before, core_grad)], axis=1)
+            turned = dot(flip, cells.astype(BF16), 1, 0)
+            fold[pl.ds(k * shape.pitch, shape.pitch), :] = turned.astype(BF16)
+
+
+def rims_kernel(shape, count_hbm, fold, *refs):
+    core_grad = refs[: shape.parts]
+    folded, first, second, count, sems = refs[shape.parts :]
     fetch = Fetch(sems, (count_hbm, count))
     for part in range(shape.parts):
-        folded[part] = core_grad[part, pl.ds(0, TILE * shape.pitch), :]
+        folded[part] = core_grad[part][pl.ds(0, TILE * shape.pitch), :]
         for k in range(HALF):
             rows = pl.ds((TILE - 1 - k) * shape.pitch, shape.pitch)
             returned = fold[pl.ds(k * shape.pitch, shape.pitch), shape.lanes(part)]
@@ -489,24 +482,52 @@
                 grad_fields[rows, shape.lanes(part)] = (flag * total).astype(BF16)
 
 
-def unpack_kernel(norm, own, came, w_in, w_out, kernel_sum, gain_sum, scale_sum):
+def write_sums(norm, has_in, sums, w_in, w_out, work_in, work_out, sems):
+    channels = sums.shape[-1]
+    blocks = w_out.shape[0] // channels
+
+    def written(of_in):
+        copies = []
+        for h in range(blocks):
+            block = slice(h * channels, (h + 1) * channels)
+            value = sums[block, :].astype(F32) * norm
+            if of_in:
+                work_in[:, block] = value
+                copy = pltpu.make_async_copy(work_in.at[:, block], w_in.at[:, block], sems.at[h])
+            else:
+                work_out[block, :] = value.T
+                copy = pltpu.make_async_copy(work_out.at[block, :], w_out.at[block, :], sems.at[h])
+            copy.start()
+            copies.append(copy)
+        for copy in copies:
+            copy.wait()
+
+    @pl.when(has_in)
+    def _():
+        written(True)
+
+    @pl.when(jnp.logical_not(has_in))
+    def _():
+        written(False)
+
+
+def own_kernel(norm, own, w_in, w_out, work_in, work_out, sems):
+    write_sums(norm, lax.axis_index("core") == 0, own, w_in, w_out, work_in, work_out, sems)
+
+
+def other_kernel(norm, w_in_old, w_out_old, own, came, w_in, w_out, kernel_sum, gain_sum, scale_sum, work_in, work_out, sems):
     is_first = lax.axis_index("core") == 0
-    channels = own.shape[-1]
     hidden = w_out.shape[0]
-    for h in range(hidden // channels):
-        rows = slice(h * channels, (h + 1) * channels)
-        mine = own[rows, :].astype(F32) * norm
-        theirs = came[rows, :].astype(F32) * norm
-        w_in[:, rows] = jnp.where(is_first, mine, theirs)
-        w_out[rows, :] = jnp.where(is_first, theirs, mine).T
     extra = (own.shape[0] - hidden) // 2
     high, low = pl.ds(hidden, extra), pl.ds(hidden + extra, extra)
-    small = own[high, :].astype(F32) + own[low, :].astype(F32)
-    small = (small + (came[high, :].astype(F32) + came[low, :].astype(F32))) * norm
+    mine = (own[high, :].astype(F32) + own[low, :].astype(F32)) * norm
+    theirs = (came[high, :].astype(F32) + came[low, :].astype(F32)) * norm
+    small = jnp.concatenate([jnp.where(is_first, mine, theirs), jnp.where(is_first, theirs, mine)])
     for above in range(KSIZE):
         kernel_sum[above] = small[above * KSIZE : (above + 1) * KSIZE, :]
     gain_sum[...] = small[KSIZE * KSIZE : KSIZE * KSIZE + 1, :]
     scale_sum[...] = small[KSIZE * KSIZE + 1 : KSIZE * KSIZE + 2, :]
+    write_sums(norm, jnp.logical_not(is_first), came, w_in, w_out, work_in, work_out, sems)
 
 
 def pairs_of(kind):
@@ -572,13 +593,28 @@
     send[...] = mine[half_rows(1 - bit_here(following), rows // 2), :].astype(BF16)
 
 
-def turn_kernel(stage, whole, came, *refs):
-    small, payload = refs[:-1], refs[-1]
-    rows = came.shape[0]
+def pack_kernel(gain_part, scale_part, *refs):
+    taps, (keep, send, work) = refs[:-3], refs[-3:]
+    half = keep.shape[0]
+    work[...] = jnp.zeros_like(work)
+    for part, ref in enumerate(taps):
+        work[pl.ds(0, ref.shape[0]), part * LANES : (part + 1) * LANES] = ref[...]
+    work[pl.ds(KSIZE * KSIZE, 1), :] = jnp.sum(gain_part[...], axis=0, keepdims=True)
+    work[pl.ds(KSIZE * KSIZE + 1, 1), :] = jnp.sum(scale_part[...], axis=0, keepdims=True)
+    core = lax.axis_index("core")
+    keep[...] = work[half_rows(core, half), :]
+    value = work[half_rows(1 - core, half), :]
+    high = value.astype(BF16)
+    send[pl.ds(0, half), :] = high
+    send[pl.ds(half, half), :] = (value - high.astype(F32)).astype(BF16)
+
+
+def turn_kernel(stage, whole, came, keep, extra, payload):
+    rows, half = came.shape[0], keep.shape[0]
     share = whole[half_rows(bit_here(stage), rows), :] + came[...].astype(F32)
     payload[pl.ds(0, rows), :] = share.astype(BF16)
-    for part, ref in enumerate(small):
-        payload[pl.ds(rows, ref.shape[0]), part * LANES : (part + 1) * LANES] = ref[...].astype(BF16)
+    small = keep[...] + (extra[pl.ds(0, half), :].astype(F32) + extra[pl.ds(half, half), :].astype(F32))
+    payload[pl.ds(rows, half), :] = small.astype(BF16)
 
 
 def add_kernel(own, came, payload):
@@ -609,7 +645,7 @@
     return mine, send
 
 
-def call(kernel, outs, scratch, hbm, vmem, copies=0, micros=1.0, after=(), limit=20):
+def call(kernel, outs, scratch, hbm, vmem, copies=0, micros=1.0, after=(), limit=20, in_hbm=0, aliases=None):
     in_specs = [pl.BlockSpec(memory_space=pl.ANY)] * len(hbm)
     in_specs += [pl.BlockSpec(memory_space=pltpu.VMEM)] * len(vmem)
     in_specs += [pl.BlockSpec(memory_space=pl.ANY)] * len(after)
@@ -625,7 +661,8 @@
         body,
         out_shape=[jax.ShapeDtypeStruct(*out) for out in outs],
         in_specs=in_specs,
-        out_specs=[pl.BlockSpec(memory_space=pltpu.VMEM)] * len(outs),
+        out_specs=[pl.BlockSpec(memory_space=pl.ANY if at < in_hbm else pltpu.VMEM) for at in range(len(outs))],
+        input_output_aliases=aliases or {},
         scratch_shapes=shapes,
         cost_estimate=pl.CostEstimate(flops=int(micros * 1e9), bytes_accessed=0, transcendentals=0),
         compiler_params=pltpu.CompilerParams(vmem_limit_bytes=limit * 1024 * 1024),
@@ -685,13 +722,10 @@
         [count_s, ocean_s, taps, ((parts, shape.early * shape.columns, LANES), F32), whole],
         [block_count, ocean], [taps_in, gain, w_out, scale, tangent, band], 2, 5.0,
     )
-    keep, give, activated, dpreact, yhat, inverse = call(
+    keep, give, activated, dpreact, yhat, inverse, top = call(
         bind(late_kernel),
-        [((hidden, channels), F32), ((hidden, channels), BF16), wide, wide, whole_f, narrow],
-        [
-            count_s, taps, strip(late + 2 * HALF), ((parts, late * shape.columns, LANES), F32), whole, flat,
-            ends_f,
-        ],
+        [((hidden, channels), F32), ((hidden, channels), BF16), wide, wide, whole_f, narrow, strip(late + 2 * HALF)],
+        [count_s, taps, ((parts, late * shape.columns, LANES), F32), whole, flat, ends_f],
         [block_count],
         [taps_in, gain, w_in, band, fold, rims, normed, yhat, inverse, dproj_t, dact], 1, 5.0,
     )
@@ -707,12 +741,20 @@
     def taps_part(part, after):
         (small,) = call(
             functools.partial(taps_kernel, shape, part), [((small_rows, LANES), F32)],
-            [count_s, ((1, (TILE + 2 * HALF) * pitch, LANES), F32), ((1, TILE * pitch, LANES), F32), ends_f],
-            [block_count], [band, fold, rims, conv_grad, gain_part, scale_part], 1, 1.8, after=after,
+            [((1, (TILE + 2 * HALF) * pitch, LANES), F32), ((1, TILE * pitch, LANES), F32)],
+            [], [band, top, conv_grad], 0, 1.8, after=after,
         )
         return small
 
-    small_rows = -(-(KSIZE * KSIZE + 2) // 16) * 16
+    def back_part(part, before, after):
+        outs = [(((TILE + HALF) * pitch, LANES), F32)] + [turned] * (part == parts - 1)
+        return call(
+            functools.partial(back_kernel, shape, part), outs,
+            [count_s, ((1, TILE * pitch, LANES), F32), ((1, KSIZE * KSIZE, 8, LANES), F32)],
+            [block_count], [taps_in, conv_grad, *before], 1, 2.0, after=after,
+        )
+
+    small_rows = -(-(KSIZE * KSIZE + 2) // 32) * 32
     came = core_swap(give)
     conv_grad, gain_part = call(
         bind(norm_grad_kernel), [whole, eight], [], [], [w_in, gain, dpreact, yhat, inverse], 0, 1.0,
@@ -722,41 +764,54 @@
         [((hidden, channels), F32), ((rows, channels), BF16)], [], [], [keep, came], after=[conv_grad], micros=0.3,
     )
     came = bit_swap(send, order[0])
+    taps_parts = [taps_part(0, [send])]
     state, scale_part = call(
         bind(state_kernel), [whole, eight], [count_s, ocean_s],
-        [block_count, ocean], [fields, tangent, w_out, scale, activated], 2, 1.5, after=[send],
-    )
-    small = [taps_part(0, [send])]
+        [block_count, ocean], [fields, tangent, w_out, scale, activated], 2, 1.5, after=taps_parts,
+    )
     body, outs = half_step(0, rows)
-    mine, send = call(body, outs, [], [], [mine, came], after=small, micros=0.3)
+    mine, send = call(body, outs, [], [], [mine, came], after=[scale_part], micros=0.3)
     came = bit_swap(send, order[1])
-    small += [taps_part(part, [send]) for part in range(1, parts)]
+    taps_parts += [taps_part(part, [send]) for part in range(1, parts)]
+    small_rows //= 2
+    small, extra = call(
+        pack_kernel, [((small_rows, channels), F32), ((2 * small_rows, channels), BF16)],
+        [((2 * small_rows, channels), F32)], [], [gain_part, scale_part, *taps_parts], micros=0.3,
+    )
     rows //= 2
     body, outs = half_step(1, rows)
-    mine, send = call(body, outs, [], [], [mine, came], after=small[1:], micros=0.3)
+    mine, send = call(body, outs, [], [], [mine, came], after=[small], micros=0.3)
+    extra = core_swap(extra)
     mine, send = halved(mine, send, order[2:-1])
     came = bit_swap(send, order[-2])
+    core_grad = []
+    for part in range(parts - 1):
+        core_grad += back_part(part, core_grad, [send])
     rows = came.shape[0]
     if rows % 16 == 0:
         (payload,) = call(
             functools.partial(turn_kernel, order[-2]), [((rows + small_rows, channels), BF16)],
-            [], [], [mine, came, *small], micros=0.3,
+            [], [], [mine, came, small, extra], after=core_grad, micros=0.3,
         )
     else:
         bit = bit_here(order[-2])
         share = lax.dynamic_index_in_dim(mine.reshape(2, rows, channels), bit, 0, keepdims=False)
-        payload = jnp.concatenate([share + came.astype(F32), jnp.concatenate(small, axis=1)]).astype(BF16)
+        small = small + (extra[:small_rows].astype(F32) + extra[small_rows:].astype(F32))
+        payload = jnp.concatenate([share + came.astype(F32), small]).astype(BF16)
     came = bit_swap(payload, order[-1])
-    core_grad, fold_back = call(
-        bind(back_kernel), [strip(TILE + HALF), turned], [count_s, strip(TILE), taps],
-        [block_count], [taps_in, conv_grad], 1, 4.0, after=[payload],
-    )
+    last_grad, fold_back = back_part(parts - 1, core_grad, [payload])
+    core_grad += [last_grad]
+    fold_back = swap(fold_back, "fold")
     (payload,) = call(
-        add_kernel, [(payload.shape, BF16)], [], [], [payload, came], after=[fold_back], micros=0.3,
-    )
-    fold_back = swap(fold_back, "fold")
+        add_kernel, [(payload.shape, BF16)], [], [], [payload, came], after=[last_grad], micros=0.3,
+    )
     came = bit_swap(payload, order[-2])
-    after = []
+    folded, first, second = call(
+        bind(rims_kernel), [strip(TILE), edge, edge], [count_s], [block_count], [fold_back, *core_grad], 1, 1.0,
+        after=[payload],
+    )
+    first, second = swap(first, "first"), swap(second, "second")
+    after = [folded]
     for at in reversed(range(len(order) - 1)):
         copies = 2 if at == 0 else 1
         if rows % 16 == 0:
@@ -766,32 +821,29 @@
                 [], [], [payload, came], after=after, micros=0.3,
             )
         else:
-            first = bit_here(order[at]) == 0
+            is_low = bit_here(order[at]) == 0
             low, high = payload[:rows], came[:rows]
             both = payload[rows:].astype(F32) + came[rows:].astype(F32)
-            joined = [jnp.where(first, low, high), jnp.where(first, high, low), both.astype(BF16)]
+            joined = [jnp.where(is_low, low, high), jnp.where(is_low, high, low), both.astype(BF16)]
             payload = jnp.concatenate(joined)
         after = []
         rows *= 2
         came = bit_swap(payload, order[at - 1]) if at else core_swap(payload)
         if at == 2:
-            folded, first, second = call(
-                bind(rims_kernel), [strip(TILE), edge, edge], [count_s], [block_count], [core_grad, fold_back], 1, 1.0,
-                after=[payload],
-            )
-            after = [folded]
-            first, second = swap(first, "first"), swap(second, "second")
-        if at == 1:
             grad_fields, done = call(
                 bind(final_kernel), [whole, ((8, LANES), F32)], [count_s, ocean_s, strip(TILE)],
                 [block_count, ocean], [tangent, folded, first, second], 2, 1.5, after=[payload],
             )
             after = [done]
     total = samples * lax.axis_size("dp") * slots * lax.axis_size(TILES) * tile_rows * tile_cols
+    norm = total ** (-0.5)
+    sums = [((channels, hidden), F32), ((hidden, channels), F32)]
+    w_in_sum, w_out_sum = call(
+        functools.partial(own_kernel, norm), sums, sums, [], [payload], hidden // channels, 1.0, in_hbm=2,
+    )
     w_in_sum, w_out_sum, kernel_sum, gain_sum, scale_sum = call(
-        functools.partial(unpack_kernel, total ** (-0.5)),
-        [((channels, hidden), F32), ((hidden, channels), F32), (kernel.shape, F32), row, row],
-        [], [], [payload, came], 0, 1.5,
+        functools.partial(other_kernel, norm), sums + [(kernel.shape, F32), row, row], sums,
+        [w_in_sum, w_out_sum], [payload, came], hidden // channels, 1.0, in_hbm=2, aliases={0: 0, 1: 1},
     )
     return (
         state.reshape(grid),

time: 67.6 us -> 67.6 us (level)
  waiting for transfers between devices: 18.2 us -> 21.9 us
  starting transfers between devices: 20 us -> 16.6 us
    ppermute x7, waiting for transfers between devices: 10.3 us -> 15.7 us  [bit_swap(): return lax.ppermute(block, ('chips', 'core', 'dp'), pairs)]
    ppermute x7, starting transfers between devices: 7.41 us -> 4.91 us  [bit_swap(): return lax.ppermute(block, ('chips', 'core', 'dp'), pairs)]
    ppermute x2 -> x3, starting transfers between devices: 1.57 us -> 0.21 us  [core_swap(): return lax.ppermute(block, 'core', [(0, 1), (1, 0)])]
    ppermute x7, waiting for transfers between devices: 5.19 us -> 4.24 us  [swap(): return lax.ppermute(block, TILES, pairs_of(kind))]
    ppermute x2 -> x3, waiting for transfers between devices: 2.73 us -> 2.03 us  [core_swap(): return lax.ppermute(block, 'core', [(0, 1), (1, 0)])]
    pallas_call x21 -> x24, Pallas kernels: 26.6 us -> 26.4 us  [call(): pl.pallas_call(body, out_shape=[jax.ShapeDtypeStruct(*out) for out in out...]
  transfers between devices with their start and end apart: 16 -> 17, of which waited for: 10 -> 11; matrix products, arithmetic and copies ran while one was open for 0% -> 0% of each run, Pallas kernels for 29% -> 28%
where the time goes in v3:
time: 67.6 us; the launch traced here: 67.5 us
  Pallas kernels  26.4 us (39%)
  waiting for transfers between devices  21.9 us (32%)
  starting transfers between devices  16.6 us (25%)
  between operations  1.59 us (2%)
  local copies, waits for them, and re-layouts  1.04 us (2%)
    pallas_call x24, Pallas kernels, call(): pl.pallas_call(body, out_shape=[jax.ShapeDtypeStruct(*out) for out in out...  26.4 us
    ppermute x7, waiting for transfers between devices, bit_swap(): return lax.ppermute(block, ('chips', 'core', 'dp'), pairs)  15.7 us
    ppermute x7, starting transfers between devices, swap(): return lax.ppermute(block, TILES, pairs_of(kind))  11.4 us
    ppermute x7, starting transfers between devices, bit_swap(): return lax.ppermute(block, ('chips', 'core', 'dp'), pairs)  4.91 us
    ppermute x7, waiting for transfers between devices, swap(): return lax.ppermute(block, TILES, pairs_of(kind))  4.24 us
    ppermute x3, waiting for transfers between devices, core_swap(): return lax.ppermute(block, 'core', [(0, 1), (1, 0)])  2.03 us
  transfers between devices with their start and end apart: 17, of which 11 were waited for; matrix products, arithmetic and copies ran while one was open for 0% of the time, Pallas kernels for 28%

profile of v3, /device:TPU:0, one launch (start us, length us, event | category | flops | bytes accessed | tf_op | source)
XLA Modules:
  0.0 67.5 jit_solution(9930063389964735646)
XLA Ops:
  1.3 0.0 copy-start.2
  1.3 1.0 %copy-done.2 = bf16[1,3,16,16,256]{4,3,2,1,0:T(8,128)(2,1)S(1)} copy-done((bf16[1,3,16,16,256]{4,3,2,1,0:T(8,128)(2,1)S(1)}, bf16[1,3,16,16,256]{4,3,2,1,0:T(8,128)(2,1)}, u32[]{:S(2)}) %copy-start.2) | copy-done | bytes 393240
  2.3 0.6 shard_map.144
  2.9 4.1 %collective-permute-start.1 = (bf16[48,256]{1,0:T(8,128)(2,1)S(1)}, bf16[48,256]{1,0:T(8,128)(2,1)S(1)}, u32[]{:S(2)}, u32[]{:S(2)}) collective-permute-start(bf16[48,256]{1,0:T(8,128)(2,1)S(1)} %get-tuple-element.50), channel_id=1, source_target_pairs={{0,16},{2,4},{4,2},{6,8},{8,6},{10,12},{12,10},{14,30},{30,14},{28... | collective-permute-start | bytes 73736 | tf_op jit(solution)/shard_map/ppermute | solution.py:546
  7.0 0.7 %shard_map.145.refs_5_ = bf16[144,256]{1,0:T(8,128)(2,1)S(1)} custom-call(s32[1]{0:T(128)S(6)} %copy.20.refs_0_, s32[3]{0:T(128)S(1)} %copy-done.8, bf16[768,256]{1,0:T(8,128)(2,1)S(1)} %bitcast.9, bf16[48,256]{1,0:T(8,128)(2,1)S(1)} %get-tuple-element.49.refs_3_), custom_call_target="tpu_custom_call" | custom-call | flops 500000000 | tf_op jit(solution)/shard_map/pallas_call | solution.py:660
  7.7 0.0 copy-start.1
  7.8 1.7 %collective-permute-start.2 = (bf16[144,256]{1,0:T(8,128)(2,1)S(1)}, bf16[144,256]{1,0:T(8,128)(2,1)S(1)}, u32[]{:S(2)}, u32[]{:S(2)}) collective-permute-start(bf16[144,256]{1,0:T(8,128)(2,1)S(1)} %shard_map.145.refs_5_), channel_id=1, source_target_pairs={{0,16},{2,18},{4,20},{6,22},{8,24},{10,26},{12,28},{14,30},{30,14}... | collective-permute-start | bytes 221192 | tf_op jit(solution)/shard_map/ppermute | solution.py:546
  9.4 0.7 %shard_map.146 = (f32[2,1216,128]{2,1,0:T(8,128)S(1)}, bf16[48,256]{1,0:T(8,128)(2,1)S(1)}) custom-call(s32[1]{0:T(128)S(6)} %copy.20.refs_0_, s32[3]{0:T(128)S(1)} %copy-done.8, bf16[768,256]{1,0:T(8,128)(2,1)S(1)} %bitcast.10, bf16[48,256]{1,0:T(8,128)(2,1)S(1)} %collective-permute-done.refs_3_, bf16[48,256]{1,0:T(8,128)(2,1)S(1)} %collective-permute-done.1.refs_4_, ...), custom_call_target="tpu_custom_call" | custom-call | flops 1000000000 | tf_op jit(solution)/shard_map/pallas_call | solution.py:660
  10.2 2.3 %collective-permute-start.3 = (bf16[48,256]{1,0:T(8,128)(2,1)S(1)}, bf16[48,256]{1,0:T(8,128)(2,1)S(1)}, u32[]{:S(2)}, u32[]{:S(2)}) collective-permute-start(bf16[48,256]{1,0:T(8,128)(2,1)S(1)} %get-tuple-element.52), channel_id=1, source_target_pairs={{0,16},{2,18},{4,20},{6,22},{8,24},{10,26},{12,28},{14,30},{30,14}... | collective-permute-start | bytes 73736 | tf_op jit(solution)/shard_map/ppermute | solution.py:546
  12.6 4.2 %shard_map.147 = (bf16[768,256]{1,0:T(8,128)(2,1)S(1)}, f32[768,256]{1,0:T(8,128)S(1)}, f32[768,128]{1,0:T(8,128)S(1)}, bf16[256,768]{1,0:T(8,128)(2,1)S(1)}, f32[768,1024]{1,0:T(8,128)S(1)}) custom-call(s32[1]{0:T(128)S(6)} %copy.20.refs_0_, s32[3]{0:T(128)S(1)} %copy-done.8, bf16[7,7,256]{2,1,0:T(8,128)(2,1)S(1)} %copy-done.5, f32[1,256]{1,0:T(1,128)S(1)} %bitcast.15, ...), custom_call_target="tpu_custom_call" | custom-call | flops 5000000000 | tf_op jit(solution)/shard_map/pallas_call | solution.py:660
  16.7 4.8 %shard_map.148 = (f32[1024,256]{1,0:T(8,128)S(1)}, bf16[1024,256]{1,0:T(8,128)(2,1)S(1)}, bf16[768,1024]{1,0:T(8,128)(2,1)S(1)}, bf16[768,1024]{1,0:T(8,128)(2,1...) custom-call(s32[1]{0:T(128)S(6)} %copy.20.refs_0_, ...), custom_call_target="tpu_custom_call" | custom-call | flops 5000000000 | tf_op jit(solution)/shard_map/pallas_call | solution.py:660
  21.5 0.1 collective-permute-start.4
  21.6 0.8 %shard_map.149 = (bf16[768,256]{1,0:T(8,128)(2,1)S(1)}, f32[8,256]{1,0:T(8,128)S(1)}) custom-call(bf16[256,1024]{1,0:T(8,128)(2,1)S(1)} %copy-done, f32[1,256]{1,0:T(1,128)S(1)} %bitcast.17, bf16[768,1024]{1,0:T(8,128)(2,1)S(1)} %get-tuple-element.60.refs_2_, f32[768,256]{1,0:T(8,128)S(1)} %get-tuple-element.61.refs_3_, f32[768,128]{1,0:T(8,128)S(1)} %get-tuple-element.62.refs_4_), custom_call_target="tpu_custom_call" | custom-call | flops 1000000000 | tf_op jit(solution)/shard_map/pallas_call | solution.py:660
  22.4 1.1 %collective-permute-done.4.refs_1_ = bf16[1024,256]{1,0:T(8,128)(2,1)S(1)} collective-permute-done((bf16[1024,256]{1,0:T(8,128)(2,1)S(1)}, bf16[1024,256]{1,0:T(8,128)(2,1)S(1)}, u32[]{:S(2)}, u32[]{:S(2)}) %collective-permute-start.4) | collective-permute-done | bytes 524320 | tf_op jit(solution)/shard_map/ppermute | solution.py:550
  23.5 0.2 shard_map.150
  23.7 0.2 collective-permute-start.5
  23.8 1.8 %shard_map.151.refs_7_.refs_2_ = f32[64,128]{1,0:T(8,128)S(1)} custom-call(f32[2,1216,128]{2,1,0:T(8,128)S(1)} %get-tuple-element.51.refs_7_.refs_4_.refs_0_, f32[2,640,128]{2,1,0:T(8,128)S(1)} %get-tuple-element.59.refs_1_, bf16[768,256]{1,0:T(8,128)(2,1)S(1)} %get-tuple-element.63.refs_2_, bf16[512,256]{1,0:T(8,128)(2,1)S(1)} %get-tuple-element.66.refs_3_), custom_call_target="tpu_custom_call" | custom-call | flops 1800000000 | tf_op jit(solution)/shard_map/pallas_call | solution.py:660
  25.6 2.0 %shard_map.152 = (bf16[768,256]{1,0:T(8,128)(2,1)}, f32[8,256]{1,0:T(8,128)S(1)}) custom-call(s32[1]{0:T(128)S(6)} %copy.20.refs_0_, s32[3]{0:T(128)S(1)} %copy-done.8, bf16[768,256]{1,0:T(8,128)(2,1)S(1)} %bitcast.11, bf16[768,256]{1,0:T(8,128)(2,1)S(1)} %bitcast.13, bf16[1024,256]{1,0:T(8,128)(2,1)S(1)} %copy-done.1, f32[1,256]{1,0:T(1,128)S(1)} %bitcast.19, ...), custom_call_target="tpu_custom_call" | custom-call | flops 1500000000 | tf_op jit(solution)/shard_map/pallas_call | solution.py:660
  27.6 2.5 %collective-permute-done.5.refs_1_ = bf16[512,256]{1,0:T(8,128)(2,1)S(1)} collective-permute-done((bf16[512,256]{1,0:T(8,128)(2,1)S(1)}, bf16[512,256]{1,0:T(8,128)(2,1)S(1)}, u32[]{:S(2)}, u32[]{:S(2)}) %collective-permute-start.5) | collective-permute-done | bytes 262176 | tf_op jit(solution)/shard_map/ppermute | solution.py:570
  30.1 0.1 shard_map.153
  30.2 1.6 %collective-permute-start.6 = (bf16[256,256]{1,0:T(8,128)(2,1)S(1)}, bf16[256,256]{1,0:T(8,128)(2,1)S(1)}, u32[]{:S(2)}, u32[]{:S(2)}) collective-permute-start(bf16[256,256]{1,0:T(8,128)(2,1)S(1)} %get-tuple-element.71.refs_3_), channel_id=1, source_target_pairs={{0,1},{1,0},{2,6},{3,7},{4,5},{5,4},{6,2},{7,3},{8,9},{9,8},{10,14... | collective-permute-start | bytes 393224 | tf_op jit(solution)/shard_map/ppermute | solution.py:570
  31.8 1.8 %shard_map.154.refs_3_ = f32[64,128]{1,0:T(8,128)S(1)} custom-call(f32[2,1216,128]{2,1,0:T(8,128)S(1)} %get-tuple-element.51.refs_7_.refs_4_.refs_0_, f32[2,640,128]{2,1,0:T(8,128)S(1)} %get-tuple-element.59.refs_1_, bf16[768,256]{1,0:T(8,128)(2,1)S(1)} %get-tuple-element.63.refs_2_, bf16[256,256]{1,0:T(8,128)(2,1)S(1)} %get-tuple-element.71.refs_3_), custom_call_target="tpu_custom_call" | custom-call | flops 1800000000 | tf_op jit(solution)/shard_map/pallas_call | solution.py:660
  33.6 0.1 collective-permute-start.8
  33.6 1.6 %collective-permute-done.6.refs_1_ = bf16[256,256]{1,0:T(8,128)(2,1)S(1)} collective-permute-done((bf16[256,256]{1,0:T(8,128)(2,1)S(1)}, bf16[256,256]{1,0:T(8,128)(2,1)S(1)}, u32[]{:S(2)}, u32[]{:S(2)}) %collective-permute-start.6) | collective-permute-done | bytes 131104 | tf_op jit(solution)/shard_map/ppermute | solution.py:570
  35.2 1.1 %collective-permute-start.7 = (bf16[128,256]{1,0:T(8,128)(2,1)S(1)}, bf16[128,256]{1,0:T(8,128)(2,1)S(1)}, u32[]{:S(2)}, u32[]{:S(2)}) collective-permute-start(bf16[128,256]{1,0:T(8,128)(2,1)S(1)} %get-tuple-element.74.refs_3_), channel_id=1, source_target_pairs={{0,8},{1,9},{2,3},{3,2},{4,12},{5,13},{6,7},{7,6},{8,0},{9,1},{10,... | collective-permute-start | bytes 196616 | tf_op jit(solution)/shard_map/ppermute | solution.py:570
  36.3 1.7 %shard_map.157.refs_4_.refs_3_.refs_2_ = f32[1216,128]{1,0:T(8,128)S(1)} custom-call(s32[1]{0:T(128)S(6)} %copy.20.refs_0_, bf16[7,7,256]{2,1,0:T(8,128)(2,1)S(1)} %copy-done.5, bf16[768,256]{1,0:T(8,128)(2,1)S(1)} %get-tuple-element.63.refs_2_, bf16[128,256]{1,0:T(8,128)(2,1)S(1)} %get-tuple-element.74.refs_3_), custom_call_target="tpu_custom_call" | custom-call | flops 2000000000 | tf_op jit(solution)/shard_map/pallas_call | solution.py:660
  38.1 1.5 %collective-permute-done.7.refs_1_ = bf16[128,256]{1,0:T(8,128)(2,1)S(1)} collective-permute-done((bf16[128,256]{1,0:T(8,128)(2,1)S(1)}, bf16[128,256]{1,0:T(8,128)(2,1)S(1)}, u32[]{:S(2)}, u32[]{:S(2)}) %collective-permute-start.7) | collective-permute-done | bytes 65568 | tf_op jit(solution)/shard_map/ppermute | solution.py:570
  39.6 0.7 %collective-permute-start.10 = (bf16[160,256]{1,0:T(8,128)(2,1)S(1)}, bf16[160,256]{1,0:T(8,128)(2,1)S(1)}, u32[]{:S(2)}, u32[]{:S(2)}) collective-permute-start(bf16[160,256]{1,0:T(8,128)(2,1)S(1)} %shard_map.158.refs_4_.refs_0_), channel_id=1, source_target_pairs={{0,16},{1,17},{2,18},{3,19},{4,20},{5,21},{6,22},{7,23},{8,24},{9,... | collective-permute-start | bytes 245768 | tf_op jit(solution)/shard_map/ppermute | solution.py:570
  40.3 1.9 %shard_map.159 = (f32[1216,128]{1,0:T(8,128)S(1)}, bf16[192,256]{1,0:T(8,128)(2,1)S(1)}) custom-call(s32[1]{0:T(128)S(6)} %copy.20.refs_0_, bf16[7,7,256]{2,1,0:T(8,128)(2,1)S(1)} %copy-done.5, bf16[768,256]{1,0:T(8,128)(2,1)S(1)} %get-tuple-element.63.refs_2_, f32[1216,128]{1,0:T(8,128)S(1)} %shard_map.157.refs_4_.refs_3_.refs_2_, ...), custom_call_target="tpu_custom_call" | custom-call | flops 2000000000 | tf_op jit(solution)/shard_map/pallas_call | solution.py:660
  42.2 2.3 %collective-permute-start.9 = (bf16[192,256]{1,0:T(8,128)(2,1)S(1)}, bf16[192,256]{1,0:T(8,128)(2,1)S(1)}, u32[]{:S(2)}, u32[]{:S(2)}) collective-permute-start(bf16[192,256]{1,0:T(8,128)(2,1)S(1)} %get-tuple-element.77), channel_id=1, source_target_pairs={{0,16},{2,18},{4,20},{6,22},{8,24},{10,26},{12,28},{14,30},{30,14}... | collective-permute-start | bytes 294920 | tf_op jit(solution)/shard_map/ppermute | solution.py:546
  44.6 2.6 %collective-permute-done.10.refs_1_ = bf16[160,256]{1,0:T(8,128)(2,1)S(1)} collective-permute-done((bf16[160,256]{1,0:T(8,128)(2,1)S(1)}, bf16[160,256]{1,0:T(8,128)(2,1)S(1)}, u32[]{:S(2)}, u32[]{:S(2)}) %collective-permute-start.10) | collective-permute-done | bytes 81952 | tf_op jit(solution)/shard_map/ppermute | solution.py:570
  47.2 0.1 collective-permute-start.13
  47.3 2.0 %collective-permute-done.9.refs_1_ = bf16[192,256]{1,0:T(8,128)(2,1)S(1)} collective-permute-done((bf16[192,256]{1,0:T(8,128)(2,1)S(1)}, bf16[192,256]{1,0:T(8,128)(2,1)S(1)}, u32[]{:S(2)}, u32[]{:S(2)}) %collective-permute-start.9) | collective-permute-done | bytes 98336 | tf_op jit(solution)/shard_map/ppermute | solution.py:546
  49.3 0.6 shard_map.161
  49.9 0.1 collective-permute-start.11
  50.0 1.0 %collective-permute-start.12 = (bf16[48,256]{1,0:T(8,128)(2,1)S(1)}, bf16[48,256]{1,0:T(8,128)(2,1)S(1)}, u32[]{:S(2)}, u32[]{:S(2)}) collective-permute-start(bf16[48,256]{1,0:T(8,128)(2,1)S(1)} %get-tuple-element.81), channel_id=1, source_target_pairs={{0,16},{2,4},{4,2},{6,8},{8,6},{10,12},{12,10},{14,30},{30,14},{28... | collective-permute-start | bytes 73736 | tf_op jit(solution)/shard_map/ppermute | solution.py:546
  50.9 0.8 %collective-permute-done.13.refs_1_ = bf16[160,256]{1,0:T(8,128)(2,1)S(1)} collective-permute-done((bf16[160,256]{1,0:T(8,128)(2,1)S(1)}, bf16[160,256]{1,0:T(8,128)(2,1)S(1)}, u32[]{:S(2)}, u32[]{:S(2)}) %collective-permute-start.13) | collective-permute-done | bytes 81952 | tf_op jit(solution)/shard_map/ppermute | solution.py:570
  51.7 0.8 %collective-permute-start.14 = (bf16[288,256]{1,0:T(8,128)(2,1)S(1)}, bf16[288,256]{1,0:T(8,128)(2,1)S(1)}, u32[]{:S(2)}, u32[]{:S(2)}) collective-permute-start(bf16[288,256]{1,0:T(8,128)(2,1)S(1)} %shard_map.162.refs_6_.refs_0_), channel_id=1, source_target_pairs={{0,1},{1,0},{2,6},{3,7},{4,5},{5,4},{6,2},{7,3},{8,9},{9,8},{10,14... | collective-permute-start | bytes 442376 | tf_op jit(solution)/shard_map/ppermute | solution.py:570
  52.6 2.2 %collective-permute-done.12.refs_5_ = bf16[48,256]{1,0:T(8,128)(2,1)S(1)} collective-permute-done((bf16[48,256]{1,0:T(8,128)(2,1)S(1)}, bf16[48,256]{1,0:T(8,128)(2,1)S(1)}, u32[]{:S(2)}, u32[]{:S(2)}) %collective-permute-start.12) | collective-permute-done | bytes 24608 | tf_op jit(solution)/shard_map/ppermute | solution.py:546
  54.8 1.6 %shard_map.163 = (bf16[768,256]{1,0:T(8,128)(2,1)}, f32[8,128]{1,0:T(8,128)S(1)}) custom-call(s32[1]{0:T(128)S(6)} %copy.20.refs_0_, s32[3]{0:T(128)S(1)} %copy-done.8, bf16[768,256]{1,0:T(8,128)(2,1)S(1)} %bitcast.14, f32[2,1024,128]{2,1,0:T(8,128)S(1)} %get-tuple-element.79.refs_2_.refs_3_, bf16[48,256]{1,0:T(8,128)(2,1)S(1)} %collective-permute-done.11.refs_4_, ...), custom_call_target="tpu_custom_call" | custom-call | flops 1500000000 | tf_op jit(solution)/shard_map/pallas_call | solution.py:660
  56.4 0.5 collective-permute-done.14.refs_1_
  57.0 0.5 collective-permute-start.15
  57.5 6.1 %collective-permute-done.15.refs_1_ = bf16[544,256]{1,0:T(8,128)(2,1)S(1)} collective-permute-done((bf16[544,256]{1,0:T(8,128)(2,1)S(1)}, bf16[544,256]{1,0:T(8,128)(2,1)S(1)}, u32[]{:S(2)}, u32[]{:S(2)}) %collective-permute-start.15) | collective-permute-done | bytes 278560 | tf_op jit(solution)/shard_map/ppermute | solution.py:570
  63.6 0.1 shard_map.165.refs_0_.refs_2_
  63.7 0.1 collective-permute-start.16
  63.7 1.0 %shard_map.166 = (f32[256,1024]{1,0:T(8,128)}, f32[1024,256]{1,0:T(8,128)}) custom-call(bf16[1088,256]{1,0:T(8,128)(2,1)S(1)} %shard_map.165.refs_0_.refs_2_), custom_call_target="tpu_custom_call" | custom-call | flops 1000000000 | tf_op jit(solution)/shard_map/pallas_call | solution.py:660
  64.8 0.9 %collective-permute-done.16.refs_3_ = bf16[1088,256]{1,0:T(8,128)(2,1)S(1)} collective-permute-done((bf16[1088,256]{1,0:T(8,128)(2,1)S(1)}, bf16[1088,256]{1,0:T(8,128)(2,1)S(1)}, u32[]{:S(2)}, u32[]{:S(2)}) %collective-permute-start.16) | collective-permute-done | bytes 557088 | tf_op jit(solution)/shard_map/ppermute | solution.py:550
  65.7 1.8 %shard_map.167 = (f32[256,1024]{1,0:T(8,128)}, f32[1024,256]{1,0:T(8,128)}, f32[7,7,256]{2,1,0:T(8,128)}, f32[1,256]{1,0:T(1,128)}, f32[1,256]{1,0:T(1,128)}) custom-call(f32[256,1024]{1,0:T(8,128)} %get-tuple-element.84.refs_0_, f32[1024,256]{1,0:T(8,128)} %get-tuple-element.85.refs_1_, ...), custom_call_target="tpu_custom_call", output_to_operand_aliasing={{0}: (0, {}), {1}: (1, {})} | custom-call | flops 1000000000 | tf_op jit(solution)/shard_map/pallas_call | solution.py:660
  (28 shorter events, 0.2 us)
Async XLA Ops:
  1.3 1.0 %copy-start.2 = (bf16[1,3,16,16,256]{4,3,2,1,0:T(8,128)(2,1)S(1)}, bf16[1,3,16,16,256]{4,3,2,1,0:T(8,128)(2,1)}, u32[]{:S(2)}) copy-start(bf16[1,3,16,16,256]{4,3,2,1,0:T(8,128)(2,1)} %param.9) | copy-start | bytes 1179652
  2.3 4.7 %copy-start.8 = (s32[3]{0:T(128)S(1)}, s32[3]{0:T(128)}, u32[]{:S(2)}) copy-start(s32[3]{0:T(128)} %refs_1_.15) | copy-start | bytes 40
  2.9 6.6 %collective-permute-start.1 = (bf16[48,256]{1,0:T(8,128)(2,1)S(1)}, bf16[48,256]{1,0:T(8,128)(2,1)S(1)}, u32[]{:S(2)}, u32[]{:S(2)}) collective-permute-start(bf16[48,256]{1,0:T(8,128)(2,1)S(1)} %get-tuple-element.50), channel_id=1, source_target_pairs={{0,16},{2,4},{4,2},{6,8},{8,6},{10,12},{12,10},{14,30},{30,14},{28... | collective-permute-start | bytes 73736 | tf_op jit(solution)/shard_map/ppermute | solution.py:546
  7.0 2.5 %collective-permute-start = (bf16[48,256]{1,0:T(8,128)(2,1)S(1)}, bf16[48,256]{1,0:T(8,128)(2,1)S(1)}, u32[]{:S(2)}, u32[]{:S(2)}) collective-permute-start(bf16[48,256]{1,0:T(8,128)(2,1)S(1)} %get-tuple-element.49.refs_3_), channel_id=1, source_target_pairs={{0,2},{2,0},{4,6},{6,4},{8,10},{10,8},{12,14},{14,12},{30,28},{28,... | collective-permute-start | bytes 73736 | tf_op jit(solution)/shard_map/ppermute | solution.py:546
  7.7 4.8 %copy-start.1 = (bf16[1024,256]{1,0:T(8,128)(2,1)S(1)}, bf16[1024,256]{1,0:T(8,128)(2,1)}, u32[]{:S(2)}) copy-start(bf16[1024,256]{1,0:T(8,128)(2,1)} %refs_4_.3) | copy-start | bytes 1572868
  7.7 4.8 %copy-start.4 = (bf16[1,3,16,16,256]{4,3,2,1,0:T(8,128)(2,1)S(1)}, bf16[1,3,16,16,256]{4,3,2,1,0:T(8,128)(2,1)}, u32[]{:S(2)}) copy-start(bf16[1,3,16,16,256]{4,3,2,1,0:T(8,128)(2,1)} %param.10) | copy-start | bytes 1179652
  7.7 4.8 %copy-start.5 = (bf16[7,7,256]{2,1,0:T(8,128)(2,1)S(1)}, bf16[7,7,256]{2,1,0:T(8,128)(2,1)}, u32[]{:S(2)}) copy-start(bf16[7,7,256]{2,1,0:T(8,128)(2,1)} %refs_1_.14) | copy-start | bytes 75268
  7.7 4.8 %copy-start.6 = (f32[256]{0:T(256)S(1)}, f32[256]{0:T(256)}, u32[]{:S(2)}) copy-start(f32[256]{0:T(256)} %param.14) | copy-start | bytes 3076
  7.8 4.8 %copy-start.7 = (f32[256]{0:T(256)S(1)}, f32[256]{0:T(256)}, u32[]{:S(2)}) copy-start(f32[256]{0:T(256)} %param.17) | copy-start | bytes 3076
  7.8 9.0 %collective-permute-start.2 = (bf16[144,256]{1,0:T(8,128)(2,1)S(1)}, bf16[144,256]{1,0:T(8,128)(2,1)S(1)}, u32[]{:S(2)}, u32[]{:S(2)}) collective-permute-start(bf16[144,256]{1,0:T(8,128)(2,1)S(1)} %shard_map.145.refs_5_), channel_id=1, source_target_pairs={{0,16},{2,18},{4,20},{6,22},{8,24},{10,26},{12,28},{14,30},{30,14}... | collective-permute-start | bytes 221192 | tf_op jit(solution)/shard_map/ppermute | solution.py:546
  10.2 6.5 %collective-permute-start.3 = (bf16[48,256]{1,0:T(8,128)(2,1)S(1)}, bf16[48,256]{1,0:T(8,128)(2,1)S(1)}, u32[]{:S(2)}, u32[]{:S(2)}) collective-permute-start(bf16[48,256]{1,0:T(8,128)(2,1)S(1)} %get-tuple-element.52), channel_id=1, source_target_pairs={{0,16},{2,18},{4,20},{6,22},{8,24},{10,26},{12,28},{14,30},{30,14}... | collective-permute-start | bytes 73736 | tf_op jit(solution)/shard_map/ppermute | solution.py:546
  12.5 4.2 %copy-start = (bf16[256,1024]{1,0:T(8,128)(2,1)S(1)}, bf16[256,1024]{1,0:T(8,128)(2,1)}, u32[]{:S(2)}) copy-start(bf16[256,1024]{1,0:T(8,128)(2,1)} %refs_0_.11) | copy-start | bytes 1572868
  21.5 2.0 %collective-permute-start.4 = (bf16[1024,256]{1,0:T(8,128)(2,1)S(1)}, bf16[1024,256]{1,0:T(8,128)(2,1)S(1)}, u32[]{:S(2)}, u32[]{:S(2)}) collective-permute-start(bf16[1024,256]{1,0:T(8,128)(2,1)S(1)} %get-tuple-element.65), channel_id=1, source_target_pairs={{0,2},{2,0},{1,3},{3,1},{4,6},{6,4},{5,7},{7,5},{8,10},{10,8},{9,1... | collective-permute-start | bytes 1572872 | tf_op jit(solution)/shard_map/ppermute | solution.py:550
  23.7 6.4 %collective-permute-start.5 = (bf16[512,256]{1,0:T(8,128)(2,1)S(1)}, bf16[512,256]{1,0:T(8,128)(2,1)S(1)}, u32[]{:S(2)}, u32[]{:S(2)}) collective-permute-start(bf16[512,256]{1,0:T(8,128)(2,1)S(1)} %get-tuple-element.66.refs_3_), channel_id=1, source_target_pairs={{0,4},{1,5},{2,10},{3,11},{4,0},{5,1},{6,14},{7,15},{8,12},{9,13},... | collective-permute-start | bytes 786440 | tf_op jit(solution)/shard_map/ppermute | solution.py:570
  23.8 1.8 %copy-start.3 = (bf16[1,3,16,16,256]{4,3,2,1,0:T(8,128)(2,1)S(1)}, bf16[1,3,16,16,256]{4,3,2,1,0:T(8,128)(2,1)}, u32[]{:S(2)}) copy-start(bf16[1,3,16,16,256]{4,3,2,1,0:T(8,128)(2,1)} %param.9) | copy-start | bytes 1179652
  30.2 5.0 %collective-permute-start.6 = (bf16[256,256]{1,0:T(8,128)(2,1)S(1)}, bf16[256,256]{1,0:T(8,128)(2,1)S(1)}, u32[]{:S(2)}, u32[]{:S(2)}) collective-permute-start(bf16[256,256]{1,0:T(8,128)(2,1)S(1)} %get-tuple-element.71.refs_3_), channel_id=1, source_target_pairs={{0,1},{1,0},{2,6},{3,7},{4,5},{5,4},{6,2},{7,3},{8,9},{9,8},{10,14... | collective-permute-start | bytes 393224 | tf_op jit(solution)/shard_map/ppermute | solution.py:570
  33.6 4.5 %collective-permute-start.8 = (bf16[64,256]{1,0:T(8,128)(2,1)S(1)}, bf16[64,256]{1,0:T(8,128)(2,1)S(1)}, u32[]{:S(2)}, u32[]{:S(2)}) collective-permute-start(bf16[64,256]{1,0:T(8,128)(2,1)S(1)} %get-tuple-element.76), channel_id=1, source_target_pairs={{0,2},{2,0},{1,3},{3,1},{4,6},{6,4},{5,7},{7,5},{8,10},{10,8},{9,1... | collective-permute-start | bytes 98312 | tf_op jit(solution)/shard_map/ppermute | solution.py:550
  35.2 4.3 %collective-permute-start.7 = (bf16[128,256]{1,0:T(8,128)(2,1)S(1)}, bf16[128,256]{1,0:T(8,128)(2,1)S(1)}, u32[]{:S(2)}, u32[]{:S(2)}) collective-permute-start(bf16[128,256]{1,0:T(8,128)(2,1)S(1)} %get-tuple-element.74.refs_3_), channel_id=1, source_target_pairs={{0,8},{1,9},{2,3},{3,2},{4,12},{5,13},{6,7},{7,6},{8,0},{9,1},{10,... | collective-permute-start | bytes 196616 | tf_op jit(solution)/shard_map/ppermute | solution.py:570
  39.6 7.6 %collective-permute-start.10 = (bf16[160,256]{1,0:T(8,128)(2,1)S(1)}, bf16[160,256]{1,0:T(8,128)(2,1)S(1)}, u32[]{:S(2)}, u32[]{:S(2)}) collective-permute-start(bf16[160,256]{1,0:T(8,128)(2,1)S(1)} %shard_map.158.refs_4_.refs_0_), channel_id=1, source_target_pairs={{0,16},{1,17},{2,18},{3,19},{4,20},{5,21},{6,22},{7,23},{8,24},{9,... | collective-permute-start | bytes 245768 | tf_op jit(solution)/shard_map/ppermute | solution.py:570
  42.2 7.0 %collective-permute-start.9 = (bf16[192,256]{1,0:T(8,128)(2,1)S(1)}, bf16[192,256]{1,0:T(8,128)(2,1)S(1)}, u32[]{:S(2)}, u32[]{:S(2)}) collective-permute-start(bf16[192,256]{1,0:T(8,128)(2,1)S(1)} %get-tuple-element.77), channel_id=1, source_target_pairs={{0,16},{2,18},{4,20},{6,22},{8,24},{10,26},{12,28},{14,30},{30,14}... | collective-permute-start | bytes 294920 | tf_op jit(solution)/shard_map/ppermute | solution.py:546
  47.2 4.5 %collective-permute-start.13 = (bf16[160,256]{1,0:T(8,128)(2,1)S(1)}, bf16[160,256]{1,0:T(8,128)(2,1)S(1)}, u32[]{:S(2)}, u32[]{:S(2)}) collective-permute-start(bf16[160,256]{1,0:T(8,128)(2,1)S(1)} %shard_map.160.refs_4_.refs_0_), channel_id=1, source_target_pairs={{0,8},{1,9},{2,3},{3,2},{4,12},{5,13},{6,7},{7,6},{8,0},{9,1},{10,... | collective-permute-start | bytes 245768 | tf_op jit(solution)/shard_map/ppermute | solution.py:570
  49.9 2.6 %collective-permute-start.11 = (bf16[48,256]{1,0:T(8,128)(2,1)S(1)}, bf16[48,256]{1,0:T(8,128)(2,1)S(1)}, u32[]{:S(2)}, u32[]{:S(2)}) collective-permute-start(bf16[48,256]{1,0:T(8,128)(2,1)S(1)} %get-tuple-element.80), channel_id=1, source_target_pairs={{0,2},{2,0},{4,6},{6,4},{8,10},{10,8},{12,14},{14,12},{30,28},{28,... | collective-permute-start | bytes 73736 | tf_op jit(solution)/shard_map/ppermute | solution.py:546
  50.0 4.8 %collective-permute-start.12 = (bf16[48,256]{1,0:T(8,128)(2,1)S(1)}, bf16[48,256]{1,0:T(8,128)(2,1)S(1)}, u32[]{:S(2)}, u32[]{:S(2)}) collective-permute-start(bf16[48,256]{1,0:T(8,128)(2,1)S(1)} %get-tuple-element.81), channel_id=1, source_target_pairs={{0,16},{2,4},{4,2},{6,8},{8,6},{10,12},{12,10},{14,30},{30,14},{28... | collective-permute-start | bytes 73736 | tf_op jit(solution)/shard_map/ppermute | solution.py:546
  51.7 5.2 %collective-permute-start.14 = (bf16[288,256]{1,0:T(8,128)(2,1)S(1)}, bf16[288,256]{1,0:T(8,128)(2,1)S(1)}, u32[]{:S(2)}, u32[]{:S(2)}) collective-permute-start(bf16[288,256]{1,0:T(8,128)(2,1)S(1)} %shard_map.162.refs_6_.refs_0_), channel_id=1, source_target_pairs={{0,1},{1,0},{2,6},{3,7},{4,5},{5,4},{6,2},{7,3},{8,9},{9,8},{10,14... | collective-permute-start | bytes 442376 | tf_op jit(solution)/shard_map/ppermute | solution.py:570
  57.0 6.6 %collective-permute-start.15 = (bf16[544,256]{1,0:T(8,128)(2,1)S(1)}, bf16[544,256]{1,0:T(8,128)(2,1)S(1)}, u32[]{:S(2)}, u32[]{:S(2)}) collective-permute-start(bf16[544,256]{1,0:T(8,128)(2,1)S(1)} %shard_map.164.refs_0_), channel_id=1, source_target_pairs={{0,4},{1,5},{2,10},{3,11},{4,0},{5,1},{6,14},{7,15},{8,12},{9,13},... | collective-permute-start | bytes 835592 | tf_op jit(solution)/shard_map/ppermute | solution.py:570
  63.7 2.0 %collective-permute-start.16 = (bf16[1088,256]{1,0:T(8,128)(2,1)S(1)}, bf16[1088,256]{1,0:T(8,128)(2,1)S(1)}, u32[]{:S(2)}, u32[]{:S(2)}) collective-permute-start(bf16[1088,256]{1,0:T(8,128)(2,1)S(1)} %shard_map.165.refs_0_.refs_2_), channel_id=1, source_target_pairs={{0,2},{2,0},{1,3},{3,1},{4,6},{6,4},{5,7},{7,5},{8,10},{10,8},{9,1... | collective-permute-start | bytes 1671176 | tf_op jit(solution)/shard_map/ppermute | solution.py:550

commit v4 on v3

--- a/solution.py
+++ b/solution.py
@@ -234,7 +234,7 @@
                 normed[out, shape.lanes(part)] = (value * gain[:, shape.lanes(part)]).astype(BF16)
         return carry
 
-    lax.fori_loop(0, rows, one_row, 0, unroll=2)
+    lax.fori_loop(0, rows, one_row, 0, unroll=4)
 
 
 def early_kernel(
@@ -262,7 +262,7 @@
 def late_kernel(
     shape, count_hbm, kernel, gain, w_in, band, fold, rims, normed_in, yhat_in, inverse_in, dproj_t, dact,
     keep, give, activated, dpreact, yhat, inverse, padded,
-    count, taps, convolved, normed, normed_t, work, sems,
+    count, taps, convolved, normed, normed_t, work, pre, sems,
 ):
     fetch = Fetch(sems, (count_hbm, count))
     late = TILE - shape.early
@@ -286,23 +286,42 @@
         normed_t[:, slot * per_slot : (slot + 1) * per_slot] = normed[pl.ds(slot * per_slot, per_slot), :].T
     keeps_in = lax.axis_index("core") == 0
     block = shape.channels
-    for h in range(shape.hidden // block):
-        cols = slice(h * block, (h + 1) * block)
-        for slot in range(shape.slots):
-            rows = pl.ds(slot * per_slot, per_slot)
-            pre = dot(normed[rows, :], w_in[:, cols], 1, 0)
-            square = pre * pre
-            inner = pre * (GELU_C + (GELU_C * GELU_A) * square)
-            gate = 0.5 + 0.5 * jnp.tanh(inner)
-            activated[rows, cols] = (pre * gate).astype(BF16)
-            slope = pre * (2.0 * GELU_C + (6.0 * GELU_C * GELU_A) * square)
-            grown = gate + slope * (gate - gate * gate)
-            dpreact[rows, cols] = (dact[rows, cols] * grown).astype(BF16)
-        rows = slice(h * block, (h + 1) * block)
-        of_in = dot(normed_t[...], dpreact[:, cols], 1, 0)
-        of_out = dot(dproj_t[...], activated[:, cols], 1, 0)
-        keep[rows, :] = jnp.where(keeps_in, of_in, of_out)
-        give[rows, :] = jnp.where(keeps_in, of_out, of_in).astype(BF16)
+    blocks = shape.hidden // block
+
+    def span(h):
+        return slice(h * block, (h + 1) * block)
+
+    def expand(step):
+        h, slot = divmod(step, shape.slots)
+        pre[step % 3] = dot(normed[pl.ds(slot * per_slot, per_slot), :], w_in[:, span(h)], 1, 0)
+
+    def activate(step):
+        h, slot = divmod(step, shape.slots)
+        rows, cols = pl.ds(slot * per_slot, per_slot), span(h)
+        value = pre[step % 3]
+        square = value * value
+        gate = 0.5 + 0.5 * jnp.tanh(value * (GELU_C + (GELU_C * GELU_A) * square))
+        activated[rows, cols] = (value * gate).astype(BF16)
+        slope = value * (2.0 * GELU_C + (6.0 * GELU_C * GELU_A) * square)
+        grown = gate + slope * (gate - gate * gate)
+        dpreact[rows, cols] = (dact[rows, cols] * grown).astype(BF16)
+
+    def reduce_rows(h):
+        of_in = dot(normed_t[...], dpreact[:, span(h)], 1, 0)
+        of_out = dot(dproj_t[...], activated[:, span(h)], 1, 0)
+        keep[span(h), :] = jnp.where(keeps_in, of_in, of_out)
+        give[span(h), :] = jnp.where(keeps_in, of_out, of_in).astype(BF16)
+
+    steps = blocks * shape.slots
+    expand(0)
+    for step in range(steps):
+        if step + 1 < steps:
+            expand(step + 1)
+        activate(step)
+        h, slot = divmod(step, shape.slots)
+        if slot == 0 and h:
+            reduce_rows(h - 1)
+    reduce_rows(blocks - 1)
 
 
 def fold_sum(value):
@@ -482,42 +501,20 @@
                 grad_fields[rows, shape.lanes(part)] = (flag * total).astype(BF16)
 
 
-def write_sums(norm, has_in, sums, w_in, w_out, work_in, work_out, sems):
-    channels = sums.shape[-1]
-    blocks = w_out.shape[0] // channels
-
-    def written(of_in):
-        copies = []
-        for h in range(blocks):
-            block = slice(h * channels, (h + 1) * channels)
-            value = sums[block, :].astype(F32) * norm
-            if of_in:
-                work_in[:, block] = value
-                copy = pltpu.make_async_copy(work_in.at[:, block], w_in.at[:, block], sems.at[h])
-            else:
-                work_out[block, :] = value.T
-                copy = pltpu.make_async_copy(work_out.at[block, :], w_out.at[block, :], sems.at[h])
-            copy.start()
-            copies.append(copy)
-        for copy in copies:
-            copy.wait()
-
-    @pl.when(has_in)
-    def _():
-        written(True)
-
-    @pl.when(jnp.logical_not(has_in))
-    def _():
-        written(False)
-
-
-def own_kernel(norm, own, w_in, w_out, work_in, work_out, sems):
-    write_sums(norm, lax.axis_index("core") == 0, own, w_in, w_out, work_in, work_out, sems)
-
-
-def other_kernel(norm, w_in_old, w_out_old, own, came, w_in, w_out, kernel_sum, gain_sum, scale_sum, work_in, work_out, sems):
+def unpack_kernel(norm, own, came, w_in, w_out, kernel_sum, gain_sum, scale_sum, work_in, work_out, sems):
     is_first = lax.axis_index("core") == 0
-    hidden = w_out.shape[0]
+    hidden, channels = w_out.shape
+    copies = []
+    for h in range(hidden // channels):
+        block = slice(h * channels, (h + 1) * channels)
+        mine = own[block, :].astype(F32) * norm
+        theirs = came[block, :].astype(F32) * norm
+        work_in[:, block] = jnp.where(is_first, mine, theirs)
+        copies.append(pltpu.make_async_copy(work_in.at[:, block], w_in.at[:, block], sems.at[2 * h]))
+        copies[-1].start()
+        work_out[block, :] = jnp.where(is_first, theirs, mine).T
+        copies.append(pltpu.make_async_copy(work_out.at[block, :], w_out.at[block, :], sems.at[2 * h + 1]))
+        copies[-1].start()
     extra = (own.shape[0] - hidden) // 2
     high, low = pl.ds(hidden, extra), pl.ds(hidden + extra, extra)
     mine = (own[high, :].astype(F32) + own[low, :].astype(F32)) * norm
@@ -527,7 +524,8 @@
         kernel_sum[above] = small[above * KSIZE : (above + 1) * KSIZE, :]
     gain_sum[...] = small[KSIZE * KSIZE : KSIZE * KSIZE + 1, :]
     scale_sum[...] = small[KSIZE * KSIZE + 1 : KSIZE * KSIZE + 2, :]
-    write_sums(norm, jnp.logical_not(is_first), came, w_in, w_out, work_in, work_out, sems)
+    for copy in copies:
+        copy.wait()
 
 
 def pairs_of(kind):
@@ -645,7 +643,7 @@
     return mine, send
 
 
-def call(kernel, outs, scratch, hbm, vmem, copies=0, micros=1.0, after=(), limit=20, in_hbm=0, aliases=None):
+def call(kernel, outs, scratch, hbm, vmem, copies=0, micros=1.0, after=(), limit=20, in_hbm=0):
     in_specs = [pl.BlockSpec(memory_space=pl.ANY)] * len(hbm)
     in_specs += [pl.BlockSpec(memory_space=pltpu.VMEM)] * len(vmem)
     in_specs += [pl.BlockSpec(memory_space=pl.ANY)] * len(after)
@@ -662,7 +660,6 @@
         out_shape=[jax.ShapeDtypeStruct(*out) for out in outs],
         in_specs=in_specs,
         out_specs=[pl.BlockSpec(memory_space=pl.ANY if at < in_hbm else pltpu.VMEM) for at in range(len(outs))],
-        input_output_aliases=aliases or {},
         scratch_shapes=shapes,
         cost_estimate=pl.CostEstimate(flops=int(micros * 1e9), bytes_accessed=0, transcendentals=0),
         compiler_params=pltpu.CompilerParams(vmem_limit_bytes=limit * 1024 * 1024),
@@ -725,7 +722,10 @@
     keep, give, activated, dpreact, yhat, inverse, top = call(
         bind(late_kernel),
         [((hidden, channels), F32), ((hidden, channels), BF16), wide, wide, whole_f, narrow, strip(late + 2 * HALF)],
-        [count_s, taps, ((parts, late * shape.columns, LANES), F32), whole, flat, ends_f],
+        [
+            count_s, taps, ((parts, late * shape.columns, LANES), F32), whole, flat, ends_f,
+            ((3, TILE * TILE, channels), F32),
+        ],
         [block_count],
         [taps_in, gain, w_in, band, fold, rims, normed, yhat, inverse, dproj_t, dact], 1, 5.0,
     )
@@ -806,12 +806,7 @@
         add_kernel, [(payload.shape, BF16)], [], [], [payload, came], after=[last_grad], micros=0.3,
     )
     came = bit_swap(payload, order[-2])
-    folded, first, second = call(
-        bind(rims_kernel), [strip(TILE), edge, edge], [count_s], [block_count], [fold_back, *core_grad], 1, 1.0,
-        after=[payload],
-    )
-    first, second = swap(first, "first"), swap(second, "second")
-    after = [folded]
+    after = [fold_back]
     for at in reversed(range(len(order) - 1)):
         copies = 2 if at == 0 else 1
         if rows % 16 == 0:
@@ -830,6 +825,13 @@
         rows *= 2
         came = bit_swap(payload, order[at - 1]) if at else core_swap(payload)
         if at == 2:
+            folded, first, second = call(
+                bind(rims_kernel), [strip(TILE), edge, edge], [count_s], [block_count], [fold_back, *core_grad], 1, 1.0,
+                after=[payload],
+            )
+            first, second = swap(first, "first"), swap(second, "second")
+            after = [first, second]
+        if at == 1:
             grad_fields, done = call(
                 bind(final_kernel), [whole, ((8, LANES), F32)], [count_s, ocean_s, strip(TILE)],
                 [block_count, ocean], [tangent, folded, first, second], 2, 1.5, after=[payload],
@@ -838,12 +840,9 @@
     total = samples * lax.axis_size("dp") * slots * lax.axis_size(TILES) * tile_rows * tile_cols
     norm = total ** (-0.5)
     sums = [((channels, hidden), F32), ((hidden, channels), F32)]
-    w_in_sum, w_out_sum = call(
-        functools.partial(own_kernel, norm), sums, sums, [], [payload], hidden // channels, 1.0, in_hbm=2,
-    )
     w_in_sum, w_out_sum, kernel_sum, gain_sum, scale_sum = call(
-        functools.partial(other_kernel, norm), sums + [(kernel.shape, F32), row, row], sums,
-        [w_in_sum, w_out_sum], [payload, came], hidden // channels, 1.0, in_hbm=2, aliases={0: 0, 1: 1},
+        functools.partial(unpack_kernel, norm), sums + [(kernel.shape, F32), row, row], sums,
+        [], [payload, came], 2 * hidden // channels, 1.5, in_hbm=2,
     )
     return (
         state.reshape(grid),

time: 67.6 us -> 68.2 us (level)
  waiting for transfers between devices: 21.9 us -> 24.6 us
  Pallas kernels: 26.4 us -> 24.4 us
    pallas_call x24 -> x23, Pallas kernels: 26.4 us -> 24.4 us  [call(): pl.pallas_call(body, out_shape=[jax.ShapeDtypeStruct(*out) for out in out...]
    ppermute x7, waiting for transfers between devices: 4.24 us -> 5.89 us  [swap(): return lax.ppermute(block, TILES, pairs_of(kind))]
    ppermute x3, waiting for transfers between devices: 2.03 us -> 3.06 us  [core_swap(): return lax.ppermute(block, 'core', [(0, 1), (1, 0)])]
  transfers between devices with their start and end apart: 17 -> 17, of which waited for: 11 -> 11; matrix products, arithmetic and copies ran while one was open for 0% -> 0% of each run, Pallas kernels for 28% -> 26%
where the time goes in v4:
time: 68.2 us; the launch traced here: 68 us
  waiting for transfers between devices  24.6 us (36%)
  Pallas kernels  24.4 us (36%)
  starting transfers between devices  16.3 us (24%)
  between operations  1.59 us (2%)
  local copies, waits for them, and re-layouts  1.04 us (2%)
    pallas_call x23, Pallas kernels, call(): pl.pallas_call(body, out_shape=[jax.ShapeDtypeStruct(*out) for out in out...  24.4 us
    ppermute x7, waiting for transfers between devices, bit_swap(): return lax.ppermute(block, ('chips', 'core', 'dp'), pairs)  15.7 us
    ppermute x7, starting transfers between devices, swap(): return lax.ppermute(block, TILES, pairs_of(kind))  11.1 us
    ppermute x7, waiting for transfers between devices, swap(): return lax.ppermute(block, TILES, pairs_of(kind))  5.89 us
    ppermute x7, starting transfers between devices, bit_swap(): return lax.ppermute(block, ('chips', 'core', 'dp'), pairs)  4.97 us
    ppermute x3, waiting for transfers between devices, core_swap(): return lax.ppermute(block, 'core', [(0, 1), (1, 0)])  3.06 us
  transfers between devices with their start and end apart: 17, of which 11 were waited for; matrix products, arithmetic and copies ran while one was open for 0% of the time, Pallas kernels for 26%

profile of v4, /device:TPU:0, one launch (start us, length us, event | category | flops | bytes accessed | tf_op | source)
XLA Modules:
  0.0 68.0 jit_solution(3452257889890625452)
XLA Ops:
  1.3 0.0 copy-start.2
  1.3 1.0 %copy-done.2 = bf16[1,3,16,16,256]{4,3,2,1,0:T(8,128)(2,1)S(1)} copy-done((bf16[1,3,16,16,256]{4,3,2,1,0:T(8,128)(2,1)S(1)}, bf16[1,3,16,16,256]{4,3,2,1,0:T(8,128)(2,1)}, u32[]{:S(2)}) %copy-start.2) | copy-done | bytes 393240
  2.3 0.6 shard_map.144
  2.9 4.1 %collective-permute-start.1 = (bf16[48,256]{1,0:T(8,128)(2,1)S(1)}, bf16[48,256]{1,0:T(8,128)(2,1)S(1)}, u32[]{:S(2)}, u32[]{:S(2)}) collective-permute-start(bf16[48,256]{1,0:T(8,128)(2,1)S(1)} %get-tuple-element.48), channel_id=1, source_target_pairs={{0,16},{2,4},{4,2},{6,8},{8,6},{10,12},{12,10},{14,30},{30,14},{28... | collective-permute-start | bytes 73736 | tf_op jit(solution)/shard_map/ppermute | solution.py:544
  7.0 0.7 %shard_map.145.refs_5_ = bf16[144,256]{1,0:T(8,128)(2,1)S(1)} custom-call(s32[1]{0:T(128)S(6)} %copy.16.refs_0_, s32[3]{0:T(128)S(1)} %copy-done.8, bf16[768,256]{1,0:T(8,128)(2,1)S(1)} %bitcast.9, bf16[48,256]{1,0:T(8,128)(2,1)S(1)} %get-tuple-element.47.refs_3_), custom_call_target="tpu_custom_call" | custom-call | flops 500000000 | tf_op jit(solution)/shard_map/pallas_call | solution.py:658
  7.7 0.0 copy-start.1
  7.7 0.0 copy-start.5
  7.8 1.7 %collective-permute-start.2 = (bf16[144,256]{1,0:T(8,128)(2,1)S(1)}, bf16[144,256]{1,0:T(8,128)(2,1)S(1)}, u32[]{:S(2)}, u32[]{:S(2)}) collective-permute-start(bf16[144,256]{1,0:T(8,128)(2,1)S(1)} %shard_map.145.refs_5_), channel_id=1, source_target_pairs={{0,16},{2,18},{4,20},{6,22},{8,24},{10,26},{12,28},{14,30},{30,14}... | collective-permute-start | bytes 221192 | tf_op jit(solution)/shard_map/ppermute | solution.py:544
  9.4 0.7 %shard_map.146 = (f32[2,1216,128]{2,1,0:T(8,128)S(1)}, bf16[48,256]{1,0:T(8,128)(2,1)S(1)}) custom-call(s32[1]{0:T(128)S(6)} %copy.16.refs_0_, s32[3]{0:T(128)S(1)} %copy-done.8, bf16[768,256]{1,0:T(8,128)(2,1)S(1)} %bitcast.10, bf16[48,256]{1,0:T(8,128)(2,1)S(1)} %collective-permute-done.refs_3_, bf16[48,256]{1,0:T(8,128)(2,1)S(1)} %collective-permute-done.1.refs_4_, ...), custom_call_target="tpu_custom_call" | custom-call | flops 1000000000 | tf_op jit(solution)/shard_map/pallas_call | solution.py:658
  10.2 2.3 %collective-permute-start.3 = (bf16[48,256]{1,0:T(8,128)(2,1)S(1)}, bf16[48,256]{1,0:T(8,128)(2,1)S(1)}, u32[]{:S(2)}, u32[]{:S(2)}) collective-permute-start(bf16[48,256]{1,0:T(8,128)(2,1)S(1)} %get-tuple-element.50), channel_id=1, source_target_pairs={{0,16},{2,18},{4,20},{6,22},{8,24},{10,26},{12,28},{14,30},{30,14}... | collective-permute-start | bytes 73736 | tf_op jit(solution)/shard_map/ppermute | solution.py:544
  12.6 3.7 %shard_map.147 = (bf16[768,256]{1,0:T(8,128)(2,1)S(1)}, f32[768,256]{1,0:T(8,128)S(1)}, f32[768,128]{1,0:T(8,128)S(1)}, bf16[256,768]{1,0:T(8,128)(2,1)S(1)}, f32[768,1024]{1,0:T(8,128)S(1)}) custom-call(s32[1]{0:T(128)S(6)} %copy.16.refs_0_, s32[3]{0:T(128)S(1)} %copy-done.8, bf16[7,7,256]{2,1,0:T(8,128)(2,1)S(1)} %copy-done.5, f32[1,256]{1,0:T(1,128)S(1)} %bitcast.15, ...), custom_call_target="tpu_custom_call" | custom-call | flops 5000000000 | tf_op jit(solution)/shard_map/pallas_call | solution.py:658
  16.3 4.1 %shard_map.148 = (f32[1024,256]{1,0:T(8,128)S(1)}, bf16[1024,256]{1,0:T(8,128)(2,1)S(1)}, bf16[768,1024]{1,0:T(8,128)(2,1)S(1)}, bf16[768,1024]{1,0:T(8,128)(2,1...) custom-call(s32[1]{0:T(128)S(6)} %copy.16.refs_0_, ...), custom_call_target="tpu_custom_call" | custom-call | flops 5000000000 | tf_op jit(solution)/shard_map/pallas_call | solution.py:658
  20.3 0.1 collective-permute-start.4
  20.4 0.8 %shard_map.149 = (bf16[768,256]{1,0:T(8,128)(2,1)S(1)}, f32[8,256]{1,0:T(8,128)S(1)}) custom-call(bf16[256,1024]{1,0:T(8,128)(2,1)S(1)} %copy-done, f32[1,256]{1,0:T(1,128)S(1)} %bitcast.17, bf16[768,1024]{1,0:T(8,128)(2,1)S(1)} %get-tuple-element.58.refs_2_, f32[768,256]{1,0:T(8,128)S(1)} %get-tuple-element.59.refs_3_, f32[768,128]{1,0:T(8,128)S(1)} %get-tuple-element.60.refs_4_), custom_call_target="tpu_custom_call" | custom-call | flops 1000000000 | tf_op jit(solution)/shard_map/pallas_call | solution.py:658
  21.2 1.1 %collective-permute-done.4.refs_1_ = bf16[1024,256]{1,0:T(8,128)(2,1)S(1)} collective-permute-done((bf16[1024,256]{1,0:T(8,128)(2,1)S(1)}, bf16[1024,256]{1,0:T(8,128)(2,1)S(1)}, u32[]{:S(2)}, u32[]{:S(2)}) %collective-permute-start.4) | collective-permute-done | bytes 524320 | tf_op jit(solution)/shard_map/ppermute | solution.py:548
  22.3 0.2 shard_map.150
  22.5 0.4 collective-permute-start.5
  22.8 1.8 %shard_map.151.refs_7_.refs_2_ = f32[64,128]{1,0:T(8,128)S(1)} custom-call(f32[2,1216,128]{2,1,0:T(8,128)S(1)} %get-tuple-element.49.refs_7_.refs_4_.refs_0_, f32[2,640,128]{2,1,0:T(8,128)S(1)} %get-tuple-element.57.refs_1_, bf16[768,256]{1,0:T(8,128)(2,1)S(1)} %get-tuple-element.61.refs_2_, bf16[512,256]{1,0:T(8,128)(2,1)S(1)} %get-tuple-element.64.refs_3_), custom_call_target="tpu_custom_call" | custom-call | flops 1800000000 | tf_op jit(solution)/shard_map/pallas_call | solution.py:658
  24.6 2.0 %shard_map.152 = (bf16[768,256]{1,0:T(8,128)(2,1)}, f32[8,256]{1,0:T(8,128)S(1)}) custom-call(s32[1]{0:T(128)S(6)} %copy.16.refs_0_, s32[3]{0:T(128)S(1)} %copy-done.8, bf16[768,256]{1,0:T(8,128)(2,1)S(1)} %bitcast.11, bf16[768,256]{1,0:T(8,128)(2,1)S(1)} %bitcast.13, bf16[1024,256]{1,0:T(8,128)(2,1)S(1)} %copy-done.1, f32[1,256]{1,0:T(1,128)S(1)} %bitcast.19, ...), custom_call_target="tpu_custom_call" | custom-call | flops 1500000000 | tf_op jit(solution)/shard_map/pallas_call | solution.py:658
  26.6 2.3 %collective-permute-done.5.refs_1_ = bf16[512,256]{1,0:T(8,128)(2,1)S(1)} collective-permute-done((bf16[512,256]{1,0:T(8,128)(2,1)S(1)}, bf16[512,256]{1,0:T(8,128)(2,1)S(1)}, u32[]{:S(2)}, u32[]{:S(2)}) %collective-permute-start.5) | collective-permute-done | bytes 262176 | tf_op jit(solution)/shard_map/ppermute | solution.py:568
  28.9 0.1 shard_map.153
  29.0 1.6 %collective-permute-start.6 = (bf16[256,256]{1,0:T(8,128)(2,1)S(1)}, bf16[256,256]{1,0:T(8,128)(2,1)S(1)}, u32[]{:S(2)}, u32[]{:S(2)}) collective-permute-start(bf16[256,256]{1,0:T(8,128)(2,1)S(1)} %get-tuple-element.69.refs_3_), channel_id=1, source_target_pairs={{0,1},{1,0},{2,6},{3,7},{4,5},{5,4},{6,2},{7,3},{8,9},{9,8},{10,14... | collective-permute-start | bytes 393224 | tf_op jit(solution)/shard_map/ppermute | solution.py:568
  30.6 1.8 %shard_map.154.refs_3_ = f32[64,128]{1,0:T(8,128)S(1)} custom-call(f32[2,1216,128]{2,1,0:T(8,128)S(1)} %get-tuple-element.49.refs_7_.refs_4_.refs_0_, f32[2,640,128]{2,1,0:T(8,128)S(1)} %get-tuple-element.57.refs_1_, bf16[768,256]{1,0:T(8,128)(2,1)S(1)} %get-tuple-element.61.refs_2_, bf16[256,256]{1,0:T(8,128)(2,1)S(1)} %get-tuple-element.69.refs_3_), custom_call_target="tpu_custom_call" | custom-call | flops 1800000000 | tf_op jit(solution)/shard_map/pallas_call | solution.py:658
  32.4 0.1 collective-permute-start.8
  32.5 1.6 %collective-permute-done.6.refs_1_ = bf16[256,256]{1,0:T(8,128)(2,1)S(1)} collective-permute-done((bf16[256,256]{1,0:T(8,128)(2,1)S(1)}, bf16[256,256]{1,0:T(8,128)(2,1)S(1)}, u32[]{:S(2)}, u32[]{:S(2)}) %collective-permute-start.6) | collective-permute-done | bytes 131104 | tf_op jit(solution)/shard_map/ppermute | solution.py:568
  34.1 1.1 %collective-permute-start.7 = (bf16[128,256]{1,0:T(8,128)(2,1)S(1)}, bf16[128,256]{1,0:T(8,128)(2,1)S(1)}, u32[]{:S(2)}, u32[]{:S(2)}) collective-permute-start(bf16[128,256]{1,0:T(8,128)(2,1)S(1)} %get-tuple-element.72.refs_3_), channel_id=1, source_target_pairs={{0,8},{1,9},{2,3},{3,2},{4,12},{5,13},{6,7},{7,6},{8,0},{9,1},{10,... | collective-permute-start | bytes 196616 | tf_op jit(solution)/shard_map/ppermute | solution.py:568
  35.1 1.7 %shard_map.157.refs_4_.refs_3_.refs_2_ = f32[1216,128]{1,0:T(8,128)S(1)} custom-call(s32[1]{0:T(128)S(6)} %copy.16.refs_0_, bf16[7,7,256]{2,1,0:T(8,128)(2,1)S(1)} %copy-done.5, bf16[768,256]{1,0:T(8,128)(2,1)S(1)} %get-tuple-element.61.refs_2_, bf16[128,256]{1,0:T(8,128)(2,1)S(1)} %get-tuple-element.72.refs_3_), custom_call_target="tpu_custom_call" | custom-call | flops 2000000000 | tf_op jit(solution)/shard_map/pallas_call | solution.py:658
  36.9 1.5 %collective-permute-done.7.refs_1_ = bf16[128,256]{1,0:T(8,128)(2,1)S(1)} collective-permute-done((bf16[128,256]{1,0:T(8,128)(2,1)S(1)}, bf16[128,256]{1,0:T(8,128)(2,1)S(1)}, u32[]{:S(2)}, u32[]{:S(2)}) %collective-permute-start.7) | collective-permute-done | bytes 65568 | tf_op jit(solution)/shard_map/ppermute | solution.py:568
  38.4 1.1 %collective-permute-start.10 = (bf16[160,256]{1,0:T(8,128)(2,1)S(1)}, bf16[160,256]{1,0:T(8,128)(2,1)S(1)}, u32[]{:S(2)}, u32[]{:S(2)}) collective-permute-start(bf16[160,256]{1,0:T(8,128)(2,1)S(1)} %shard_map.158.refs_4_.refs_0_), channel_id=1, source_target_pairs={{0,16},{1,17},{2,18},{3,19},{4,20},{5,21},{6,22},{7,23},{8,24},{9,... | collective-permute-start | bytes 245768 | tf_op jit(solution)/shard_map/ppermute | solution.py:568
  39.5 1.9 %shard_map.159 = (f32[1216,128]{1,0:T(8,128)S(1)}, bf16[192,256]{1,0:T(8,128)(2,1)S(1)}) custom-call(s32[1]{0:T(128)S(6)} %copy.16.refs_0_, bf16[7,7,256]{2,1,0:T(8,128)(2,1)S(1)} %copy-done.5, bf16[768,256]{1,0:T(8,128)(2,1)S(1)} %get-tuple-element.61.refs_2_, f32[1216,128]{1,0:T(8,128)S(1)} %shard_map.157.refs_4_.refs_3_.refs_2_, ...), custom_call_target="tpu_custom_call" | custom-call | flops 2000000000 | tf_op jit(solution)/shard_map/pallas_call | solution.py:658
  41.4 2.0 %collective-permute-start.9 = (bf16[192,256]{1,0:T(8,128)(2,1)S(1)}, bf16[192,256]{1,0:T(8,128)(2,1)S(1)}, u32[]{:S(2)}, u32[]{:S(2)}) collective-permute-start(bf16[192,256]{1,0:T(8,128)(2,1)S(1)} %get-tuple-element.75), channel_id=1, source_target_pairs={{0,16},{2,18},{4,20},{6,22},{8,24},{10,26},{12,28},{14,30},{30,14}... | collective-permute-start | bytes 294920 | tf_op jit(solution)/shard_map/ppermute | solution.py:544
  43.4 2.9 %collective-permute-done.10.refs_1_ = bf16[160,256]{1,0:T(8,128)(2,1)S(1)} collective-permute-done((bf16[160,256]{1,0:T(8,128)(2,1)S(1)}, bf16[160,256]{1,0:T(8,128)(2,1)S(1)}, u32[]{:S(2)}, u32[]{:S(2)}) %collective-permute-start.10) | collective-permute-done | bytes 81952 | tf_op jit(solution)/shard_map/ppermute | solution.py:568
  46.3 0.1 collective-permute-start.11
  46.4 2.0 %collective-permute-done.9.refs_2_.refs_1_ = bf16[192,256]{1,0:T(8,128)(2,1)S(1)} collective-permute-done((bf16[192,256]{1,0:T(8,128)(2,1)S(1)}, bf16[192,256]{1,0:T(8,128)(2,1)S(1)}, u32[]{:S(2)}, u32[]{:S(2)}) %collective-permute-start.9) | collective-permute-done | bytes 98336 | tf_op jit(solution)/shard_map/ppermute | solution.py:544
  48.4 2.4 %collective-permute-done.11.refs_1_ = bf16[160,256]{1,0:T(8,128)(2,1)S(1)} collective-permute-done((bf16[160,256]{1,0:T(8,128)(2,1)S(1)}, bf16[160,256]{1,0:T(8,128)(2,1)S(1)}, u32[]{:S(2)}, u32[]{:S(2)}) %collective-permute-start.11) | collective-permute-done | bytes 81952 | tf_op jit(solution)/shard_map/ppermute | solution.py:568
  50.9 0.8 %collective-permute-start.14 = (bf16[288,256]{1,0:T(8,128)(2,1)S(1)}, bf16[288,256]{1,0:T(8,128)(2,1)S(1)}, u32[]{:S(2)}, u32[]{:S(2)}) collective-permute-start(bf16[288,256]{1,0:T(8,128)(2,1)S(1)} %shard_map.161.refs_4_.refs_0_), channel_id=1, source_target_pairs={{0,1},{1,0},{2,6},{3,7},{4,5},{5,4},{6,2},{7,3},{8,9},{9,8},{10,14... | collective-permute-start | bytes 442376 | tf_op jit(solution)/shard_map/ppermute | solution.py:568
  51.6 0.6 shard_map.162
  52.3 0.1 collective-permute-start.12
  52.3 1.0 %collective-permute-start.13 = (bf16[48,256]{1,0:T(8,128)(2,1)S(1)}, bf16[48,256]{1,0:T(8,128)(2,1)S(1)}, u32[]{:S(2)}, u32[]{:S(2)}) collective-permute-start(bf16[48,256]{1,0:T(8,128)(2,1)S(1)} %get-tuple-element.79), channel_id=1, source_target_pairs={{0,16},{2,4},{4,2},{6,8},{8,6},{10,12},{12,10},{14,30},{30,14},{28... | collective-permute-start | bytes 73736 | tf_op jit(solution)/shard_map/ppermute | solution.py:544
  53.3 0.2 collective-permute-done.12.refs_2_.refs_4_
  53.5 3.7 %collective-permute-done.13.refs_3_.refs_5_ = bf16[48,256]{1,0:T(8,128)(2,1)S(1)} collective-permute-done((bf16[48,256]{1,0:T(8,128)(2,1)S(1)}, bf16[48,256]{1,0:T(8,128)(2,1)S(1)}, u32[]{:S(2)}, u32[]{:S(2)}) %collective-permute-start.13) | collective-permute-done | bytes 24608 | tf_op jit(solution)/shard_map/ppermute | solution.py:544
  57.2 0.1 collective-permute-start.15
  57.3 1.6 %shard_map.164 = (bf16[768,256]{1,0:T(8,128)(2,1)}, f32[8,128]{1,0:T(8,128)S(1)}) custom-call(s32[1]{0:T(128)S(6)} %copy.16.refs_0_, s32[3]{0:T(128)S(1)} %copy-done.8, bf16[768,256]{1,0:T(8,128)(2,1)S(1)} %bitcast.14, f32[2,1024,128]{2,1,0:T(8,128)S(1)} %get-tuple-element.77.refs_3_, bf16[48,256]{1,0:T(8,128)(2,1)S(1)} %collective-permute-done.12.refs_2_.refs_4_, ...), custom_call_target="tpu_custom_call" | custom-call | flops 1500000000 | tf_op jit(solution)/shard_map/pallas_call | solution.py:658
  59.0 4.9 %collective-permute-done.15.refs_1_ = bf16[544,256]{1,0:T(8,128)(2,1)S(1)} collective-permute-done((bf16[544,256]{1,0:T(8,128)(2,1)S(1)}, bf16[544,256]{1,0:T(8,128)(2,1)S(1)}, u32[]{:S(2)}, u32[]{:S(2)}) %collective-permute-start.15) | collective-permute-done | bytes 278560 | tf_op jit(solution)/shard_map/ppermute | solution.py:568
  63.9 0.1 shard_map.165.refs_0_
  63.9 0.1 collective-permute-start.16
  64.0 1.9 %collective-permute-done.16.refs_1_ = bf16[1088,256]{1,0:T(8,128)(2,1)S(1)} collective-permute-done((bf16[1088,256]{1,0:T(8,128)(2,1)S(1)}, bf16[1088,256]{1,0:T(8,128)(2,1)S(1)}, u32[]{:S(2)}, u32[]{:S(2)}) %collective-permute-start.16) | collective-permute-done | bytes 557088 | tf_op jit(solution)/shard_map/ppermute | solution.py:548
  65.9 2.1 %shard_map.166 = (f32[256,1024]{1,0:T(8,128)}, f32[1024,256]{1,0:T(8,128)}, f32[7,7,256]{2,1,0:T(8,128)}, f32[1,256]{1,0:T(1,128)}, f32[1,256]{1,0:T(1,128)}) custom-call(bf16[1088,256]{1,0:T(8,128)(2,1)S(1)} %shard_map.165.refs_0_, bf16[1088,256]{1,0:T(8,128)(2,1)S(1)} %collective-permute-done.16.refs_1_), custom_call_target="tpu_custom_call" | custom-call | flops 1500000000 | tf_op jit(solution)/shard_map/pallas_call | solution.py:658
  (27 shorter events, 0.2 us)
Async XLA Ops:
  1.3 1.0 %copy-start.2 = (bf16[1,3,16,16,256]{4,3,2,1,0:T(8,128)(2,1)S(1)}, bf16[1,3,16,16,256]{4,3,2,1,0:T(8,128)(2,1)}, u32[]{:S(2)}) copy-start(bf16[1,3,16,16,256]{4,3,2,1,0:T(8,128)(2,1)} %param.9) | copy-start | bytes 1179652
  2.3 4.7 %copy-start.8 = (s32[3]{0:T(128)S(1)}, s32[3]{0:T(128)}, u32[]{:S(2)}) copy-start(s32[3]{0:T(128)} %refs_1_.15) | copy-start | bytes 40
  2.9 6.6 %collective-permute-start.1 = (bf16[48,256]{1,0:T(8,128)(2,1)S(1)}, bf16[48,256]{1,0:T(8,128)(2,1)S(1)}, u32[]{:S(2)}, u32[]{:S(2)}) collective-permute-start(bf16[48,256]{1,0:T(8,128)(2,1)S(1)} %get-tuple-element.48), channel_id=1, source_target_pairs={{0,16},{2,4},{4,2},{6,8},{8,6},{10,12},{12,10},{14,30},{30,14},{28... | collective-permute-start | bytes 73736 | tf_op jit(solution)/shard_map/ppermute | solution.py:544
  7.0 2.5 %collective-permute-start = (bf16[48,256]{1,0:T(8,128)(2,1)S(1)}, bf16[48,256]{1,0:T(8,128)(2,1)S(1)}, u32[]{:S(2)}, u32[]{:S(2)}) collective-permute-start(bf16[48,256]{1,0:T(8,128)(2,1)S(1)} %get-tuple-element.47.refs_3_), channel_id=1, source_target_pairs={{0,2},{2,0},{4,6},{6,4},{8,10},{10,8},{12,14},{14,12},{30,28},{28,... | collective-permute-start | bytes 73736 | tf_op jit(solution)/shard_map/ppermute | solution.py:544
  7.7 4.8 %copy-start.1 = (bf16[1024,256]{1,0:T(8,128)(2,1)S(1)}, bf16[1024,256]{1,0:T(8,128)(2,1)}, u32[]{:S(2)}) copy-start(bf16[1024,256]{1,0:T(8,128)(2,1)} %refs_4_.3) | copy-start | bytes 1572868
  7.7 4.8 %copy-start.4 = (bf16[1,3,16,16,256]{4,3,2,1,0:T(8,128)(2,1)S(1)}, bf16[1,3,16,16,256]{4,3,2,1,0:T(8,128)(2,1)}, u32[]{:S(2)}) copy-start(bf16[1,3,16,16,256]{4,3,2,1,0:T(8,128)(2,1)} %param.10) | copy-start | bytes 1179652
  7.7 4.8 %copy-start.5 = (bf16[7,7,256]{2,1,0:T(8,128)(2,1)S(1)}, bf16[7,7,256]{2,1,0:T(8,128)(2,1)}, u32[]{:S(2)}) copy-start(bf16[7,7,256]{2,1,0:T(8,128)(2,1)} %refs_1_.14) | copy-start | bytes 75268
  7.7 4.8 %copy-start.6 = (f32[256]{0:T(256)S(1)}, f32[256]{0:T(256)}, u32[]{:S(2)}) copy-start(f32[256]{0:T(256)} %param.14) | copy-start | bytes 3076
  7.8 4.8 %copy-start.7 = (f32[256]{0:T(256)S(1)}, f32[256]{0:T(256)}, u32[]{:S(2)}) copy-start(f32[256]{0:T(256)} %param.17) | copy-start | bytes 3076
  7.8 8.5 %collective-permute-start.2 = (bf16[144,256]{1,0:T(8,128)(2,1)S(1)}, bf16[144,256]{1,0:T(8,128)(2,1)S(1)}, u32[]{:S(2)}, u32[]{:S(2)}) collective-permute-start(bf16[144,256]{1,0:T(8,128)(2,1)S(1)} %shard_map.145.refs_5_), channel_id=1, source_target_pairs={{0,16},{2,18},{4,20},{6,22},{8,24},{10,26},{12,28},{14,30},{30,14}... | collective-permute-start | bytes 221192 | tf_op jit(solution)/shard_map/ppermute | solution.py:544
  10.2 6.0 %collective-permute-start.3 = (bf16[48,256]{1,0:T(8,128)(2,1)S(1)}, bf16[48,256]{1,0:T(8,128)(2,1)S(1)}, u32[]{:S(2)}, u32[]{:S(2)}) collective-permute-start(bf16[48,256]{1,0:T(8,128)(2,1)S(1)} %get-tuple-element.50), channel_id=1, source_target_pairs={{0,16},{2,18},{4,20},{6,22},{8,24},{10,26},{12,28},{14,30},{30,14}... | collective-permute-start | bytes 73736 | tf_op jit(solution)/shard_map/ppermute | solution.py:544
  12.5 3.7 %copy-start = (bf16[256,1024]{1,0:T(8,128)(2,1)S(1)}, bf16[256,1024]{1,0:T(8,128)(2,1)}, u32[]{:S(2)}) copy-start(bf16[256,1024]{1,0:T(8,128)(2,1)} %refs_0_.11) | copy-start | bytes 1572868
  20.3 2.0 %collective-permute-start.4 = (bf16[1024,256]{1,0:T(8,128)(2,1)S(1)}, bf16[1024,256]{1,0:T(8,128)(2,1)S(1)}, u32[]{:S(2)}, u32[]{:S(2)}) collective-permute-start(bf16[1024,256]{1,0:T(8,128)(2,1)S(1)} %get-tuple-element.63), channel_id=1, source_target_pairs={{0,2},{2,0},{1,3},{3,1},{4,6},{6,4},{5,7},{7,5},{8,10},{10,8},{9,1... | collective-permute-start | bytes 1572872 | tf_op jit(solution)/shard_map/ppermute | solution.py:548
  22.5 6.4 %collective-permute-start.5 = (bf16[512,256]{1,0:T(8,128)(2,1)S(1)}, bf16[512,256]{1,0:T(8,128)(2,1)S(1)}, u32[]{:S(2)}, u32[]{:S(2)}) collective-permute-start(bf16[512,256]{1,0:T(8,128)(2,1)S(1)} %get-tuple-element.64.refs_3_), channel_id=1, source_target_pairs={{0,4},{1,5},{2,10},{3,11},{4,0},{5,1},{6,14},{7,15},{8,12},{9,13},... | collective-permute-start | bytes 786440 | tf_op jit(solution)/shard_map/ppermute | solution.py:568
  22.8 1.8 %copy-start.3 = (bf16[1,3,16,16,256]{4,3,2,1,0:T(8,128)(2,1)S(1)}, bf16[1,3,16,16,256]{4,3,2,1,0:T(8,128)(2,1)}, u32[]{:S(2)}) copy-start(bf16[1,3,16,16,256]{4,3,2,1,0:T(8,128)(2,1)} %param.9) | copy-start | bytes 1179652
  29.0 5.0 %collective-permute-start.6 = (bf16[256,256]{1,0:T(8,128)(2,1)S(1)}, bf16[256,256]{1,0:T(8,128)(2,1)S(1)}, u32[]{:S(2)}, u32[]{:S(2)}) collective-permute-start(bf16[256,256]{1,0:T(8,128)(2,1)S(1)} %get-tuple-element.69.refs_3_), channel_id=1, source_target_pairs={{0,1},{1,0},{2,6},{3,7},{4,5},{5,4},{6,2},{7,3},{8,9},{9,8},{10,14... | collective-permute-start | bytes 393224 | tf_op jit(solution)/shard_map/ppermute | solution.py:568
  32.4 4.5 %collective-permute-start.8 = (bf16[64,256]{1,0:T(8,128)(2,1)S(1)}, bf16[64,256]{1,0:T(8,128)(2,1)S(1)}, u32[]{:S(2)}, u32[]{:S(2)}) collective-permute-start(bf16[64,256]{1,0:T(8,128)(2,1)S(1)} %get-tuple-element.74), channel_id=1, source_target_pairs={{0,2},{2,0},{1,3},{3,1},{4,6},{6,4},{5,7},{7,5},{8,10},{10,8},{9,1... | collective-permute-start | bytes 98312 | tf_op jit(solution)/shard_map/ppermute | solution.py:548
  34.1 4.3 %collective-permute-start.7 = (bf16[128,256]{1,0:T(8,128)(2,1)S(1)}, bf16[128,256]{1,0:T(8,128)(2,1)S(1)}, u32[]{:S(2)}, u32[]{:S(2)}) collective-permute-start(bf16[128,256]{1,0:T(8,128)(2,1)S(1)} %get-tuple-element.72.refs_3_), channel_id=1, source_target_pairs={{0,8},{1,9},{2,3},{3,2},{4,12},{5,13},{6,7},{7,6},{8,0},{9,1},{10,... | collective-permute-start | bytes 196616 | tf_op jit(solution)/shard_map/ppermute | solution.py:568
  38.4 7.9 %collective-permute-start.10 = (bf16[160,256]{1,0:T(8,128)(2,1)S(1)}, bf16[160,256]{1,0:T(8,128)(2,1)S(1)}, u32[]{:S(2)}, u32[]{:S(2)}) collective-permute-start(bf16[160,256]{1,0:T(8,128)(2,1)S(1)} %shard_map.158.refs_4_.refs_0_), channel_id=1, source_target_pairs={{0,16},{1,17},{2,18},{3,19},{4,20},{5,21},{6,22},{7,23},{8,24},{9,... | collective-permute-start | bytes 245768 | tf_op jit(solution)/shard_map/ppermute | solution.py:568
  41.4 7.0 %collective-permute-start.9 = (bf16[192,256]{1,0:T(8,128)(2,1)S(1)}, bf16[192,256]{1,0:T(8,128)(2,1)S(1)}, u32[]{:S(2)}, u32[]{:S(2)}) collective-permute-start(bf16[192,256]{1,0:T(8,128)(2,1)S(1)} %get-tuple-element.75), channel_id=1, source_target_pairs={{0,16},{2,18},{4,20},{6,22},{8,24},{10,26},{12,28},{14,30},{30,14}... | collective-permute-start | bytes 294920 | tf_op jit(solution)/shard_map/ppermute | solution.py:544
  46.3 4.5 %collective-permute-start.11 = (bf16[160,256]{1,0:T(8,128)(2,1)S(1)}, bf16[160,256]{1,0:T(8,128)(2,1)S(1)}, u32[]{:S(2)}, u32[]{:S(2)}) collective-permute-start(bf16[160,256]{1,0:T(8,128)(2,1)S(1)} %shard_map.160.refs_0_), channel_id=1, source_target_pairs={{0,8},{1,9},{2,3},{3,2},{4,12},{5,13},{6,7},{7,6},{8,0},{9,1},{10,... | collective-permute-start | bytes 245768 | tf_op jit(solution)/shard_map/ppermute | solution.py:568
  50.9 6.3 %collective-permute-start.14 = (bf16[288,256]{1,0:T(8,128)(2,1)S(1)}, bf16[288,256]{1,0:T(8,128)(2,1)S(1)}, u32[]{:S(2)}, u32[]{:S(2)}) collective-permute-start(bf16[288,256]{1,0:T(8,128)(2,1)S(1)} %shard_map.161.refs_4_.refs_0_), channel_id=1, source_target_pairs={{0,1},{1,0},{2,6},{3,7},{4,5},{5,4},{6,2},{7,3},{8,9},{9,8},{10,14... | collective-permute-start | bytes 442376 | tf_op jit(solution)/shard_map/ppermute | solution.py:568
  52.3 1.3 %collective-permute-start.12 = (bf16[48,256]{1,0:T(8,128)(2,1)S(1)}, bf16[48,256]{1,0:T(8,128)(2,1)S(1)}, u32[]{:S(2)}, u32[]{:S(2)}) collective-permute-start(bf16[48,256]{1,0:T(8,128)(2,1)S(1)} %get-tuple-element.78), channel_id=1, source_target_pairs={{0,2},{2,0},{4,6},{6,4},{8,10},{10,8},{12,14},{14,12},{30,28},{28,... | collective-permute-start | bytes 73736 | tf_op jit(solution)/shard_map/ppermute | solution.py:544
  52.3 4.9 %collective-permute-start.13 = (bf16[48,256]{1,0:T(8,128)(2,1)S(1)}, bf16[48,256]{1,0:T(8,128)(2,1)S(1)}, u32[]{:S(2)}, u32[]{:S(2)}) collective-permute-start(bf16[48,256]{1,0:T(8,128)(2,1)S(1)} %get-tuple-element.79), channel_id=1, source_target_pairs={{0,16},{2,4},{4,2},{6,8},{8,6},{10,12},{12,10},{14,30},{30,14},{28... | collective-permute-start | bytes 73736 | tf_op jit(solution)/shard_map/ppermute | solution.py:544
  57.2 6.6 %collective-permute-start.15 = (bf16[544,256]{1,0:T(8,128)(2,1)S(1)}, bf16[544,256]{1,0:T(8,128)(2,1)S(1)}, u32[]{:S(2)}, u32[]{:S(2)}) collective-permute-start(bf16[544,256]{1,0:T(8,128)(2,1)S(1)} %shard_map.163.refs_6_.refs_0_), channel_id=1, source_target_pairs={{0,4},{1,5},{2,10},{3,11},{4,0},{5,1},{6,14},{7,15},{8,12},{9,13},... | collective-permute-start | bytes 835592 | tf_op jit(solution)/shard_map/ppermute | solution.py:568
  63.9 2.0 %collective-permute-start.16 = (bf16[1088,256]{1,0:T(8,128)(2,1)S(1)}, bf16[1088,256]{1,0:T(8,128)(2,1)S(1)}, u32[]{:S(2)}, u32[]{:S(2)}) collective-permute-start(bf16[1088,256]{1,0:T(8,128)(2,1)S(1)} %shard_map.165.refs_0_), channel_id=1, source_target_pairs={{0,2},{2,0},{1,3},{3,1},{4,6},{6,4},{5,7},{7,5},{8,10},{10,8},{9,1... | collective-permute-start | bytes 1671176 | tf_op jit(solution)/shard_map/ppermute | solution.py:548

commit v5 on v4

--- a/solution.py
+++ b/solution.py
@@ -239,7 +239,7 @@
 
 def early_kernel(
     shape, count_hbm, ocean_hbm, kernel, gain, w_out, scale, tangent, band,
-    normed, yhat, inverse, dproj_t, dact,
+    normed, yhat, inverse, dproj_t, dact, live,
     count, ocean, taps, convolved, dproj, sems,
 ):
     fetch = Fetch(sems, (count_hbm, count), (ocean_hbm, ocean))
@@ -251,6 +251,7 @@
     for slot in range(shape.slots):
         rows = pl.ds(slot * per_slot, per_slot)
         flag = slot_flag(count, ocean, slot)
+        live[slot] = jnp.full((8, shape.channels), flag, F32)
         scaled = (tangent[rows, :].astype(F32) * (scale[...] * flag)).astype(BF16)
         dproj[rows, :] = scaled
         dproj_t[:, slot * per_slot : (slot + 1) * per_slot] = scaled.T
@@ -328,39 +329,37 @@
     return jnp.sum(value.reshape(-1, 8, value.shape[-1]), axis=0)
 
 
-def norm_grad_kernel(shape, w_in, gain, dpreact, yhat, inverse, conv_grad, gain_part):
+def norm_grad_kernel(
+    shape, w_in, w_out, gain, dpreact, yhat, inverse, activated, tangent, live,
+    conv_grad, projected, gain_part, scale_part,
+):
     chunk = TILE * TILE
-    total = jnp.zeros((8, shape.channels), F32)
+    of_gain = jnp.zeros((8, shape.channels), F32)
+    of_scale = jnp.zeros((8, shape.channels), F32)
     for slot in range(shape.slots):
         rows = pl.ds(slot * chunk, chunk)
         dnormed = dot(dpreact[rows, :], w_in[...], 1, 1)
         unit = yhat[rows, :]
-        total += fold_sum(dnormed * unit)
+        of_gain += fold_sum(dnormed * unit)
         dhat = dnormed * gain[...]
         mean = jnp.sum(dhat, axis=-1, keepdims=True) * (1.0 / shape.channels)
         along = jnp.sum(dhat * unit, axis=-1, keepdims=True) * (1.0 / shape.channels)
         scale = jnp.concatenate([inverse[rows, :]] * shape.parts, axis=1)
         conv_grad[rows, :] = (scale * (dhat - mean - unit * along)).astype(BF16)
-    gain_part[...] = total
-
-
-def state_kernel(
-    shape, count_hbm, ocean_hbm, fields, tangent, w_out, scale, activated,
-    state, scale_part,
-    count, ocean, sems,
-):
-    fetch = Fetch(sems, (count_hbm, count), (ocean_hbm, ocean))
-    fetch.wait(0, 1)
+        value = dot(activated[rows, :], w_out[...], 1, 0)
+        projected[rows, :] = value
+        of_scale += live[slot] * fold_sum(tangent[rows, :].astype(F32) * value)
+    gain_part[...] = of_gain
+    scale_part[...] = of_scale
+
+
+def state_kernel(shape, fields, scale, projected, live, state, done):
+    done[...] = jnp.zeros_like(done)
     chunk = TILE * TILE
-    total = jnp.zeros((8, shape.channels), F32)
     for slot in range(shape.slots):
         rows = pl.ds(slot * chunk, chunk)
-        flag = slot_flag(count, ocean, slot)
-        projected = dot(activated[rows, :], w_out[...], 1, 0)
-        kept = fields[rows, :].astype(F32) + scale[...] * projected
-        state[rows, :] = (flag * kept).astype(BF16)
-        total += fold_sum(flag * tangent[rows, :].astype(F32) * projected)
-    scale_part[...] = total
+        kept = fields[rows, :].astype(F32) + scale[...] * projected[rows, :]
+        state[rows, :] = (live[slot, 0:1, :] * kept).astype(BF16)
 
 
 def place_grad(shape, conv_grad, parts, spaced):
@@ -501,20 +500,15 @@
                 grad_fields[rows, shape.lanes(part)] = (flag * total).astype(BF16)
 
 
-def unpack_kernel(norm, own, came, w_in, w_out, kernel_sum, gain_sum, scale_sum, work_in, work_out, sems):
+def unpack_kernel(norm, own, came, w_in, w_out, kernel_sum, gain_sum, scale_sum):
     is_first = lax.axis_index("core") == 0
     hidden, channels = w_out.shape
-    copies = []
     for h in range(hidden // channels):
         block = slice(h * channels, (h + 1) * channels)
         mine = own[block, :].astype(F32) * norm
         theirs = came[block, :].astype(F32) * norm
-        work_in[:, block] = jnp.where(is_first, mine, theirs)
-        copies.append(pltpu.make_async_copy(work_in.at[:, block], w_in.at[:, block], sems.at[2 * h]))
-        copies[-1].start()
-        work_out[block, :] = jnp.where(is_first, theirs, mine).T
-        copies.append(pltpu.make_async_copy(work_out.at[block, :], w_out.at[block, :], sems.at[2 * h + 1]))
-        copies[-1].start()
+        w_in[:, block] = jnp.where(is_first, mine, theirs)
+        w_out[block, :] = jnp.where(is_first, theirs, mine).T
     extra = (own.shape[0] - hidden) // 2
     high, low = pl.ds(hidden, extra), pl.ds(hidden + extra, extra)
     mine = (own[high, :].astype(F32) + own[low, :].astype(F32)) * norm
@@ -524,8 +518,6 @@
         kernel_sum[above] = small[above * KSIZE : (above + 1) * KSIZE, :]
     gain_sum[...] = small[KSIZE * KSIZE : KSIZE * KSIZE + 1, :]
     scale_sum[...] = small[KSIZE * KSIZE + 1 : KSIZE * KSIZE + 2, :]
-    for copy in copies:
-        copy.wait()
 
 
 def pairs_of(kind):
@@ -643,7 +635,7 @@
     return mine, send
 
 
-def call(kernel, outs, scratch, hbm, vmem, copies=0, micros=1.0, after=(), limit=20, in_hbm=0):
+def call(kernel, outs, scratch, hbm, vmem, copies=0, micros=1.0, after=(), limit=20):
     in_specs = [pl.BlockSpec(memory_space=pl.ANY)] * len(hbm)
     in_specs += [pl.BlockSpec(memory_space=pltpu.VMEM)] * len(vmem)
     in_specs += [pl.BlockSpec(memory_space=pl.ANY)] * len(after)
@@ -659,7 +651,7 @@
         body,
         out_shape=[jax.ShapeDtypeStruct(*out) for out in outs],
         in_specs=in_specs,
-        out_specs=[pl.BlockSpec(memory_space=pl.ANY if at < in_hbm else pltpu.VMEM) for at in range(len(outs))],
+        out_specs=[pl.BlockSpec(memory_space=pltpu.VMEM)] * len(outs),
         scratch_shapes=shapes,
         cost_estimate=pl.CostEstimate(flops=int(micros * 1e9), bytes_accessed=0, transcendentals=0),
         compiler_params=pltpu.CompilerParams(vmem_limit_bytes=limit * 1024 * 1024),
@@ -714,8 +706,8 @@
         [block_count, ocean], [fields, first, second], 2, 1.0, after=[fold],
     )
     fold, rims = swap(fold, "fold"), swap(rims, "fold")
-    normed, yhat, inverse, dproj_t, dact = call(
-        bind(early_kernel), [whole, whole_f, narrow, flat, ((cells, hidden), F32)],
+    normed, yhat, inverse, dproj_t, dact, live = call(
+        bind(early_kernel), [whole, whole_f, narrow, flat, ((cells, hidden), F32), ((slots, 8, channels), F32)],
         [count_s, ocean_s, taps, ((parts, shape.early * shape.columns, LANES), F32), whole],
         [block_count, ocean], [taps_in, gain, w_out, scale, tangent, band], 2, 5.0,
     )
@@ -756,21 +748,25 @@
 
     small_rows = -(-(KSIZE * KSIZE + 2) // 32) * 32
     came = core_swap(give)
-    conv_grad, gain_part = call(
-        bind(norm_grad_kernel), [whole, eight], [], [], [w_in, gain, dpreact, yhat, inverse], 0, 1.0,
+    conv_grad, projected, gain_part, scale_part = call(
+        bind(norm_grad_kernel), [whole, whole_f, eight, eight], [], [],
+        [w_in, w_out, gain, dpreact, yhat, inverse, activated, tangent, live], 0, 1.3,
     )
     mine, send = call(
         functools.partial(join_kernel, order[0]),
-        [((hidden, channels), F32), ((rows, channels), BF16)], [], [], [keep, came], after=[conv_grad], micros=0.3,
+        [((hidden, channels), F32), ((rows, channels), BF16)], [], [], [keep, came], after=[gain_part], micros=0.3,
     )
     came = bit_swap(send, order[0])
-    taps_parts = [taps_part(0, [send])]
-    state, scale_part = call(
-        bind(state_kernel), [whole, eight], [count_s, ocean_s],
-        [block_count, ocean], [fields, tangent, w_out, scale, activated], 2, 1.5, after=taps_parts,
-    )
+    core_grad = []
+    after = [send]
+    for part in range(parts):
+        one, *fold_back = back_part(part, core_grad, after)
+        core_grad += [one]
+        after = [one]
+    taps_parts = [taps_part(0, after)]
+    fold_back = swap(fold_back[0], "fold")
     body, outs = half_step(0, rows)
-    mine, send = call(body, outs, [], [], [mine, came], after=[scale_part], micros=0.3)
+    mine, send = call(body, outs, [], [], [mine, came], after=taps_parts, micros=0.3)
     came = bit_swap(send, order[1])
     taps_parts += [taps_part(part, [send]) for part in range(1, parts)]
     small_rows //= 2
@@ -778,20 +774,22 @@
         pack_kernel, [((small_rows, channels), F32), ((2 * small_rows, channels), BF16)],
         [((2 * small_rows, channels), F32)], [], [gain_part, scale_part, *taps_parts], micros=0.3,
     )
+    extra = core_swap(extra)
     rows //= 2
     body, outs = half_step(1, rows)
     mine, send = call(body, outs, [], [], [mine, came], after=[small], micros=0.3)
-    extra = core_swap(extra)
     mine, send = halved(mine, send, order[2:-1])
     came = bit_swap(send, order[-2])
-    core_grad = []
-    for part in range(parts - 1):
-        core_grad += back_part(part, core_grad, [send])
+    folded, first, second = call(
+        bind(rims_kernel), [strip(TILE), edge, edge], [count_s], [block_count], [fold_back, *core_grad], 1, 1.0,
+        after=[send],
+    )
+    first, second = swap(first, "first"), swap(second, "second")
     rows = came.shape[0]
     if rows % 16 == 0:
         (payload,) = call(
             functools.partial(turn_kernel, order[-2]), [((rows + small_rows, channels), BF16)],
-            [], [], [mine, came, small, extra], after=core_grad, micros=0.3,
+            [], [], [mine, came, small, extra], after=[folded], micros=0.3,
         )
     else:
         bit = bit_here(order[-2])
@@ -799,14 +797,15 @@
         small = small + (extra[:small_rows].astype(F32) + extra[small_rows:].astype(F32))
         payload = jnp.concatenate([share + came.astype(F32), small]).astype(BF16)
     came = bit_swap(payload, order[-1])
-    last_grad, fold_back = back_part(parts - 1, core_grad, [payload])
-    core_grad += [last_grad]
-    fold_back = swap(fold_back, "fold")
+    grad_fields, done = call(
+        bind(final_kernel), [whole, ((8, LANES), F32)], [count_s, ocean_s, strip(TILE)],
+        [block_count, ocean], [tangent, folded, first, second], 2, 1.5, after=[payload],
+    )
     (payload,) = call(
-        add_kernel, [(payload.shape, BF16)], [], [], [payload, came], after=[last_grad], micros=0.3,
+        add_kernel, [(payload.shape, BF16)], [], [], [payload, came], after=[done], micros=0.3,
     )
     came = bit_swap(payload, order[-2])
-    after = [fold_back]
+    after = []
     for at in reversed(range(len(order) - 1)):
         copies = 2 if at == 0 else 1
         if rows % 16 == 0:
@@ -824,25 +823,18 @@
         after = []
         rows *= 2
         came = bit_swap(payload, order[at - 1]) if at else core_swap(payload)
-        if at == 2:
-            folded, first, second = call(
-                bind(rims_kernel), [strip(TILE), edge, edge], [count_s], [block_count], [fold_back, *core_grad], 1, 1.0,
+        if at == 1:
+            state, done = call(
+                bind(state_kernel), [whole, ((8, LANES), F32)], [], [], [fields, scale, projected, live], 0, 1.5,
                 after=[payload],
-            )
-            first, second = swap(first, "first"), swap(second, "second")
-            after = [first, second]
-        if at == 1:
-            grad_fields, done = call(
-                bind(final_kernel), [whole, ((8, LANES), F32)], [count_s, ocean_s, strip(TILE)],
-                [block_count, ocean], [tangent, folded, first, second], 2, 1.5, after=[payload],
             )
             after = [done]
     total = samples * lax.axis_size("dp") * slots * lax.axis_size(TILES) * tile_rows * tile_cols
     norm = total ** (-0.5)
     sums = [((channels, hidden), F32), ((hidden, channels), F32)]
     w_in_sum, w_out_sum, kernel_sum, gain_sum, scale_sum = call(
-        functools.partial(unpack_kernel, norm), sums + [(kernel.shape, F32), row, row], sums,
-        [], [payload, came], 2 * hidden // channels, 1.5, in_hbm=2,
+        functools.partial(unpack_kernel, norm), sums + [(kernel.shape, F32), row, row], [],
+        [], [payload, came], 0, 1.5,
     )
     return (
         state.reshape(grid),

time: 68.2 us -> 66.4 us (0.974)
  waiting for transfers between devices: 24.6 us -> 21.8 us
  starting transfers between devices: 16.3 us -> 18.5 us
  Pallas kernels: 24.4 us -> 23.3 us
    ppermute x7, waiting for transfers between devices: 5.89 us -> 0.98 us  [swap(): return lax.ppermute(block, TILES, pairs_of(kind))]
    ppermute x7, waiting for transfers between devices: 15.7 us -> 18.1 us  [bit_swap(): return lax.ppermute(block, ('chips', 'core', 'dp'), pairs)]
    ppermute x7, starting transfers between devices: 4.97 us -> 6.4 us  [bit_swap(): return lax.ppermute(block, ('chips', 'core', 'dp'), pairs)]
    pallas_call x23, Pallas kernels: 24.4 us -> 23.3 us  [call(): pl.pallas_call(body, out_shape=[jax.ShapeDtypeStruct(*out) for out in out...]
    ppermute x7, starting transfers between devices: 11.1 us -> 11.9 us  [swap(): return lax.ppermute(block, TILES, pairs_of(kind))]
  transfers between devices with their start and end apart: 17 -> 17, of which waited for: 11 -> 9; matrix products, arithmetic and copies ran while one was open for 0% -> 0% of each run, Pallas kernels for 26% -> 25%
where the time goes in v5:
time: 66.4 us; the launch traced here: 66.2 us
  Pallas kernels  23.3 us (35%)
  waiting for transfers between devices  21.8 us (33%)
  starting transfers between devices  18.5 us (28%)
  between operations  1.57 us (2%)
  local copies, waits for them, and re-layouts  1.04 us (2%)
    pallas_call x23, Pallas kernels, call(): pl.pallas_call(body, out_shape=[jax.ShapeDtypeStruct(*out) for out in out...  23.3 us
    ppermute x7, waiting for transfers between devices, bit_swap(): return lax.ppermute(block, ('chips', 'core', 'dp'), pairs)  18.1 us
    ppermute x7, starting transfers between devices, swap(): return lax.ppermute(block, TILES, pairs_of(kind))  11.9 us
    ppermute x7, starting transfers between devices, bit_swap(): return lax.ppermute(block, ('chips', 'core', 'dp'), pairs)  6.4 us
    ppermute x3, waiting for transfers between devices, core_swap(): return lax.ppermute(block, 'core', [(0, 1), (1, 0)])  2.75 us
  transfers between devices with their start and end apart: 17, of which 9 were waited for; matrix products, arithmetic and copies ran while one was open for 0% of the time, Pallas kernels for 25%

profile of v5, /device:TPU:0, one launch (start us, length us, event | category | flops | bytes accessed | tf_op | source)
XLA Modules:
  0.0 66.2 jit_solution(10406376661314854667)
XLA Ops:
  1.3 0.0 copy-start.4
  1.3 1.0 %copy-done.4 = bf16[1,3,16,16,256]{4,3,2,1,0:T(8,128)(2,1)S(1)} copy-done((bf16[1,3,16,16,256]{4,3,2,1,0:T(8,128)(2,1)S(1)}, bf16[1,3,16,16,256]{4,3,2,1,0:T(8,128)(2,1)}, u32[]{:S(2)}) %copy-start.4) | copy-done | bytes 393240
  2.3 0.6 shard_map.144
  2.9 4.1 %collective-permute-start.1 = (bf16[48,256]{1,0:T(8,128)(2,1)S(1)}, bf16[48,256]{1,0:T(8,128)(2,1)S(1)}, u32[]{:S(2)}, u32[]{:S(2)}) collective-permute-start(bf16[48,256]{1,0:T(8,128)(2,1)S(1)} %get-tuple-element.51), channel_id=1, source_target_pairs={{0,16},{2,4},{4,2},{6,8},{8,6},{10,12},{12,10},{14,30},{30,14},{28... | collective-permute-start | bytes 73736 | tf_op jit(solution)/shard_map/ppermute | solution.py:536
  7.0 0.7 %shard_map.145.refs_5_ = bf16[144,256]{1,0:T(8,128)(2,1)S(1)} custom-call(s32[1]{0:T(128)S(6)} %copy.16.refs_0_, s32[3]{0:T(128)S(1)} %copy-done.8, bf16[768,256]{1,0:T(8,128)(2,1)S(1)} %bitcast.15, bf16[48,256]{1,0:T(8,128)(2,1)S(1)} %get-tuple-element.50.refs_3_), custom_call_target="tpu_custom_call" | custom-call | flops 500000000 | tf_op jit(solution)/shard_map/pallas_call | solution.py:650
  7.7 0.0 copy-start.1
  7.7 0.0 copy-start.2
  7.7 0.0 copy-start.3
  7.8 1.7 %collective-permute-start.2 = (bf16[144,256]{1,0:T(8,128)(2,1)S(1)}, bf16[144,256]{1,0:T(8,128)(2,1)S(1)}, u32[]{:S(2)}, u32[]{:S(2)}) collective-permute-start(bf16[144,256]{1,0:T(8,128)(2,1)S(1)} %shard_map.145.refs_5_), channel_id=1, source_target_pairs={{0,16},{2,18},{4,20},{6,22},{8,24},{10,26},{12,28},{14,30},{30,14}... | collective-permute-start | bytes 221192 | tf_op jit(solution)/shard_map/ppermute | solution.py:536
  9.4 0.7 %shard_map.146 = (f32[2,1216,128]{2,1,0:T(8,128)S(1)}, bf16[48,256]{1,0:T(8,128)(2,1)S(1)}) custom-call(s32[1]{0:T(128)S(6)} %copy.16.refs_0_, s32[3]{0:T(128)S(1)} %copy-done.8, bf16[768,256]{1,0:T(8,128)(2,1)S(1)} %bitcast.16, bf16[48,256]{1,0:T(8,128)(2,1)S(1)} %collective-permute-done.refs_3_, bf16[48,256]{1,0:T(8,128)(2,1)S(1)} %collective-permute-done.1.refs_4_, ...), custom_call_target="tpu_custom_call" | custom-call | flops 1000000000 | tf_op jit(solution)/shard_map/pallas_call | solution.py:650
  10.2 2.3 %collective-permute-start.3 = (bf16[48,256]{1,0:T(8,128)(2,1)S(1)}, bf16[48,256]{1,0:T(8,128)(2,1)S(1)}, u32[]{:S(2)}, u32[]{:S(2)}) collective-permute-start(bf16[48,256]{1,0:T(8,128)(2,1)S(1)} %get-tuple-element.53), channel_id=1, source_target_pairs={{0,16},{2,18},{4,20},{6,22},{8,24},{10,26},{12,28},{14,30},{30,14}... | collective-permute-start | bytes 73736 | tf_op jit(solution)/shard_map/ppermute | solution.py:536
  12.5 0.0 copy-start
  12.6 3.7 %shard_map.147 = (bf16[768,256]{1,0:T(8,128)(2,1)S(1)}, f32[768,256]{1,0:T(8,128)S(1)}, f32[768,128]{1,0:T(8,128)S(1)}, bf16[256,768]{1,0:T(8,128)(2,1)S(1)}, f3...) custom-call(s32[1]{0:T(128)S(6)} %copy.16.refs_0_, s32[3]{0:T(128)S(1)} %copy-done.8, bf16[7,7,256]{2,1,0:T(8,128)(2,1)S(1)} %copy-done.6, ...), custom_call_target="tpu_custom_call" | custom-call | flops 5000000000 | tf_op jit(solution)/shard_map/pallas_call | solution.py:650
  16.3 4.1 %shard_map.148 = (f32[1024,256]{1,0:T(8,128)S(1)}, bf16[1024,256]{1,0:T(8,128)(2,1)S(1)}, bf16[768,1024]{1,0:T(8,128)(2,1)S(1)}, bf16[768,1024]{1,0:T(8,128)(2,1...) custom-call(s32[1]{0:T(128)S(6)} %copy.16.refs_0_, ...), custom_call_target="tpu_custom_call" | custom-call | flops 5000000000 | tf_op jit(solution)/shard_map/pallas_call | solution.py:650
  20.4 0.1 collective-permute-start.4
  20.5 1.1 %shard_map.149 = (bf16[768,256]{1,0:T(8,128)(2,1)S(1)}, f32[768,256]{1,0:T(8,128)S(1)}, f32[8,256]{1,0:T(8,128)S(1)}, f32[8,256]{1,0:T(8,128)S(1)}) custom-call(bf16[256,1024]{1,0:T(8,128)(2,1)S(1)} %copy-done, bf16[1024,256]{1,0:T(8,128)(2,1)S(1)} %copy-done.1, f32[1,256]{1,0:T(1,128)S(1)} %bitcast.13, bf16[768,1024]{1,0:T(8,128)(2,1)S(1)} %get-tuple-element.59.refs_3_, ...), custom_call_target="tpu_custom_call" | custom-call | flops 1300000000 | tf_op jit(solution)/shard_map/pallas_call | solution.py:650
  21.6 0.8 %collective-permute-done.4.refs_1_ = bf16[1024,256]{1,0:T(8,128)(2,1)S(1)} collective-permute-done((bf16[1024,256]{1,0:T(8,128)(2,1)S(1)}, bf16[1024,256]{1,0:T(8,128)(2,1)S(1)}, u32[]{:S(2)}, u32[]{:S(2)}) %collective-permute-start.4) | collective-permute-done | bytes 524320 | tf_op jit(solution)/shard_map/ppermute | solution.py:540
  22.4 0.2 shard_map.150
  22.5 0.4 collective-permute-start.5
  22.9 1.7 %shard_map.151.refs_3_.refs_4_.refs_2_ = f32[1216,128]{1,0:T(8,128)S(1)} custom-call(s32[1]{0:T(128)S(6)} %copy.16.refs_0_, bf16[7,7,256]{2,1,0:T(8,128)(2,1)S(1)} %copy-done.6, bf16[768,256]{1,0:T(8,128)(2,1)S(1)} %get-tuple-element.71.refs_2_, bf16[512,256]{1,0:T(8,128)(2,1)S(1)} %get-tuple-element.69.refs_3_), custom_call_target="tpu_custom_call" | custom-call | flops 2000000000 | tf_op jit(solution)/shard_map/pallas_call | solution.py:650
  24.6 1.9 %shard_map.152 = (f32[1216,128]{1,0:T(8,128)S(1)}, bf16[192,256]{1,0:T(8,128)(2,1)S(1)}) custom-call(s32[1]{0:T(128)S(6)} %copy.16.refs_0_, bf16[7,7,256]{2,1,0:T(8,128)(2,1)S(1)} %copy-done.6, bf16[768,256]{1,0:T(8,128)(2,1)S(1)} %get-tuple-element.71.refs_2_, f32[1216,128]{1,0:T(8,128)S(1)} %shard_map.151.refs_3_.refs_4_.refs_2_, ...), custom_call_target="tpu_custom_call" | custom-call | flops 2000000000 | tf_op jit(solution)/shard_map/pallas_call | solution.py:650
  26.5 2.0 %collective-permute-start.9 = (bf16[192,256]{1,0:T(8,128)(2,1)S(1)}, bf16[192,256]{1,0:T(8,128)(2,1)S(1)}, u32[]{:S(2)}, u32[]{:S(2)}) collective-permute-start(bf16[192,256]{1,0:T(8,128)(2,1)S(1)} %get-tuple-element.80), channel_id=1, source_target_pairs={{0,16},{2,18},{4,20},{6,22},{8,24},{10,26},{12,28},{14,30},{30,14}... | collective-permute-start | bytes 294920 | tf_op jit(solution)/shard_map/ppermute | solution.py:536
  28.5 1.8 %shard_map.153.refs_2_ = f32[64,128]{1,0:T(8,128)S(1)} custom-call(f32[2,1216,128]{2,1,0:T(8,128)S(1)} %get-tuple-element.52.refs_7_.refs_4_.refs_0_, f32[2,640,128]{2,1,0:T(8,128)S(1)} %get-tuple-element.70.refs_1_, bf16[768,256]{1,0:T(8,128)(2,1)S(1)} %get-tuple-element.71.refs_2_, f32[1216,128]{1,0:T(8,128)S(1)} %get-tuple-element.72.refs_3_), custom_call_target="tpu_custom_call" | custom-call | flops 1800000000 | tf_op jit(solution)/shard_map/pallas_call | solution.py:650
  30.3 0.1 shard_map.154
  30.4 1.6 %collective-permute-start.6 = (bf16[256,256]{1,0:T(8,128)(2,1)S(1)}, bf16[256,256]{1,0:T(8,128)(2,1)S(1)}, u32[]{:S(2)}, u32[]{:S(2)}) collective-permute-start(bf16[256,256]{1,0:T(8,128)(2,1)S(1)} %get-tuple-element.74.refs_3_), channel_id=1, source_target_pairs={{0,1},{1,0},{2,6},{3,7},{4,5},{5,4},{6,2},{7,3},{8,9},{9,8},{10,14... | collective-permute-start | bytes 393224 | tf_op jit(solution)/shard_map/ppermute | solution.py:560
  32.0 1.8 %shard_map.155.refs_3_ = f32[64,128]{1,0:T(8,128)S(1)} custom-call(f32[2,1216,128]{2,1,0:T(8,128)S(1)} %get-tuple-element.52.refs_7_.refs_4_.refs_0_, f32[2,640,128]{2,1,0:T(8,128)S(1)} %get-tuple-element.70.refs_1_, bf16[768,256]{1,0:T(8,128)(2,1)S(1)} %get-tuple-element.71.refs_2_, bf16[256,256]{1,0:T(8,128)(2,1)S(1)} %get-tuple-element.74.refs_3_), custom_call_target="tpu_custom_call" | custom-call | flops 1800000000 | tf_op jit(solution)/shard_map/pallas_call | solution.py:650
  33.8 0.1 collective-permute-start.8
  33.9 1.6 %collective-permute-done.6.refs_1_ = bf16[256,256]{1,0:T(8,128)(2,1)S(1)} collective-permute-done((bf16[256,256]{1,0:T(8,128)(2,1)S(1)}, bf16[256,256]{1,0:T(8,128)(2,1)S(1)}, u32[]{:S(2)}, u32[]{:S(2)}) %collective-permute-start.6) | collective-permute-done | bytes 131104 | tf_op jit(solution)/shard_map/ppermute | solution.py:560
  35.5 0.8 %collective-permute-start.7 = (bf16[128,256]{1,0:T(8,128)(2,1)S(1)}, bf16[128,256]{1,0:T(8,128)(2,1)S(1)}, u32[]{:S(2)}, u32[]{:S(2)}) collective-permute-start(bf16[128,256]{1,0:T(8,128)(2,1)S(1)} %get-tuple-element.78.refs_4_), channel_id=1, source_target_pairs={{0,8},{1,9},{2,3},{3,2},{4,12},{5,13},{6,7},{7,6},{8,0},{9,1},{10,... | collective-permute-start | bytes 196616 | tf_op jit(solution)/shard_map/ppermute | solution.py:560
  36.3 0.6 shard_map.158
  36.9 0.1 collective-permute-start.11
  37.0 1.7 %collective-permute-start.12 = (bf16[48,256]{1,0:T(8,128)(2,1)S(1)}, bf16[48,256]{1,0:T(8,128)(2,1)S(1)}, u32[]{:S(2)}, u32[]{:S(2)}) collective-permute-start(bf16[48,256]{1,0:T(8,128)(2,1)S(1)} %get-tuple-element.83), channel_id=1, source_target_pairs={{0,16},{2,4},{4,2},{6,8},{8,6},{10,12},{12,10},{14,30},{30,14},{28... | collective-permute-start | bytes 73736 | tf_op jit(solution)/shard_map/ppermute | solution.py:536
  38.7 1.1 %collective-permute-done.7.refs_1_ = bf16[128,256]{1,0:T(8,128)(2,1)S(1)} collective-permute-done((bf16[128,256]{1,0:T(8,128)(2,1)S(1)}, bf16[128,256]{1,0:T(8,128)(2,1)S(1)}, u32[]{:S(2)}, u32[]{:S(2)}) %collective-permute-start.7) | collective-permute-done | bytes 65568 | tf_op jit(solution)/shard_map/ppermute | solution.py:560
  39.8 1.1 %collective-permute-start.10 = (bf16[160,256]{1,0:T(8,128)(2,1)S(1)}, bf16[160,256]{1,0:T(8,128)(2,1)S(1)}, u32[]{:S(2)}, u32[]{:S(2)}) collective-permute-start(bf16[160,256]{1,0:T(8,128)(2,1)S(1)} %shard_map.159.refs_6_.refs_0_), channel_id=1, source_target_pairs={{0,16},{1,17},{2,18},{3,19},{4,20},{5,21},{6,22},{7,23},{8,24},{9,... | collective-permute-start | bytes 245768 | tf_op jit(solution)/shard_map/ppermute | solution.py:560
  40.9 1.0 %collective-permute-done.12.refs_5_ = bf16[48,256]{1,0:T(8,128)(2,1)S(1)} collective-permute-done((bf16[48,256]{1,0:T(8,128)(2,1)S(1)}, bf16[48,256]{1,0:T(8,128)(2,1)S(1)}, u32[]{:S(2)}, u32[]{:S(2)}) %collective-permute-start.12) | collective-permute-done | bytes 24608 | tf_op jit(solution)/shard_map/ppermute | solution.py:536
  41.9 1.6 %shard_map.160 = (bf16[768,256]{1,0:T(8,128)(2,1)}, f32[8,128]{1,0:T(8,128)S(1)}) custom-call(s32[1]{0:T(128)S(6)} %copy.16.refs_0_, s32[3]{0:T(128)S(1)} %copy-done.8, bf16[768,256]{1,0:T(8,128)(2,1)S(1)} %bitcast.10, f32[2,1024,128]{2,1,0:T(8,128)S(1)} %get-tuple-element.81.refs_4_.refs_3_, bf16[48,256]{1,0:T(8,128)(2,1)S(1)} %collective-permute-done.11.refs_4_, ...), custom_call_target="tpu_custom_call" | custom-call | flops 1500000000 | tf_op jit(solution)/shard_map/pallas_call | solution.py:650
  43.5 2.6 %collective-permute-done.10.refs_1_ = bf16[160,256]{1,0:T(8,128)(2,1)S(1)} collective-permute-done((bf16[160,256]{1,0:T(8,128)(2,1)S(1)}, bf16[160,256]{1,0:T(8,128)(2,1)S(1)}, u32[]{:S(2)}, u32[]{:S(2)}) %collective-permute-start.10) | collective-permute-done | bytes 81952 | tf_op jit(solution)/shard_map/ppermute | solution.py:560
  46.1 0.1 collective-permute-start.13
  46.2 4.4 %collective-permute-done.13.refs_1_ = bf16[160,256]{1,0:T(8,128)(2,1)S(1)} collective-permute-done((bf16[160,256]{1,0:T(8,128)(2,1)S(1)}, bf16[160,256]{1,0:T(8,128)(2,1)S(1)}, u32[]{:S(2)}, u32[]{:S(2)}) %collective-permute-start.13) | collective-permute-done | bytes 81952 | tf_op jit(solution)/shard_map/ppermute | solution.py:560
  50.7 1.6 %collective-permute-start.14 = (bf16[288,256]{1,0:T(8,128)(2,1)S(1)}, bf16[288,256]{1,0:T(8,128)(2,1)S(1)}, u32[]{:S(2)}, u32[]{:S(2)}) collective-permute-start(bf16[288,256]{1,0:T(8,128)(2,1)S(1)} %shard_map.162.refs_0_), channel_id=1, source_target_pairs={{0,1},{1,0},{2,6},{3,7},{4,5},{5,4},{6,2},{7,3},{8,9},{9,8},{10,14... | collective-permute-start | bytes 442376 | tf_op jit(solution)/shard_map/ppermute | solution.py:560
  52.3 3.6 %collective-permute-done.14.refs_1_ = bf16[288,256]{1,0:T(8,128)(2,1)S(1)} collective-permute-done((bf16[288,256]{1,0:T(8,128)(2,1)S(1)}, bf16[288,256]{1,0:T(8,128)(2,1)S(1)}, u32[]{:S(2)}, u32[]{:S(2)}) %collective-permute-start.14) | collective-permute-done | bytes 147488 | tf_op jit(solution)/shard_map/ppermute | solution.py:560
  55.9 1.0 %collective-permute-start.15 = (bf16[544,256]{1,0:T(8,128)(2,1)S(1)}, bf16[544,256]{1,0:T(8,128)(2,1)S(1)}, u32[]{:S(2)}, u32[]{:S(2)}) collective-permute-start(bf16[544,256]{1,0:T(8,128)(2,1)S(1)} %shard_map.163.refs_4_.refs_0_), channel_id=1, source_target_pairs={{0,4},{1,5},{2,10},{3,11},{4,0},{5,1},{6,14},{7,15},{8,12},{9,13},... | collective-permute-start | bytes 835592 | tf_op jit(solution)/shard_map/ppermute | solution.py:560
  56.9 0.9 %shard_map.164 = (bf16[768,256]{1,0:T(8,128)(2,1)}, f32[8,128]{1,0:T(8,128)S(1)}) custom-call(bf16[768,256]{1,0:T(8,128)(2,1)S(1)} %bitcast.17, f32[1,256]{1,0:T(1,128)S(1)} %bitcast.19, f32[768,256]{1,0:T(8,128)S(1)} %get-tuple-element.64.refs_2_, f32[3,8,256]{2,1,0:T(8,128)S(1)} %get-tuple-element.63.refs_8_.refs_3_, ...), custom_call_target="tpu_custom_call" | custom-call | flops 1500000000 | tf_op jit(solution)/shard_map/pallas_call | solution.py:650
  57.8 4.8 %collective-permute-done.15.refs_1_ = bf16[544,256]{1,0:T(8,128)(2,1)S(1)} collective-permute-done((bf16[544,256]{1,0:T(8,128)(2,1)S(1)}, bf16[544,256]{1,0:T(8,128)(2,1)S(1)}, u32[]{:S(2)}, u32[]{:S(2)}) %collective-permute-start.15) | collective-permute-done | bytes 278560 | tf_op jit(solution)/shard_map/ppermute | solution.py:560
  62.5 0.1 shard_map.165.refs_0_
  62.6 0.1 collective-permute-start.16
  62.7 1.9 %collective-permute-done.16.refs_1_ = bf16[1088,256]{1,0:T(8,128)(2,1)S(1)} collective-permute-done((bf16[1088,256]{1,0:T(8,128)(2,1)S(1)}, bf16[1088,256]{1,0:T(8,128)(2,1)S(1)}, u32[]{:S(2)}, u32[]{:S(2)}) %collective-permute-start.16) | collective-permute-done | bytes 557088 | tf_op jit(solution)/shard_map/ppermute | solution.py:540
  64.6 1.6 %shard_map.166 = (f32[256,1024]{1,0:T(8,128)}, f32[1024,256]{1,0:T(8,128)}, f32[7,7,256]{2,1,0:T(8,128)}, f32[1,256]{1,0:T(1,128)}, f32[1,256]{1,0:T(1,128)}) custom-call(bf16[1088,256]{1,0:T(8,128)(2,1)S(1)} %shard_map.165.refs_0_, bf16[1088,256]{1,0:T(8,128)(2,1)S(1)} %collective-permute-done.16.refs_1_), custom_call_target="tpu_custom_call" | custom-call | flops 1500000000 | tf_op jit(solution)/shard_map/pallas_call | solution.py:650
  (27 shorter events, 0.2 us)
Async XLA Ops:
  1.3 1.0 %copy-start.4 = (bf16[1,3,16,16,256]{4,3,2,1,0:T(8,128)(2,1)S(1)}, bf16[1,3,16,16,256]{4,3,2,1,0:T(8,128)(2,1)}, u32[]{:S(2)}) copy-start(bf16[1,3,16,16,256]{4,3,2,1,0:T(8,128)(2,1)} %param.9) | copy-start | bytes 1179652
  2.3 4.7 %copy-start.8 = (s32[3]{0:T(128)S(1)}, s32[3]{0:T(128)}, u32[]{:S(2)}) copy-start(s32[3]{0:T(128)} %refs_1_.15) | copy-start | bytes 40
  2.9 6.6 %collective-permute-start.1 = (bf16[48,256]{1,0:T(8,128)(2,1)S(1)}, bf16[48,256]{1,0:T(8,128)(2,1)S(1)}, u32[]{:S(2)}, u32[]{:S(2)}) collective-permute-start(bf16[48,256]{1,0:T(8,128)(2,1)S(1)} %get-tuple-element.51), channel_id=1, source_target_pairs={{0,16},{2,4},{4,2},{6,8},{8,6},{10,12},{12,10},{14,30},{30,14},{28... | collective-permute-start | bytes 73736 | tf_op jit(solution)/shard_map/ppermute | solution.py:536
  7.0 2.5 %collective-permute-start = (bf16[48,256]{1,0:T(8,128)(2,1)S(1)}, bf16[48,256]{1,0:T(8,128)(2,1)S(1)}, u32[]{:S(2)}, u32[]{:S(2)}) collective-permute-start(bf16[48,256]{1,0:T(8,128)(2,1)S(1)} %get-tuple-element.50.refs_3_), channel_id=1, source_target_pairs={{0,2},{2,0},{4,6},{6,4},{8,10},{10,8},{12,14},{14,12},{30,28},{28,... | collective-permute-start | bytes 73736 | tf_op jit(solution)/shard_map/ppermute | solution.py:536
  7.7 4.8 %copy-start.1 = (bf16[1024,256]{1,0:T(8,128)(2,1)S(1)}, bf16[1024,256]{1,0:T(8,128)(2,1)}, u32[]{:S(2)}) copy-start(bf16[1024,256]{1,0:T(8,128)(2,1)} %refs_1_.12) | copy-start | bytes 1572868
  7.7 4.8 %copy-start.2 = (bf16[1,3,16,16,256]{4,3,2,1,0:T(8,128)(2,1)S(1)}, bf16[1,3,16,16,256]{4,3,2,1,0:T(8,128)(2,1)}, u32[]{:S(2)}) copy-start(bf16[1,3,16,16,256]{4,3,2,1,0:T(8,128)(2,1)} %param.10) | copy-start | bytes 1179652
  7.7 4.8 %copy-start.3 = (f32[256]{0:T(256)S(1)}, f32[256]{0:T(256)}, u32[]{:S(2)}) copy-start(f32[256]{0:T(256)} %param.14) | copy-start | bytes 3076
  7.7 4.8 %copy-start.6 = (bf16[7,7,256]{2,1,0:T(8,128)(2,1)S(1)}, bf16[7,7,256]{2,1,0:T(8,128)(2,1)}, u32[]{:S(2)}) copy-start(bf16[7,7,256]{2,1,0:T(8,128)(2,1)} %refs_1_.14) | copy-start | bytes 75268
  7.8 4.8 %copy-start.7 = (f32[256]{0:T(256)S(1)}, f32[256]{0:T(256)}, u32[]{:S(2)}) copy-start(f32[256]{0:T(256)} %param.17) | copy-start | bytes 3076
  7.8 8.5 %collective-permute-start.2 = (bf16[144,256]{1,0:T(8,128)(2,1)S(1)}, bf16[144,256]{1,0:T(8,128)(2,1)S(1)}, u32[]{:S(2)}, u32[]{:S(2)}) collective-permute-start(bf16[144,256]{1,0:T(8,128)(2,1)S(1)} %shard_map.145.refs_5_), channel_id=1, source_target_pairs={{0,16},{2,18},{4,20},{6,22},{8,24},{10,26},{12,28},{14,30},{30,14}... | collective-permute-start | bytes 221192 | tf_op jit(solution)/shard_map/ppermute | solution.py:536
  10.2 6.0 %collective-permute-start.3 = (bf16[48,256]{1,0:T(8,128)(2,1)S(1)}, bf16[48,256]{1,0:T(8,128)(2,1)S(1)}, u32[]{:S(2)}, u32[]{:S(2)}) collective-permute-start(bf16[48,256]{1,0:T(8,128)(2,1)S(1)} %get-tuple-element.53), channel_id=1, source_target_pairs={{0,16},{2,18},{4,20},{6,22},{8,24},{10,26},{12,28},{14,30},{30,14}... | collective-permute-start | bytes 73736 | tf_op jit(solution)/shard_map/ppermute | solution.py:536
  12.5 3.7 %copy-start = (bf16[256,1024]{1,0:T(8,128)(2,1)S(1)}, bf16[256,1024]{1,0:T(8,128)(2,1)}, u32[]{:S(2)}) copy-start(bf16[256,1024]{1,0:T(8,128)(2,1)} %refs_0_.10) | copy-start | bytes 1572868
  20.4 2.0 %collective-permute-start.4 = (bf16[1024,256]{1,0:T(8,128)(2,1)S(1)}, bf16[1024,256]{1,0:T(8,128)(2,1)S(1)}, u32[]{:S(2)}, u32[]{:S(2)}) collective-permute-start(bf16[1024,256]{1,0:T(8,128)(2,1)S(1)} %get-tuple-element.66), channel_id=1, source_target_pairs={{0,2},{2,0},{1,3},{3,1},{4,6},{6,4},{5,7},{7,5},{8,10},{10,8},{9,1... | collective-permute-start | bytes 1572872 | tf_op jit(solution)/shard_map/ppermute | solution.py:540
  22.5 7.8 %collective-permute-start.5 = (bf16[512,256]{1,0:T(8,128)(2,1)S(1)}, bf16[512,256]{1,0:T(8,128)(2,1)S(1)}, u32[]{:S(2)}, u32[]{:S(2)}) collective-permute-start(bf16[512,256]{1,0:T(8,128)(2,1)S(1)} %get-tuple-element.69.refs_3_), channel_id=1, source_target_pairs={{0,4},{1,5},{2,10},{3,11},{4,0},{5,1},{6,14},{7,15},{8,12},{9,13},... | collective-permute-start | bytes 786440 | tf_op jit(solution)/shard_map/ppermute | solution.py:560
  26.5 9.7 %collective-permute-start.9 = (bf16[192,256]{1,0:T(8,128)(2,1)S(1)}, bf16[192,256]{1,0:T(8,128)(2,1)S(1)}, u32[]{:S(2)}, u32[]{:S(2)}) collective-permute-start(bf16[192,256]{1,0:T(8,128)(2,1)S(1)} %get-tuple-element.80), channel_id=1, source_target_pairs={{0,16},{2,18},{4,20},{6,22},{8,24},{10,26},{12,28},{14,30},{30,14}... | collective-permute-start | bytes 294920 | tf_op jit(solution)/shard_map/ppermute | solution.py:536
  30.4 5.0 %collective-permute-start.6 = (bf16[256,256]{1,0:T(8,128)(2,1)S(1)}, bf16[256,256]{1,0:T(8,128)(2,1)S(1)}, u32[]{:S(2)}, u32[]{:S(2)}) collective-permute-start(bf16[256,256]{1,0:T(8,128)(2,1)S(1)} %get-tuple-element.74.refs_3_), channel_id=1, source_target_pairs={{0,1},{1,0},{2,6},{3,7},{4,5},{5,4},{6,2},{7,3},{8,9},{9,8},{10,14... | collective-permute-start | bytes 393224 | tf_op jit(solution)/shard_map/ppermute | solution.py:560
  33.8 4.9 %collective-permute-start.8 = (bf16[64,256]{1,0:T(8,128)(2,1)S(1)}, bf16[64,256]{1,0:T(8,128)(2,1)S(1)}, u32[]{:S(2)}, u32[]{:S(2)}) collective-permute-start(bf16[64,256]{1,0:T(8,128)(2,1)S(1)} %get-tuple-element.79), channel_id=1, source_target_pairs={{0,2},{2,0},{1,3},{3,1},{4,6},{6,4},{5,7},{7,5},{8,10},{10,8},{9,1... | collective-permute-start | bytes 98312 | tf_op jit(solution)/shard_map/ppermute | solution.py:540
  35.5 4.3 %collective-permute-start.7 = (bf16[128,256]{1,0:T(8,128)(2,1)S(1)}, bf16[128,256]{1,0:T(8,128)(2,1)S(1)}, u32[]{:S(2)}, u32[]{:S(2)}) collective-permute-start(bf16[128,256]{1,0:T(8,128)(2,1)S(1)} %get-tuple-element.78.refs_4_), channel_id=1, source_target_pairs={{0,8},{1,9},{2,3},{3,2},{4,12},{5,13},{6,7},{7,6},{8,0},{9,1},{10,... | collective-permute-start | bytes 196616 | tf_op jit(solution)/shard_map/ppermute | solution.py:560
  36.9 4.0 %collective-permute-start.11 = (bf16[48,256]{1,0:T(8,128)(2,1)S(1)}, bf16[48,256]{1,0:T(8,128)(2,1)S(1)}, u32[]{:S(2)}, u32[]{:S(2)}) collective-permute-start(bf16[48,256]{1,0:T(8,128)(2,1)S(1)} %get-tuple-element.82), channel_id=1, source_target_pairs={{0,2},{2,0},{4,6},{6,4},{8,10},{10,8},{12,14},{14,12},{30,28},{28,... | collective-permute-start | bytes 73736 | tf_op jit(solution)/shard_map/ppermute | solution.py:536
  37.0 4.9 %collective-permute-start.12 = (bf16[48,256]{1,0:T(8,128)(2,1)S(1)}, bf16[48,256]{1,0:T(8,128)(2,1)S(1)}, u32[]{:S(2)}, u32[]{:S(2)}) collective-permute-start(bf16[48,256]{1,0:T(8,128)(2,1)S(1)} %get-tuple-element.83), channel_id=1, source_target_pairs={{0,16},{2,4},{4,2},{6,8},{8,6},{10,12},{12,10},{14,30},{30,14},{28... | collective-permute-start | bytes 73736 | tf_op jit(solution)/shard_map/ppermute | solution.py:536
  39.8 6.3 %collective-permute-start.10 = (bf16[160,256]{1,0:T(8,128)(2,1)S(1)}, bf16[160,256]{1,0:T(8,128)(2,1)S(1)}, u32[]{:S(2)}, u32[]{:S(2)}) collective-permute-start(bf16[160,256]{1,0:T(8,128)(2,1)S(1)} %shard_map.159.refs_6_.refs_0_), channel_id=1, source_target_pairs={{0,16},{1,17},{2,18},{3,19},{4,20},{5,21},{6,22},{7,23},{8,24},{9,... | collective-permute-start | bytes 245768 | tf_op jit(solution)/shard_map/ppermute | solution.py:560
  46.1 10.8 %copy-start.5 = (bf16[1,3,16,16,256]{4,3,2,1,0:T(8,128)(2,1)S(1)}, bf16[1,3,16,16,256]{4,3,2,1,0:T(8,128)(2,1)}, u32[]{:S(2)}) copy-start(bf16[1,3,16,16,256]{4,3,2,1,0:T(8,128)(2,1)} %param.9) | copy-start | bytes 1179652
  46.1 4.5 %collective-permute-start.13 = (bf16[160,256]{1,0:T(8,128)(2,1)S(1)}, bf16[160,256]{1,0:T(8,128)(2,1)S(1)}, u32[]{:S(2)}, u32[]{:S(2)}) collective-permute-start(bf16[160,256]{1,0:T(8,128)(2,1)S(1)} %shard_map.161.refs_0_), channel_id=1, source_target_pairs={{0,8},{1,9},{2,3},{3,2},{4,12},{5,13},{6,7},{7,6},{8,0},{9,1},{10,... | collective-permute-start | bytes 245768 | tf_op jit(solution)/shard_map/ppermute | solution.py:560
  50.7 5.2 %collective-permute-start.14 = (bf16[288,256]{1,0:T(8,128)(2,1)S(1)}, bf16[288,256]{1,0:T(8,128)(2,1)S(1)}, u32[]{:S(2)}, u32[]{:S(2)}) collective-permute-start(bf16[288,256]{1,0:T(8,128)(2,1)S(1)} %shard_map.162.refs_0_), channel_id=1, source_target_pairs={{0,1},{1,0},{2,6},{3,7},{4,5},{5,4},{6,2},{7,3},{8,9},{9,8},{10,14... | collective-permute-start | bytes 442376 | tf_op jit(solution)/shard_map/ppermute | solution.py:560
  55.9 6.6 %collective-permute-start.15 = (bf16[544,256]{1,0:T(8,128)(2,1)S(1)}, bf16[544,256]{1,0:T(8,128)(2,1)S(1)}, u32[]{:S(2)}, u32[]{:S(2)}) collective-permute-start(bf16[544,256]{1,0:T(8,128)(2,1)S(1)} %shard_map.163.refs_4_.refs_0_), channel_id=1, source_target_pairs={{0,4},{1,5},{2,10},{3,11},{4,0},{5,1},{6,14},{7,15},{8,12},{9,13},... | collective-permute-start | bytes 835592 | tf_op jit(solution)/shard_map/ppermute | solution.py:560
  62.6 2.0 %collective-permute-start.16 = (bf16[1088,256]{1,0:T(8,128)(2,1)S(1)}, bf16[1088,256]{1,0:T(8,128)(2,1)S(1)}, u32[]{:S(2)}, u32[]{:S(2)}) collective-permute-start(bf16[1088,256]{1,0:T(8,128)(2,1)S(1)} %shard_map.165.refs_0_), channel_id=1, source_target_pairs={{0,2},{2,0},{1,3},{3,1},{4,6},{6,4},{5,7},{7,5},{8,10},{10,8},{9,1... | collective-permute-start | bytes 1671176 | tf_op jit(solution)/shard_map/ppermute | solution.py:540

commit v6 on v5

--- a/solution.py
+++ b/solution.py
@@ -763,12 +763,11 @@
         one, *fold_back = back_part(part, core_grad, after)
         core_grad += [one]
         after = [one]
-    taps_parts = [taps_part(0, after)]
     fold_back = swap(fold_back[0], "fold")
     body, outs = half_step(0, rows)
-    mine, send = call(body, outs, [], [], [mine, came], after=taps_parts, micros=0.3)
+    mine, send = call(body, outs, [], [], [mine, came], after=after, micros=0.3)
     came = bit_swap(send, order[1])
-    taps_parts += [taps_part(part, [send]) for part in range(1, parts)]
+    taps_parts = [taps_part(part, [send]) for part in range(parts)]
     small_rows //= 2
     small, extra = call(
         pack_kernel, [((small_rows, channels), F32), ((2 * small_rows, channels), BF16)],

time: 66.4 us -> 65.7 us (0.989)
  starting transfers between devices: 18.5 us -> 17.3 us
    ppermute x7, starting transfers between devices: 6.4 us -> 5.61 us  [bit_swap(): return lax.ppermute(block, ('chips', 'core', 'dp'), pairs)]
where the time goes in v6:
time: 65.7 us; the launch traced here: 65.5 us
  Pallas kernels  23.3 us (35%)
  waiting for transfers between devices  22.3 us (34%)
  starting transfers between devices  17.3 us (26%)
  between operations  1.57 us (2%)
  local copies, waits for them, and re-layouts  1.04 us (2%)
    pallas_call x23, Pallas kernels, call(): pl.pallas_call(body, out_shape=[jax.ShapeDtypeStruct(*out) for out in out...  23.3 us
    ppermute x7, waiting for transfers between devices, bit_swap(): return lax.ppermute(block, ('chips', 'core', 'dp'), pairs)  18.4 us
    ppermute x7, starting transfers between devices, swap(): return lax.ppermute(block, TILES, pairs_of(kind))  11.5 us
    ppermute x7, starting transfers between devices, bit_swap(): return lax.ppermute(block, ('chips', 'core', 'dp'), pairs)  5.61 us
    ppermute x3, waiting for transfers between devices, core_swap(): return lax.ppermute(block, 'core', [(0, 1), (1, 0)])  2.75 us
  transfers between devices with their start and end apart: 17, of which 9 were waited for; matrix products, arithmetic and copies ran while one was open for 0% of the time, Pallas kernels for 25%

profile of v6, /device:TPU:0, one launch (start us, length us, event | category | flops | bytes accessed | tf_op | source)
XLA Modules:
  0.0 65.5 jit_solution(308463168420006247)
XLA Ops:
  1.3 0.0 copy-start.4
  1.3 1.0 %copy-done.4 = bf16[1,3,16,16,256]{4,3,2,1,0:T(8,128)(2,1)S(1)} copy-done((bf16[1,3,16,16,256]{4,3,2,1,0:T(8,128)(2,1)S(1)}, bf16[1,3,16,16,256]{4,3,2,1,0:T(8,128)(2,1)}, u32[]{:S(2)}) %copy-start.4) | copy-done | bytes 393240
  2.3 0.6 shard_map.144
  2.9 4.1 %collective-permute-start.1 = (bf16[48,256]{1,0:T(8,128)(2,1)S(1)}, bf16[48,256]{1,0:T(8,128)(2,1)S(1)}, u32[]{:S(2)}, u32[]{:S(2)}) collective-permute-start(bf16[48,256]{1,0:T(8,128)(2,1)S(1)} %get-tuple-element.51), channel_id=1, source_target_pairs={{0,16},{2,4},{4,2},{6,8},{8,6},{10,12},{12,10},{14,30},{30,14},{28... | collective-permute-start | bytes 73736 | tf_op jit(solution)/shard_map/ppermute | solution.py:536
  7.0 0.7 %shard_map.145.refs_5_ = bf16[144,256]{1,0:T(8,128)(2,1)S(1)} custom-call(s32[1]{0:T(128)S(6)} %copy.16.refs_0_, s32[3]{0:T(128)S(1)} %copy-done.8, bf16[768,256]{1,0:T(8,128)(2,1)S(1)} %bitcast.15, bf16[48,256]{1,0:T(8,128)(2,1)S(1)} %get-tuple-element.50.refs_3_), custom_call_target="tpu_custom_call" | custom-call | flops 500000000 | tf_op jit(solution)/shard_map/pallas_call | solution.py:650
  7.7 0.0 copy-start.1
  7.7 0.0 copy-start.3
  7.7 0.0 copy-start.6
  7.8 1.7 %collective-permute-start.2 = (bf16[144,256]{1,0:T(8,128)(2,1)S(1)}, bf16[144,256]{1,0:T(8,128)(2,1)S(1)}, u32[]{:S(2)}, u32[]{:S(2)}) collective-permute-start(bf16[144,256]{1,0:T(8,128)(2,1)S(1)} %shard_map.145.refs_5_), channel_id=1, source_target_pairs={{0,16},{2,18},{4,20},{6,22},{8,24},{10,26},{12,28},{14,30},{30,14}... | collective-permute-start | bytes 221192 | tf_op jit(solution)/shard_map/ppermute | solution.py:536
  9.4 0.7 %shard_map.146 = (f32[2,1216,128]{2,1,0:T(8,128)S(1)}, bf16[48,256]{1,0:T(8,128)(2,1)S(1)}) custom-call(s32[1]{0:T(128)S(6)} %copy.16.refs_0_, s32[3]{0:T(128)S(1)} %copy-done.8, bf16[768,256]{1,0:T(8,128)(2,1)S(1)} %bitcast.16, bf16[48,256]{1,0:T(8,128)(2,1)S(1)} %collective-permute-done.refs_3_, bf16[48,256]{1,0:T(8,128)(2,1)S(1)} %collective-permute-done.1.refs_4_, ...), custom_call_target="tpu_custom_call" | custom-call | flops 1000000000 | tf_op jit(solution)/shard_map/pallas_call | solution.py:650
  10.2 2.3 %collective-permute-start.3 = (bf16[48,256]{1,0:T(8,128)(2,1)S(1)}, bf16[48,256]{1,0:T(8,128)(2,1)S(1)}, u32[]{:S(2)}, u32[]{:S(2)}) collective-permute-start(bf16[48,256]{1,0:T(8,128)(2,1)S(1)} %get-tuple-element.53), channel_id=1, source_target_pairs={{0,16},{2,18},{4,20},{6,22},{8,24},{10,26},{12,28},{14,30},{30,14}... | collective-permute-start | bytes 73736 | tf_op jit(solution)/shard_map/ppermute | solution.py:536
  12.5 0.0 copy-start
  12.6 3.7 %shard_map.147 = (bf16[768,256]{1,0:T(8,128)(2,1)S(1)}, f32[768,256]{1,0:T(8,128)S(1)}, f32[768,128]{1,0:T(8,128)S(1)}, bf16[256,768]{1,0:T(8,128)(2,1)S(1)}, f3...) custom-call(s32[1]{0:T(128)S(6)} %copy.16.refs_0_, s32[3]{0:T(128)S(1)} %copy-done.8, bf16[7,7,256]{2,1,0:T(8,128)(2,1)S(1)} %copy-done.6, ...), custom_call_target="tpu_custom_call" | custom-call | flops 5000000000 | tf_op jit(solution)/shard_map/pallas_call | solution.py:650
  16.3 4.1 %shard_map.148 = (f32[1024,256]{1,0:T(8,128)S(1)}, bf16[1024,256]{1,0:T(8,128)(2,1)S(1)}, bf16[768,1024]{1,0:T(8,128)(2,1)S(1)}, bf16[768,1024]{1,0:T(8,128)(2,1...) custom-call(s32[1]{0:T(128)S(6)} %copy.16.refs_0_, ...), custom_call_target="tpu_custom_call" | custom-call | flops 5000000000 | tf_op jit(solution)/shard_map/pallas_call | solution.py:650
  20.4 0.1 collective-permute-start.4
  20.5 1.1 %shard_map.149 = (bf16[768,256]{1,0:T(8,128)(2,1)S(1)}, f32[768,256]{1,0:T(8,128)S(1)}, f32[8,256]{1,0:T(8,128)S(1)}, f32[8,256]{1,0:T(8,128)S(1)}) custom-call(bf16[256,1024]{1,0:T(8,128)(2,1)S(1)} %copy-done, bf16[1024,256]{1,0:T(8,128)(2,1)S(1)} %copy-done.1, f32[1,256]{1,0:T(1,128)S(1)} %bitcast.13, bf16[768,1024]{1,0:T(8,128)(2,1)S(1)} %get-tuple-element.59.refs_3_, ...), custom_call_target="tpu_custom_call" | custom-call | flops 1300000000 | tf_op jit(solution)/shard_map/pallas_call | solution.py:650
  21.6 0.8 %collective-permute-done.4.refs_1_ = bf16[1024,256]{1,0:T(8,128)(2,1)S(1)} collective-permute-done((bf16[1024,256]{1,0:T(8,128)(2,1)S(1)}, bf16[1024,256]{1,0:T(8,128)(2,1)S(1)}, u32[]{:S(2)}, u32[]{:S(2)}) %collective-permute-start.4) | collective-permute-done | bytes 524320 | tf_op jit(solution)/shard_map/ppermute | solution.py:540
  22.4 0.2 shard_map.150
  22.5 0.4 collective-permute-start.5
  22.9 1.7 %shard_map.151.refs_3_.refs_4_.refs_2_ = f32[1216,128]{1,0:T(8,128)S(1)} custom-call(s32[1]{0:T(128)S(6)} %copy.16.refs_0_, bf16[7,7,256]{2,1,0:T(8,128)(2,1)S(1)} %copy-done.6, bf16[768,256]{1,0:T(8,128)(2,1)S(1)} %get-tuple-element.70.refs_2_, bf16[512,256]{1,0:T(8,128)(2,1)S(1)} %get-tuple-element.69.refs_3_), custom_call_target="tpu_custom_call" | custom-call | flops 2000000000 | tf_op jit(solution)/shard_map/pallas_call | solution.py:650
  24.6 1.9 %shard_map.152 = (f32[1216,128]{1,0:T(8,128)S(1)}, bf16[192,256]{1,0:T(8,128)(2,1)S(1)}) custom-call(s32[1]{0:T(128)S(6)} %copy.16.refs_0_, bf16[7,7,256]{2,1,0:T(8,128)(2,1)S(1)} %copy-done.6, bf16[768,256]{1,0:T(8,128)(2,1)S(1)} %get-tuple-element.70.refs_2_, f32[1216,128]{1,0:T(8,128)S(1)} %shard_map.151.refs_3_.refs_4_.refs_2_, ...), custom_call_target="tpu_custom_call" | custom-call | flops 2000000000 | tf_op jit(solution)/shard_map/pallas_call | solution.py:650
  26.5 2.0 %collective-permute-start.9 = (bf16[192,256]{1,0:T(8,128)(2,1)S(1)}, bf16[192,256]{1,0:T(8,128)(2,1)S(1)}, u32[]{:S(2)}, u32[]{:S(2)}) collective-permute-start(bf16[192,256]{1,0:T(8,128)(2,1)S(1)} %get-tuple-element.80), channel_id=1, source_target_pairs={{0,16},{2,18},{4,20},{6,22},{8,24},{10,26},{12,28},{14,30},{30,14}... | collective-permute-start | bytes 294920 | tf_op jit(solution)/shard_map/ppermute | solution.py:536
  28.5 0.4 collective-permute-done.5.refs_1_
  29.0 0.1 shard_map.153
  29.0 1.6 %collective-permute-start.6 = (bf16[256,256]{1,0:T(8,128)(2,1)S(1)}, bf16[256,256]{1,0:T(8,128)(2,1)S(1)}, u32[]{:S(2)}, u32[]{:S(2)}) collective-permute-start(bf16[256,256]{1,0:T(8,128)(2,1)S(1)} %get-tuple-element.73.refs_3_), channel_id=1, source_target_pairs={{0,1},{1,0},{2,6},{3,7},{4,5},{5,4},{6,2},{7,3},{8,9},{9,8},{10,14... | collective-permute-start | bytes 393224 | tf_op jit(solution)/shard_map/ppermute | solution.py:560
  30.6 1.8 %shard_map.155.refs_3_ = f32[64,128]{1,0:T(8,128)S(1)} custom-call(f32[2,1216,128]{2,1,0:T(8,128)S(1)} %get-tuple-element.52.refs_7_.refs_4_.refs_0_, f32[2,640,128]{2,1,0:T(8,128)S(1)} %get-tuple-element.75.refs_1_, bf16[768,256]{1,0:T(8,128)(2,1)S(1)} %get-tuple-element.70.refs_2_, bf16[256,256]{1,0:T(8,128)(2,1)S(1)} %get-tuple-element.73.refs_3_), custom_call_target="tpu_custom_call" | custom-call | flops 1800000000 | tf_op jit(solution)/shard_map/pallas_call | solution.py:650
  32.4 1.8 %shard_map.154.refs_2_ = f32[64,128]{1,0:T(8,128)S(1)} custom-call(f32[2,1216,128]{2,1,0:T(8,128)S(1)} %get-tuple-element.52.refs_7_.refs_4_.refs_0_, f32[2,640,128]{2,1,0:T(8,128)S(1)} %get-tuple-element.75.refs_1_, bf16[768,256]{1,0:T(8,128)(2,1)S(1)} %get-tuple-element.70.refs_2_, bf16[256,256]{1,0:T(8,128)(2,1)S(1)} %get-tuple-element.73.refs_3_), custom_call_target="tpu_custom_call" | custom-call | flops 1800000000 | tf_op jit(solution)/shard_map/pallas_call | solution.py:650
  34.2 0.1 collective-permute-start.8
  34.4 1.1 %collective-permute-start.7 = (bf16[128,256]{1,0:T(8,128)(2,1)S(1)}, bf16[128,256]{1,0:T(8,128)(2,1)S(1)}, u32[]{:S(2)}, u32[]{:S(2)}) collective-permute-start(bf16[128,256]{1,0:T(8,128)(2,1)S(1)} %get-tuple-element.78.refs_4_), channel_id=1, source_target_pairs={{0,8},{1,9},{2,3},{3,2},{4,12},{5,13},{6,7},{7,6},{8,0},{9,1},{10,... | collective-permute-start | bytes 196616 | tf_op jit(solution)/shard_map/ppermute | solution.py:560
  35.4 0.6 shard_map.158
  36.1 0.1 collective-permute-start.11
  36.1 1.3 %collective-permute-start.12 = (bf16[48,256]{1,0:T(8,128)(2,1)S(1)}, bf16[48,256]{1,0:T(8,128)(2,1)S(1)}, u32[]{:S(2)}, u32[]{:S(2)}) collective-permute-start(bf16[48,256]{1,0:T(8,128)(2,1)S(1)} %get-tuple-element.83), channel_id=1, source_target_pairs={{0,16},{2,4},{4,2},{6,8},{8,6},{10,12},{12,10},{14,30},{30,14},{28... | collective-permute-start | bytes 73736 | tf_op jit(solution)/shard_map/ppermute | solution.py:536
  37.5 1.2 %collective-permute-done.7.refs_1_ = bf16[128,256]{1,0:T(8,128)(2,1)S(1)} collective-permute-done((bf16[128,256]{1,0:T(8,128)(2,1)S(1)}, bf16[128,256]{1,0:T(8,128)(2,1)S(1)}, u32[]{:S(2)}, u32[]{:S(2)}) %collective-permute-start.7) | collective-permute-done | bytes 65568 | tf_op jit(solution)/shard_map/ppermute | solution.py:560
  38.7 1.1 %collective-permute-start.10 = (bf16[160,256]{1,0:T(8,128)(2,1)S(1)}, bf16[160,256]{1,0:T(8,128)(2,1)S(1)}, u32[]{:S(2)}, u32[]{:S(2)}) collective-permute-start(bf16[160,256]{1,0:T(8,128)(2,1)S(1)} %shard_map.159.refs_6_.refs_0_), channel_id=1, source_target_pairs={{0,16},{1,17},{2,18},{3,19},{4,20},{5,21},{6,22},{7,23},{8,24},{9,... | collective-permute-start | bytes 245768 | tf_op jit(solution)/shard_map/ppermute | solution.py:560
  39.8 1.1 %collective-permute-done.12.refs_5_ = bf16[48,256]{1,0:T(8,128)(2,1)S(1)} collective-permute-done((bf16[48,256]{1,0:T(8,128)(2,1)S(1)}, bf16[48,256]{1,0:T(8,128)(2,1)S(1)}, u32[]{:S(2)}, u32[]{:S(2)}) %collective-permute-start.12) | collective-permute-done | bytes 24608 | tf_op jit(solution)/shard_map/ppermute | solution.py:536
  40.9 1.6 %shard_map.160 = (bf16[768,256]{1,0:T(8,128)(2,1)}, f32[8,128]{1,0:T(8,128)S(1)}) custom-call(s32[1]{0:T(128)S(6)} %copy.16.refs_0_, s32[3]{0:T(128)S(1)} %copy-done.8, bf16[768,256]{1,0:T(8,128)(2,1)S(1)} %bitcast.10, f32[2,1024,128]{2,1,0:T(8,128)S(1)} %get-tuple-element.81.refs_4_.refs_3_, bf16[48,256]{1,0:T(8,128)(2,1)S(1)} %collective-permute-done.11.refs_4_, ...), custom_call_target="tpu_custom_call" | custom-call | flops 1500000000 | tf_op jit(solution)/shard_map/pallas_call | solution.py:650
  42.6 2.9 %collective-permute-done.10.refs_1_ = bf16[160,256]{1,0:T(8,128)(2,1)S(1)} collective-permute-done((bf16[160,256]{1,0:T(8,128)(2,1)S(1)}, bf16[160,256]{1,0:T(8,128)(2,1)S(1)}, u32[]{:S(2)}, u32[]{:S(2)}) %collective-permute-start.10) | collective-permute-done | bytes 81952 | tf_op jit(solution)/shard_map/ppermute | solution.py:560
  45.5 0.1 collective-permute-start.13
  45.5 4.4 %collective-permute-done.13.refs_1_ = bf16[160,256]{1,0:T(8,128)(2,1)S(1)} collective-permute-done((bf16[160,256]{1,0:T(8,128)(2,1)S(1)}, bf16[160,256]{1,0:T(8,128)(2,1)S(1)}, u32[]{:S(2)}, u32[]{:S(2)}) %collective-permute-start.13) | collective-permute-done | bytes 81952 | tf_op jit(solution)/shard_map/ppermute | solution.py:560
  50.0 0.9 %collective-permute-start.14 = (bf16[288,256]{1,0:T(8,128)(2,1)S(1)}, bf16[288,256]{1,0:T(8,128)(2,1)S(1)}, u32[]{:S(2)}, u32[]{:S(2)}) collective-permute-start(bf16[288,256]{1,0:T(8,128)(2,1)S(1)} %shard_map.162.refs_0_), channel_id=1, source_target_pairs={{0,1},{1,0},{2,6},{3,7},{4,5},{5,4},{6,2},{7,3},{8,9},{9,8},{10,14... | collective-permute-start | bytes 442376 | tf_op jit(solution)/shard_map/ppermute | solution.py:560
  50.9 4.3 %collective-permute-done.14.refs_1_ = bf16[288,256]{1,0:T(8,128)(2,1)S(1)} collective-permute-done((bf16[288,256]{1,0:T(8,128)(2,1)S(1)}, bf16[288,256]{1,0:T(8,128)(2,1)S(1)}, u32[]{:S(2)}, u32[]{:S(2)}) %collective-permute-start.14) | collective-permute-done | bytes 147488 | tf_op jit(solution)/shard_map/ppermute | solution.py:560
  55.2 0.6 collective-permute-start.15
  55.8 0.9 %shard_map.164 = (bf16[768,256]{1,0:T(8,128)(2,1)}, f32[8,128]{1,0:T(8,128)S(1)}) custom-call(bf16[768,256]{1,0:T(8,128)(2,1)S(1)} %bitcast.17, f32[1,256]{1,0:T(1,128)S(1)} %bitcast.19, f32[768,256]{1,0:T(8,128)S(1)} %get-tuple-element.64.refs_2_, f32[3,8,256]{2,1,0:T(8,128)S(1)} %get-tuple-element.63.refs_8_.refs_3_, ...), custom_call_target="tpu_custom_call" | custom-call | flops 1500000000 | tf_op jit(solution)/shard_map/pallas_call | solution.py:650
  56.7 5.2 %collective-permute-done.15.refs_1_ = bf16[544,256]{1,0:T(8,128)(2,1)S(1)} collective-permute-done((bf16[544,256]{1,0:T(8,128)(2,1)S(1)}, bf16[544,256]{1,0:T(8,128)(2,1)S(1)}, u32[]{:S(2)}, u32[]{:S(2)}) %collective-permute-start.15) | collective-permute-done | bytes 278560 | tf_op jit(solution)/shard_map/ppermute | solution.py:560
  61.8 0.1 shard_map.165.refs_0_
  61.9 0.1 collective-permute-start.16
  62.0 1.9 %collective-permute-done.16.refs_1_ = bf16[1088,256]{1,0:T(8,128)(2,1)S(1)} collective-permute-done((bf16[1088,256]{1,0:T(8,128)(2,1)S(1)}, bf16[1088,256]{1,0:T(8,128)(2,1)S(1)}, u32[]{:S(2)}, u32[]{:S(2)}) %collective-permute-start.16) | collective-permute-done | bytes 557088 | tf_op jit(solution)/shard_map/ppermute | solution.py:540
  63.9 1.6 %shard_map.166 = (f32[256,1024]{1,0:T(8,128)}, f32[1024,256]{1,0:T(8,128)}, f32[7,7,256]{2,1,0:T(8,128)}, f32[1,256]{1,0:T(1,128)}, f32[1,256]{1,0:T(1,128)}) custom-call(bf16[1088,256]{1,0:T(8,128)(2,1)S(1)} %shard_map.165.refs_0_, bf16[1088,256]{1,0:T(8,128)(2,1)S(1)} %collective-permute-done.16.refs_1_), custom_call_target="tpu_custom_call" | custom-call | flops 1500000000 | tf_op jit(solution)/shard_map/pallas_call | solution.py:650
  (27 shorter events, 0.2 us)
Async XLA Ops:
  1.3 1.0 %copy-start.4 = (bf16[1,3,16,16,256]{4,3,2,1,0:T(8,128)(2,1)S(1)}, bf16[1,3,16,16,256]{4,3,2,1,0:T(8,128)(2,1)}, u32[]{:S(2)}) copy-start(bf16[1,3,16,16,256]{4,3,2,1,0:T(8,128)(2,1)} %param.9) | copy-start | bytes 1179652
  2.3 4.7 %copy-start.8 = (s32[3]{0:T(128)S(1)}, s32[3]{0:T(128)}, u32[]{:S(2)}) copy-start(s32[3]{0:T(128)} %refs_1_.15) | copy-start | bytes 40
  2.9 6.6 %collective-permute-start.1 = (bf16[48,256]{1,0:T(8,128)(2,1)S(1)}, bf16[48,256]{1,0:T(8,128)(2,1)S(1)}, u32[]{:S(2)}, u32[]{:S(2)}) collective-permute-start(bf16[48,256]{1,0:T(8,128)(2,1)S(1)} %get-tuple-element.51), channel_id=1, source_target_pairs={{0,16},{2,4},{4,2},{6,8},{8,6},{10,12},{12,10},{14,30},{30,14},{28... | collective-permute-start | bytes 73736 | tf_op jit(solution)/shard_map/ppermute | solution.py:536
  7.0 2.5 %collective-permute-start = (bf16[48,256]{1,0:T(8,128)(2,1)S(1)}, bf16[48,256]{1,0:T(8,128)(2,1)S(1)}, u32[]{:S(2)}, u32[]{:S(2)}) collective-permute-start(bf16[48,256]{1,0:T(8,128)(2,1)S(1)} %get-tuple-element.50.refs_3_), channel_id=1, source_target_pairs={{0,2},{2,0},{4,6},{6,4},{8,10},{10,8},{12,14},{14,12},{30,28},{28,... | collective-permute-start | bytes 73736 | tf_op jit(solution)/shard_map/ppermute | solution.py:536
  7.7 4.8 %copy-start.1 = (bf16[1024,256]{1,0:T(8,128)(2,1)S(1)}, bf16[1024,256]{1,0:T(8,128)(2,1)}, u32[]{:S(2)}) copy-start(bf16[1024,256]{1,0:T(8,128)(2,1)} %refs_1_.12) | copy-start | bytes 1572868
  7.7 4.8 %copy-start.2 = (bf16[1,3,16,16,256]{4,3,2,1,0:T(8,128)(2,1)S(1)}, bf16[1,3,16,16,256]{4,3,2,1,0:T(8,128)(2,1)}, u32[]{:S(2)}) copy-start(bf16[1,3,16,16,256]{4,3,2,1,0:T(8,128)(2,1)} %param.10) | copy-start | bytes 1179652
  7.7 4.8 %copy-start.3 = (f32[256]{0:T(256)S(1)}, f32[256]{0:T(256)}, u32[]{:S(2)}) copy-start(f32[256]{0:T(256)} %param.14) | copy-start | bytes 3076
  7.7 4.8 %copy-start.6 = (bf16[7,7,256]{2,1,0:T(8,128)(2,1)S(1)}, bf16[7,7,256]{2,1,0:T(8,128)(2,1)}, u32[]{:S(2)}) copy-start(bf16[7,7,256]{2,1,0:T(8,128)(2,1)} %refs_1_.14) | copy-start | bytes 75268
  7.8 4.8 %copy-start.7 = (f32[256]{0:T(256)S(1)}, f32[256]{0:T(256)}, u32[]{:S(2)}) copy-start(f32[256]{0:T(256)} %param.17) | copy-start | bytes 3076
  7.8 8.5 %collective-permute-start.2 = (bf16[144,256]{1,0:T(8,128)(2,1)S(1)}, bf16[144,256]{1,0:T(8,128)(2,1)S(1)}, u32[]{:S(2)}, u32[]{:S(2)}) collective-permute-start(bf16[144,256]{1,0:T(8,128)(2,1)S(1)} %shard_map.145.refs_5_), channel_id=1, source_target_pairs={{0,16},{2,18},{4,20},{6,22},{8,24},{10,26},{12,28},{14,30},{30,14}... | collective-permute-start | bytes 221192 | tf_op jit(solution)/shard_map/ppermute | solution.py:536
  10.2 6.0 %collective-permute-start.3 = (bf16[48,256]{1,0:T(8,128)(2,1)S(1)}, bf16[48,256]{1,0:T(8,128)(2,1)S(1)}, u32[]{:S(2)}, u32[]{:S(2)}) collective-permute-start(bf16[48,256]{1,0:T(8,128)(2,1)S(1)} %get-tuple-element.53), channel_id=1, source_target_pairs={{0,16},{2,18},{4,20},{6,22},{8,24},{10,26},{12,28},{14,30},{30,14}... | collective-permute-start | bytes 73736 | tf_op jit(solution)/shard_map/ppermute | solution.py:536
  12.5 3.7 %copy-start = (bf16[256,1024]{1,0:T(8,128)(2,1)S(1)}, bf16[256,1024]{1,0:T(8,128)(2,1)}, u32[]{:S(2)}) copy-start(bf16[256,1024]{1,0:T(8,128)(2,1)} %refs_0_.10) | copy-start | bytes 1572868
  20.4 2.0 %collective-permute-start.4 = (bf16[1024,256]{1,0:T(8,128)(2,1)S(1)}, bf16[1024,256]{1,0:T(8,128)(2,1)S(1)}, u32[]{:S(2)}, u32[]{:S(2)}) collective-permute-start(bf16[1024,256]{1,0:T(8,128)(2,1)S(1)} %get-tuple-element.66), channel_id=1, source_target_pairs={{0,2},{2,0},{1,3},{3,1},{4,6},{6,4},{5,7},{7,5},{8,10},{10,8},{9,1... | collective-permute-start | bytes 1572872 | tf_op jit(solution)/shard_map/ppermute | solution.py:540
  22.5 6.4 %collective-permute-start.5 = (bf16[512,256]{1,0:T(8,128)(2,1)S(1)}, bf16[512,256]{1,0:T(8,128)(2,1)S(1)}, u32[]{:S(2)}, u32[]{:S(2)}) collective-permute-start(bf16[512,256]{1,0:T(8,128)(2,1)S(1)} %get-tuple-element.69.refs_3_), channel_id=1, source_target_pairs={{0,4},{1,5},{2,10},{3,11},{4,0},{5,1},{6,14},{7,15},{8,12},{9,13},... | collective-permute-start | bytes 786440 | tf_op jit(solution)/shard_map/ppermute | solution.py:560
  26.5 8.9 %collective-permute-start.9 = (bf16[192,256]{1,0:T(8,128)(2,1)S(1)}, bf16[192,256]{1,0:T(8,128)(2,1)S(1)}, u32[]{:S(2)}, u32[]{:S(2)}) collective-permute-start(bf16[192,256]{1,0:T(8,128)(2,1)S(1)} %get-tuple-element.80), channel_id=1, source_target_pairs={{0,16},{2,18},{4,20},{6,22},{8,24},{10,26},{12,28},{14,30},{30,14}... | collective-permute-start | bytes 294920 | tf_op jit(solution)/shard_map/ppermute | solution.py:536
  29.0 5.3 %collective-permute-start.6 = (bf16[256,256]{1,0:T(8,128)(2,1)S(1)}, bf16[256,256]{1,0:T(8,128)(2,1)S(1)}, u32[]{:S(2)}, u32[]{:S(2)}) collective-permute-start(bf16[256,256]{1,0:T(8,128)(2,1)S(1)} %get-tuple-element.73.refs_3_), channel_id=1, source_target_pairs={{0,1},{1,0},{2,6},{3,7},{4,5},{5,4},{6,2},{7,3},{8,9},{9,8},{10,14... | collective-permute-start | bytes 393224 | tf_op jit(solution)/shard_map/ppermute | solution.py:560
  34.2 3.2 %collective-permute-start.8 = (bf16[64,256]{1,0:T(8,128)(2,1)S(1)}, bf16[64,256]{1,0:T(8,128)(2,1)S(1)}, u32[]{:S(2)}, u32[]{:S(2)}) collective-permute-start(bf16[64,256]{1,0:T(8,128)(2,1)S(1)} %get-tuple-element.79), channel_id=1, source_target_pairs={{0,2},{2,0},{1,3},{3,1},{4,6},{6,4},{5,7},{7,5},{8,10},{10,8},{9,1... | collective-permute-start | bytes 98312 | tf_op jit(solution)/shard_map/ppermute | solution.py:540
  34.4 4.3 %collective-permute-start.7 = (bf16[128,256]{1,0:T(8,128)(2,1)S(1)}, bf16[128,256]{1,0:T(8,128)(2,1)S(1)}, u32[]{:S(2)}, u32[]{:S(2)}) collective-permute-start(bf16[128,256]{1,0:T(8,128)(2,1)S(1)} %get-tuple-element.78.refs_4_), channel_id=1, source_target_pairs={{0,8},{1,9},{2,3},{3,2},{4,12},{5,13},{6,7},{7,6},{8,0},{9,1},{10,... | collective-permute-start | bytes 196616 | tf_op jit(solution)/shard_map/ppermute | solution.py:560
  36.1 3.7 %collective-permute-start.11 = (bf16[48,256]{1,0:T(8,128)(2,1)S(1)}, bf16[48,256]{1,0:T(8,128)(2,1)S(1)}, u32[]{:S(2)}, u32[]{:S(2)}) collective-permute-start(bf16[48,256]{1,0:T(8,128)(2,1)S(1)} %get-tuple-element.82), channel_id=1, source_target_pairs={{0,2},{2,0},{4,6},{6,4},{8,10},{10,8},{12,14},{14,12},{30,28},{28,... | collective-permute-start | bytes 73736 | tf_op jit(solution)/shard_map/ppermute | solution.py:536
  36.1 4.8 %collective-permute-start.12 = (bf16[48,256]{1,0:T(8,128)(2,1)S(1)}, bf16[48,256]{1,0:T(8,128)(2,1)S(1)}, u32[]{:S(2)}, u32[]{:S(2)}) collective-permute-start(bf16[48,256]{1,0:T(8,128)(2,1)S(1)} %get-tuple-element.83), channel_id=1, source_target_pairs={{0,16},{2,4},{4,2},{6,8},{8,6},{10,12},{12,10},{14,30},{30,14},{28... | collective-permute-start | bytes 73736 | tf_op jit(solution)/shard_map/ppermute | solution.py:536
  38.7 6.7 %collective-permute-start.10 = (bf16[160,256]{1,0:T(8,128)(2,1)S(1)}, bf16[160,256]{1,0:T(8,128)(2,1)S(1)}, u32[]{:S(2)}, u32[]{:S(2)}) collective-permute-start(bf16[160,256]{1,0:T(8,128)(2,1)S(1)} %shard_map.159.refs_6_.refs_0_), channel_id=1, source_target_pairs={{0,16},{1,17},{2,18},{3,19},{4,20},{5,21},{6,22},{7,23},{8,24},{9,... | collective-permute-start | bytes 245768 | tf_op jit(solution)/shard_map/ppermute | solution.py:560
  45.4 10.4 %copy-start.5 = (bf16[1,3,16,16,256]{4,3,2,1,0:T(8,128)(2,1)S(1)}, bf16[1,3,16,16,256]{4,3,2,1,0:T(8,128)(2,1)}, u32[]{:S(2)}) copy-start(bf16[1,3,16,16,256]{4,3,2,1,0:T(8,128)(2,1)} %param.9) | copy-start | bytes 1179652
  45.5 4.5 %collective-permute-start.13 = (bf16[160,256]{1,0:T(8,128)(2,1)S(1)}, bf16[160,256]{1,0:T(8,128)(2,1)S(1)}, u32[]{:S(2)}, u32[]{:S(2)}) collective-permute-start(bf16[160,256]{1,0:T(8,128)(2,1)S(1)} %shard_map.161.refs_0_), channel_id=1, source_target_pairs={{0,8},{1,9},{2,3},{3,2},{4,12},{5,13},{6,7},{7,6},{8,0},{9,1},{10,... | collective-permute-start | bytes 245768 | tf_op jit(solution)/shard_map/ppermute | solution.py:560
  50.0 5.2 %collective-permute-start.14 = (bf16[288,256]{1,0:T(8,128)(2,1)S(1)}, bf16[288,256]{1,0:T(8,128)(2,1)S(1)}, u32[]{:S(2)}, u32[]{:S(2)}) collective-permute-start(bf16[288,256]{1,0:T(8,128)(2,1)S(1)} %shard_map.162.refs_0_), channel_id=1, source_target_pairs={{0,1},{1,0},{2,6},{3,7},{4,5},{5,4},{6,2},{7,3},{8,9},{9,8},{10,14... | collective-permute-start | bytes 442376 | tf_op jit(solution)/shard_map/ppermute | solution.py:560
  55.2 6.6 %collective-permute-start.15 = (bf16[544,256]{1,0:T(8,128)(2,1)S(1)}, bf16[544,256]{1,0:T(8,128)(2,1)S(1)}, u32[]{:S(2)}, u32[]{:S(2)}) collective-permute-start(bf16[544,256]{1,0:T(8,128)(2,1)S(1)} %shard_map.163.refs_4_.refs_0_), channel_id=1, source_target_pairs={{0,4},{1,5},{2,10},{3,11},{4,0},{5,1},{6,14},{7,15},{8,12},{9,13},... | collective-permute-start | bytes 835592 | tf_op jit(solution)/shard_map/ppermute | solution.py:560
  61.9 2.0 %collective-permute-start.16 = (bf16[1088,256]{1,0:T(8,128)(2,1)S(1)}, bf16[1088,256]{1,0:T(8,128)(2,1)S(1)}, u32[]{:S(2)}, u32[]{:S(2)}) collective-permute-start(bf16[1088,256]{1,0:T(8,128)(2,1)S(1)} %shard_map.165.refs_0_), channel_id=1, source_target_pairs={{0,2},{2,0},{1,3},{3,1},{4,6},{6,4},{5,7},{7,5},{8,10},{10,8},{9,1... | collective-permute-start | bytes 1671176 | tf_op jit(solution)/shard_map/ppermute | solution.py:540

commit v7 on v6

--- a/solution.py
+++ b/solution.py
@@ -11,7 +11,8 @@
 HALF = KSIZE // 2
 TILE = 16
 EPS = 1e-06
-TILES = ("chips", "core")
+CHIPS = ("far", "near")
+TILES = CHIPS + ("core",)
 F32 = jnp.float32
 BF16 = jnp.bfloat16
 LANES = 128
@@ -26,9 +27,13 @@
     )
 
 
+def chip_index():
+    return lax.axis_index("far") * lax.axis_size("near") + lax.axis_index("near")
+
+
 def cycle_rank():
     count = lax.axis_size(TILES)
-    here = lax.axis_index("chips") * lax.axis_size("core") + lax.axis_index("core")
+    here = chip_index() * lax.axis_size("core") + lax.axis_index("core")
     return jnp.where(here < count // 2, here, count - 1 + count // 2 - here)
 
 
@@ -541,13 +546,13 @@
 
 
 def stages():
-    chip_bits = lax.axis_size("chips").bit_length() - 1
+    chip_bits = lax.axis_size(CHIPS).bit_length() - 1
     rest = list(range(2, chip_bits))
     return list(zip([0, -1, 1] + rest, [1, 0, -1] + rest))
 
 
 def bit_swap(block, stage):
-    chips, cores, samples = (lax.axis_size(axis) for axis in ("chips", "core", "dp"))
+    chips, cores, samples = (lax.axis_size(axis) for axis in (CHIPS, "core", "dp"))
     pairs = []
     for chip in range(chips):
         for core in range(cores):
@@ -557,12 +562,12 @@
                 pairs.append(
                     ((chip * cores + core) * samples + sample, (to[0] * cores + core) * samples + to[1])
                 )
-    return lax.ppermute(block, ("chips", "core", "dp"), pairs)
+    return lax.ppermute(block, TILES + ("dp",), pairs)
 
 
 def bit_here(stage):
     bits = [
-        lax.axis_index("dp") if bit < 0 else lax.axis_index("chips") >> bit & 1 for bit in stage
+        lax.axis_index("dp") if bit < 0 else chip_index() >> bit & 1 for bit in stage
     ]
     return jnp.where(lax.axis_index("core") == 0, bits[0], bits[1])
 
@@ -608,7 +613,34 @@
 
 
 def add_kernel(own, came, payload):
-    payload[...] = (own[...].astype(F32) + came[...].astype(F32)).astype(BF16)
+    total = (own[...].astype(F32) + came[...].astype(F32)).astype(BF16)
+    if payload.shape == total.shape:
+        payload[...] = total
+    else:
+        for at in range(payload.shape[0]):
+            payload[at] = total
+
+
+def gather_kernel(order, extra, came, payload):
+    rows = came.shape[1] - extra
+    samples = lax.axis_size("dp")
+    is_first = lax.axis_index("core") == 0
+    total = jnp.zeros((extra, came.shape[2]), F32)
+    for at in range(came.shape[0]):
+        near, sample = divmod(at, samples)
+        places = []
+        for core in range(2):
+            place = 0
+            for stage in order:
+                place = 2 * place + (sample if stage[core] < 0 else near >> stage[core] & 1)
+            places.append(place)
+        place = jnp.where(is_first, places[0], places[1])
+        payload[half_rows(place, rows), :] = came[at, pl.ds(0, rows), :]
+        total += came[at, pl.ds(rows, extra), :].astype(F32)
+    high = total.astype(BF16)
+    full = rows * came.shape[0]
+    payload[pl.ds(full, extra), :] = high
+    payload[pl.ds(full + extra, extra), :] = (total - high.astype(F32)).astype(BF16)
 
 
 def double_kernel(stage, extra, own, came, payload):
@@ -800,18 +832,22 @@
         bind(final_kernel), [whole, ((8, LANES), F32)], [count_s, ocean_s, strip(TILE)],
         [block_count, ocean], [tangent, folded, first, second], 2, 1.5, after=[payload],
     )
+    state, done_too = call(
+        bind(state_kernel), [whole, ((8, LANES), F32)], [], [], [fields, scale, projected, live], 0, 1.0, after=[done],
+    )
+    block = lax.axis_size("near") * lax.axis_size("dp")
+    copied = (block, *payload.shape)
+    outer = range(block.bit_length() - 1, len(order) - 1)
     (payload,) = call(
-        add_kernel, [(payload.shape, BF16)], [], [], [payload, came], after=[done], micros=0.3,
-    )
-    came = bit_swap(payload, order[-2])
-    after = []
-    for at in reversed(range(len(order) - 1)):
-        copies = 2 if at == 0 else 1
+        add_kernel, [(payload.shape if outer else copied, BF16)], [], [], [payload, came], after=[done, done_too],
+        micros=0.3,
+    )
+    for at in reversed(outer):
+        came = bit_swap(payload, order[at])
         if rows % 16 == 0:
             (payload,) = call(
                 functools.partial(double_kernel, order[at], small_rows),
-                [((2 * rows + copies * small_rows, channels), BF16)],
-                [], [], [payload, came], after=after, micros=0.3,
+                [((2 * rows + small_rows, channels), BF16)], [], [], [payload, came], micros=0.3,
             )
         else:
             is_low = bit_here(order[at]) == 0
@@ -819,15 +855,15 @@
             both = payload[rows:].astype(F32) + came[rows:].astype(F32)
             joined = [jnp.where(is_low, low, high), jnp.where(is_low, high, low), both.astype(BF16)]
             payload = jnp.concatenate(joined)
-        after = []
         rows *= 2
-        came = bit_swap(payload, order[at - 1]) if at else core_swap(payload)
-        if at == 1:
-            state, done = call(
-                bind(state_kernel), [whole, ((8, LANES), F32)], [], [], [fields, scale, projected, live], 0, 1.5,
-                after=[payload],
-            )
-            after = [done]
+    if outer:
+        payload = jnp.broadcast_to(payload, (block, *payload.shape))
+    came = lax.all_to_all(payload, ("near", "dp"), 0, 0, tiled=True)
+    (payload,) = call(
+        functools.partial(gather_kernel, order[: block.bit_length() - 1], small_rows),
+        [((hidden + 2 * small_rows, channels), BF16)], [], [], [came], micros=0.3,
+    )
+    came = core_swap(payload)
     total = samples * lax.axis_size("dp") * slots * lax.axis_size(TILES) * tile_rows * tile_cols
     norm = total ** (-0.5)
     sums = [((channels, hidden), F32), ((hidden, channels), F32)]
@@ -847,7 +883,7 @@
 
 
 def solution(mesh):
-    cores = Mesh(mesh.devices.reshape(-1, 2, mesh.devices.shape[1]), ("chips", "core", "dp"))
+    cores = Mesh(mesh.devices.reshape(-1, 4, 2, mesh.devices.shape[1]), TILES + ("dp",))
     banded = P("dp", TILES, None, None, None)
     placed = (banded, banded, P(TILES), P(TILES), P(), P(), P(), P(), P())
     return jax.shard_map(

time: 65.7 us -> 62.8 us (0.956)
  waiting for transfers between devices: 22.3 us -> 7.57 us
  blocking collectives: 0 us -> 13.4 us
  starting transfers between devices: 17.3 us -> 15.8 us
    ppermute x7 -> x4, waiting for transfers between devices: 18.4 us -> 3.69 us  [bit_swap(): return lax.ppermute(block, TILES + ('dp',), pairs)]
    all_to_all x0 -> x1, blocking collectives: none -> 13.4 us  [shards(): came = lax.all_to_all(payload, ('near', 'dp'), 0, 0, tiled=True)]
    ppermute x7 -> x4, starting transfers between devices: 5.61 us -> 4.07 us  [bit_swap(): return lax.ppermute(block, TILES + ('dp',), pairs)]
    pallas_call x23 -> x21, Pallas kernels: 23.3 us -> 23.3 us  [call(): pl.pallas_call(body, out_shape=[jax.ShapeDtypeStruct(*out) for out in out...]
  transfers between devices with their start and end apart: 17 -> 14, of which waited for: 9 -> 6; matrix products, arithmetic and copies ran while one was open for 0% -> 0% of each run, Pallas kernels for 25% -> 27%
where the time goes in v7:
time: 62.8 us; the launch traced here: 62.6 us
  Pallas kernels  23.3 us (37%)
  starting transfers between devices  15.8 us (25%)
  blocking collectives  13.4 us (21%)
  waiting for transfers between devices  7.57 us (12%)
  between operations  1.57 us (2%)
  local copies, waits for them, and re-layouts  1.04 us (2%)
    pallas_call x21, Pallas kernels, call(): pl.pallas_call(body, out_shape=[jax.ShapeDtypeStruct(*out) for out in out...  23.3 us
    all_to_all x1, blocking collectives, shards(): came = lax.all_to_all(payload, ('near', 'dp'), 0, 0, tiled=True)  13.4 us
    ppermute x7, starting transfers between devices, swap(): return lax.ppermute(block, TILES, pairs_of(kind))  11.5 us
    ppermute x4, starting transfers between devices, bit_swap(): return lax.ppermute(block, TILES + ('dp',), pairs)  4.07 us
    ppermute x4, waiting for transfers between devices, bit_swap(): return lax.ppermute(block, TILES + ('dp',), pairs)  3.69 us
    ppermute x3, waiting for transfers between devices, core_swap(): return lax.ppermute(block, 'core', [(0, 1), (1, 0)])  2.75 us
  transfers between devices with their start and end apart: 14, of which 6 were waited for; matrix products, arithmetic and copies ran while one was open for 0% of the time, Pallas kernels for 27%

profile of v7, /device:TPU:0, one launch (start us, length us, event | category | flops | bytes accessed | tf_op | source)
XLA Modules:
  0.0 62.6 jit_solution(9280230649163591922)
XLA Ops:
  1.3 0.0 copy-start.4
  1.3 1.0 %copy-done.4 = bf16[1,3,16,16,256]{4,3,2,1,0:T(8,128)(2,1)S(1)} copy-done((bf16[1,3,16,16,256]{4,3,2,1,0:T(8,128)(2,1)S(1)}, bf16[1,3,16,16,256]{4,3,2,1,0:T(8,128)(2,1)}, u32[]{:S(2)}) %copy-start.4) | copy-done | bytes 393240
  2.3 0.6 shard_map.144
  2.9 4.1 %collective-permute-start.1 = (bf16[48,256]{1,0:T(8,128)(2,1)S(1)}, bf16[48,256]{1,0:T(8,128)(2,1)S(1)}, u32[]{:S(2)}, u32[]{:S(2)}) collective-permute-start(bf16[48,256]{1,0:T(8,128)(2,1)S(1)} %get-tuple-element.51), channel_id=1, source_target_pairs={{0,16},{2,4},{4,2},{6,8},{8,6},{10,12},{12,10},{14,30},{30,14},{28... | collective-permute-start | bytes 73736 | tf_op jit(solution)/shard_map/ppermute | solution.py:541
  7.0 0.0 collective-permute-start
  7.0 0.7 %shard_map.145.refs_5_ = bf16[144,256]{1,0:T(8,128)(2,1)S(1)} custom-call(s32[1]{0:T(128)S(6)} %copy.16.refs_0_, s32[3]{0:T(128)S(1)} %copy-done.8, bf16[768,256]{1,0:T(8,128)(2,1)S(1)} %bitcast.15, bf16[48,256]{1,0:T(8,128)(2,1)S(1)} %get-tuple-element.50.refs_3_), custom_call_target="tpu_custom_call" | custom-call | flops 500000000 | tf_op jit(solution)/shard_map/pallas_call | solution.py:682
  7.7 0.0 copy-start.1
  7.7 0.0 copy-start.2
  7.7 0.0 copy-start.3
  7.7 0.0 copy-start.6
  7.8 0.0 copy-start.7
  7.8 1.7 %collective-permute-start.2 = (bf16[144,256]{1,0:T(8,128)(2,1)S(1)}, bf16[144,256]{1,0:T(8,128)(2,1)S(1)}, u32[]{:S(2)}, u32[]{:S(2)}) collective-permute-start(bf16[144,256]{1,0:T(8,128)(2,1)S(1)} %shard_map.145.refs_5_), channel_id=1, source_target_pairs={{0,16},{2,18},{4,20},{6,22},{8,24},{10,26},{12,28},{14,30},{30,14}... | collective-permute-start | bytes 221192 | tf_op jit(solution)/shard_map/ppermute | solution.py:541
  9.4 0.7 %shard_map.146 = (f32[2,1216,128]{2,1,0:T(8,128)S(1)}, bf16[48,256]{1,0:T(8,128)(2,1)S(1)}) custom-call(s32[1]{0:T(128)S(6)} %copy.16.refs_0_, s32[3]{0:T(128)S(1)} %copy-done.8, bf16[768,256]{1,0:T(8,128)(2,1)S(1)} %bitcast.16, bf16[48,256]{1,0:T(8,128)(2,1)S(1)} %collective-permute-done.refs_3_, bf16[48,256]{1,0:T(8,128)(2,1)S(1)} %collective-permute-done.1.refs_4_, ...), custom_call_target="tpu_custom_call" | custom-call | flops 1000000000 | tf_op jit(solution)/shard_map/pallas_call | solution.py:682
  10.2 2.3 %collective-permute-start.3 = (bf16[48,256]{1,0:T(8,128)(2,1)S(1)}, bf16[48,256]{1,0:T(8,128)(2,1)S(1)}, u32[]{:S(2)}, u32[]{:S(2)}) collective-permute-start(bf16[48,256]{1,0:T(8,128)(2,1)S(1)} %get-tuple-element.53), channel_id=1, source_target_pairs={{0,16},{2,18},{4,20},{6,22},{8,24},{10,26},{12,28},{14,30},{30,14}... | collective-permute-start | bytes 73736 | tf_op jit(solution)/shard_map/ppermute | solution.py:541
  12.5 0.0 copy-start
  12.6 3.7 %shard_map.147 = (bf16[768,256]{1,0:T(8,128)(2,1)S(1)}, f32[768,256]{1,0:T(8,128)S(1)}, f32[768,128]{1,0:T(8,128)S(1)}, bf16[256,768]{1,0:T(8,128)(2,1)S(1)}, f3...) custom-call(s32[1]{0:T(128)S(6)} %copy.16.refs_0_, s32[3]{0:T(128)S(1)} %copy-done.8, bf16[7,7,256]{2,1,0:T(8,128)(2,1)S(1)} %copy-done.6, ...), custom_call_target="tpu_custom_call" | custom-call | flops 5000000000 | tf_op jit(solution)/shard_map/pallas_call | solution.py:682
  16.3 4.1 %shard_map.148 = (f32[1024,256]{1,0:T(8,128)S(1)}, bf16[1024,256]{1,0:T(8,128)(2,1)S(1)}, bf16[768,1024]{1,0:T(8,128)(2,1)S(1)}, bf16[768,1024]{1,0:T(8,128)(2,1...) custom-call(s32[1]{0:T(128)S(6)} %copy.16.refs_0_, ...), custom_call_target="tpu_custom_call" | custom-call | flops 5000000000 | tf_op jit(solution)/shard_map/pallas_call | solution.py:682
  20.4 0.1 collective-permute-start.4
  20.5 1.1 %shard_map.149 = (bf16[768,256]{1,0:T(8,128)(2,1)S(1)}, f32[768,256]{1,0:T(8,128)S(1)}, f32[8,256]{1,0:T(8,128)S(1)}, f32[8,256]{1,0:T(8,128)S(1)}) custom-call(bf16[256,1024]{1,0:T(8,128)(2,1)S(1)} %copy-done, bf16[1024,256]{1,0:T(8,128)(2,1)S(1)} %copy-done.1, f32[1,256]{1,0:T(1,128)S(1)} %bitcast.13, bf16[768,1024]{1,0:T(8,128)(2,1)S(1)} %get-tuple-element.59.refs_3_, ...), custom_call_target="tpu_custom_call" | custom-call | flops 1300000000 | tf_op jit(solution)/shard_map/pallas_call | solution.py:682
  21.6 0.8 %collective-permute-done.4.refs_1_ = bf16[1024,256]{1,0:T(8,128)(2,1)S(1)} collective-permute-done((bf16[1024,256]{1,0:T(8,128)(2,1)S(1)}, bf16[1024,256]{1,0:T(8,128)(2,1)S(1)}, u32[]{:S(2)}, u32[]{:S(2)}) %collective-permute-start.4) | collective-permute-done | bytes 524320 | tf_op jit(solution)/shard_map/ppermute | solution.py:545
  22.4 0.2 shard_map.150
  22.5 0.4 collective-permute-start.6
  22.9 1.7 %shard_map.151.refs_3_.refs_4_.refs_2_ = f32[1216,128]{1,0:T(8,128)S(1)} custom-call(s32[1]{0:T(128)S(6)} %copy.16.refs_0_, bf16[7,7,256]{2,1,0:T(8,128)(2,1)S(1)} %copy-done.6, bf16[768,256]{1,0:T(8,128)(2,1)S(1)} %get-tuple-element.65.refs_2_, bf16[512,256]{1,0:T(8,128)(2,1)S(1)} %get-tuple-element.69.refs_3_), custom_call_target="tpu_custom_call" | custom-call | flops 2000000000 | tf_op jit(solution)/shard_map/pallas_call | solution.py:682
  24.6 1.9 %shard_map.152 = (f32[1216,128]{1,0:T(8,128)S(1)}, bf16[192,256]{1,0:T(8,128)(2,1)S(1)}) custom-call(s32[1]{0:T(128)S(6)} %copy.16.refs_0_, bf16[7,7,256]{2,1,0:T(8,128)(2,1)S(1)} %copy-done.6, bf16[768,256]{1,0:T(8,128)(2,1)S(1)} %get-tuple-element.65.refs_2_, f32[1216,128]{1,0:T(8,128)S(1)} %shard_map.151.refs_3_.refs_4_.refs_2_, ...), custom_call_target="tpu_custom_call" | custom-call | flops 2000000000 | tf_op jit(solution)/shard_map/pallas_call | solution.py:682
  26.5 2.0 %collective-permute-start.5 = (bf16[192,256]{1,0:T(8,128)(2,1)S(1)}, bf16[192,256]{1,0:T(8,128)(2,1)S(1)}, u32[]{:S(2)}, u32[]{:S(2)}) collective-permute-start(bf16[192,256]{1,0:T(8,128)(2,1)S(1)} %get-tuple-element.70), channel_id=1, source_target_pairs={{0,16},{2,18},{4,20},{6,22},{8,24},{10,26},{12,28},{14,30},{30,14}... | collective-permute-start | bytes 294920 | tf_op jit(solution)/shard_map/ppermute | solution.py:541
  28.5 0.4 collective-permute-done.6.refs_1_
  29.0 0.1 shard_map.153
  29.0 1.6 %collective-permute-start.7 = (bf16[256,256]{1,0:T(8,128)(2,1)S(1)}, bf16[256,256]{1,0:T(8,128)(2,1)S(1)}, u32[]{:S(2)}, u32[]{:S(2)}) collective-permute-start(bf16[256,256]{1,0:T(8,128)(2,1)S(1)} %get-tuple-element.74.refs_3_), channel_id=1, source_target_pairs={{0,1},{1,0},{2,6},{3,7},{4,5},{5,4},{6,2},{7,3},{8,9},{9,8},{10,14... | collective-permute-start | bytes 393224 | tf_op jit(solution)/shard_map/ppermute | solution.py:565
  30.6 1.8 %shard_map.155.refs_3_ = f32[64,128]{1,0:T(8,128)S(1)} custom-call(f32[2,1216,128]{2,1,0:T(8,128)S(1)} %get-tuple-element.52.refs_7_.refs_4_.refs_0_, f32[2,640,128]{2,1,0:T(8,128)S(1)} %get-tuple-element.76.refs_1_, bf16[768,256]{1,0:T(8,128)(2,1)S(1)} %get-tuple-element.65.refs_2_, bf16[256,256]{1,0:T(8,128)(2,1)S(1)} %get-tuple-element.74.refs_3_), custom_call_target="tpu_custom_call" | custom-call | flops 1800000000 | tf_op jit(solution)/shard_map/pallas_call | solution.py:682
  32.4 1.8 %shard_map.154.refs_2_ = f32[64,128]{1,0:T(8,128)S(1)} custom-call(f32[2,1216,128]{2,1,0:T(8,128)S(1)} %get-tuple-element.52.refs_7_.refs_4_.refs_0_, f32[2,640,128]{2,1,0:T(8,128)S(1)} %get-tuple-element.76.refs_1_, bf16[768,256]{1,0:T(8,128)(2,1)S(1)} %get-tuple-element.65.refs_2_, bf16[256,256]{1,0:T(8,128)(2,1)S(1)} %get-tuple-element.74.refs_3_), custom_call_target="tpu_custom_call" | custom-call | flops 1800000000 | tf_op jit(solution)/shard_map/pallas_call | solution.py:682
  34.2 0.1 collective-permute-start.11
  34.3 0.1 shard_map.157
  34.4 1.1 %collective-permute-start.10 = (bf16[128,256]{1,0:T(8,128)(2,1)S(1)}, bf16[128,256]{1,0:T(8,128)(2,1)S(1)}, u32[]{:S(2)}, u32[]{:S(2)}) collective-permute-start(bf16[128,256]{1,0:T(8,128)(2,1)S(1)} %get-tuple-element.78.refs_4_), channel_id=1, source_target_pairs={{0,8},{1,9},{2,3},{3,2},{4,12},{5,13},{6,7},{7,6},{8,0},{9,1},{10,... | collective-permute-start | bytes 196616 | tf_op jit(solution)/shard_map/ppermute | solution.py:565
  35.4 0.6 shard_map.158
  36.1 0.1 collective-permute-start.8
  36.1 1.3 %collective-permute-start.9 = (bf16[48,256]{1,0:T(8,128)(2,1)S(1)}, bf16[48,256]{1,0:T(8,128)(2,1)S(1)}, u32[]{:S(2)}, u32[]{:S(2)}) collective-permute-start(bf16[48,256]{1,0:T(8,128)(2,1)S(1)} %get-tuple-element.81), channel_id=1, source_target_pairs={{0,16},{2,4},{4,2},{6,8},{8,6},{10,12},{12,10},{14,30},{30,14},{28... | collective-permute-start | bytes 73736 | tf_op jit(solution)/shard_map/ppermute | solution.py:541
  37.5 1.2 %collective-permute-done.10.refs_1_ = bf16[128,256]{1,0:T(8,128)(2,1)S(1)} collective-permute-done((bf16[128,256]{1,0:T(8,128)(2,1)S(1)}, bf16[128,256]{1,0:T(8,128)(2,1)S(1)}, u32[]{:S(2)}, u32[]{:S(2)}) %collective-permute-start.10) | collective-permute-done | bytes 65568 | tf_op jit(solution)/shard_map/ppermute | solution.py:565
  38.7 0.0 copy-start.5
  38.8 1.1 %collective-permute-start.12 = (bf16[160,256]{1,0:T(8,128)(2,1)S(1)}, bf16[160,256]{1,0:T(8,128)(2,1)S(1)}, u32[]{:S(2)}, u32[]{:S(2)}) collective-permute-start(bf16[160,256]{1,0:T(8,128)(2,1)S(1)} %shard_map.159.refs_6_.refs_0_), channel_id=1, source_target_pairs={{0,16},{1,17},{2,18},{3,19},{4,20},{5,21},{6,22},{7,23},{8,24},{9,... | collective-permute-start | bytes 245768 | tf_op jit(solution)/shard_map/ppermute | solution.py:565
  39.8 1.1 %collective-permute-done.9.refs_5_ = bf16[48,256]{1,0:T(8,128)(2,1)S(1)} collective-permute-done((bf16[48,256]{1,0:T(8,128)(2,1)S(1)}, bf16[48,256]{1,0:T(8,128)(2,1)S(1)}, u32[]{:S(2)}, u32[]{:S(2)}) %collective-permute-start.9) | collective-permute-done | bytes 24608 | tf_op jit(solution)/shard_map/ppermute | solution.py:541
  40.9 1.6 %shard_map.160 = (bf16[768,256]{1,0:T(8,128)(2,1)}, f32[8,128]{1,0:T(8,128)S(1)}) custom-call(s32[1]{0:T(128)S(6)} %copy.16.refs_0_, s32[3]{0:T(128)S(1)} %copy-done.8, bf16[768,256]{1,0:T(8,128)(2,1)S(1)} %bitcast.10, f32[2,1024,128]{2,1,0:T(8,128)S(1)} %get-tuple-element.79.refs_4_.refs_3_, bf16[48,256]{1,0:T(8,128)(2,1)S(1)} %collective-permute-done.8.refs_4_, ...), custom_call_target="tpu_custom_call" | custom-call | flops 1500000000 | tf_op jit(solution)/shard_map/pallas_call | solution.py:682
  42.6 0.9 %shard_map.161 = (bf16[768,256]{1,0:T(8,128)(2,1)}, f32[8,128]{1,0:T(8,128)S(1)}) custom-call(bf16[768,256]{1,0:T(8,128)(2,1)S(1)} %bitcast.17, f32[1,256]{1,0:T(1,128)S(1)} %bitcast.19, f32[768,256]{1,0:T(8,128)S(1)} %get-tuple-element.64.refs_2_, f32[3,8,256]{2,1,0:T(8,128)S(1)} %get-tuple-element.63.refs_8_.refs_3_, ...), custom_call_target="tpu_custom_call" | custom-call | flops 1000000000 | tf_op jit(solution)/shard_map/pallas_call | solution.py:682
  43.5 2.0 %collective-permute-done.12.refs_1_ = bf16[160,256]{1,0:T(8,128)(2,1)S(1)} collective-permute-done((bf16[160,256]{1,0:T(8,128)(2,1)S(1)}, bf16[160,256]{1,0:T(8,128)(2,1)S(1)}, u32[]{:S(2)}, u32[]{:S(2)}) %collective-permute-start.12) | collective-permute-done | bytes 81952 | tf_op jit(solution)/shard_map/ppermute | solution.py:565
  45.5 13.4 %all_to_all.5.refs_0_ = bf16[8,160,256]{2,1,0:T(8,128)(2,1)S(1)} all-to-all(bf16[8,160,256]{2,1,0:T(8,128)(2,1)S(1)} %shard_map.162), channel_id=1, replica_groups=mesh['far'=2,'near'=4,'core'=2,'dp'=2] {'near','dp'}, dimensions={0} | all-to-all | bytes 1310720 | tf_op jit(solution)/shard_map/all_to_all | solution.py:861
  58.9 0.1 shard_map.163.refs_0_
  59.0 0.1 collective-permute-start.13
  59.1 1.9 %collective-permute-done.13.refs_1_ = bf16[1088,256]{1,0:T(8,128)(2,1)S(1)} collective-permute-done((bf16[1088,256]{1,0:T(8,128)(2,1)S(1)}, bf16[1088,256]{1,0:T(8,128)(2,1)S(1)}, u32[]{:S(2)}, u32[]{:S(2)}) %collective-permute-start.13) | collective-permute-done | bytes 557088 | tf_op jit(solution)/shard_map/ppermute | solution.py:545
  61.0 1.6 %shard_map.164 = (f32[256,1024]{1,0:T(8,128)}, f32[1024,256]{1,0:T(8,128)}, f32[7,7,256]{2,1,0:T(8,128)}, f32[1,256]{1,0:T(1,128)}, f32[1,256]{1,0:T(1,128)}) custom-call(bf16[1088,256]{1,0:T(8,128)(2,1)S(1)} %shard_map.163.refs_0_, bf16[1088,256]{1,0:T(8,128)(2,1)S(1)} %collective-permute-done.13.refs_1_), custom_call_target="tpu_custom_call" | custom-call | flops 1500000000 | tf_op jit(solution)/shard_map/pallas_call | solution.py:682
  (20 shorter events, 0.1 us)
Async XLA Ops:
  1.3 1.0 %copy-start.4 = (bf16[1,3,16,16,256]{4,3,2,1,0:T(8,128)(2,1)S(1)}, bf16[1,3,16,16,256]{4,3,2,1,0:T(8,128)(2,1)}, u32[]{:S(2)}) copy-start(bf16[1,3,16,16,256]{4,3,2,1,0:T(8,128)(2,1)} %param.9) | copy-start | bytes 1179652
  2.3 4.7 %copy-start.8 = (s32[3]{0:T(128)S(1)}, s32[3]{0:T(128)}, u32[]{:S(2)}) copy-start(s32[3]{0:T(128)} %refs_1_.15) | copy-start | bytes 40
  2.9 6.6 %collective-permute-start.1 = (bf16[48,256]{1,0:T(8,128)(2,1)S(1)}, bf16[48,256]{1,0:T(8,128)(2,1)S(1)}, u32[]{:S(2)}, u32[]{:S(2)}) collective-permute-start(bf16[48,256]{1,0:T(8,128)(2,1)S(1)} %get-tuple-element.51), channel_id=1, source_target_pairs={{0,16},{2,4},{4,2},{6,8},{8,6},{10,12},{12,10},{14,30},{30,14},{28... | collective-permute-start | bytes 73736 | tf_op jit(solution)/shard_map/ppermute | solution.py:541
  7.0 2.5 %collective-permute-start = (bf16[48,256]{1,0:T(8,128)(2,1)S(1)}, bf16[48,256]{1,0:T(8,128)(2,1)S(1)}, u32[]{:S(2)}, u32[]{:S(2)}) collective-permute-start(bf16[48,256]{1,0:T(8,128)(2,1)S(1)} %get-tuple-element.50.refs_3_), channel_id=1, source_target_pairs={{0,2},{2,0},{4,6},{6,4},{8,10},{10,8},{12,14},{14,12},{30,28},{28,... | collective-permute-start | bytes 73736 | tf_op jit(solution)/shard_map/ppermute | solution.py:541
  7.7 4.8 %copy-start.1 = (bf16[1024,256]{1,0:T(8,128)(2,1)S(1)}, bf16[1024,256]{1,0:T(8,128)(2,1)}, u32[]{:S(2)}) copy-start(bf16[1024,256]{1,0:T(8,128)(2,1)} %refs_1_.12) | copy-start | bytes 1572868
  7.7 4.8 %copy-start.2 = (bf16[1,3,16,16,256]{4,3,2,1,0:T(8,128)(2,1)S(1)}, bf16[1,3,16,16,256]{4,3,2,1,0:T(8,128)(2,1)}, u32[]{:S(2)}) copy-start(bf16[1,3,16,16,256]{4,3,2,1,0:T(8,128)(2,1)} %param.10) | copy-start | bytes 1179652
  7.7 4.8 %copy-start.3 = (f32[256]{0:T(256)S(1)}, f32[256]{0:T(256)}, u32[]{:S(2)}) copy-start(f32[256]{0:T(256)} %param.14) | copy-start | bytes 3076
  7.7 4.8 %copy-start.6 = (bf16[7,7,256]{2,1,0:T(8,128)(2,1)S(1)}, bf16[7,7,256]{2,1,0:T(8,128)(2,1)}, u32[]{:S(2)}) copy-start(bf16[7,7,256]{2,1,0:T(8,128)(2,1)} %refs_1_.14) | copy-start | bytes 75268
  7.8 4.8 %copy-start.7 = (f32[256]{0:T(256)S(1)}, f32[256]{0:T(256)}, u32[]{:S(2)}) copy-start(f32[256]{0:T(256)} %param.17) | copy-start | bytes 3076
  7.8 8.5 %collective-permute-start.2 = (bf16[144,256]{1,0:T(8,128)(2,1)S(1)}, bf16[144,256]{1,0:T(8,128)(2,1)S(1)}, u32[]{:S(2)}, u32[]{:S(2)}) collective-permute-start(bf16[144,256]{1,0:T(8,128)(2,1)S(1)} %shard_map.145.refs_5_), channel_id=1, source_target_pairs={{0,16},{2,18},{4,20},{6,22},{8,24},{10,26},{12,28},{14,30},{30,14}... | collective-permute-start | bytes 221192 | tf_op jit(solution)/shard_map/ppermute | solution.py:541
  10.2 6.0 %collective-permute-start.3 = (bf16[48,256]{1,0:T(8,128)(2,1)S(1)}, bf16[48,256]{1,0:T(8,128)(2,1)S(1)}, u32[]{:S(2)}, u32[]{:S(2)}) collective-permute-start(bf16[48,256]{1,0:T(8,128)(2,1)S(1)} %get-tuple-element.53), channel_id=1, source_target_pairs={{0,16},{2,18},{4,20},{6,22},{8,24},{10,26},{12,28},{14,30},{30,14}... | collective-permute-start | bytes 73736 | tf_op jit(solution)/shard_map/ppermute | solution.py:541
  12.5 3.7 %copy-start = (bf16[256,1024]{1,0:T(8,128)(2,1)S(1)}, bf16[256,1024]{1,0:T(8,128)(2,1)}, u32[]{:S(2)}) copy-start(bf16[256,1024]{1,0:T(8,128)(2,1)} %refs_0_.10) | copy-start | bytes 1572868
  20.4 2.0 %collective-permute-start.4 = (bf16[1024,256]{1,0:T(8,128)(2,1)S(1)}, bf16[1024,256]{1,0:T(8,128)(2,1)S(1)}, u32[]{:S(2)}, u32[]{:S(2)}) collective-permute-start(bf16[1024,256]{1,0:T(8,128)(2,1)S(1)} %get-tuple-element.67), channel_id=1, source_target_pairs={{0,2},{2,0},{1,3},{3,1},{4,6},{6,4},{5,7},{7,5},{8,10},{10,8},{9,1... | collective-permute-start | bytes 1572872 | tf_op jit(solution)/shard_map/ppermute | solution.py:545
  22.5 6.4 %collective-permute-start.6 = (bf16[512,256]{1,0:T(8,128)(2,1)S(1)}, bf16[512,256]{1,0:T(8,128)(2,1)S(1)}, u32[]{:S(2)}, u32[]{:S(2)}) collective-permute-start(bf16[512,256]{1,0:T(8,128)(2,1)S(1)} %get-tuple-element.69.refs_3_), channel_id=1, source_target_pairs={{0,4},{1,5},{2,10},{3,11},{4,0},{5,1},{6,14},{7,15},{8,12},{9,13},... | collective-permute-start | bytes 786440 | tf_op jit(solution)/shard_map/ppermute | solution.py:565
  26.5 8.9 %collective-permute-start.5 = (bf16[192,256]{1,0:T(8,128)(2,1)S(1)}, bf16[192,256]{1,0:T(8,128)(2,1)S(1)}, u32[]{:S(2)}, u32[]{:S(2)}) collective-permute-start(bf16[192,256]{1,0:T(8,128)(2,1)S(1)} %get-tuple-element.70), channel_id=1, source_target_pairs={{0,16},{2,18},{4,20},{6,22},{8,24},{10,26},{12,28},{14,30},{30,14}... | collective-permute-start | bytes 294920 | tf_op jit(solution)/shard_map/ppermute | solution.py:541
  29.0 5.3 %collective-permute-start.7 = (bf16[256,256]{1,0:T(8,128)(2,1)S(1)}, bf16[256,256]{1,0:T(8,128)(2,1)S(1)}, u32[]{:S(2)}, u32[]{:S(2)}) collective-permute-start(bf16[256,256]{1,0:T(8,128)(2,1)S(1)} %get-tuple-element.74.refs_3_), channel_id=1, source_target_pairs={{0,1},{1,0},{2,6},{3,7},{4,5},{5,4},{6,2},{7,3},{8,9},{9,8},{10,14... | collective-permute-start | bytes 393224 | tf_op jit(solution)/shard_map/ppermute | solution.py:565
  34.2 3.2 %collective-permute-start.11 = (bf16[64,256]{1,0:T(8,128)(2,1)S(1)}, bf16[64,256]{1,0:T(8,128)(2,1)S(1)}, u32[]{:S(2)}, u32[]{:S(2)}) collective-permute-start(bf16[64,256]{1,0:T(8,128)(2,1)S(1)} %get-tuple-element.83), channel_id=1, source_target_pairs={{0,2},{2,0},{1,3},{3,1},{4,6},{6,4},{5,7},{7,5},{8,10},{10,8},{9,1... | collective-permute-start | bytes 98312 | tf_op jit(solution)/shard_map/ppermute | solution.py:545
  34.4 4.3 %collective-permute-start.10 = (bf16[128,256]{1,0:T(8,128)(2,1)S(1)}, bf16[128,256]{1,0:T(8,128)(2,1)S(1)}, u32[]{:S(2)}, u32[]{:S(2)}) collective-permute-start(bf16[128,256]{1,0:T(8,128)(2,1)S(1)} %get-tuple-element.78.refs_4_), channel_id=1, source_target_pairs={{0,8},{1,9},{2,3},{3,2},{4,12},{5,13},{6,7},{7,6},{8,0},{9,1},{10,... | collective-permute-start | bytes 196616 | tf_op jit(solution)/shard_map/ppermute | solution.py:565
  36.1 3.7 %collective-permute-start.8 = (bf16[48,256]{1,0:T(8,128)(2,1)S(1)}, bf16[48,256]{1,0:T(8,128)(2,1)S(1)}, u32[]{:S(2)}, u32[]{:S(2)}) collective-permute-start(bf16[48,256]{1,0:T(8,128)(2,1)S(1)} %get-tuple-element.80), channel_id=1, source_target_pairs={{0,2},{2,0},{4,6},{6,4},{8,10},{10,8},{12,14},{14,12},{30,28},{28,... | collective-permute-start | bytes 73736 | tf_op jit(solution)/shard_map/ppermute | solution.py:541
  36.1 4.8 %collective-permute-start.9 = (bf16[48,256]{1,0:T(8,128)(2,1)S(1)}, bf16[48,256]{1,0:T(8,128)(2,1)S(1)}, u32[]{:S(2)}, u32[]{:S(2)}) collective-permute-start(bf16[48,256]{1,0:T(8,128)(2,1)S(1)} %get-tuple-element.81), channel_id=1, source_target_pairs={{0,16},{2,4},{4,2},{6,8},{8,6},{10,12},{12,10},{14,30},{30,14},{28... | collective-permute-start | bytes 73736 | tf_op jit(solution)/shard_map/ppermute | solution.py:541
  38.7 3.8 %copy-start.5 = (bf16[1,3,16,16,256]{4,3,2,1,0:T(8,128)(2,1)S(1)}, bf16[1,3,16,16,256]{4,3,2,1,0:T(8,128)(2,1)}, u32[]{:S(2)}) copy-start(bf16[1,3,16,16,256]{4,3,2,1,0:T(8,128)(2,1)} %param.9) | copy-start | bytes 1179652
  38.8 6.7 %collective-permute-start.12 = (bf16[160,256]{1,0:T(8,128)(2,1)S(1)}, bf16[160,256]{1,0:T(8,128)(2,1)S(1)}, u32[]{:S(2)}, u32[]{:S(2)}) collective-permute-start(bf16[160,256]{1,0:T(8,128)(2,1)S(1)} %shard_map.159.refs_6_.refs_0_), channel_id=1, source_target_pairs={{0,16},{1,17},{2,18},{3,19},{4,20},{5,21},{6,22},{7,23},{8,24},{9,... | collective-permute-start | bytes 245768 | tf_op jit(solution)/shard_map/ppermute | solution.py:565
  59.0 2.0 %collective-permute-start.13 = (bf16[1088,256]{1,0:T(8,128)(2,1)S(1)}, bf16[1088,256]{1,0:T(8,128)(2,1)S(1)}, u32[]{:S(2)}, u32[]{:S(2)}) collective-permute-start(bf16[1088,256]{1,0:T(8,128)(2,1)S(1)} %shard_map.163.refs_0_), channel_id=1, source_target_pairs={{0,2},{2,0},{1,3},{3,1},{4,6},{6,4},{5,7},{7,5},{8,10},{10,8},{9,1... | collective-permute-start | bytes 1671176 | tf_op jit(solution)/shard_map/ppermute | solution.py:545

commit v8 on v7

--- a/solution.py
+++ b/solution.py
@@ -576,16 +576,22 @@
     return pl.ds(pl.multiple_of(bit * rows, rows), rows)
 
 
-def join_kernel(stage, keep, came, mine, send):
-    rows = send.shape[0]
-    mine[...] = keep[...] + came[...].astype(F32)
-    send[...] = mine[half_rows(1 - bit_here(stage), rows), :].astype(BF16)
-
-
-def halve_kernel(stage, following, whole, came, mine, send):
-    rows = mine.shape[0]
-    mine[...] = whole[half_rows(bit_here(stage), rows), :] + came[...].astype(F32)
-    send[...] = mine[half_rows(1 - bit_here(following), rows // 2), :].astype(BF16)
+def place_of(order, at):
+    near, sample = divmod(at, lax.axis_size("dp"))
+    places = []
+    for core in range(2):
+        place = 0
+        for stage in order:
+            place = 2 * place + (sample if stage[core] < 0 else near >> stage[core] & 1)
+        places.append(place)
+    return jnp.where(lax.axis_index("core") == 0, places[0], places[1])
+
+
+def join_kernel(order, keep, came, pieces):
+    rows = pieces.shape[1]
+    for at in range(pieces.shape[0]):
+        share = half_rows(place_of(order, at), rows)
+        pieces[at] = (keep[share, :] + came[share, :].astype(F32)).astype(BF16)
 
 
 def pack_kernel(gain_part, scale_part, *refs):
@@ -604,9 +610,9 @@
     send[pl.ds(half, half), :] = (value - high.astype(F32)).astype(BF16)
 
 
-def turn_kernel(stage, whole, came, keep, extra, payload):
-    rows, half = came.shape[0], keep.shape[0]
-    share = whole[half_rows(bit_here(stage), rows), :] + came[...].astype(F32)
+def turn_kernel(came, keep, extra, payload):
+    rows, half = came.shape[1], keep.shape[0]
+    share = sum(came[at].astype(F32) for at in range(came.shape[0]))
     payload[pl.ds(0, rows), :] = share.astype(BF16)
     small = keep[...] + (extra[pl.ds(0, half), :].astype(F32) + extra[pl.ds(half, half), :].astype(F32))
     payload[pl.ds(rows, half), :] = small.astype(BF16)
@@ -623,19 +629,9 @@
 
 def gather_kernel(order, extra, came, payload):
     rows = came.shape[1] - extra
-    samples = lax.axis_size("dp")
-    is_first = lax.axis_index("core") == 0
     total = jnp.zeros((extra, came.shape[2]), F32)
     for at in range(came.shape[0]):
-        near, sample = divmod(at, samples)
-        places = []
-        for core in range(2):
-            place = 0
-            for stage in order:
-                place = 2 * place + (sample if stage[core] < 0 else near >> stage[core] & 1)
-            places.append(place)
-        place = jnp.where(is_first, places[0], places[1])
-        payload[half_rows(place, rows), :] = came[at, pl.ds(0, rows), :]
+        payload[half_rows(place_of(order, at), rows), :] = came[at, pl.ds(0, rows), :]
         total += came[at, pl.ds(rows, extra), :].astype(F32)
     high = total.astype(BF16)
     full = rows * came.shape[0]
@@ -655,16 +651,13 @@
         payload[pl.ds(2 * rows + extra, extra), :] = (total - high.astype(F32)).astype(BF16)
 
 
-def halved(mine, send, order):
-    for at, stage in enumerate(order[:-1]):
-        came = bit_swap(send, stage)
-        rows = came.shape[0]
+def halved(mine, order):
+    for stage in order:
         bit = bit_here(stage)
-        mine = lax.dynamic_index_in_dim(mine.reshape(2, rows, -1), bit, 0, keepdims=False) + came.astype(F32)
-        bit = bit_here(order[at + 1])
-        halves = mine.reshape(2, rows // 2, -1)
+        halves = mine.reshape(2, -1, mine.shape[-1])
         send = lax.dynamic_index_in_dim(halves, 1 - bit, 0, keepdims=False).astype(BF16)
-    return mine, send
+        mine = lax.dynamic_index_in_dim(halves, bit, 0, keepdims=False) + bit_swap(send, stage).astype(F32)
+    return mine
 
 
 def call(kernel, outs, scratch, hbm, vmem, copies=0, micros=1.0, after=(), limit=20):
@@ -755,12 +748,9 @@
     )
 
     order = stages()
-    rows = hidden // 2
-
-    def half_step(at, rows):
-        return functools.partial(halve_kernel, order[at], order[at + 1]), [
-            ((rows, channels), F32), ((rows // 2, channels), BF16),
-        ]
+    block = lax.axis_size("near") * lax.axis_size("dp")
+    inner = block.bit_length() - 1
+    rows = hidden // block
 
     def taps_part(part, after):
         (small,) = call(
@@ -784,11 +774,11 @@
         bind(norm_grad_kernel), [whole, whole_f, eight, eight], [], [],
         [w_in, w_out, gain, dpreact, yhat, inverse, activated, tangent, live], 0, 1.3,
     )
-    mine, send = call(
-        functools.partial(join_kernel, order[0]),
-        [((hidden, channels), F32), ((rows, channels), BF16)], [], [], [keep, came], after=[gain_part], micros=0.3,
-    )
-    came = bit_swap(send, order[0])
+    (send,) = call(
+        functools.partial(join_kernel, order[:inner]), [((block, rows, channels), BF16)],
+        [], [], [keep, came], after=[gain_part], micros=0.3,
+    )
+    came = lax.all_to_all(send, ("near", "dp"), 0, 0, tiled=True)
     core_grad = []
     after = [send]
     for part in range(parts):
@@ -796,37 +786,27 @@
         core_grad += [one]
         after = [one]
     fold_back = swap(fold_back[0], "fold")
-    body, outs = half_step(0, rows)
-    mine, send = call(body, outs, [], [], [mine, came], after=after, micros=0.3)
-    came = bit_swap(send, order[1])
-    taps_parts = [taps_part(part, [send]) for part in range(parts)]
+    taps_parts = [taps_part(part, after) for part in range(parts)]
     small_rows //= 2
     small, extra = call(
         pack_kernel, [((small_rows, channels), F32), ((2 * small_rows, channels), BF16)],
         [((2 * small_rows, channels), F32)], [], [gain_part, scale_part, *taps_parts], micros=0.3,
     )
     extra = core_swap(extra)
-    rows //= 2
-    body, outs = half_step(1, rows)
-    mine, send = call(body, outs, [], [], [mine, came], after=[small], micros=0.3)
-    mine, send = halved(mine, send, order[2:-1])
-    came = bit_swap(send, order[-2])
     folded, first, second = call(
         bind(rims_kernel), [strip(TILE), edge, edge], [count_s], [block_count], [fold_back, *core_grad], 1, 1.0,
-        after=[send],
+        after=[small],
     )
     first, second = swap(first, "first"), swap(second, "second")
-    rows = came.shape[0]
-    if rows % 16 == 0:
+    if len(order) == inner + 1:
         (payload,) = call(
-            functools.partial(turn_kernel, order[-2]), [((rows + small_rows, channels), BF16)],
-            [], [], [mine, came, small, extra], after=[folded], micros=0.3,
+            turn_kernel, [((rows + small_rows, channels), BF16)], [], [], [came, small, extra], after=[folded], micros=0.3,
         )
     else:
-        bit = bit_here(order[-2])
-        share = lax.dynamic_index_in_dim(mine.reshape(2, rows, channels), bit, 0, keepdims=False)
+        share = halved(jnp.sum(came.astype(F32), axis=0), order[inner:-1])
+        rows = share.shape[0]
         small = small + (extra[:small_rows].astype(F32) + extra[small_rows:].astype(F32))
-        payload = jnp.concatenate([share + came.astype(F32), small]).astype(BF16)
+        payload = jnp.concatenate([share, small]).astype(BF16)
     came = bit_swap(payload, order[-1])
     grad_fields, done = call(
         bind(final_kernel), [whole, ((8, LANES), F32)], [count_s, ocean_s, strip(TILE)],
@@ -835,9 +815,8 @@
     state, done_too = call(
         bind(state_kernel), [whole, ((8, LANES), F32)], [], [], [fields, scale, projected, live], 0, 1.0, after=[done],
     )
-    block = lax.axis_size("near") * lax.axis_size("dp")
     copied = (block, *payload.shape)
-    outer = range(block.bit_length() - 1, len(order) - 1)
+    outer = range(inner, len(order) - 1)
     (payload,) = call(
         add_kernel, [(payload.shape if outer else copied, BF16)], [], [], [payload, came], after=[done, done_too],
         micros=0.3,
@@ -860,7 +839,7 @@
         payload = jnp.broadcast_to(payload, (block, *payload.shape))
     came = lax.all_to_all(payload, ("near", "dp"), 0, 0, tiled=True)
     (payload,) = call(
-        functools.partial(gather_kernel, order[: block.bit_length() - 1], small_rows),
+        functools.partial(gather_kernel, order[:inner], small_rows),
         [((hidden + 2 * small_rows, channels), BF16)], [], [], [came], micros=0.3,
     )
     came = core_swap(payload)

time: 62.8 us -> 65.4 us (1.041)
  waiting for transfers between devices: 7.57 us -> 8.49 us
    ppermute x7, waiting for transfers between devices: 1.14 us -> 4.8 us  [swap(): return lax.ppermute(block, TILES, pairs_of(kind))]
    all_to_all x0 -> x1, starting transfers between devices: none -> 3.49 us  [shards(): came = lax.all_to_all(send, ('near', 'dp'), 0, 0, tiled=True)]
    ppermute x4 -> x1, waiting for transfers between devices: 3.69 us -> 0.94 us  [bit_swap(): return lax.ppermute(block, TILES + ('dp',), pairs)]
    ppermute x7, starting transfers between devices: 11.5 us -> 9.72 us  [swap(): return lax.ppermute(block, TILES, pairs_of(kind))]
    ppermute x4 -> x1, starting transfers between devices: 4.07 us -> 2.67 us  [bit_swap(): return lax.ppermute(block, TILES + ('dp',), pairs)]
    pallas_call x21 -> x19, Pallas kernels: 23.3 us -> 23.9 us  [call(): pl.pallas_call(body, out_shape=[jax.ShapeDtypeStruct(*out) for out in out...]
  transfers between devices with their start and end apart: 14 -> 12, of which waited for: 6 -> 5; matrix products, arithmetic and copies ran while one was open for 0% -> 0% of each run, Pallas kernels for 27% -> 26%
where the time goes in v8:
time: 65.4 us; the launch traced here: 65.1 us
  Pallas kernels  23.9 us (37%)
  starting transfers between devices  16.1 us (25%)
  blocking collectives  14 us (21%)
  waiting for transfers between devices  8.49 us (13%)
  between operations  1.57 us (2%)
  local copies, waits for them, and re-layouts  1.05 us (2%)
    pallas_call x19, Pallas kernels, call(): pl.pallas_call(body, out_shape=[jax.ShapeDtypeStruct(*out) for out in out...  23.9 us
    all_to_all x1, blocking collectives, shards(): came = lax.all_to_all(payload, ('near', 'dp'), 0, 0, tiled=True)  14 us
    ppermute x7, starting transfers between devices, swap(): return lax.ppermute(block, TILES, pairs_of(kind))  9.72 us
    ppermute x7, waiting for transfers between devices, swap(): return lax.ppermute(block, TILES, pairs_of(kind))  4.8 us
    all_to_all x1, starting transfers between devices, shards(): came = lax.all_to_all(send, ('near', 'dp'), 0, 0, tiled=True)  3.49 us
    ppermute x3, waiting for transfers between devices, core_swap(): return lax.ppermute(block, 'core', [(0, 1), (1, 0)])  2.74 us
    ppermute x1, starting transfers between devices, bit_swap(): return lax.ppermute(block, TILES + ('dp',), pairs)  2.67 us
  transfers between devices with their start and end apart: 12, of which 5 were waited for; matrix products, arithmetic and copies ran while one was open for 0% of the time, Pallas kernels for 26%

profile of v8, /device:TPU:0, one launch (start us, length us, event | category | flops | bytes accessed | tf_op | source)
XLA Modules:
  0.0 65.1 jit_solution(5276065083857073596)
XLA Ops:
  1.3 0.0 copy-start.4
  1.3 1.0 %copy-done.4 = bf16[1,3,16,16,256]{4,3,2,1,0:T(8,128)(2,1)S(1)} copy-done((bf16[1,3,16,16,256]{4,3,2,1,0:T(8,128)(2,1)S(1)}, bf16[1,3,16,16,256]{4,3,2,1,0:T(8,128)(2,1)}, u32[]{:S(2)}) %copy-start.4) | copy-done | bytes 393240
  2.3 0.6 shard_map.144
  2.9 4.1 %collective-permute-start.1 = (bf16[48,256]{1,0:T(8,128)(2,1)S(1)}, bf16[48,256]{1,0:T(8,128)(2,1)S(1)}, u32[]{:S(2)}, u32[]{:S(2)}) collective-permute-start(bf16[48,256]{1,0:T(8,128)(2,1)S(1)} %get-tuple-element.45), channel_id=1, source_target_pairs={{0,16},{2,4},{4,2},{6,8},{8,6},{10,12},{12,10},{14,30},{30,14},{28... | collective-permute-start | bytes 73736 | tf_op jit(solution)/shard_map/ppermute | solution.py:541
  7.0 0.0 collective-permute-start
  7.0 0.7 %shard_map.145.refs_5_ = bf16[144,256]{1,0:T(8,128)(2,1)S(1)} custom-call(s32[1]{0:T(128)S(6)} %copy.16.refs_0_, s32[3]{0:T(128)S(1)} %copy-done.8, bf16[768,256]{1,0:T(8,128)(2,1)S(1)} %bitcast.15, bf16[48,256]{1,0:T(8,128)(2,1)S(1)} %get-tuple-element.44.refs_3_), custom_call_target="tpu_custom_call" | custom-call | flops 500000000 | tf_op jit(solution)/shard_map/pallas_call | solution.py:675
  7.7 0.0 copy-start.1
  7.7 0.0 copy-start.2
  7.7 0.0 copy-start.3
  7.7 0.0 copy-start.6
  7.8 0.0 copy-start.7
  7.8 1.7 %collective-permute-start.2 = (bf16[144,256]{1,0:T(8,128)(2,1)S(1)}, bf16[144,256]{1,0:T(8,128)(2,1)S(1)}, u32[]{:S(2)}, u32[]{:S(2)}) collective-permute-start(bf16[144,256]{1,0:T(8,128)(2,1)S(1)} %shard_map.145.refs_5_), channel_id=1, source_target_pairs={{0,16},{2,18},{4,20},{6,22},{8,24},{10,26},{12,28},{14,30},{30,14}... | collective-permute-start | bytes 221192 | tf_op jit(solution)/shard_map/ppermute | solution.py:541
  9.4 0.0 collective-permute-done.1.refs_4_
  9.4 0.7 %shard_map.146 = (f32[2,1216,128]{2,1,0:T(8,128)S(1)}, bf16[48,256]{1,0:T(8,128)(2,1)S(1)}) custom-call(s32[1]{0:T(128)S(6)} %copy.16.refs_0_, s32[3]{0:T(128)S(1)} %copy-done.8, bf16[768,256]{1,0:T(8,128)(2,1)S(1)} %bitcast.16, bf16[48,256]{1,0:T(8,128)(2,1)S(1)} %collective-permute-done.refs_3_, bf16[48,256]{1,0:T(8,128)(2,1)S(1)} %collective-permute-done.1.refs_4_, ...), custom_call_target="tpu_custom_call" | custom-call | flops 1000000000 | tf_op jit(solution)/shard_map/pallas_call | solution.py:675
  10.2 2.3 %collective-permute-start.3 = (bf16[48,256]{1,0:T(8,128)(2,1)S(1)}, bf16[48,256]{1,0:T(8,128)(2,1)S(1)}, u32[]{:S(2)}, u32[]{:S(2)}) collective-permute-start(bf16[48,256]{1,0:T(8,128)(2,1)S(1)} %get-tuple-element.47), channel_id=1, source_target_pairs={{0,16},{2,18},{4,20},{6,22},{8,24},{10,26},{12,28},{14,30},{30,14}... | collective-permute-start | bytes 73736 | tf_op jit(solution)/shard_map/ppermute | solution.py:541
  12.6 0.0 copy-start
  12.6 3.7 %shard_map.147 = (bf16[768,256]{1,0:T(8,128)(2,1)S(1)}, f32[768,256]{1,0:T(8,128)S(1)}, f32[768,128]{1,0:T(8,128)S(1)}, bf16[256,768]{1,0:T(8,128)(2,1)S(1)}, f3...) custom-call(s32[1]{0:T(128)S(6)} %copy.16.refs_0_, s32[3]{0:T(128)S(1)} %copy-done.8, bf16[7,7,256]{2,1,0:T(8,128)(2,1)S(1)} %copy-done.6, ...), custom_call_target="tpu_custom_call" | custom-call | flops 5000000000 | tf_op jit(solution)/shard_map/pallas_call | solution.py:675
  16.3 4.1 %shard_map.148 = (f32[1024,256]{1,0:T(8,128)S(1)}, bf16[1024,256]{1,0:T(8,128)(2,1)S(1)}, bf16[768,1024]{1,0:T(8,128)(2,1)S(1)}, bf16[768,1024]{1,0:T(8,128)(2,1...) custom-call(s32[1]{0:T(128)S(6)} %copy.16.refs_0_, ...), custom_call_target="tpu_custom_call" | custom-call | flops 5000000000 | tf_op jit(solution)/shard_map/pallas_call | solution.py:675
  20.4 0.1 collective-permute-start.4
  20.4 1.1 %shard_map.149 = (bf16[768,256]{1,0:T(8,128)(2,1)S(1)}, f32[768,256]{1,0:T(8,128)S(1)}, f32[8,256]{1,0:T(8,128)S(1)}, f32[8,256]{1,0:T(8,128)S(1)}) custom-call(bf16[256,1024]{1,0:T(8,128)(2,1)S(1)} %copy-done, bf16[1024,256]{1,0:T(8,128)(2,1)S(1)} %copy-done.1, f32[1,256]{1,0:T(1,128)S(1)} %bitcast.13, bf16[768,1024]{1,0:T(8,128)(2,1)S(1)} %get-tuple-element.53.refs_3_, ...), custom_call_target="tpu_custom_call" | custom-call | flops 1300000000 | tf_op jit(solution)/shard_map/pallas_call | solution.py:675
  21.5 0.8 %collective-permute-done.4.refs_1_ = bf16[1024,256]{1,0:T(8,128)(2,1)S(1)} collective-permute-done((bf16[1024,256]{1,0:T(8,128)(2,1)S(1)}, bf16[1024,256]{1,0:T(8,128)(2,1)S(1)}, u32[]{:S(2)}, u32[]{:S(2)}) %collective-permute-start.4) | collective-permute-done | bytes 524320 | tf_op jit(solution)/shard_map/ppermute | solution.py:545
  22.3 0.9 %shard_map.150.refs_3_ = bf16[8,128,256]{2,1,0:T(8,128)(2,1)} custom-call(f32[1024,256]{1,0:T(8,128)S(1)} %get-tuple-element.60.refs_0_, bf16[1024,256]{1,0:T(8,128)(2,1)S(1)} %collective-permute-done.4.refs_1_, f32[8,256]{1,0:T(8,128)S(1)} %get-tuple-element.62.refs_2_.refs_0_), custom_call_target="tpu_custom_call" | custom-call | flops 300000000 | tf_op jit(solution)/shard_map/pallas_call | solution.py:675
  23.2 3.5 %all-to-all-start = ((bf16[8,128,256]{2,1,0:T(8,128)(2,1)}), bf16[8,128,256]{2,1,0:T(8,128)(2,1)S(1)}, u32[]{:S(2)}, u32[]{:S(2)}) async-start(bf16[8,128,256]{2,1,0:T(8,128)(2,1)} %shard_map.150.refs_3_), calls=%async_computation | async-start | bytes 1048576 | tf_op jit(solution)/shard_map/all_to_all | solution.py:781
  26.7 1.7 %shard_map.151.refs_3_.refs_4_.refs_2_ = f32[1216,128]{1,0:T(8,128)S(1)} custom-call(s32[1]{0:T(128)S(6)} %copy.16.refs_0_, bf16[7,7,256]{2,1,0:T(8,128)(2,1)S(1)} %copy-done.6, bf16[768,256]{1,0:T(8,128)(2,1)S(1)} %get-tuple-element.59.refs_2_, bf16[8,128,256]{2,1,0:T(8,128)(2,1)} %shard_map.150.refs_3_), custom_call_target="tpu_custom_call" | custom-call | flops 2000000000 | tf_op jit(solution)/shard_map/pallas_call | solution.py:675
  28.5 1.9 %shard_map.152 = (f32[1216,128]{1,0:T(8,128)S(1)}, bf16[192,256]{1,0:T(8,128)(2,1)S(1)}) custom-call(s32[1]{0:T(128)S(6)} %copy.16.refs_0_, bf16[7,7,256]{2,1,0:T(8,128)(2,1)S(1)} %copy-done.6, bf16[768,256]{1,0:T(8,128)(2,1)S(1)} %get-tuple-element.59.refs_2_, f32[1216,128]{1,0:T(8,128)S(1)} %shard_map.151.refs_3_.refs_4_.refs_2_, ...), custom_call_target="tpu_custom_call" | custom-call | flops 2000000000 | tf_op jit(solution)/shard_map/pallas_call | solution.py:675
  30.4 1.2 %collective-permute-start.5 = (bf16[192,256]{1,0:T(8,128)(2,1)S(1)}, bf16[192,256]{1,0:T(8,128)(2,1)S(1)}, u32[]{:S(2)}, u32[]{:S(2)}) collective-permute-start(bf16[192,256]{1,0:T(8,128)(2,1)S(1)} %get-tuple-element.63), channel_id=1, source_target_pairs={{0,16},{2,18},{4,20},{6,22},{8,24},{10,26},{12,28},{14,30},{30,14}... | collective-permute-start | bytes 294920 | tf_op jit(solution)/shard_map/ppermute | solution.py:541
  31.6 1.8 %shard_map.154.refs_3_ = f32[64,128]{1,0:T(8,128)S(1)} custom-call(f32[2,1216,128]{2,1,0:T(8,128)S(1)} %copy-done.10, f32[2,640,128]{2,1,0:T(8,128)S(1)} %get-tuple-element.66.refs_1_, bf16[768,256]{1,0:T(8,128)(2,1)S(1)} %get-tuple-element.59.refs_2_, f32[1216,128]{1,0:T(8,128)S(1)} %get-tuple-element.64.refs_3_), custom_call_target="tpu_custom_call" | custom-call | flops 1800000000 | tf_op jit(solution)/shard_map/pallas_call | solution.py:675
  33.3 1.8 %shard_map.153.refs_2_ = f32[64,128]{1,0:T(8,128)S(1)} custom-call(f32[2,1216,128]{2,1,0:T(8,128)S(1)} %copy-done.10, f32[2,640,128]{2,1,0:T(8,128)S(1)} %get-tuple-element.66.refs_1_, bf16[768,256]{1,0:T(8,128)(2,1)S(1)} %get-tuple-element.59.refs_2_, f32[1216,128]{1,0:T(8,128)S(1)} %get-tuple-element.64.refs_3_), custom_call_target="tpu_custom_call" | custom-call | flops 1800000000 | tf_op jit(solution)/shard_map/pallas_call | solution.py:675
  35.2 0.1 collective-permute-start.8
  35.2 3.1 %collective-permute-done.5.refs_1_ = bf16[192,256]{1,0:T(8,128)(2,1)S(1)} collective-permute-done((bf16[192,256]{1,0:T(8,128)(2,1)S(1)}, bf16[192,256]{1,0:T(8,128)(2,1)S(1)}, u32[]{:S(2)}, u32[]{:S(2)}) %collective-permute-start.5) | collective-permute-done | bytes 98336 | tf_op jit(solution)/shard_map/ppermute | solution.py:541
  38.4 0.6 shard_map.156
  39.0 0.1 collective-permute-start.6
  39.1 0.4 collective-permute-start.7
  39.4 0.0 collective-permute-done.8.refs_2_
  39.4 0.0 all-to-all-done.refs_0_
  39.5 0.1 shard_map.157.refs_6_.refs_0_
  39.5 0.0 copy-start.5
  39.5 2.7 %collective-permute-start.9 = (bf16[160,256]{1,0:T(8,128)(2,1)S(1)}, bf16[160,256]{1,0:T(8,128)(2,1)S(1)}, u32[]{:S(2)}, u32[]{:S(2)}) collective-permute-start(bf16[160,256]{1,0:T(8,128)(2,1)S(1)} %shard_map.157.refs_6_.refs_0_), channel_id=1, source_target_pairs={{0,16},{1,17},{2,18},{3,19},{4,20},{5,21},{6,22},{7,23},{8,24},{9,... | collective-permute-start | bytes 245768 | tf_op jit(solution)/shard_map/ppermute | solution.py:565
  42.2 0.0 collective-permute-done.6.refs_4_
  42.2 1.7 %collective-permute-done.7.refs_5_ = bf16[48,256]{1,0:T(8,128)(2,1)S(1)} collective-permute-done((bf16[48,256]{1,0:T(8,128)(2,1)S(1)}, bf16[48,256]{1,0:T(8,128)(2,1)S(1)}, u32[]{:S(2)}, u32[]{:S(2)}) %collective-permute-start.7) | collective-permute-done | bytes 24608 | tf_op jit(solution)/shard_map/ppermute | solution.py:541
  43.9 1.6 %shard_map.158 = (bf16[768,256]{1,0:T(8,128)(2,1)}, f32[8,128]{1,0:T(8,128)S(1)}) custom-call(s32[1]{0:T(128)S(6)} %copy.16.refs_0_, s32[3]{0:T(128)S(1)} %copy-done.8, bf16[768,256]{1,0:T(8,128)(2,1)S(1)} %bitcast.10, f32[2,1024,128]{2,1,0:T(8,128)S(1)} %get-tuple-element.68.refs_3_, bf16[48,256]{1,0:T(8,128)(2,1)S(1)} %collective-permute-done.6.refs_4_, ...), custom_call_target="tpu_custom_call" | custom-call | flops 1500000000 | tf_op jit(solution)/shard_map/pallas_call | solution.py:675
  45.5 0.9 %shard_map.159 = (bf16[768,256]{1,0:T(8,128)(2,1)}, f32[8,128]{1,0:T(8,128)S(1)}) custom-call(bf16[768,256]{1,0:T(8,128)(2,1)S(1)} %bitcast.17, f32[1,256]{1,0:T(1,128)S(1)} %bitcast.19, f32[768,256]{1,0:T(8,128)S(1)} %get-tuple-element.58.refs_2_, f32[3,8,256]{2,1,0:T(8,128)S(1)} %get-tuple-element.57.refs_8_.refs_3_, ...), custom_call_target="tpu_custom_call" | custom-call | flops 1000000000 | tf_op jit(solution)/shard_map/pallas_call | solution.py:675
  46.4 0.9 %collective-permute-done.9.refs_1_ = bf16[160,256]{1,0:T(8,128)(2,1)S(1)} collective-permute-done((bf16[160,256]{1,0:T(8,128)(2,1)S(1)}, bf16[160,256]{1,0:T(8,128)(2,1)S(1)}, u32[]{:S(2)}, u32[]{:S(2)}) %collective-permute-start.9) | collective-permute-done | bytes 81952 | tf_op jit(solution)/shard_map/ppermute | solution.py:565
  47.4 14.0 %all_to_all.10.refs_0_ = bf16[8,160,256]{2,1,0:T(8,128)(2,1)S(1)} all-to-all(bf16[8,160,256]{2,1,0:T(8,128)(2,1)S(1)} %shard_map.160), channel_id=1, replica_groups=mesh['far'=2,'near'=4,'core'=2,'dp'=2] {'near','dp'}, dimensions={0} | all-to-all | bytes 1310720 | tf_op jit(solution)/shard_map/all_to_all | solution.py:840
  61.4 0.1 shard_map.161.refs_0_
  61.5 0.1 collective-permute-start.10
  61.5 1.9 %collective-permute-done.10.refs_1_ = bf16[1088,256]{1,0:T(8,128)(2,1)S(1)} collective-permute-done((bf16[1088,256]{1,0:T(8,128)(2,1)S(1)}, bf16[1088,256]{1,0:T(8,128)(2,1)S(1)}, u32[]{:S(2)}, u32[]{:S(2)}) %collective-permute-start.10) | collective-permute-done | bytes 557088 | tf_op jit(solution)/shard_map/ppermute | solution.py:545
  63.5 1.6 %shard_map.162 = (f32[256,1024]{1,0:T(8,128)}, f32[1024,256]{1,0:T(8,128)}, f32[7,7,256]{2,1,0:T(8,128)}, f32[1,256]{1,0:T(1,128)}, f32[1,256]{1,0:T(1,128)}) custom-call(bf16[1088,256]{1,0:T(8,128)(2,1)S(1)} %shard_map.161.refs_0_, bf16[1088,256]{1,0:T(8,128)(2,1)S(1)} %collective-permute-done.10.refs_1_), custom_call_target="tpu_custom_call" | custom-call | flops 1500000000 | tf_op jit(solution)/shard_map/pallas_call | solution.py:675
  (18 shorter events, 0.1 us)
Async XLA Ops:
  1.3 1.0 %copy-start.4 = (bf16[1,3,16,16,256]{4,3,2,1,0:T(8,128)(2,1)S(1)}, bf16[1,3,16,16,256]{4,3,2,1,0:T(8,128)(2,1)}, u32[]{:S(2)}) copy-start(bf16[1,3,16,16,256]{4,3,2,1,0:T(8,128)(2,1)} %param.9) | copy-start | bytes 1179652
  2.3 4.7 %copy-start.8 = (s32[3]{0:T(128)S(1)}, s32[3]{0:T(128)}, u32[]{:S(2)}) copy-start(s32[3]{0:T(128)} %refs_1_.15) | copy-start | bytes 40
  2.9 6.6 %collective-permute-start.1 = (bf16[48,256]{1,0:T(8,128)(2,1)S(1)}, bf16[48,256]{1,0:T(8,128)(2,1)S(1)}, u32[]{:S(2)}, u32[]{:S(2)}) collective-permute-start(bf16[48,256]{1,0:T(8,128)(2,1)S(1)} %get-tuple-element.45), channel_id=1, source_target_pairs={{0,16},{2,4},{4,2},{6,8},{8,6},{10,12},{12,10},{14,30},{30,14},{28... | collective-permute-start | bytes 73736 | tf_op jit(solution)/shard_map/ppermute | solution.py:541
  7.0 2.5 %collective-permute-start = (bf16[48,256]{1,0:T(8,128)(2,1)S(1)}, bf16[48,256]{1,0:T(8,128)(2,1)S(1)}, u32[]{:S(2)}, u32[]{:S(2)}) collective-permute-start(bf16[48,256]{1,0:T(8,128)(2,1)S(1)} %get-tuple-element.44.refs_3_), channel_id=1, source_target_pairs={{0,2},{2,0},{4,6},{6,4},{8,10},{10,8},{12,14},{14,12},{30,28},{28,... | collective-permute-start | bytes 73736 | tf_op jit(solution)/shard_map/ppermute | solution.py:541
  7.7 4.8 %copy-start.1 = (bf16[1024,256]{1,0:T(8,128)(2,1)S(1)}, bf16[1024,256]{1,0:T(8,128)(2,1)}, u32[]{:S(2)}) copy-start(bf16[1024,256]{1,0:T(8,128)(2,1)} %refs_1_.12) | copy-start | bytes 1572868
  7.7 4.8 %copy-start.2 = (bf16[1,3,16,16,256]{4,3,2,1,0:T(8,128)(2,1)S(1)}, bf16[1,3,16,16,256]{4,3,2,1,0:T(8,128)(2,1)}, u32[]{:S(2)}) copy-start(bf16[1,3,16,16,256]{4,3,2,1,0:T(8,128)(2,1)} %param.10) | copy-start | bytes 1179652
  7.7 4.8 %copy-start.3 = (f32[256]{0:T(256)S(1)}, f32[256]{0:T(256)}, u32[]{:S(2)}) copy-start(f32[256]{0:T(256)} %param.14) | copy-start | bytes 3076
  7.7 4.8 %copy-start.6 = (bf16[7,7,256]{2,1,0:T(8,128)(2,1)S(1)}, bf16[7,7,256]{2,1,0:T(8,128)(2,1)}, u32[]{:S(2)}) copy-start(bf16[7,7,256]{2,1,0:T(8,128)(2,1)} %refs_1_.14) | copy-start | bytes 75268
  7.8 4.8 %copy-start.7 = (f32[256]{0:T(256)S(1)}, f32[256]{0:T(256)}, u32[]{:S(2)}) copy-start(f32[256]{0:T(256)} %param.17) | copy-start | bytes 3076
  7.8 8.5 %collective-permute-start.2 = (bf16[144,256]{1,0:T(8,128)(2,1)S(1)}, bf16[144,256]{1,0:T(8,128)(2,1)S(1)}, u32[]{:S(2)}, u32[]{:S(2)}) collective-permute-start(bf16[144,256]{1,0:T(8,128)(2,1)S(1)} %shard_map.145.refs_5_), channel_id=1, source_target_pairs={{0,16},{2,18},{4,20},{6,22},{8,24},{10,26},{12,28},{14,30},{30,14}... | collective-permute-start | bytes 221192 | tf_op jit(solution)/shard_map/ppermute | solution.py:541
  10.2 6.1 %copy-start.9 = (f32[2,1216,128]{2,1,0:T(8,128)}, f32[2,1216,128]{2,1,0:T(8,128)S(1)}, u32[]{:S(2)}) copy-start(f32[2,1216,128]{2,1,0:T(8,128)S(1)} %get-tuple-element.46.refs_7_.refs_4_.refs_0_) | copy-start | bytes 3735556
  10.2 6.0 %collective-permute-start.3 = (bf16[48,256]{1,0:T(8,128)(2,1)S(1)}, bf16[48,256]{1,0:T(8,128)(2,1)S(1)}, u32[]{:S(2)}, u32[]{:S(2)}) collective-permute-start(bf16[48,256]{1,0:T(8,128)(2,1)S(1)} %get-tuple-element.47), channel_id=1, source_target_pairs={{0,16},{2,18},{4,20},{6,22},{8,24},{10,26},{12,28},{14,30},{30,14}... | collective-permute-start | bytes 73736 | tf_op jit(solution)/shard_map/ppermute | solution.py:541
  12.6 3.7 %copy-start = (bf16[256,1024]{1,0:T(8,128)(2,1)S(1)}, bf16[256,1024]{1,0:T(8,128)(2,1)}, u32[]{:S(2)}) copy-start(bf16[256,1024]{1,0:T(8,128)(2,1)} %refs_0_.10) | copy-start | bytes 1572868
  20.4 2.0 %collective-permute-start.4 = (bf16[1024,256]{1,0:T(8,128)(2,1)S(1)}, bf16[1024,256]{1,0:T(8,128)(2,1)S(1)}, u32[]{:S(2)}, u32[]{:S(2)}) collective-permute-start(bf16[1024,256]{1,0:T(8,128)(2,1)S(1)} %get-tuple-element.61), channel_id=1, source_target_pairs={{0,2},{2,0},{1,3},{3,1},{4,6},{6,4},{5,7},{7,5},{8,10},{10,8},{9,1... | collective-permute-start | bytes 1572872 | tf_op jit(solution)/shard_map/ppermute | solution.py:545
  23.2 16.2 %all-to-all-start = ((bf16[8,128,256]{2,1,0:T(8,128)(2,1)}), bf16[8,128,256]{2,1,0:T(8,128)(2,1)S(1)}, u32[]{:S(2)}, u32[]{:S(2)}) async-start(bf16[8,128,256]{2,1,0:T(8,128)(2,1)} %shard_map.150.refs_3_), calls=%async_computation | async-start | bytes 1048576 | tf_op jit(solution)/shard_map/all_to_all | solution.py:781
  28.5 3.1 %copy-start.10 = (f32[2,1216,128]{2,1,0:T(8,128)S(1)}, f32[2,1216,128]{2,1,0:T(8,128)}, u32[]{:S(2)}) copy-start(f32[2,1216,128]{2,1,0:T(8,128)} %copy-done.9) | copy-start | bytes 3735556
  30.4 8.0 %collective-permute-start.5 = (bf16[192,256]{1,0:T(8,128)(2,1)S(1)}, bf16[192,256]{1,0:T(8,128)(2,1)S(1)}, u32[]{:S(2)}, u32[]{:S(2)}) collective-permute-start(bf16[192,256]{1,0:T(8,128)(2,1)S(1)} %get-tuple-element.63), channel_id=1, source_target_pairs={{0,16},{2,18},{4,20},{6,22},{8,24},{10,26},{12,28},{14,30},{30,14}... | collective-permute-start | bytes 294920 | tf_op jit(solution)/shard_map/ppermute | solution.py:541
  35.2 4.3 %collective-permute-start.8 = (bf16[64,256]{1,0:T(8,128)(2,1)S(1)}, bf16[64,256]{1,0:T(8,128)(2,1)S(1)}, u32[]{:S(2)}, u32[]{:S(2)}) collective-permute-start(bf16[64,256]{1,0:T(8,128)(2,1)S(1)} %get-tuple-element.71), channel_id=1, source_target_pairs={{0,2},{2,0},{1,3},{3,1},{4,6},{6,4},{5,7},{7,5},{8,10},{10,8},{9,1... | collective-permute-start | bytes 98312 | tf_op jit(solution)/shard_map/ppermute | solution.py:545
  39.0 3.2 %collective-permute-start.6 = (bf16[48,256]{1,0:T(8,128)(2,1)S(1)}, bf16[48,256]{1,0:T(8,128)(2,1)S(1)}, u32[]{:S(2)}, u32[]{:S(2)}) collective-permute-start(bf16[48,256]{1,0:T(8,128)(2,1)S(1)} %get-tuple-element.69), channel_id=1, source_target_pairs={{0,2},{2,0},{4,6},{6,4},{8,10},{10,8},{12,14},{14,12},{30,28},{28,... | collective-permute-start | bytes 73736 | tf_op jit(solution)/shard_map/ppermute | solution.py:541
  39.1 4.8 %collective-permute-start.7 = (bf16[48,256]{1,0:T(8,128)(2,1)S(1)}, bf16[48,256]{1,0:T(8,128)(2,1)S(1)}, u32[]{:S(2)}, u32[]{:S(2)}) collective-permute-start(bf16[48,256]{1,0:T(8,128)(2,1)S(1)} %get-tuple-element.70), channel_id=1, source_target_pairs={{0,16},{2,4},{4,2},{6,8},{8,6},{10,12},{12,10},{14,30},{30,14},{28... | collective-permute-start | bytes 73736 | tf_op jit(solution)/shard_map/ppermute | solution.py:541
  39.5 6.0 %copy-start.5 = (bf16[1,3,16,16,256]{4,3,2,1,0:T(8,128)(2,1)S(1)}, bf16[1,3,16,16,256]{4,3,2,1,0:T(8,128)(2,1)}, u32[]{:S(2)}) copy-start(bf16[1,3,16,16,256]{4,3,2,1,0:T(8,128)(2,1)} %param.9) | copy-start | bytes 1179652
  39.5 7.8 %collective-permute-start.9 = (bf16[160,256]{1,0:T(8,128)(2,1)S(1)}, bf16[160,256]{1,0:T(8,128)(2,1)S(1)}, u32[]{:S(2)}, u32[]{:S(2)}) collective-permute-start(bf16[160,256]{1,0:T(8,128)(2,1)S(1)} %shard_map.157.refs_6_.refs_0_), channel_id=1, source_target_pairs={{0,16},{1,17},{2,18},{3,19},{4,20},{5,21},{6,22},{7,23},{8,24},{9,... | collective-permute-start | bytes 245768 | tf_op jit(solution)/shard_map/ppermute | solution.py:565
  61.5 2.0 %collective-permute-start.10 = (bf16[1088,256]{1,0:T(8,128)(2,1)S(1)}, bf16[1088,256]{1,0:T(8,128)(2,1)S(1)}, u32[]{:S(2)}, u32[]{:S(2)}) collective-permute-start(bf16[1088,256]{1,0:T(8,128)(2,1)S(1)} %shard_map.161.refs_0_), channel_id=1, source_target_pairs={{0,2},{2,0},{1,3},{3,1},{4,6},{6,4},{5,7},{7,5},{8,10},{10,8},{9,1... | collective-permute-start | bytes 1671176 | tf_op jit(solution)/shard_map/ppermute | solution.py:545

commit v9 on v8

--- a/solution.py
+++ b/solution.py
@@ -779,28 +779,16 @@
         [], [], [keep, came], after=[gain_part], micros=0.3,
     )
     came = lax.all_to_all(send, ("near", "dp"), 0, 0, tiled=True)
-    core_grad = []
-    after = [send]
-    for part in range(parts):
-        one, *fold_back = back_part(part, core_grad, after)
-        core_grad += [one]
-        after = [one]
-    fold_back = swap(fold_back[0], "fold")
-    taps_parts = [taps_part(part, after) for part in range(parts)]
+    taps_parts = [taps_part(part, [send]) for part in range(parts)]
     small_rows //= 2
     small, extra = call(
         pack_kernel, [((small_rows, channels), F32), ((2 * small_rows, channels), BF16)],
         [((2 * small_rows, channels), F32)], [], [gain_part, scale_part, *taps_parts], micros=0.3,
     )
     extra = core_swap(extra)
-    folded, first, second = call(
-        bind(rims_kernel), [strip(TILE), edge, edge], [count_s], [block_count], [fold_back, *core_grad], 1, 1.0,
-        after=[small],
-    )
-    first, second = swap(first, "first"), swap(second, "second")
     if len(order) == inner + 1:
         (payload,) = call(
-            turn_kernel, [((rows + small_rows, channels), BF16)], [], [], [came, small, extra], after=[folded], micros=0.3,
+            turn_kernel, [((rows + small_rows, channels), BF16)], [], [], [came, small, extra], micros=0.3,
         )
     else:
         share = halved(jnp.sum(came.astype(F32), axis=0), order[inner:-1])
@@ -808,18 +796,17 @@
         small = small + (extra[:small_rows].astype(F32) + extra[small_rows:].astype(F32))
         payload = jnp.concatenate([share, small]).astype(BF16)
     came = bit_swap(payload, order[-1])
-    grad_fields, done = call(
-        bind(final_kernel), [whole, ((8, LANES), F32)], [count_s, ocean_s, strip(TILE)],
-        [block_count, ocean], [tangent, folded, first, second], 2, 1.5, after=[payload],
-    )
-    state, done_too = call(
-        bind(state_kernel), [whole, ((8, LANES), F32)], [], [], [fields, scale, projected, live], 0, 1.0, after=[done],
-    )
+    core_grad = []
+    after = [payload]
+    for part in range(parts):
+        one, *fold_back = back_part(part, core_grad, after)
+        core_grad += [one]
+        after = [one]
+    fold_back = swap(fold_back[0], "fold")
     copied = (block, *payload.shape)
     outer = range(inner, len(order) - 1)
     (payload,) = call(
-        add_kernel, [(payload.shape if outer else copied, BF16)], [], [], [payload, came], after=[done, done_too],
-        micros=0.3,
+        add_kernel, [(payload.shape if outer else copied, BF16)], [], [], [payload, came], after=after, micros=0.3,
     )
     for at in reversed(outer):
         came = bit_swap(payload, order[at])
@@ -838,9 +825,22 @@
     if outer:
         payload = jnp.broadcast_to(payload, (block, *payload.shape))
     came = lax.all_to_all(payload, ("near", "dp"), 0, 0, tiled=True)
+    folded, first, second = call(
+        bind(rims_kernel), [strip(TILE), edge, edge], [count_s], [block_count], [fold_back, *core_grad], 1, 1.0,
+        after=[payload],
+    )
+    first, second = swap(first, "first"), swap(second, "second")
+    state, done_too = call(
+        bind(state_kernel), [whole, ((8, LANES), F32)], [], [], [fields, scale, projected, live], 0, 1.0,
+        after=[folded],
+    )
+    grad_fields, done = call(
+        bind(final_kernel), [whole, ((8, LANES), F32)], [count_s, ocean_s, strip(TILE)],
+        [block_count, ocean], [tangent, folded, first, second], 2, 1.5, after=[done_too],
+    )
     (payload,) = call(
         functools.partial(gather_kernel, order[:inner], small_rows),
-        [((hidden + 2 * small_rows, channels), BF16)], [], [], [came], micros=0.3,
+        [((hidden + 2 * small_rows, channels), BF16)], [], [], [came], after=[done], micros=0.3,
     )
     came = core_swap(payload)
     total = samples * lax.axis_size("dp") * slots * lax.axis_size(TILES) * tile_rows * tile_cols

time: 65.4 us -> 67.9 us (1.038)
  blocking collectives: 14 us -> 0 us
  waiting for transfers between devices: 8.49 us -> 17.2 us
  starting transfers between devices: 16.1 us -> 20.5 us
  local copies, waits for them, and re-layouts: 1.05 us -> 3.41 us
  Pallas kernels: 23.9 us -> 24.8 us
    all_to_all x1 -> x0, blocking collectives: 14 us -> none  [shards(): came = lax.all_to_all(payload, ('near', 'dp'), 0, 0, tiled=True)]
    ppermute x7, waiting for transfers between devices: 4.8 us -> 8.4 us  [swap(): return lax.ppermute(block, TILES, pairs_of(kind))]
    all_to_all x0 -> x1, starting transfers between devices: none -> 3.54 us  [shards(): came = lax.all_to_all(payload, ('near', 'dp'), 0, 0, tiled=True)]
    all_to_all x1, waiting for transfers between devices: 0.01 us -> 3.42 us  [shards(): came = lax.all_to_all(send, ('near', 'dp'), 0, 0, tiled=True)]
    unnamed x22 -> x26, local copies, waits for them, and re-layouts: 1.05 us -> 3.41 us
    ppermute x7, starting transfers between devices: 9.72 us -> 12.1 us  [swap(): return lax.ppermute(block, TILES, pairs_of(kind))]
    ppermute x1, starting transfers between devices: 2.67 us -> 1.06 us  [bit_swap(): return lax.ppermute(block, TILES + ('dp',), pairs)]
    ppermute x3, waiting for transfers between devices: 2.74 us -> 3.81 us  [core_swap(): return lax.ppermute(block, 'core', [(0, 1), (1, 0)])]
  transfers between devices with their start and end apart: 12 -> 13, of which waited for: 5 -> 7; matrix products, arithmetic and copies ran while one was open for 0% -> 0% of each run, Pallas kernels for 26% -> 24%
where the time goes in v9:
time: 67.9 us; the launch traced here: 67.5 us
  Pallas kernels  24.8 us (37%)
  starting transfers between devices  20.5 us (30%)
  waiting for transfers between devices  17.2 us (25%)
  local copies, waits for them, and re-layouts  3.41 us (5%)
  between operations  1.59 us (2%)
    pallas_call x19, Pallas kernels, call(): pl.pallas_call(body, out_shape=[jax.ShapeDtypeStruct(*out) for out in out...  24.8 us
    ppermute x7, starting transfers between devices, swap(): return lax.ppermute(block, TILES, pairs_of(kind))  12.1 us
    ppermute x7, waiting for transfers between devices, swap(): return lax.ppermute(block, TILES, pairs_of(kind))  8.4 us
    ppermute x3, waiting for transfers between devices, core_swap(): return lax.ppermute(block, 'core', [(0, 1), (1, 0)])  3.81 us
    all_to_all x1, starting transfers between devices, shards(): came = lax.all_to_all(payload, ('near', 'dp'), 0, 0, tiled=True)  3.54 us
    all_to_all x1, starting transfers between devices, shards(): came = lax.all_to_all(send, ('near', 'dp'), 0, 0, tiled=True)  3.49 us
    all_to_all x1, waiting for transfers between devices, shards(): came = lax.all_to_all(send, ('near', 'dp'), 0, 0, tiled=True)  3.42 us
    unnamed x26, local copies, waits for them, and re-layouts  3.41 us
  transfers between devices with their start and end apart: 13, of which 7 were waited for; matrix products, arithmetic and copies ran while one was open for 0% of the time, Pallas kernels for 24%

profile of v9, /device:TPU:0, one launch (start us, length us, event | category | flops | bytes accessed | tf_op | source)
XLA Modules:
  0.0 67.5 jit_solution(577538912235057392)
XLA Ops:
  1.3 0.0 copy-start.4
  1.3 1.0 %copy-done.4 = bf16[1,3,16,16,256]{4,3,2,1,0:T(8,128)(2,1)S(1)} copy-done((bf16[1,3,16,16,256]{4,3,2,1,0:T(8,128)(2,1)S(1)}, bf16[1,3,16,16,256]{4,3,2,1,0:T(8,128)(2,1)}, u32[]{:S(2)}) %copy-start.4) | copy-done | bytes 393240
  2.3 0.6 shard_map.144
  2.9 4.1 %collective-permute-start.1 = (bf16[48,256]{1,0:T(8,128)(2,1)S(1)}, bf16[48,256]{1,0:T(8,128)(2,1)S(1)}, u32[]{:S(2)}, u32[]{:S(2)}) collective-permute-start(bf16[48,256]{1,0:T(8,128)(2,1)S(1)} %get-tuple-element.45), channel_id=1, source_target_pairs={{0,16},{2,4},{4,2},{6,8},{8,6},{10,12},{12,10},{14,30},{30,14},{28... | collective-permute-start | bytes 73736 | tf_op jit(solution)/shard_map/ppermute | solution.py:541
  7.0 0.7 %shard_map.145.refs_5_ = bf16[144,256]{1,0:T(8,128)(2,1)S(1)} custom-call(s32[1]{0:T(128)S(6)} %copy.16.refs_0_, s32[3]{0:T(128)S(1)} %copy-done.8, bf16[768,256]{1,0:T(8,128)(2,1)S(1)} %bitcast.15, bf16[48,256]{1,0:T(8,128)(2,1)S(1)} %get-tuple-element.44.refs_3_), custom_call_target="tpu_custom_call" | custom-call | flops 500000000 | tf_op jit(solution)/shard_map/pallas_call | solution.py:675
  7.7 0.0 copy-start.1
  7.7 0.0 copy-start.2
  7.7 0.0 copy-start.3
  7.7 0.0 copy-start.6
  7.8 0.0 copy-start.7
  7.8 1.7 %collective-permute-start.2 = (bf16[144,256]{1,0:T(8,128)(2,1)S(1)}, bf16[144,256]{1,0:T(8,128)(2,1)S(1)}, u32[]{:S(2)}, u32[]{:S(2)}) collective-permute-start(bf16[144,256]{1,0:T(8,128)(2,1)S(1)} %shard_map.145.refs_5_), channel_id=1, source_target_pairs={{0,16},{2,18},{4,20},{6,22},{8,24},{10,26},{12,28},{14,30},{30,14}... | collective-permute-start | bytes 221192 | tf_op jit(solution)/shard_map/ppermute | solution.py:541
  9.4 0.7 %shard_map.146 = (f32[2,1216,128]{2,1,0:T(8,128)S(1)}, bf16[48,256]{1,0:T(8,128)(2,1)S(1)}) custom-call(s32[1]{0:T(128)S(6)} %copy.16.refs_0_, s32[3]{0:T(128)S(1)} %copy-done.8, bf16[768,256]{1,0:T(8,128)(2,1)S(1)} %bitcast.16, bf16[48,256]{1,0:T(8,128)(2,1)S(1)} %collective-permute-done.refs_3_, bf16[48,256]{1,0:T(8,128)(2,1)S(1)} %collective-permute-done.1.refs_4_, ...), custom_call_target="tpu_custom_call" | custom-call | flops 1000000000 | tf_op jit(solution)/shard_map/pallas_call | solution.py:675
  10.2 2.3 %collective-permute-start.3 = (bf16[48,256]{1,0:T(8,128)(2,1)S(1)}, bf16[48,256]{1,0:T(8,128)(2,1)S(1)}, u32[]{:S(2)}, u32[]{:S(2)}) collective-permute-start(bf16[48,256]{1,0:T(8,128)(2,1)S(1)} %get-tuple-element.47), channel_id=1, source_target_pairs={{0,16},{2,18},{4,20},{6,22},{8,24},{10,26},{12,28},{14,30},{30,14}... | collective-permute-start | bytes 73736 | tf_op jit(solution)/shard_map/ppermute | solution.py:541
  12.6 0.0 copy-start
  12.6 3.7 %shard_map.147 = (bf16[768,256]{1,0:T(8,128)(2,1)S(1)}, f32[768,256]{1,0:T(8,128)S(1)}, f32[768,128]{1,0:T(8,128)S(1)}, bf16[256,768]{1,0:T(8,128)(2,1)S(1)}, f3...) custom-call(s32[1]{0:T(128)S(6)} %copy.16.refs_0_, s32[3]{0:T(128)S(1)} %copy-done.8, bf16[7,7,256]{2,1,0:T(8,128)(2,1)S(1)} %copy-done.6, ...), custom_call_target="tpu_custom_call" | custom-call | flops 5000000000 | tf_op jit(solution)/shard_map/pallas_call | solution.py:675
  16.3 4.1 %shard_map.148 = (f32[1024,256]{1,0:T(8,128)S(1)}, bf16[1024,256]{1,0:T(8,128)(2,1)S(1)}, bf16[768,1024]{1,0:T(8,128)(2,1)S(1)}, bf16[768,1024]{1,0:T(8,128)(2,1...) custom-call(s32[1]{0:T(128)S(6)} %copy.16.refs_0_, ...), custom_call_target="tpu_custom_call" | custom-call | flops 5000000000 | tf_op jit(solution)/shard_map/pallas_call | solution.py:675
  20.4 0.1 collective-permute-start.4
  20.5 1.1 %shard_map.149 = (bf16[768,256]{1,0:T(8,128)(2,1)S(1)}, f32[768,256]{1,0:T(8,128)S(1)}, f32[8,256]{1,0:T(8,128)S(1)}, f32[8,256]{1,0:T(8,128)S(1)}) custom-call(bf16[256,1024]{1,0:T(8,128)(2,1)S(1)} %copy-done, bf16[1024,256]{1,0:T(8,128)(2,1)S(1)} %copy-done.1, f32[1,256]{1,0:T(1,128)S(1)} %bitcast.13, bf16[768,1024]{1,0:T(8,128)(2,1)S(1)} %get-tuple-element.53.refs_3_, ...), custom_call_target="tpu_custom_call" | custom-call | flops 1300000000 | tf_op jit(solution)/shard_map/pallas_call | solution.py:675
  21.6 0.8 %collective-permute-done.4.refs_1_ = bf16[1024,256]{1,0:T(8,128)(2,1)S(1)} collective-permute-done((bf16[1024,256]{1,0:T(8,128)(2,1)S(1)}, bf16[1024,256]{1,0:T(8,128)(2,1)S(1)}, u32[]{:S(2)}, u32[]{:S(2)}) %collective-permute-start.4) | collective-permute-done | bytes 524320 | tf_op jit(solution)/shard_map/ppermute | solution.py:545
  22.4 0.9 %shard_map.150.refs_3_ = bf16[8,128,256]{2,1,0:T(8,128)(2,1)} custom-call(f32[1024,256]{1,0:T(8,128)S(1)} %get-tuple-element.60.refs_0_, bf16[1024,256]{1,0:T(8,128)(2,1)S(1)} %collective-permute-done.4.refs_1_, f32[8,256]{1,0:T(8,128)S(1)} %get-tuple-element.62.refs_2_.refs_0_), custom_call_target="tpu_custom_call" | custom-call | flops 300000000 | tf_op jit(solution)/shard_map/pallas_call | solution.py:675
  23.3 3.5 %all-to-all-start = ((bf16[8,128,256]{2,1,0:T(8,128)(2,1)}), bf16[8,128,256]{2,1,0:T(8,128)(2,1)S(1)}, u32[]{:S(2)}, u32[]{:S(2)}) async-start(bf16[8,128,256]{2,1,0:T(8,128)(2,1)} %shard_map.150.refs_3_), calls=%async_computation | async-start | bytes 1048576 | tf_op jit(solution)/shard_map/all_to_all | solution.py:781
  26.8 1.3 %copy-done.12 = f32[2,1216,128]{2,1,0:T(8,128)S(1)} copy-done((f32[2,1216,128]{2,1,0:T(8,128)S(1)}, f32[2,1216,128]{2,1,0:T(8,128)}, u32[]{:S(2)}) %copy-start.12) | copy-done | bytes 1245208
  28.1 1.8 %shard_map.152.refs_3_ = f32[64,128]{1,0:T(8,128)S(1)} custom-call(f32[2,1216,128]{2,1,0:T(8,128)S(1)} %copy-done.12, f32[2,640,128]{2,1,0:T(8,128)S(1)} %get-tuple-element.64.refs_1_, bf16[768,256]{1,0:T(8,128)(2,1)S(1)} %get-tuple-element.59.refs_2_, bf16[8,128,256]{2,1,0:T(8,128)(2,1)} %shard_map.150.refs_3_), custom_call_target="tpu_custom_call" | custom-call | flops 1800000000 | tf_op jit(solution)/shard_map/pallas_call | solution.py:675
  29.8 1.8 %shard_map.151.refs_2_ = f32[64,128]{1,0:T(8,128)S(1)} custom-call(f32[2,1216,128]{2,1,0:T(8,128)S(1)} %copy-done.12, f32[2,640,128]{2,1,0:T(8,128)S(1)} %get-tuple-element.64.refs_1_, bf16[768,256]{1,0:T(8,128)(2,1)S(1)} %get-tuple-element.59.refs_2_, bf16[8,128,256]{2,1,0:T(8,128)(2,1)} %shard_map.150.refs_3_), custom_call_target="tpu_custom_call" | custom-call | flops 1800000000 | tf_op jit(solution)/shard_map/pallas_call | solution.py:675
  31.7 0.2 collective-permute-start.5
  31.9 1.1 %collective-permute-done.5.refs_2_ = bf16[64,256]{1,0:T(8,128)(2,1)S(1)} collective-permute-done((bf16[64,256]{1,0:T(8,128)(2,1)S(1)}, bf16[64,256]{1,0:T(8,128)(2,1)S(1)}, u32[]{:S(2)}, u32[]{:S(2)}) %collective-permute-start.5) | collective-permute-done | bytes 32800 | tf_op jit(solution)/shard_map/ppermute | solution.py:545
  32.9 3.4 %all-to-all-done.refs_0_ = bf16[8,128,256]{2,1,0:T(8,128)(2,1)S(1)} async-done(((bf16[8,128,256]{2,1,0:T(8,128)(2,1)}), bf16[8,128,256]{2,1,0:T(8,128)(2,1)S(1)}, u32[]{:S(2)}, u32[]{:S(2)}) %all-to-all-start) | async-done | bytes 524320 | tf_op jit(solution)/shard_map/all_to_all | solution.py:781
  36.4 0.1 shard_map.154.refs_3_.refs_0_
  36.4 1.1 %collective-permute-start.7 = (bf16[160,256]{1,0:T(8,128)(2,1)S(1)}, bf16[160,256]{1,0:T(8,128)(2,1)S(1)}, u32[]{:S(2)}, u32[]{:S(2)}) collective-permute-start(bf16[160,256]{1,0:T(8,128)(2,1)S(1)} %shard_map.154.refs_3_.refs_0_), channel_id=1, source_target_pairs={{0,16},{1,17},{2,18},{3,19},{4,20},{5,21},{6,22},{7,23},{8,24},{9,... | collective-permute-start | bytes 245768 | tf_op jit(solution)/shard_map/ppermute | solution.py:565
  37.5 1.7 %shard_map.155.refs_3_.refs_4_.refs_2_ = f32[1216,128]{1,0:T(8,128)S(1)} custom-call(s32[1]{0:T(128)S(6)} %copy.16.refs_0_, bf16[7,7,256]{2,1,0:T(8,128)(2,1)S(1)} %copy-done.6, bf16[768,256]{1,0:T(8,128)(2,1)S(1)} %get-tuple-element.59.refs_2_, bf16[160,256]{1,0:T(8,128)(2,1)S(1)} %shard_map.154.refs_3_.refs_0_), custom_call_target="tpu_custom_call" | custom-call | flops 2000000000 | tf_op jit(solution)/shard_map/pallas_call | solution.py:675
  39.2 0.0 copy-start.9
  39.2 1.9 %shard_map.156 = (f32[1216,128]{1,0:T(8,128)S(1)}, bf16[192,256]{1,0:T(8,128)(2,1)S(1)}) custom-call(s32[1]{0:T(128)S(6)} %copy.16.refs_0_, bf16[7,7,256]{2,1,0:T(8,128)(2,1)S(1)} %copy-done.6, bf16[768,256]{1,0:T(8,128)(2,1)S(1)} %get-tuple-element.59.refs_2_, f32[1216,128]{1,0:T(8,128)S(1)} %shard_map.155.refs_3_.refs_4_.refs_2_, ...), custom_call_target="tpu_custom_call" | custom-call | flops 2000000000 | tf_op jit(solution)/shard_map/pallas_call | solution.py:675
  41.2 1.6 %collective-permute-done.7.refs_1_ = bf16[160,256]{1,0:T(8,128)(2,1)S(1)} collective-permute-done((bf16[160,256]{1,0:T(8,128)(2,1)S(1)}, bf16[160,256]{1,0:T(8,128)(2,1)S(1)}, u32[]{:S(2)}, u32[]{:S(2)}) %collective-permute-start.7) | collective-permute-done | bytes 81952 | tf_op jit(solution)/shard_map/ppermute | solution.py:565
  42.7 0.9 %shard_map.157.refs_4_ = bf16[8,160,256]{2,1,0:T(8,128)(2,1)} custom-call(bf16[160,256]{1,0:T(8,128)(2,1)S(1)} %shard_map.154.refs_3_.refs_0_, bf16[160,256]{1,0:T(8,128)(2,1)S(1)} %collective-permute-done.7.refs_1_, f32[1216,128]{1,0:T(8,128)S(1)} %get-tuple-element.68.refs_2_.refs_3_), custom_call_target="tpu_custom_call" | custom-call | flops 300000000 | tf_op jit(solution)/shard_map/pallas_call | solution.py:675
  43.6 3.5 %all-to-all-start.1 = ((bf16[8,160,256]{2,1,0:T(8,128)(2,1)}), bf16[8,160,256]{2,1,0:T(8,128)(2,1)S(1)}, u32[]{:S(2)}, u32[]{:S(2)}) async-start(bf16[8,160,256]{2,1,0:T(8,128)(2,1)} %shard_map.157.refs_4_), calls=%async_computation.1 | async-start | bytes 1310720 | tf_op jit(solution)/shard_map/all_to_all | solution.py:827
  47.2 0.5 collective-permute-start.6
  47.6 7.4 %collective-permute-done.6.refs_1_ = bf16[192,256]{1,0:T(8,128)(2,1)S(1)} collective-permute-done((bf16[192,256]{1,0:T(8,128)(2,1)S(1)}, bf16[192,256]{1,0:T(8,128)(2,1)S(1)}, u32[]{:S(2)}, u32[]{:S(2)}) %collective-permute-start.6) | collective-permute-done | bytes 98336 | tf_op jit(solution)/shard_map/ppermute | solution.py:541
  55.0 1.1 %copy-done.10 = f32[1216,128]{1,0:T(8,128)S(1)} copy-done((f32[1216,128]{1,0:T(8,128)S(1)}, f32[1216,128]{1,0:T(8,128)}, u32[]{:S(2)}) %copy-start.10) | copy-done | bytes 622616
  56.1 0.6 shard_map.158
  56.7 0.1 collective-permute-start.8
  56.8 3.4 %collective-permute-start.9 = (bf16[48,256]{1,0:T(8,128)(2,1)S(1)}, bf16[48,256]{1,0:T(8,128)(2,1)S(1)}, u32[]{:S(2)}, u32[]{:S(2)}) collective-permute-start(bf16[48,256]{1,0:T(8,128)(2,1)S(1)} %get-tuple-element.72), channel_id=1, source_target_pairs={{0,16},{2,4},{4,2},{6,8},{8,6},{10,12},{12,10},{14,30},{30,14},{28... | collective-permute-start | bytes 73736 | tf_op jit(solution)/shard_map/ppermute | solution.py:541
  60.2 0.9 %shard_map.159 = (bf16[768,256]{1,0:T(8,128)(2,1)}, f32[8,128]{1,0:T(8,128)S(1)}) custom-call(bf16[768,256]{1,0:T(8,128)(2,1)S(1)} %bitcast.17, f32[1,256]{1,0:T(1,128)S(1)} %bitcast.19, f32[768,256]{1,0:T(8,128)S(1)} %get-tuple-element.58.refs_2_, f32[3,8,256]{2,1,0:T(8,128)S(1)} %get-tuple-element.57.refs_8_.refs_3_, ...), custom_call_target="tpu_custom_call" | custom-call | flops 1000000000 | tf_op jit(solution)/shard_map/pallas_call | solution.py:675
  61.1 1.0 %collective-permute-done.9.refs_5_ = bf16[48,256]{1,0:T(8,128)(2,1)S(1)} collective-permute-done((bf16[48,256]{1,0:T(8,128)(2,1)S(1)}, bf16[48,256]{1,0:T(8,128)(2,1)S(1)}, u32[]{:S(2)}, u32[]{:S(2)}) %collective-permute-start.9) | collective-permute-done | bytes 24608 | tf_op jit(solution)/shard_map/ppermute | solution.py:541
  62.1 1.6 %shard_map.160 = (bf16[768,256]{1,0:T(8,128)(2,1)}, f32[8,128]{1,0:T(8,128)S(1)}) custom-call(s32[1]{0:T(128)S(6)} %copy.16.refs_0_, s32[3]{0:T(128)S(1)} %copy-done.8, bf16[768,256]{1,0:T(8,128)(2,1)S(1)} %bitcast.10, f32[2,1024,128]{2,1,0:T(8,128)S(1)} %get-tuple-element.69.refs_4_.refs_3_, bf16[48,256]{1,0:T(8,128)(2,1)S(1)} %collective-permute-done.8.refs_4_, ...), custom_call_target="tpu_custom_call" | custom-call | flops 1500000000 | tf_op jit(solution)/shard_map/pallas_call | solution.py:675
  63.8 0.1 shard_map.161.refs_0_
  63.8 0.1 collective-permute-start.10
  63.9 1.9 %collective-permute-done.10.refs_1_ = bf16[1088,256]{1,0:T(8,128)(2,1)S(1)} collective-permute-done((bf16[1088,256]{1,0:T(8,128)(2,1)S(1)}, bf16[1088,256]{1,0:T(8,128)(2,1)S(1)}, u32[]{:S(2)}, u32[]{:S(2)}) %collective-permute-start.10) | collective-permute-done | bytes 557088 | tf_op jit(solution)/shard_map/ppermute | solution.py:545
  65.8 1.6 %shard_map.162 = (f32[256,1024]{1,0:T(8,128)}, f32[1024,256]{1,0:T(8,128)}, f32[7,7,256]{2,1,0:T(8,128)}, f32[1,256]{1,0:T(1,128)}, f32[1,256]{1,0:T(1,128)}) custom-call(bf16[1088,256]{1,0:T(8,128)(2,1)S(1)} %shard_map.161.refs_0_, bf16[1088,256]{1,0:T(8,128)(2,1)S(1)} %collective-permute-done.10.refs_1_), custom_call_target="tpu_custom_call" | custom-call | flops 1500000000 | tf_op jit(solution)/shard_map/pallas_call | solution.py:675
  (23 shorter events, 0.1 us)
Async XLA Ops:
  1.3 1.0 %copy-start.4 = (bf16[1,3,16,16,256]{4,3,2,1,0:T(8,128)(2,1)S(1)}, bf16[1,3,16,16,256]{4,3,2,1,0:T(8,128)(2,1)}, u32[]{:S(2)}) copy-start(bf16[1,3,16,16,256]{4,3,2,1,0:T(8,128)(2,1)} %param.9) | copy-start | bytes 1179652
  2.3 4.7 %copy-start.8 = (s32[3]{0:T(128)S(1)}, s32[3]{0:T(128)}, u32[]{:S(2)}) copy-start(s32[3]{0:T(128)} %refs_1_.15) | copy-start | bytes 40
  2.9 6.6 %collective-permute-start.1 = (bf16[48,256]{1,0:T(8,128)(2,1)S(1)}, bf16[48,256]{1,0:T(8,128)(2,1)S(1)}, u32[]{:S(2)}, u32[]{:S(2)}) collective-permute-start(bf16[48,256]{1,0:T(8,128)(2,1)S(1)} %get-tuple-element.45), channel_id=1, source_target_pairs={{0,16},{2,4},{4,2},{6,8},{8,6},{10,12},{12,10},{14,30},{30,14},{28... | collective-permute-start | bytes 73736 | tf_op jit(solution)/shard_map/ppermute | solution.py:541
  7.0 2.5 %collective-permute-start = (bf16[48,256]{1,0:T(8,128)(2,1)S(1)}, bf16[48,256]{1,0:T(8,128)(2,1)S(1)}, u32[]{:S(2)}, u32[]{:S(2)}) collective-permute-start(bf16[48,256]{1,0:T(8,128)(2,1)S(1)} %get-tuple-element.44.refs_3_), channel_id=1, source_target_pairs={{0,2},{2,0},{4,6},{6,4},{8,10},{10,8},{12,14},{14,12},{30,28},{28,... | collective-permute-start | bytes 73736 | tf_op jit(solution)/shard_map/ppermute | solution.py:541
  7.7 4.8 %copy-start.1 = (bf16[1024,256]{1,0:T(8,128)(2,1)S(1)}, bf16[1024,256]{1,0:T(8,128)(2,1)}, u32[]{:S(2)}) copy-start(bf16[1024,256]{1,0:T(8,128)(2,1)} %refs_1_.12) | copy-start | bytes 1572868
  7.7 4.8 %copy-start.2 = (bf16[1,3,16,16,256]{4,3,2,1,0:T(8,128)(2,1)S(1)}, bf16[1,3,16,16,256]{4,3,2,1,0:T(8,128)(2,1)}, u32[]{:S(2)}) copy-start(bf16[1,3,16,16,256]{4,3,2,1,0:T(8,128)(2,1)} %param.10) | copy-start | bytes 1179652
  7.7 4.8 %copy-start.3 = (f32[256]{0:T(256)S(1)}, f32[256]{0:T(256)}, u32[]{:S(2)}) copy-start(f32[256]{0:T(256)} %param.14) | copy-start | bytes 3076
  7.7 4.8 %copy-start.6 = (bf16[7,7,256]{2,1,0:T(8,128)(2,1)S(1)}, bf16[7,7,256]{2,1,0:T(8,128)(2,1)}, u32[]{:S(2)}) copy-start(bf16[7,7,256]{2,1,0:T(8,128)(2,1)} %refs_1_.14) | copy-start | bytes 75268
  7.8 4.8 %copy-start.7 = (f32[256]{0:T(256)S(1)}, f32[256]{0:T(256)}, u32[]{:S(2)}) copy-start(f32[256]{0:T(256)} %param.17) | copy-start | bytes 3076
  7.8 8.5 %collective-permute-start.2 = (bf16[144,256]{1,0:T(8,128)(2,1)S(1)}, bf16[144,256]{1,0:T(8,128)(2,1)S(1)}, u32[]{:S(2)}, u32[]{:S(2)}) collective-permute-start(bf16[144,256]{1,0:T(8,128)(2,1)S(1)} %shard_map.145.refs_5_), channel_id=1, source_target_pairs={{0,16},{2,18},{4,20},{6,22},{8,24},{10,26},{12,28},{14,30},{30,14}... | collective-permute-start | bytes 221192 | tf_op jit(solution)/shard_map/ppermute | solution.py:541
  10.2 6.1 %copy-start.11 = (f32[2,1216,128]{2,1,0:T(8,128)}, f32[2,1216,128]{2,1,0:T(8,128)S(1)}, u32[]{:S(2)}) copy-start(f32[2,1216,128]{2,1,0:T(8,128)S(1)} %get-tuple-element.46.refs_7_.refs_4_.refs_0_) | copy-start | bytes 3735556
  10.2 6.0 %collective-permute-start.3 = (bf16[48,256]{1,0:T(8,128)(2,1)S(1)}, bf16[48,256]{1,0:T(8,128)(2,1)S(1)}, u32[]{:S(2)}, u32[]{:S(2)}) collective-permute-start(bf16[48,256]{1,0:T(8,128)(2,1)S(1)} %get-tuple-element.47), channel_id=1, source_target_pairs={{0,16},{2,18},{4,20},{6,22},{8,24},{10,26},{12,28},{14,30},{30,14}... | collective-permute-start | bytes 73736 | tf_op jit(solution)/shard_map/ppermute | solution.py:541
  12.6 3.7 %copy-start = (bf16[256,1024]{1,0:T(8,128)(2,1)S(1)}, bf16[256,1024]{1,0:T(8,128)(2,1)}, u32[]{:S(2)}) copy-start(bf16[256,1024]{1,0:T(8,128)(2,1)} %refs_0_.10) | copy-start | bytes 1572868
  20.4 2.0 %collective-permute-start.4 = (bf16[1024,256]{1,0:T(8,128)(2,1)S(1)}, bf16[1024,256]{1,0:T(8,128)(2,1)S(1)}, u32[]{:S(2)}, u32[]{:S(2)}) collective-permute-start(bf16[1024,256]{1,0:T(8,128)(2,1)S(1)} %get-tuple-element.61), channel_id=1, source_target_pairs={{0,2},{2,0},{1,3},{3,1},{4,6},{6,4},{5,7},{7,5},{8,10},{10,8},{9,1... | collective-permute-start | bytes 1572872 | tf_op jit(solution)/shard_map/ppermute | solution.py:545
  23.3 13.1 %all-to-all-start = ((bf16[8,128,256]{2,1,0:T(8,128)(2,1)}), bf16[8,128,256]{2,1,0:T(8,128)(2,1)S(1)}, u32[]{:S(2)}, u32[]{:S(2)}) async-start(bf16[8,128,256]{2,1,0:T(8,128)(2,1)} %shard_map.150.refs_3_), calls=%async_computation | async-start | bytes 1048576 | tf_op jit(solution)/shard_map/all_to_all | solution.py:781
  26.8 1.3 %copy-start.12 = (f32[2,1216,128]{2,1,0:T(8,128)S(1)}, f32[2,1216,128]{2,1,0:T(8,128)}, u32[]{:S(2)}) copy-start(f32[2,1216,128]{2,1,0:T(8,128)} %copy-done.11) | copy-start | bytes 3735556
  31.7 1.3 %collective-permute-start.5 = (bf16[64,256]{1,0:T(8,128)(2,1)S(1)}, bf16[64,256]{1,0:T(8,128)(2,1)S(1)}, u32[]{:S(2)}, u32[]{:S(2)}) collective-permute-start(bf16[64,256]{1,0:T(8,128)(2,1)S(1)} %get-tuple-element.66), channel_id=1, source_target_pairs={{0,2},{2,0},{1,3},{3,1},{4,6},{6,4},{5,7},{7,5},{8,10},{10,8},{9,1... | collective-permute-start | bytes 98312 | tf_op jit(solution)/shard_map/ppermute | solution.py:545
  36.4 6.3 %collective-permute-start.7 = (bf16[160,256]{1,0:T(8,128)(2,1)S(1)}, bf16[160,256]{1,0:T(8,128)(2,1)S(1)}, u32[]{:S(2)}, u32[]{:S(2)}) collective-permute-start(bf16[160,256]{1,0:T(8,128)(2,1)S(1)} %shard_map.154.refs_3_.refs_0_), channel_id=1, source_target_pairs={{0,16},{1,17},{2,18},{3,19},{4,20},{5,21},{6,22},{7,23},{8,24},{9,... | collective-permute-start | bytes 245768 | tf_op jit(solution)/shard_map/ppermute | solution.py:565
  39.2 1.9 %copy-start.9 = (f32[1216,128]{1,0:T(8,128)}, f32[1216,128]{1,0:T(8,128)S(1)}, u32[]{:S(2)}) copy-start(f32[1216,128]{1,0:T(8,128)S(1)} %shard_map.155.refs_3_.refs_4_.refs_2_) | copy-start | bytes 1867780
  43.6 20.1 %all-to-all-start.1 = ((bf16[8,160,256]{2,1,0:T(8,128)(2,1)}), bf16[8,160,256]{2,1,0:T(8,128)(2,1)S(1)}, u32[]{:S(2)}, u32[]{:S(2)}) async-start(bf16[8,160,256]{2,1,0:T(8,128)(2,1)} %shard_map.157.refs_4_), calls=%async_computation.1 | async-start | bytes 1310720 | tf_op jit(solution)/shard_map/all_to_all | solution.py:827
  47.2 13.1 %copy-start.5 = (bf16[1,3,16,16,256]{4,3,2,1,0:T(8,128)(2,1)S(1)}, bf16[1,3,16,16,256]{4,3,2,1,0:T(8,128)(2,1)}, u32[]{:S(2)}) copy-start(bf16[1,3,16,16,256]{4,3,2,1,0:T(8,128)(2,1)} %param.9) | copy-start | bytes 1179652
  47.2 7.8 %collective-permute-start.6 = (bf16[192,256]{1,0:T(8,128)(2,1)S(1)}, bf16[192,256]{1,0:T(8,128)(2,1)S(1)}, u32[]{:S(2)}, u32[]{:S(2)}) collective-permute-start(bf16[192,256]{1,0:T(8,128)(2,1)S(1)} %get-tuple-element.67), channel_id=1, source_target_pairs={{0,16},{2,18},{4,20},{6,22},{8,24},{10,26},{12,28},{14,30},{30,14}... | collective-permute-start | bytes 294920 | tf_op jit(solution)/shard_map/ppermute | solution.py:541
  55.0 1.1 %copy-start.10 = (f32[1216,128]{1,0:T(8,128)S(1)}, f32[1216,128]{1,0:T(8,128)}, u32[]{:S(2)}) copy-start(f32[1216,128]{1,0:T(8,128)} %copy-done.9) | copy-start | bytes 1867780
  56.7 4.4 %collective-permute-start.8 = (bf16[48,256]{1,0:T(8,128)(2,1)S(1)}, bf16[48,256]{1,0:T(8,128)(2,1)S(1)}, u32[]{:S(2)}, u32[]{:S(2)}) collective-permute-start(bf16[48,256]{1,0:T(8,128)(2,1)S(1)} %get-tuple-element.71), channel_id=1, source_target_pairs={{0,2},{2,0},{4,6},{6,4},{8,10},{10,8},{12,14},{14,12},{30,28},{28,... | collective-permute-start | bytes 73736 | tf_op jit(solution)/shard_map/ppermute | solution.py:541
  56.8 5.4 %collective-permute-start.9 = (bf16[48,256]{1,0:T(8,128)(2,1)S(1)}, bf16[48,256]{1,0:T(8,128)(2,1)S(1)}, u32[]{:S(2)}, u32[]{:S(2)}) collective-permute-start(bf16[48,256]{1,0:T(8,128)(2,1)S(1)} %get-tuple-element.72), channel_id=1, source_target_pairs={{0,16},{2,4},{4,2},{6,8},{8,6},{10,12},{12,10},{14,30},{30,14},{28... | collective-permute-start | bytes 73736 | tf_op jit(solution)/shard_map/ppermute | solution.py:541
  63.8 2.0 %collective-permute-start.10 = (bf16[1088,256]{1,0:T(8,128)(2,1)S(1)}, bf16[1088,256]{1,0:T(8,128)(2,1)S(1)}, u32[]{:S(2)}, u32[]{:S(2)}) collective-permute-start(bf16[1088,256]{1,0:T(8,128)(2,1)S(1)} %shard_map.161.refs_0_), channel_id=1, source_target_pairs={{0,2},{2,0},{1,3},{3,1},{4,6},{6,4},{5,7},{7,5},{8,10},{10,8},{9,1... | collective-permute-start | bytes 1671176 | tf_op jit(solution)/shard_map/ppermute | solution.py:545

commit v10 on v7

--- a/solution.py
+++ b/solution.py
@@ -54,11 +54,6 @@
             self.copies[at].wait()
 
 
-def slot_flag(count_ref, ocean_ref, slot):
-    live = jnp.logical_and(slot < count_ref[0], ocean_ref[slot] > 0)
-    return jnp.where(live, 1.0, 0.0).astype(F32)
-
-
 class Shape:
     def __init__(self, slots, channels, hidden):
         self.slots = slots
@@ -98,7 +93,11 @@
     return jnp.where(to + frm == last, 1.0, 0.0).astype(BF16)
 
 
-def prep_kernel(shape, count_hbm, fields, first, second, count, work, sems):
+def owned_of(info):
+    return jnp.max(info[...]).astype(jnp.int32)
+
+
+def prep_kernel(shape, count_hbm, fields, first, second, info, count, work, sems):
     fetch = Fetch(sems, (count_hbm, count))
     for part in range(shape.parts):
         work[part] = fields[:, shape.lanes(part)].astype(F32)
@@ -106,17 +105,22 @@
     fetch.wait(0)
     right = edge_planes(shape, work, (count[0] - 1) * TILE * TILE + TILE - HALF, TILE)
     send_edges(shape, left, right, first, second)
-
-
-def top_kernel(shape, count_hbm, ocean_hbm, fields, fold, count, ocean, sems):
-    fetch = Fetch(sems, (count_hbm, count), (ocean_hbm, ocean))
-    fetch.wait(0, 1)
-    flip = flip_matrix(shape.columns, count[0] * TILE - 1)
+    info[...] = jnp.full(info.shape, count[0].astype(F32), F32)
+
+
+def top_kernel(shape, info, ocean, fields, fold, live):
+    column = lax.broadcasted_iota(jnp.int32, ocean.shape, 1)
+    wet = jnp.where(ocean[...] > 0, 1.0, 0.0).astype(F32)
+    for slot in range(shape.slots):
+        one = jnp.sum(jnp.where(column == slot, wet, 0.0), axis=1, keepdims=True)
+        one = jnp.where(info[0:1, 0:1] > slot + 0.5, one, 0.0)
+        live[slot] = jnp.broadcast_to(one, live.shape[1:])
+    flip = flip_matrix(shape.columns, owned_of(info) * TILE - 1)
     for k in range(HALF):
         cells = jnp.concatenate(
             [
                 fields[pl.ds(slot * TILE * TILE + (TILE - 1 - k) * TILE, TILE), :].astype(F32)
-                * slot_flag(count, ocean, slot)
+                * live[slot, 0:1, :]
                 for slot in range(shape.slots)
             ]
         )
@@ -124,8 +128,8 @@
         fold[pl.ds(k * shape.columns, shape.columns), :] = turned.astype(BF16)
 
 
-def band_kernel(shape, count_hbm, ocean_hbm, fields, first, second, band, rims, count, ocean, sems):
-    fetch = Fetch(sems, (count_hbm, count), (ocean_hbm, ocean))
+def band_kernel(shape, info, live, fields, first, second, band, rims):
+    used = owned_of(info) * TILE
     even = is_even()
     blank = jnp.zeros((LEFT, LANES), F32)
     per_slot = TILE * TILE
@@ -135,16 +139,13 @@
             base = (row + HALF) * shape.pitch
             band[part, pl.ds(base, LEFT), :] = blank
             band[part, pl.ds(base + LEFT + shape.columns, LEFT), :] = blank
-    fetch.wait(0, 1)
-    used = count[0] * TILE
-    flags = [slot_flag(count, ocean, slot) for slot in range(shape.slots)]
     top = HALF * shape.pitch
     for part in range(shape.parts):
         for row in range(TILE):
             base = (row + HALF) * shape.pitch
             for slot in range(shape.slots):
                 cells = fields[pl.ds(slot * per_slot + row * TILE, TILE), shape.lanes(part)]
-                band[part, pl.ds(base + LEFT + slot * TILE, TILE), :] = cells.astype(F32) * flags[slot]
+                band[part, pl.ds(base + LEFT + slot * TILE, TILE), :] = cells.astype(F32) * live[slot, 0:1, shape.lanes(part)]
         for col in range(HALF):
             rows = pl.ds(col * TILE, TILE)
             one = first[rows, shape.lanes(part)].astype(F32)
@@ -243,21 +244,17 @@
 
 
 def early_kernel(
-    shape, count_hbm, ocean_hbm, kernel, gain, w_out, scale, tangent, band,
-    normed, yhat, inverse, dproj_t, dact, live,
-    count, ocean, taps, convolved, dproj, sems,
+    shape, live, kernel, gain, w_out, scale, tangent, band,
+    normed, yhat, inverse, dproj_t, dact,
+    taps, convolved, dproj,
 ):
-    fetch = Fetch(sems, (count_hbm, count), (ocean_hbm, ocean))
     spread_taps(shape, kernel, range(shape.parts), taps)
     convolve(shape, shape.early, band, taps, convolved)
     normalise(shape, shape.early, 0, convolved, gain, normed, yhat, inverse)
-    fetch.wait(0, 1)
     per_slot = TILE * TILE
     for slot in range(shape.slots):
         rows = pl.ds(slot * per_slot, per_slot)
-        flag = slot_flag(count, ocean, slot)
-        live[slot] = jnp.full((8, shape.channels), flag, F32)
-        scaled = (tangent[rows, :].astype(F32) * (scale[...] * flag)).astype(BF16)
+        scaled = (tangent[rows, :].astype(F32) * (scale[...] * live[slot, 0:1, :])).astype(BF16)
         dproj[rows, :] = scaled
         dproj_t[:, slot * per_slot : (slot + 1) * per_slot] = scaled.T
         for h in range(shape.hidden // shape.channels):
@@ -266,11 +263,10 @@
 
 
 def late_kernel(
-    shape, count_hbm, kernel, gain, w_in, band, fold, rims, normed_in, yhat_in, inverse_in, dproj_t, dact,
+    shape, info, kernel, gain, w_in, band, fold, rims, normed_in, yhat_in, inverse_in, dproj_t, dact,
     keep, give, activated, dpreact, yhat, inverse, padded,
-    count, taps, convolved, normed, normed_t, work, pre, sems,
+    taps, convolved, normed, normed_t, work, pre,
 ):
-    fetch = Fetch(sems, (count_hbm, count))
     late = TILE - shape.early
     kept = late + HALF
     for part in range(shape.parts):
@@ -283,8 +279,7 @@
         yhat[rows, :] = yhat_in[rows, :]
         inverse[rows, :] = inverse_in[rows, :]
     spread_taps(shape, kernel, range(shape.parts), taps)
-    fetch.wait(0)
-    put_fold(shape, count[0] * TILE, fold, rims, range(shape.parts), padded, kept, work)
+    put_fold(shape, owned_of(info) * TILE, fold, rims, range(shape.parts), padded, kept, work)
     convolve(shape, late, padded, taps, convolved)
     normalise(shape, late, shape.early, convolved, gain, normed, yhat, inverse)
     per_slot = TILE * TILE
@@ -405,14 +400,13 @@
             small[pl.ds(above * KSIZE + shift, 1), :] = jnp.sum(sums[shift], axis=0, keepdims=True)
 
 
-def back_kernel(shape, part, count_hbm, kernel, conv_grad, *refs):
+def back_kernel(shape, part, info, kernel, conv_grad, *refs):
     before = refs[:part]
     turns = part == shape.parts - 1
     core_grad, *refs = refs[part:]
     if turns:
         fold, *refs = refs
-    count, spaced, taps, sems = refs
-    fetch = Fetch(sems, (count_hbm, count))
+    spaced, taps = refs
     place_grad(shape, conv_grad, [part], spaced)
     blank = jnp.zeros((LEFT, LANES), F32)
     for row in range(TILE + HALF):
@@ -448,9 +442,8 @@
         return carry
 
     lax.fori_loop(inner[0], inner[1] + 1, inner_row, 0)
-    fetch.wait(0)
     if turns:
-        flip = flip_matrix(shape.pitch, count[0] * TILE + 2 * LEFT - 1)
+        flip = flip_matrix(shape.pitch, owned_of(info) * TILE + 2 * LEFT - 1)
         for k in range(HALF):
             at = pl.ds((TILE + k) * shape.pitch, shape.pitch)
             cells = jnp.concatenate([one[at, :] for one in (*before, core_grad)], axis=1)
@@ -458,33 +451,30 @@
             fold[pl.ds(k * shape.pitch, shape.pitch), :] = turned.astype(BF16)
 
 
-def rims_kernel(shape, count_hbm, fold, *refs):
+def rims_kernel(shape, info, fold, *refs):
     core_grad = refs[: shape.parts]
-    folded, first, second, count, sems = refs[shape.parts :]
-    fetch = Fetch(sems, (count_hbm, count))
+    folded, first, second = refs[shape.parts :]
+    used = owned_of(info) * TILE
     for part in range(shape.parts):
         folded[part] = core_grad[part][pl.ds(0, TILE * shape.pitch), :]
         for k in range(HALF):
             rows = pl.ds((TILE - 1 - k) * shape.pitch, shape.pitch)
             returned = fold[pl.ds(k * shape.pitch, shape.pitch), shape.lanes(part)]
             folded[part, rows, :] += returned.astype(F32)
-    fetch.wait(0)
     west = edge_planes(shape, folded, LEFT - HALF, shape.pitch)
-    east = edge_planes(shape, folded, LEFT + count[0] * TILE, shape.pitch)
+    east = edge_planes(shape, folded, LEFT + used, shape.pitch)
     send_edges(shape, west, east, first, second)
 
 
 def final_kernel(
-    shape, count_hbm, ocean_hbm, tangent, folded, first, second,
+    shape, info, live, tangent, folded, first, second,
     grad_fields, done,
-    count, ocean, work, sems,
+    work,
 ):
-    fetch = Fetch(sems, (count_hbm, count), (ocean_hbm, ocean))
+    used = owned_of(info) * TILE
     even = is_even()
     done[...] = jnp.zeros_like(done)
     work[...] = folded[...]
-    fetch.wait(0, 1)
-    used = count[0] * TILE
     for part in range(shape.parts):
         for col in range(HALF):
             planes = pl.ds(col * TILE, TILE)
@@ -497,7 +487,7 @@
             tail = pl.ds(LEFT + used - HALF + col, TILE, stride=shape.pitch)
             work[part, tail, :] = work[part, tail, :] + to_tail
         for slot in range(shape.slots):
-            flag = slot_flag(count, ocean, slot)
+            flag = live[slot, 0:1, shape.lanes(part)]
             for row in range(TILE):
                 rows = pl.ds(slot * TILE * TILE + row * TILE, TILE)
                 cells = work[part, pl.ds(row * shape.pitch + LEFT + slot * TILE, TILE), :]
@@ -718,40 +708,39 @@
     eight = ((8, channels), F32)
     taps = ((parts, KSIZE * KSIZE, 8, LANES), F32)
     count_s = (block_count.shape, jnp.int32)
-    ocean_s = (ocean.shape, jnp.int32)
     flat = ((channels, cells), BF16)
     ends = ((HALF * 2 * LEFT, channels), BF16)
     ends_f = ((parts, HALF * 2 * LEFT, LANES), F32)
     late = TILE - shape.early
 
-    first, second = call(
-        bind(prep_kernel), [edge, edge], [count_s, ((parts, cells, LANES), F32)],
-        [block_count], [fields], 1, 1.0,
-    )
-    (fold,) = call(
-        bind(top_kernel), [((HALF * shape.columns, channels), BF16)], [count_s, ocean_s],
-        [block_count, ocean], [fields], 2, 0.5, after=[first],
+    first, second, info = call(
+        bind(prep_kernel), [edge, edge, ((8, LANES), F32)],
+        [count_s, ((parts, cells, LANES), F32)], [block_count], [fields], 1, 1.0,
+    )
+    fold, live = call(
+        bind(top_kernel), [((HALF * shape.columns, channels), BF16), ((slots, 8, channels), F32)], [],
+        [], [info, ocean.reshape(1, slots), fields], 0, 0.5, after=[first],
     )
     first, second = swap(first, "first"), swap(second, "second")
     band, rims = call(
-        bind(band_kernel), [strip(TILE + HALF), ends], [count_s, ocean_s],
-        [block_count, ocean], [fields, first, second], 2, 1.0, after=[fold],
+        bind(band_kernel), [strip(TILE + HALF), ends], [],
+        [], [info, live, fields, first, second], 0, 1.0, after=[fold],
     )
     fold, rims = swap(fold, "fold"), swap(rims, "fold")
-    normed, yhat, inverse, dproj_t, dact, live = call(
-        bind(early_kernel), [whole, whole_f, narrow, flat, ((cells, hidden), F32), ((slots, 8, channels), F32)],
-        [count_s, ocean_s, taps, ((parts, shape.early * shape.columns, LANES), F32), whole],
-        [block_count, ocean], [taps_in, gain, w_out, scale, tangent, band], 2, 5.0,
+    normed, yhat, inverse, dproj_t, dact = call(
+        bind(early_kernel), [whole, whole_f, narrow, flat, ((cells, hidden), F32)],
+        [taps, ((parts, shape.early * shape.columns, LANES), F32), whole],
+        [], [live, taps_in, gain, w_out, scale, tangent, band], 0, 5.0,
     )
     keep, give, activated, dpreact, yhat, inverse, top = call(
         bind(late_kernel),
         [((hidden, channels), F32), ((hidden, channels), BF16), wide, wide, whole_f, narrow, strip(late + 2 * HALF)],
         [
-            count_s, taps, ((parts, late * shape.columns, LANES), F32), whole, flat, ends_f,
+            taps, ((parts, late * shape.columns, LANES), F32), whole, flat, ends_f,
             ((3, TILE * TILE, channels), F32),
         ],
-        [block_count],
-        [taps_in, gain, w_in, band, fold, rims, normed, yhat, inverse, dproj_t, dact], 1, 5.0,
+        [],
+        [info, taps_in, gain, w_in, band, fold, rims, normed, yhat, inverse, dproj_t, dact], 0, 5.0,
     )
 
     order = stages()
@@ -774,8 +763,8 @@
         outs = [(((TILE + HALF) * pitch, LANES), F32)] + [turned] * (part == parts - 1)
         return call(
             functools.partial(back_kernel, shape, part), outs,
-            [count_s, ((1, TILE * pitch, LANES), F32), ((1, KSIZE * KSIZE, 8, LANES), F32)],
-            [block_count], [taps_in, conv_grad, *before], 1, 2.0, after=after,
+            [((1, TILE * pitch, LANES), F32), ((1, KSIZE * KSIZE, 8, LANES), F32)],
+            [], [info, taps_in, conv_grad, *before], 0, 2.0, after=after,
         )
 
     small_rows = -(-(KSIZE * KSIZE + 2) // 32) * 32
@@ -812,7 +801,7 @@
     mine, send = halved(mine, send, order[2:-1])
     came = bit_swap(send, order[-2])
     folded, first, second = call(
-        bind(rims_kernel), [strip(TILE), edge, edge], [count_s], [block_count], [fold_back, *core_grad], 1, 1.0,
+        bind(rims_kernel), [strip(TILE), edge, edge], [], [], [info, fold_back, *core_grad], 0, 1.0,
         after=[send],
     )
     first, second = swap(first, "first"), swap(second, "second")
@@ -829,8 +818,8 @@
         payload = jnp.concatenate([share + came.astype(F32), small]).astype(BF16)
     came = bit_swap(payload, order[-1])
     grad_fields, done = call(
-        bind(final_kernel), [whole, ((8, LANES), F32)], [count_s, ocean_s, strip(TILE)],
-        [block_count, ocean], [tangent, folded, first, second], 2, 1.5, after=[payload],
+        bind(final_kernel), [whole, ((8, LANES), F32)], [strip(TILE)],
+        [], [info, live, tangent, folded, first, second], 0, 1.5, after=[payload],
     )
     state, done_too = call(
         bind(state_kernel), [whole, ((8, LANES), F32)], [], [], [fields, scale, projected, live], 0, 1.0, after=[done],

time: 62.8 us -> 61.9 us (0.986)
  Pallas kernels: 23.3 us -> 21.1 us
  waiting for transfers between devices: 7.57 us -> 8.95 us
    pallas_call x21, Pallas kernels: 23.3 us -> 21.1 us  [call(): pl.pallas_call(body, out_shape=[jax.ShapeDtypeStruct(*out) for out in out...]
    ppermute x4, waiting for transfers between devices: 3.69 us -> 5.63 us  [bit_swap(): return lax.ppermute(block, TILES + ('dp',), pairs)]
  transfers between devices with their start and end apart: 14 -> 14, of which waited for: 6 -> 6; matrix products, arithmetic and copies ran while one was open for 0% -> 0% of each run, Pallas kernels for 27% -> 24%
where the time goes in v10:
time: 61.9 us; the launch traced here: 61.7 us
  Pallas kernels  21.1 us (34%)
  starting transfers between devices  15.7 us (25%)
  blocking collectives  13.4 us (22%)
  waiting for transfers between devices  8.95 us (14%)
  between operations  1.53 us (2%)
  local copies, waits for them, and re-layouts  1.04 us (2%)
    pallas_call x21, Pallas kernels, call(): pl.pallas_call(body, out_shape=[jax.ShapeDtypeStruct(*out) for out in out...  21.1 us
    all_to_all x1, blocking collectives, shards(): came = lax.all_to_all(payload, ('near', 'dp'), 0, 0, tiled=True)  13.4 us
    ppermute x7, starting transfers between devices, swap(): return lax.ppermute(block, TILES, pairs_of(kind))  11.6 us
    ppermute x4, waiting for transfers between devices, bit_swap(): return lax.ppermute(block, TILES + ('dp',), pairs)  5.63 us
    ppermute x4, starting transfers between devices, bit_swap(): return lax.ppermute(block, TILES + ('dp',), pairs)  3.96 us
    ppermute x3, waiting for transfers between devices, core_swap(): return lax.ppermute(block, 'core', [(0, 1), (1, 0)])  2.71 us
  transfers between devices with their start and end apart: 14, of which 6 were waited for; matrix products, arithmetic and copies ran while one was open for 0% of the time, Pallas kernels for 24%

profile of v10, /device:TPU:0, one launch (start us, length us, event | category | flops | bytes accessed | tf_op | source)
XLA Modules:
  0.0 61.7 jit_solution(12530397543543591016)
XLA Ops:
  1.3 0.0 copy-start.4
  1.3 1.0 %copy-done.4 = bf16[1,3,16,16,256]{4,3,2,1,0:T(8,128)(2,1)S(1)} copy-done((bf16[1,3,16,16,256]{4,3,2,1,0:T(8,128)(2,1)S(1)}, bf16[1,3,16,16,256]{4,3,2,1,0:T(8,128)(2,1)}, u32[]{:S(2)}) %copy-start.4) | copy-done | bytes 393240
  2.3 0.6 shard_map.144
  2.9 4.1 %collective-permute-start.1 = (bf16[48,256]{1,0:T(8,128)(2,1)S(1)}, bf16[48,256]{1,0:T(8,128)(2,1)S(1)}, u32[]{:S(2)}, u32[]{:S(2)}) collective-permute-start(bf16[48,256]{1,0:T(8,128)(2,1)S(1)} %get-tuple-element.55), channel_id=1, source_target_pairs={{0,16},{2,4},{4,2},{6,8},{8,6},{10,12},{12,10},{14,30},{30,14},{28... | collective-permute-start | bytes 73736 | tf_op jit(solution)/shard_map/ppermute | solution.py:531
  7.0 0.0 collective-permute-start
  7.0 0.3 shard_map.145
  7.2 1.7 %collective-permute-start.2 = (bf16[144,256]{1,0:T(8,128)(2,1)S(1)}, bf16[144,256]{1,0:T(8,128)(2,1)S(1)}, u32[]{:S(2)}, u32[]{:S(2)}) collective-permute-start(bf16[144,256]{1,0:T(8,128)(2,1)S(1)} %get-tuple-element.56.refs_5_), channel_id=1, source_target_pairs={{0,16},{2,18},{4,20},{6,22},{8,24},{10,26},{12,28},{14,30},{30,14}... | collective-permute-start | bytes 221192 | tf_op jit(solution)/shard_map/ppermute | solution.py:531
  8.9 0.0 collective-permute-done.1.refs_4_
  8.9 0.0 copy-start.2
  8.9 0.0 copy-start.3
  8.9 0.0 copy-start.6
  9.0 0.0 copy-start.7
  9.0 0.2 shard_map.146
  9.2 2.8 %collective-permute-start.3 = (bf16[48,256]{1,0:T(8,128)(2,1)S(1)}, bf16[48,256]{1,0:T(8,128)(2,1)S(1)}, u32[]{:S(2)}, u32[]{:S(2)}) collective-permute-start(bf16[48,256]{1,0:T(8,128)(2,1)S(1)} %get-tuple-element.58), channel_id=1, source_target_pairs={{0,16},{2,18},{4,20},{6,22},{8,24},{10,26},{12,28},{14,30},{30,14}... | collective-permute-start | bytes 73736 | tf_op jit(solution)/shard_map/ppermute | solution.py:531
  12.1 0.0 copy-start
  12.1 3.6 %shard_map.147 = (bf16[768,256]{1,0:T(8,128)(2,1)S(1)}, f32[768,256]{1,0:T(8,128)S(1)}, f32[768,128]{1,0:T(8,128)S(1)}, bf16[256,768]{1,0:T(8,128)(2,1)S(1)}, f32[768,1024]{1,0:T(8,128)S(1)}) custom-call(f32[3,8,256]{2,1,0:T(8,128)S(1)} %get-tuple-element.54.refs_1_.refs_0_.refs_8_.refs_3_, bf16[7,7,256]{2,1,0:T(8,128)(2,1)S(1)} %copy-done.6, ...), custom_call_target="tpu_custom_call" | custom-call | flops 5000000000 | tf_op jit(solution)/shard_map/pallas_call | solution.py:672
  15.7 3.8 %shard_map.148 = (f32[1024,256]{1,0:T(8,128)S(1)}, bf16[1024,256]{1,0:T(8,128)(2,1)S(1)}, bf16[768,1024]{1,0:T(8,128)(2,1)S(1)}, bf16[768,1024]{1,0:T(8,128)(2,1...) custom-call(f32[8,128]{1,0:T(8,128)S(1)} %get-tuple-element.52.refs_0_, ...), custom_call_target="tpu_custom_call" | custom-call | flops 5000000000 | tf_op jit(solution)/shard_map/pallas_call | solution.py:672
  19.5 0.1 collective-permute-start.4
  19.6 1.1 %shard_map.149 = (bf16[768,256]{1,0:T(8,128)(2,1)S(1)}, f32[768,256]{1,0:T(8,128)S(1)}, f32[8,256]{1,0:T(8,128)S(1)}, f32[8,256]{1,0:T(8,128)S(1)}) custom-call(bf16[256,1024]{1,0:T(8,128)(2,1)S(1)} %copy-done, bf16[1024,256]{1,0:T(8,128)(2,1)S(1)} %copy-done.1, f32[1,256]{1,0:T(1,128)S(1)} %bitcast.14, bf16[768,1024]{1,0:T(8,128)(2,1)S(1)} %get-tuple-element.64.refs_3_, ...), custom_call_target="tpu_custom_call" | custom-call | flops 1300000000 | tf_op jit(solution)/shard_map/pallas_call | solution.py:672
  20.7 0.8 %collective-permute-done.4.refs_1_ = bf16[1024,256]{1,0:T(8,128)(2,1)S(1)} collective-permute-done((bf16[1024,256]{1,0:T(8,128)(2,1)S(1)}, bf16[1024,256]{1,0:T(8,128)(2,1)S(1)}, u32[]{:S(2)}, u32[]{:S(2)}) %collective-permute-start.4) | collective-permute-done | bytes 524320 | tf_op jit(solution)/shard_map/ppermute | solution.py:535
  21.5 0.2 shard_map.150
  21.6 0.2 collective-permute-start.6
  21.8 1.7 %shard_map.151.refs_3_.refs_4_.refs_2_ = f32[1216,128]{1,0:T(8,128)S(1)} custom-call(f32[8,128]{1,0:T(8,128)S(1)} %get-tuple-element.52.refs_0_, bf16[7,7,256]{2,1,0:T(8,128)(2,1)S(1)} %copy-done.6, bf16[768,256]{1,0:T(8,128)(2,1)S(1)} %get-tuple-element.69.refs_2_, bf16[512,256]{1,0:T(8,128)(2,1)S(1)} %get-tuple-element.73.refs_3_), custom_call_target="tpu_custom_call" | custom-call | flops 2000000000 | tf_op jit(solution)/shard_map/pallas_call | solution.py:672
  23.5 1.9 %shard_map.152 = (f32[1216,128]{1,0:T(8,128)S(1)}, bf16[192,256]{1,0:T(8,128)(2,1)S(1)}) custom-call(f32[8,128]{1,0:T(8,128)S(1)} %get-tuple-element.52.refs_0_, bf16[7,7,256]{2,1,0:T(8,128)(2,1)S(1)} %copy-done.6, bf16[768,256]{1,0:T(8,128)(2,1)S(1)} %get-tuple-element.69.refs_2_, f32[1216,128]{1,0:T(8,128)S(1)} %shard_map.151.refs_3_.refs_4_.refs_2_, ...), custom_call_target="tpu_custom_call" | custom-call | flops 2000000000 | tf_op jit(solution)/shard_map/pallas_call | solution.py:672
  25.5 1.7 %collective-permute-start.5 = (bf16[192,256]{1,0:T(8,128)(2,1)S(1)}, bf16[192,256]{1,0:T(8,128)(2,1)S(1)}, u32[]{:S(2)}, u32[]{:S(2)}) collective-permute-start(bf16[192,256]{1,0:T(8,128)(2,1)S(1)} %get-tuple-element.74), channel_id=1, source_target_pairs={{0,16},{2,18},{4,20},{6,22},{8,24},{10,26},{12,28},{14,30},{30,14}... | collective-permute-start | bytes 294920 | tf_op jit(solution)/shard_map/ppermute | solution.py:531
  27.1 0.9 %collective-permute-done.6.refs_1_ = bf16[512,256]{1,0:T(8,128)(2,1)S(1)} collective-permute-done((bf16[512,256]{1,0:T(8,128)(2,1)S(1)}, bf16[512,256]{1,0:T(8,128)(2,1)S(1)}, u32[]{:S(2)}, u32[]{:S(2)}) %collective-permute-start.6) | collective-permute-done | bytes 262176 | tf_op jit(solution)/shard_map/ppermute | solution.py:555
  28.1 0.1 shard_map.153
  28.1 1.6 %collective-permute-start.7 = (bf16[256,256]{1,0:T(8,128)(2,1)S(1)}, bf16[256,256]{1,0:T(8,128)(2,1)S(1)}, u32[]{:S(2)}, u32[]{:S(2)}) collective-permute-start(bf16[256,256]{1,0:T(8,128)(2,1)S(1)} %get-tuple-element.78.refs_3_), channel_id=1, source_target_pairs={{0,1},{1,0},{2,6},{3,7},{4,5},{5,4},{6,2},{7,3},{8,9},{9,8},{10,14... | collective-permute-start | bytes 393224 | tf_op jit(solution)/shard_map/ppermute | solution.py:555
  29.7 1.8 %shard_map.155.refs_3_ = f32[64,128]{1,0:T(8,128)S(1)} custom-call(f32[2,1216,128]{2,1,0:T(8,128)S(1)} %get-tuple-element.57.refs_6_.refs_4_.refs_0_, f32[2,640,128]{2,1,0:T(8,128)S(1)} %get-tuple-element.80.refs_1_, bf16[768,256]{1,0:T(8,128)(2,1)S(1)} %get-tuple-element.69.refs_2_, bf16[256,256]{1,0:T(8,128)(2,1)S(1)} %get-tuple-element.78.refs_3_), custom_call_target="tpu_custom_call" | custom-call | flops 1800000000 | tf_op jit(solution)/shard_map/pallas_call | solution.py:672
  31.5 1.8 %shard_map.154.refs_2_ = f32[64,128]{1,0:T(8,128)S(1)} custom-call(f32[2,1216,128]{2,1,0:T(8,128)S(1)} %get-tuple-element.57.refs_6_.refs_4_.refs_0_, f32[2,640,128]{2,1,0:T(8,128)S(1)} %get-tuple-element.80.refs_1_, bf16[768,256]{1,0:T(8,128)(2,1)S(1)} %get-tuple-element.69.refs_2_, bf16[256,256]{1,0:T(8,128)(2,1)S(1)} %get-tuple-element.78.refs_3_), custom_call_target="tpu_custom_call" | custom-call | flops 1800000000 | tf_op jit(solution)/shard_map/pallas_call | solution.py:672
  33.3 0.1 collective-permute-start.11
  33.4 0.1 shard_map.157
  33.5 1.1 %collective-permute-start.10 = (bf16[128,256]{1,0:T(8,128)(2,1)S(1)}, bf16[128,256]{1,0:T(8,128)(2,1)S(1)}, u32[]{:S(2)}, u32[]{:S(2)}) collective-permute-start(bf16[128,256]{1,0:T(8,128)(2,1)S(1)} %get-tuple-element.82.refs_4_), channel_id=1, source_target_pairs={{0,8},{1,9},{2,3},{3,2},{4,12},{5,13},{6,7},{7,6},{8,0},{9,1},{10,... | collective-permute-start | bytes 196616 | tf_op jit(solution)/shard_map/ppermute | solution.py:555
  34.5 0.2 shard_map.158
  34.7 0.1 collective-permute-start.8
  34.8 1.2 %collective-permute-start.9 = (bf16[48,256]{1,0:T(8,128)(2,1)S(1)}, bf16[48,256]{1,0:T(8,128)(2,1)S(1)}, u32[]{:S(2)}, u32[]{:S(2)}) collective-permute-start(bf16[48,256]{1,0:T(8,128)(2,1)S(1)} %get-tuple-element.85), channel_id=1, source_target_pairs={{0,16},{2,4},{4,2},{6,8},{8,6},{10,12},{12,10},{14,30},{30,14},{28... | collective-permute-start | bytes 73736 | tf_op jit(solution)/shard_map/ppermute | solution.py:531
  36.0 1.8 %collective-permute-done.10.refs_1_ = bf16[128,256]{1,0:T(8,128)(2,1)S(1)} collective-permute-done((bf16[128,256]{1,0:T(8,128)(2,1)S(1)}, bf16[128,256]{1,0:T(8,128)(2,1)S(1)}, u32[]{:S(2)}, u32[]{:S(2)}) %collective-permute-start.10) | collective-permute-done | bytes 65568 | tf_op jit(solution)/shard_map/ppermute | solution.py:555
  37.8 0.0 copy-start.5
  37.8 1.1 %collective-permute-start.12 = (bf16[160,256]{1,0:T(8,128)(2,1)S(1)}, bf16[160,256]{1,0:T(8,128)(2,1)S(1)}, u32[]{:S(2)}, u32[]{:S(2)}) collective-permute-start(bf16[160,256]{1,0:T(8,128)(2,1)S(1)} %shard_map.159.refs_6_.refs_0_), channel_id=1, source_target_pairs={{0,16},{1,17},{2,18},{3,19},{4,20},{5,21},{6,22},{7,23},{8,24},{9,... | collective-permute-start | bytes 245768 | tf_op jit(solution)/shard_map/ppermute | solution.py:555
  39.0 0.6 collective-permute-done.9.refs_5_
  39.6 1.2 %shard_map.160 = (bf16[768,256]{1,0:T(8,128)(2,1)}, f32[8,128]{1,0:T(8,128)S(1)}) custom-call(f32[8,128]{1,0:T(8,128)S(1)} %get-tuple-element.52.refs_0_, f32[3,8,256]{2,1,0:T(8,128)S(1)} %get-tuple-element.54.refs_1_.refs_0_.refs_8_.refs_3_, bf16[768,256]{1,0:T(8,128)(2,1)S(1)} %bitcast.11, f32[2,1024,128]{2,1,0:T(8,128)S(1)} %get-tuple-element.83.refs_4_.refs_3_, ...), custom_call_target="tpu_custom_call" | custom-call | flops 1500000000 | tf_op jit(solution)/shard_map/pallas_call | solution.py:672
  40.8 0.9 %shard_map.161 = (bf16[768,256]{1,0:T(8,128)(2,1)}, f32[8,128]{1,0:T(8,128)S(1)}) custom-call(bf16[768,256]{1,0:T(8,128)(2,1)S(1)} %bitcast.18, f32[1,256]{1,0:T(1,128)S(1)} %bitcast.20, f32[768,256]{1,0:T(8,128)S(1)} %get-tuple-element.68.refs_2_, f32[3,8,256]{2,1,0:T(8,128)S(1)} %get-tuple-element.54.refs_1_.refs_0_.refs_8_.refs_3_, ...), custom_call_target="tpu_custom_call" | custom-call | flops 1000000000 | tf_op jit(solution)/shard_map/pallas_call | solution.py:672
  41.6 2.9 %collective-permute-done.12.refs_1_ = bf16[160,256]{1,0:T(8,128)(2,1)S(1)} collective-permute-done((bf16[160,256]{1,0:T(8,128)(2,1)S(1)}, bf16[160,256]{1,0:T(8,128)(2,1)S(1)}, u32[]{:S(2)}, u32[]{:S(2)}) %collective-permute-start.12) | collective-permute-done | bytes 81952 | tf_op jit(solution)/shard_map/ppermute | solution.py:555
  44.6 13.4 %all_to_all.5.refs_0_ = bf16[8,160,256]{2,1,0:T(8,128)(2,1)S(1)} all-to-all(bf16[8,160,256]{2,1,0:T(8,128)(2,1)S(1)} %shard_map.162), channel_id=1, replica_groups=mesh['far'=2,'near'=4,'core'=2,'dp'=2] {'near','dp'}, dimensions={0} | all-to-all | bytes 1310720 | tf_op jit(solution)/shard_map/all_to_all | solution.py:850
  58.0 0.1 shard_map.163.refs_0_
  58.1 0.1 collective-permute-start.13
  58.1 1.9 %collective-permute-done.13.refs_1_ = bf16[1088,256]{1,0:T(8,128)(2,1)S(1)} collective-permute-done((bf16[1088,256]{1,0:T(8,128)(2,1)S(1)}, bf16[1088,256]{1,0:T(8,128)(2,1)S(1)}, u32[]{:S(2)}, u32[]{:S(2)}) %collective-permute-start.13) | collective-permute-done | bytes 557088 | tf_op jit(solution)/shard_map/ppermute | solution.py:535
  60.1 1.6 %shard_map.164 = (f32[256,1024]{1,0:T(8,128)}, f32[1024,256]{1,0:T(8,128)}, f32[7,7,256]{2,1,0:T(8,128)}, f32[1,256]{1,0:T(1,128)}, f32[1,256]{1,0:T(1,128)}) custom-call(bf16[1088,256]{1,0:T(8,128)(2,1)S(1)} %shard_map.163.refs_0_, bf16[1088,256]{1,0:T(8,128)(2,1)S(1)} %collective-permute-done.13.refs_1_), custom_call_target="tpu_custom_call" | custom-call | flops 1500000000 | tf_op jit(solution)/shard_map/pallas_call | solution.py:672
  (20 shorter events, 0.1 us)
Async XLA Ops:
  1.3 1.0 %copy-start.4 = (bf16[1,3,16,16,256]{4,3,2,1,0:T(8,128)(2,1)S(1)}, bf16[1,3,16,16,256]{4,3,2,1,0:T(8,128)(2,1)}, u32[]{:S(2)}) copy-start(bf16[1,3,16,16,256]{4,3,2,1,0:T(8,128)(2,1)} %param.9) | copy-start | bytes 1179652
  2.3 4.7 %copy-start.8 = (s32[3]{0:T(128)S(1)}, s32[3]{0:T(128)}, u32[]{:S(2)}) copy-start(s32[3]{0:T(128)} %param.12) | copy-start | bytes 40
  2.9 6.0 %collective-permute-start.1 = (bf16[48,256]{1,0:T(8,128)(2,1)S(1)}, bf16[48,256]{1,0:T(8,128)(2,1)S(1)}, u32[]{:S(2)}, u32[]{:S(2)}) collective-permute-start(bf16[48,256]{1,0:T(8,128)(2,1)S(1)} %get-tuple-element.55), channel_id=1, source_target_pairs={{0,16},{2,4},{4,2},{6,8},{8,6},{10,12},{12,10},{14,30},{30,14},{28... | collective-permute-start | bytes 73736 | tf_op jit(solution)/shard_map/ppermute | solution.py:531
  7.0 1.9 %collective-permute-start = (bf16[48,256]{1,0:T(8,128)(2,1)S(1)}, bf16[48,256]{1,0:T(8,128)(2,1)S(1)}, u32[]{:S(2)}, u32[]{:S(2)}) collective-permute-start(bf16[48,256]{1,0:T(8,128)(2,1)S(1)} %get-tuple-element.53.refs_3_), channel_id=1, source_target_pairs={{0,2},{2,0},{4,6},{6,4},{8,10},{10,8},{12,14},{14,12},{30,28},{28,... | collective-permute-start | bytes 73736 | tf_op jit(solution)/shard_map/ppermute | solution.py:531
  7.2 8.4 %collective-permute-start.2 = (bf16[144,256]{1,0:T(8,128)(2,1)S(1)}, bf16[144,256]{1,0:T(8,128)(2,1)S(1)}, u32[]{:S(2)}, u32[]{:S(2)}) collective-permute-start(bf16[144,256]{1,0:T(8,128)(2,1)S(1)} %get-tuple-element.56.refs_5_), channel_id=1, source_target_pairs={{0,16},{2,18},{4,20},{6,22},{8,24},{10,26},{12,28},{14,30},{30,14}... | collective-permute-start | bytes 221192 | tf_op jit(solution)/shard_map/ppermute | solution.py:531
  8.9 3.1 %copy-start.1 = (bf16[1024,256]{1,0:T(8,128)(2,1)S(1)}, bf16[1024,256]{1,0:T(8,128)(2,1)}, u32[]{:S(2)}) copy-start(bf16[1024,256]{1,0:T(8,128)(2,1)} %refs_1_.7) | copy-start | bytes 1572868
  8.9 3.1 %copy-start.2 = (bf16[1,3,16,16,256]{4,3,2,1,0:T(8,128)(2,1)S(1)}, bf16[1,3,16,16,256]{4,3,2,1,0:T(8,128)(2,1)}, u32[]{:S(2)}) copy-start(bf16[1,3,16,16,256]{4,3,2,1,0:T(8,128)(2,1)} %param.10) | copy-start | bytes 1179652
  8.9 3.1 %copy-start.3 = (f32[256]{0:T(256)S(1)}, f32[256]{0:T(256)}, u32[]{:S(2)}) copy-start(f32[256]{0:T(256)} %param.14) | copy-start | bytes 3076
  8.9 3.1 %copy-start.6 = (bf16[7,7,256]{2,1,0:T(8,128)(2,1)S(1)}, bf16[7,7,256]{2,1,0:T(8,128)(2,1)}, u32[]{:S(2)}) copy-start(bf16[7,7,256]{2,1,0:T(8,128)(2,1)} %refs_1_.9) | copy-start | bytes 75268
  9.0 3.1 %copy-start.7 = (f32[256]{0:T(256)S(1)}, f32[256]{0:T(256)}, u32[]{:S(2)}) copy-start(f32[256]{0:T(256)} %param.17) | copy-start | bytes 3076
  9.2 6.4 %collective-permute-start.3 = (bf16[48,256]{1,0:T(8,128)(2,1)S(1)}, bf16[48,256]{1,0:T(8,128)(2,1)S(1)}, u32[]{:S(2)}, u32[]{:S(2)}) collective-permute-start(bf16[48,256]{1,0:T(8,128)(2,1)S(1)} %get-tuple-element.58), channel_id=1, source_target_pairs={{0,16},{2,18},{4,20},{6,22},{8,24},{10,26},{12,28},{14,30},{30,14}... | collective-permute-start | bytes 73736 | tf_op jit(solution)/shard_map/ppermute | solution.py:531
  12.1 3.6 %copy-start = (bf16[256,1024]{1,0:T(8,128)(2,1)S(1)}, bf16[256,1024]{1,0:T(8,128)(2,1)}, u32[]{:S(2)}) copy-start(bf16[256,1024]{1,0:T(8,128)(2,1)} %refs_0_.2) | copy-start | bytes 1572868
  19.5 2.0 %collective-permute-start.4 = (bf16[1024,256]{1,0:T(8,128)(2,1)S(1)}, bf16[1024,256]{1,0:T(8,128)(2,1)S(1)}, u32[]{:S(2)}, u32[]{:S(2)}) collective-permute-start(bf16[1024,256]{1,0:T(8,128)(2,1)S(1)} %get-tuple-element.71), channel_id=1, source_target_pairs={{0,2},{2,0},{1,3},{3,1},{4,6},{6,4},{5,7},{7,5},{8,10},{10,8},{9,1... | collective-permute-start | bytes 1572872 | tf_op jit(solution)/shard_map/ppermute | solution.py:535
  21.6 6.4 %collective-permute-start.6 = (bf16[512,256]{1,0:T(8,128)(2,1)S(1)}, bf16[512,256]{1,0:T(8,128)(2,1)S(1)}, u32[]{:S(2)}, u32[]{:S(2)}) collective-permute-start(bf16[512,256]{1,0:T(8,128)(2,1)S(1)} %get-tuple-element.73.refs_3_), channel_id=1, source_target_pairs={{0,4},{1,5},{2,10},{3,11},{4,0},{5,1},{6,14},{7,15},{8,12},{9,13},... | collective-permute-start | bytes 786440 | tf_op jit(solution)/shard_map/ppermute | solution.py:555
  25.5 9.1 %collective-permute-start.5 = (bf16[192,256]{1,0:T(8,128)(2,1)S(1)}, bf16[192,256]{1,0:T(8,128)(2,1)S(1)}, u32[]{:S(2)}, u32[]{:S(2)}) collective-permute-start(bf16[192,256]{1,0:T(8,128)(2,1)S(1)} %get-tuple-element.74), channel_id=1, source_target_pairs={{0,16},{2,18},{4,20},{6,22},{8,24},{10,26},{12,28},{14,30},{30,14}... | collective-permute-start | bytes 294920 | tf_op jit(solution)/shard_map/ppermute | solution.py:531
  28.1 5.3 %collective-permute-start.7 = (bf16[256,256]{1,0:T(8,128)(2,1)S(1)}, bf16[256,256]{1,0:T(8,128)(2,1)S(1)}, u32[]{:S(2)}, u32[]{:S(2)}) collective-permute-start(bf16[256,256]{1,0:T(8,128)(2,1)S(1)} %get-tuple-element.78.refs_3_), channel_id=1, source_target_pairs={{0,1},{1,0},{2,6},{3,7},{4,5},{5,4},{6,2},{7,3},{8,9},{9,8},{10,14... | collective-permute-start | bytes 393224 | tf_op jit(solution)/shard_map/ppermute | solution.py:555
  33.3 2.7 %collective-permute-start.11 = (bf16[64,256]{1,0:T(8,128)(2,1)S(1)}, bf16[64,256]{1,0:T(8,128)(2,1)S(1)}, u32[]{:S(2)}, u32[]{:S(2)}) collective-permute-start(bf16[64,256]{1,0:T(8,128)(2,1)S(1)} %get-tuple-element.87), channel_id=1, source_target_pairs={{0,2},{2,0},{1,3},{3,1},{4,6},{6,4},{5,7},{7,5},{8,10},{10,8},{9,1... | collective-permute-start | bytes 98312 | tf_op jit(solution)/shard_map/ppermute | solution.py:535
  33.5 4.3 %collective-permute-start.10 = (bf16[128,256]{1,0:T(8,128)(2,1)S(1)}, bf16[128,256]{1,0:T(8,128)(2,1)S(1)}, u32[]{:S(2)}, u32[]{:S(2)}) collective-permute-start(bf16[128,256]{1,0:T(8,128)(2,1)S(1)} %get-tuple-element.82.refs_4_), channel_id=1, source_target_pairs={{0,8},{1,9},{2,3},{3,2},{4,12},{5,13},{6,7},{7,6},{8,0},{9,1},{10,... | collective-permute-start | bytes 196616 | tf_op jit(solution)/shard_map/ppermute | solution.py:555
  34.7 4.3 %collective-permute-start.8 = (bf16[48,256]{1,0:T(8,128)(2,1)S(1)}, bf16[48,256]{1,0:T(8,128)(2,1)S(1)}, u32[]{:S(2)}, u32[]{:S(2)}) collective-permute-start(bf16[48,256]{1,0:T(8,128)(2,1)S(1)} %get-tuple-element.84), channel_id=1, source_target_pairs={{0,2},{2,0},{4,6},{6,4},{8,10},{10,8},{12,14},{14,12},{30,28},{28,... | collective-permute-start | bytes 73736 | tf_op jit(solution)/shard_map/ppermute | solution.py:531
  34.8 4.8 %collective-permute-start.9 = (bf16[48,256]{1,0:T(8,128)(2,1)S(1)}, bf16[48,256]{1,0:T(8,128)(2,1)S(1)}, u32[]{:S(2)}, u32[]{:S(2)}) collective-permute-start(bf16[48,256]{1,0:T(8,128)(2,1)S(1)} %get-tuple-element.85), channel_id=1, source_target_pairs={{0,16},{2,4},{4,2},{6,8},{8,6},{10,12},{12,10},{14,30},{30,14},{28... | collective-permute-start | bytes 73736 | tf_op jit(solution)/shard_map/ppermute | solution.py:531
  37.8 2.9 %copy-start.5 = (bf16[1,3,16,16,256]{4,3,2,1,0:T(8,128)(2,1)S(1)}, bf16[1,3,16,16,256]{4,3,2,1,0:T(8,128)(2,1)}, u32[]{:S(2)}) copy-start(bf16[1,3,16,16,256]{4,3,2,1,0:T(8,128)(2,1)} %param.9) | copy-start | bytes 1179652
  37.8 6.7 %collective-permute-start.12 = (bf16[160,256]{1,0:T(8,128)(2,1)S(1)}, bf16[160,256]{1,0:T(8,128)(2,1)S(1)}, u32[]{:S(2)}, u32[]{:S(2)}) collective-permute-start(bf16[160,256]{1,0:T(8,128)(2,1)S(1)} %shard_map.159.refs_6_.refs_0_), channel_id=1, source_target_pairs={{0,16},{1,17},{2,18},{3,19},{4,20},{5,21},{6,22},{7,23},{8,24},{9,... | collective-permute-start | bytes 245768 | tf_op jit(solution)/shard_map/ppermute | solution.py:555
  58.1 2.0 %collective-permute-start.13 = (bf16[1088,256]{1,0:T(8,128)(2,1)S(1)}, bf16[1088,256]{1,0:T(8,128)(2,1)S(1)}, u32[]{:S(2)}, u32[]{:S(2)}) collective-permute-start(bf16[1088,256]{1,0:T(8,128)(2,1)S(1)} %shard_map.163.refs_0_), channel_id=1, source_target_pairs={{0,2},{2,0},{1,3},{3,1},{4,6},{6,4},{5,7},{7,5},{8,10},{10,8},{9,1... | collective-permute-start | bytes 1671176 | tf_op jit(solution)/shard_map/ppermute | solution.py:535

commit v11 on v10

--- a/solution.py
+++ b/solution.py
@@ -179,6 +179,13 @@
                 padded[at, pl.ds(base + LEFT + used + col, 1), :] = west
 
 
+def tree_sum(terms):
+    while len(terms) > 1:
+        pairs = [terms[at] + terms[at + 1] for at in range(0, len(terms) - 1, 2)]
+        terms = pairs + terms[len(pairs) * 2 :]
+    return terms[0]
+
+
 def spread_taps(shape, kernel, parts, taps):
     for above in range(KSIZE):
         rows = kernel[above].astype(F32)
@@ -390,8 +397,7 @@
             grads = [spaced[0, pl.ds(start + at, 8, stride=run), :] for at in range(run)]
             sums = list(sums)
             for shift in range(KSIZE):
-                for at in range(run):
-                    sums[shift] = sums[shift] + grads[at] * loaded[at + shift]
+                sums[shift] = sums[shift] + tree_sum([grads[at] * loaded[at + shift] for at in range(run)])
             return tuple(sums)
 
         blank = tuple(jnp.zeros((8, LANES), F32) for _ in range(KSIZE))
@@ -422,11 +428,10 @@
             loaded = [
                 spaced[0, pl.ds(base + at - KSIZE + 1, 8, stride=run), :] for at in range(run + KSIZE - 1)
             ]
-            for shift in range(KSIZE):
-                weight = taps[0, above * KSIZE + shift]
-                for at in range(run):
-                    term = weight * loaded[at - shift + KSIZE - 1]
-                    sums[at] = term if sums[at] is None else sums[at] + term
+            weights = [taps[0, above * KSIZE + shift] for shift in range(KSIZE)]
+            for at in range(run):
+                row_sum = tree_sum([weights[shift] * loaded[at - shift + KSIZE - 1] for shift in range(KSIZE)])
+                sums[at] = row_sum if sums[at] is None else sums[at] + row_sum
         start = (row - HALF) * shape.pitch + LEFT - HALF
         for at in range(run):
             core_grad[pl.ds(start + at, 8, stride=run), :] = sums[at]

time: 61.9 us -> 62 us (level)
  no operation moved by 1% of the time
where the time goes in v11:
time: 62 us; the launch traced here: 61.8 us
  Pallas kernels  20.9 us (34%)
  starting transfers between devices  15.7 us (25%)
  blocking collectives  13.4 us (22%)
  waiting for transfers between devices  9.16 us (15%)
  between operations  1.53 us (2%)
  local copies, waits for them, and re-layouts  1.04 us (2%)
    pallas_call x21, Pallas kernels, call(): pl.pallas_call(body, out_shape=[jax.ShapeDtypeStruct(*out) for out in out...  20.9 us
    all_to_all x1, blocking collectives, shards(): came = lax.all_to_all(payload, ('near', 'dp'), 0, 0, tiled=True)  13.4 us
    ppermute x7, starting transfers between devices, swap(): return lax.ppermute(block, TILES, pairs_of(kind))  11.6 us
    ppermute x4, waiting for transfers between devices, bit_swap(): return lax.ppermute(block, TILES + ('dp',), pairs)  5.83 us
    ppermute x4, starting transfers between devices, bit_swap(): return lax.ppermute(block, TILES + ('dp',), pairs)  3.96 us
    ppermute x3, waiting for transfers between devices, core_swap(): return lax.ppermute(block, 'core', [(0, 1), (1, 0)])  2.71 us
  transfers between devices with their start and end apart: 14, of which 6 were waited for; matrix products, arithmetic and copies ran while one was open for 0% of the time, Pallas kernels for 24%

profile of v11, /device:TPU:0, one launch (start us, length us, event | category | flops | bytes accessed | tf_op | source)
XLA Modules:
  0.0 61.8 jit_solution(10409143920066354047)
XLA Ops:
  1.3 0.0 copy-start.4
  1.3 1.0 %copy-done.4 = bf16[1,3,16,16,256]{4,3,2,1,0:T(8,128)(2,1)S(1)} copy-done((bf16[1,3,16,16,256]{4,3,2,1,0:T(8,128)(2,1)S(1)}, bf16[1,3,16,16,256]{4,3,2,1,0:T(8,128)(2,1)}, u32[]{:S(2)}) %copy-start.4) | copy-done | bytes 393240
  2.3 0.6 shard_map.144
  2.9 4.1 %collective-permute-start.1 = (bf16[48,256]{1,0:T(8,128)(2,1)S(1)}, bf16[48,256]{1,0:T(8,128)(2,1)S(1)}, u32[]{:S(2)}, u32[]{:S(2)}) collective-permute-start(bf16[48,256]{1,0:T(8,128)(2,1)S(1)} %get-tuple-element.55), channel_id=1, source_target_pairs={{0,16},{2,4},{4,2},{6,8},{8,6},{10,12},{12,10},{14,30},{30,14},{28... | collective-permute-start | bytes 73736 | tf_op jit(solution)/shard_map/ppermute | solution.py:536
  7.0 0.0 collective-permute-start
  7.0 0.3 shard_map.145
  7.2 1.7 %collective-permute-start.2 = (bf16[144,256]{1,0:T(8,128)(2,1)S(1)}, bf16[144,256]{1,0:T(8,128)(2,1)S(1)}, u32[]{:S(2)}, u32[]{:S(2)}) collective-permute-start(bf16[144,256]{1,0:T(8,128)(2,1)S(1)} %get-tuple-element.56.refs_5_), channel_id=1, source_target_pairs={{0,16},{2,18},{4,20},{6,22},{8,24},{10,26},{12,28},{14,30},{30,14}... | collective-permute-start | bytes 221192 | tf_op jit(solution)/shard_map/ppermute | solution.py:536
  8.9 0.0 collective-permute-done.1.refs_4_
  8.9 0.0 copy-start.2
  8.9 0.0 copy-start.3
  8.9 0.0 copy-start.6
  9.0 0.0 copy-start.7
  9.0 0.2 shard_map.146
  9.2 2.8 %collective-permute-start.3 = (bf16[48,256]{1,0:T(8,128)(2,1)S(1)}, bf16[48,256]{1,0:T(8,128)(2,1)S(1)}, u32[]{:S(2)}, u32[]{:S(2)}) collective-permute-start(bf16[48,256]{1,0:T(8,128)(2,1)S(1)} %get-tuple-element.58), channel_id=1, source_target_pairs={{0,16},{2,18},{4,20},{6,22},{8,24},{10,26},{12,28},{14,30},{30,14}... | collective-permute-start | bytes 73736 | tf_op jit(solution)/shard_map/ppermute | solution.py:536
  12.1 0.0 copy-start
  12.1 3.6 %shard_map.147 = (bf16[768,256]{1,0:T(8,128)(2,1)S(1)}, f32[768,256]{1,0:T(8,128)S(1)}, f32[768,128]{1,0:T(8,128)S(1)}, bf16[256,768]{1,0:T(8,128)(2,1)S(1)}, f32[768,1024]{1,0:T(8,128)S(1)}) custom-call(f32[3,8,256]{2,1,0:T(8,128)S(1)} %get-tuple-element.54.refs_1_.refs_0_.refs_8_.refs_3_, bf16[7,7,256]{2,1,0:T(8,128)(2,1)S(1)} %copy-done.6, ...), custom_call_target="tpu_custom_call" | custom-call | flops 5000000000 | tf_op jit(solution)/shard_map/pallas_call | solution.py:677
  15.7 3.8 %shard_map.148 = (f32[1024,256]{1,0:T(8,128)S(1)}, bf16[1024,256]{1,0:T(8,128)(2,1)S(1)}, bf16[768,1024]{1,0:T(8,128)(2,1)S(1)}, bf16[768,1024]{1,0:T(8,128)(2,1...) custom-call(f32[8,128]{1,0:T(8,128)S(1)} %get-tuple-element.52.refs_0_, ...), custom_call_target="tpu_custom_call" | custom-call | flops 5000000000 | tf_op jit(solution)/shard_map/pallas_call | solution.py:677
  19.5 0.1 collective-permute-start.4
  19.6 1.1 %shard_map.149 = (bf16[768,256]{1,0:T(8,128)(2,1)S(1)}, f32[768,256]{1,0:T(8,128)S(1)}, f32[8,256]{1,0:T(8,128)S(1)}, f32[8,256]{1,0:T(8,128)S(1)}) custom-call(bf16[256,1024]{1,0:T(8,128)(2,1)S(1)} %copy-done, bf16[1024,256]{1,0:T(8,128)(2,1)S(1)} %copy-done.1, f32[1,256]{1,0:T(1,128)S(1)} %bitcast.14, bf16[768,1024]{1,0:T(8,128)(2,1)S(1)} %get-tuple-element.64.refs_3_, ...), custom_call_target="tpu_custom_call" | custom-call | flops 1300000000 | tf_op jit(solution)/shard_map/pallas_call | solution.py:677
  20.7 0.8 %collective-permute-done.4.refs_1_ = bf16[1024,256]{1,0:T(8,128)(2,1)S(1)} collective-permute-done((bf16[1024,256]{1,0:T(8,128)(2,1)S(1)}, bf16[1024,256]{1,0:T(8,128)(2,1)S(1)}, u32[]{:S(2)}, u32[]{:S(2)}) %collective-permute-start.4) | collective-permute-done | bytes 524320 | tf_op jit(solution)/shard_map/ppermute | solution.py:540
  21.5 0.2 shard_map.150
  21.6 0.2 collective-permute-start.6
  21.8 1.6 %shard_map.151.refs_3_.refs_4_.refs_2_ = f32[1216,128]{1,0:T(8,128)S(1)} custom-call(f32[8,128]{1,0:T(8,128)S(1)} %get-tuple-element.52.refs_0_, bf16[7,7,256]{2,1,0:T(8,128)(2,1)S(1)} %copy-done.6, bf16[768,256]{1,0:T(8,128)(2,1)S(1)} %get-tuple-element.69.refs_2_, bf16[512,256]{1,0:T(8,128)(2,1)S(1)} %get-tuple-element.73.refs_3_), custom_call_target="tpu_custom_call" | custom-call | flops 2000000000 | tf_op jit(solution)/shard_map/pallas_call | solution.py:677
  23.4 1.9 %shard_map.152 = (f32[1216,128]{1,0:T(8,128)S(1)}, bf16[192,256]{1,0:T(8,128)(2,1)S(1)}) custom-call(f32[8,128]{1,0:T(8,128)S(1)} %get-tuple-element.52.refs_0_, bf16[7,7,256]{2,1,0:T(8,128)(2,1)S(1)} %copy-done.6, bf16[768,256]{1,0:T(8,128)(2,1)S(1)} %get-tuple-element.69.refs_2_, f32[1216,128]{1,0:T(8,128)S(1)} %shard_map.151.refs_3_.refs_4_.refs_2_, ...), custom_call_target="tpu_custom_call" | custom-call | flops 2000000000 | tf_op jit(solution)/shard_map/pallas_call | solution.py:677
  25.3 1.7 %collective-permute-start.5 = (bf16[192,256]{1,0:T(8,128)(2,1)S(1)}, bf16[192,256]{1,0:T(8,128)(2,1)S(1)}, u32[]{:S(2)}, u32[]{:S(2)}) collective-permute-start(bf16[192,256]{1,0:T(8,128)(2,1)S(1)} %get-tuple-element.74), channel_id=1, source_target_pairs={{0,16},{2,18},{4,20},{6,22},{8,24},{10,26},{12,28},{14,30},{30,14}... | collective-permute-start | bytes 294920 | tf_op jit(solution)/shard_map/ppermute | solution.py:536
  26.9 1.1 %collective-permute-done.6.refs_1_ = bf16[512,256]{1,0:T(8,128)(2,1)S(1)} collective-permute-done((bf16[512,256]{1,0:T(8,128)(2,1)S(1)}, bf16[512,256]{1,0:T(8,128)(2,1)S(1)}, u32[]{:S(2)}, u32[]{:S(2)}) %collective-permute-start.6) | collective-permute-done | bytes 262176 | tf_op jit(solution)/shard_map/ppermute | solution.py:560
  28.1 0.1 shard_map.153
  28.1 1.6 %collective-permute-start.7 = (bf16[256,256]{1,0:T(8,128)(2,1)S(1)}, bf16[256,256]{1,0:T(8,128)(2,1)S(1)}, u32[]{:S(2)}, u32[]{:S(2)}) collective-permute-start(bf16[256,256]{1,0:T(8,128)(2,1)S(1)} %get-tuple-element.78.refs_3_), channel_id=1, source_target_pairs={{0,1},{1,0},{2,6},{3,7},{4,5},{5,4},{6,2},{7,3},{8,9},{9,8},{10,14... | collective-permute-start | bytes 393224 | tf_op jit(solution)/shard_map/ppermute | solution.py:560
  29.7 1.8 %shard_map.155.refs_3_ = f32[64,128]{1,0:T(8,128)S(1)} custom-call(f32[2,1216,128]{2,1,0:T(8,128)S(1)} %get-tuple-element.57.refs_6_.refs_4_.refs_0_, f32[2,640,128]{2,1,0:T(8,128)S(1)} %get-tuple-element.80.refs_1_, bf16[768,256]{1,0:T(8,128)(2,1)S(1)} %get-tuple-element.69.refs_2_, bf16[256,256]{1,0:T(8,128)(2,1)S(1)} %get-tuple-element.78.refs_3_), custom_call_target="tpu_custom_call" | custom-call | flops 1800000000 | tf_op jit(solution)/shard_map/pallas_call | solution.py:677
  31.5 1.8 %shard_map.154.refs_2_ = f32[64,128]{1,0:T(8,128)S(1)} custom-call(f32[2,1216,128]{2,1,0:T(8,128)S(1)} %get-tuple-element.57.refs_6_.refs_4_.refs_0_, f32[2,640,128]{2,1,0:T(8,128)S(1)} %get-tuple-element.80.refs_1_, bf16[768,256]{1,0:T(8,128)(2,1)S(1)} %get-tuple-element.69.refs_2_, bf16[256,256]{1,0:T(8,128)(2,1)S(1)} %get-tuple-element.78.refs_3_), custom_call_target="tpu_custom_call" | custom-call | flops 1800000000 | tf_op jit(solution)/shard_map/pallas_call | solution.py:677
  33.4 0.1 collective-permute-start.11
  33.5 0.1 shard_map.157
  33.5 1.1 %collective-permute-start.10 = (bf16[128,256]{1,0:T(8,128)(2,1)S(1)}, bf16[128,256]{1,0:T(8,128)(2,1)S(1)}, u32[]{:S(2)}, u32[]{:S(2)}) collective-permute-start(bf16[128,256]{1,0:T(8,128)(2,1)S(1)} %get-tuple-element.82.refs_4_), channel_id=1, source_target_pairs={{0,8},{1,9},{2,3},{3,2},{4,12},{5,13},{6,7},{7,6},{8,0},{9,1},{10,... | collective-permute-start | bytes 196616 | tf_op jit(solution)/shard_map/ppermute | solution.py:560
  34.6 0.2 shard_map.158
  34.8 0.1 collective-permute-start.8
  34.9 1.2 %collective-permute-start.9 = (bf16[48,256]{1,0:T(8,128)(2,1)S(1)}, bf16[48,256]{1,0:T(8,128)(2,1)S(1)}, u32[]{:S(2)}, u32[]{:S(2)}) collective-permute-start(bf16[48,256]{1,0:T(8,128)(2,1)S(1)} %get-tuple-element.85), channel_id=1, source_target_pairs={{0,16},{2,4},{4,2},{6,8},{8,6},{10,12},{12,10},{14,30},{30,14},{28... | collective-permute-start | bytes 73736 | tf_op jit(solution)/shard_map/ppermute | solution.py:536
  36.1 1.8 %collective-permute-done.10.refs_1_ = bf16[128,256]{1,0:T(8,128)(2,1)S(1)} collective-permute-done((bf16[128,256]{1,0:T(8,128)(2,1)S(1)}, bf16[128,256]{1,0:T(8,128)(2,1)S(1)}, u32[]{:S(2)}, u32[]{:S(2)}) %collective-permute-start.10) | collective-permute-done | bytes 65568 | tf_op jit(solution)/shard_map/ppermute | solution.py:560
  37.9 0.0 copy-start.5
  37.9 1.1 %collective-permute-start.12 = (bf16[160,256]{1,0:T(8,128)(2,1)S(1)}, bf16[160,256]{1,0:T(8,128)(2,1)S(1)}, u32[]{:S(2)}, u32[]{:S(2)}) collective-permute-start(bf16[160,256]{1,0:T(8,128)(2,1)S(1)} %shard_map.159.refs_6_.refs_0_), channel_id=1, source_target_pairs={{0,16},{1,17},{2,18},{3,19},{4,20},{5,21},{6,22},{7,23},{8,24},{9,... | collective-permute-start | bytes 245768 | tf_op jit(solution)/shard_map/ppermute | solution.py:560
  39.0 0.6 collective-permute-done.9.refs_5_
  39.6 1.2 %shard_map.160 = (bf16[768,256]{1,0:T(8,128)(2,1)}, f32[8,128]{1,0:T(8,128)S(1)}) custom-call(f32[8,128]{1,0:T(8,128)S(1)} %get-tuple-element.52.refs_0_, f32[3,8,256]{2,1,0:T(8,128)S(1)} %get-tuple-element.54.refs_1_.refs_0_.refs_8_.refs_3_, bf16[768,256]{1,0:T(8,128)(2,1)S(1)} %bitcast.11, f32[2,1024,128]{2,1,0:T(8,128)S(1)} %get-tuple-element.83.refs_4_.refs_3_, ...), custom_call_target="tpu_custom_call" | custom-call | flops 1500000000 | tf_op jit(solution)/shard_map/pallas_call | solution.py:677
  40.8 0.9 %shard_map.161 = (bf16[768,256]{1,0:T(8,128)(2,1)}, f32[8,128]{1,0:T(8,128)S(1)}) custom-call(bf16[768,256]{1,0:T(8,128)(2,1)S(1)} %bitcast.18, f32[1,256]{1,0:T(1,128)S(1)} %bitcast.20, f32[768,256]{1,0:T(8,128)S(1)} %get-tuple-element.68.refs_2_, f32[3,8,256]{2,1,0:T(8,128)S(1)} %get-tuple-element.54.refs_1_.refs_0_.refs_8_.refs_3_, ...), custom_call_target="tpu_custom_call" | custom-call | flops 1000000000 | tf_op jit(solution)/shard_map/pallas_call | solution.py:677
  41.7 2.9 %collective-permute-done.12.refs_1_ = bf16[160,256]{1,0:T(8,128)(2,1)S(1)} collective-permute-done((bf16[160,256]{1,0:T(8,128)(2,1)S(1)}, bf16[160,256]{1,0:T(8,128)(2,1)S(1)}, u32[]{:S(2)}, u32[]{:S(2)}) %collective-permute-start.12) | collective-permute-done | bytes 81952 | tf_op jit(solution)/shard_map/ppermute | solution.py:560
  44.6 13.4 %all_to_all.5.refs_0_ = bf16[8,160,256]{2,1,0:T(8,128)(2,1)S(1)} all-to-all(bf16[8,160,256]{2,1,0:T(8,128)(2,1)S(1)} %shard_map.162), channel_id=1, replica_groups=mesh['far'=2,'near'=4,'core'=2,'dp'=2] {'near','dp'}, dimensions={0} | all-to-all | bytes 1310720 | tf_op jit(solution)/shard_map/all_to_all | solution.py:855
  58.1 0.1 shard_map.163.refs_0_
  58.1 0.1 collective-permute-start.13
  58.2 1.9 %collective-permute-done.13.refs_1_ = bf16[1088,256]{1,0:T(8,128)(2,1)S(1)} collective-permute-done((bf16[1088,256]{1,0:T(8,128)(2,1)S(1)}, bf16[1088,256]{1,0:T(8,128)(2,1)S(1)}, u32[]{:S(2)}, u32[]{:S(2)}) %collective-permute-start.13) | collective-permute-done | bytes 557088 | tf_op jit(solution)/shard_map/ppermute | solution.py:540
  60.1 1.6 %shard_map.164 = (f32[256,1024]{1,0:T(8,128)}, f32[1024,256]{1,0:T(8,128)}, f32[7,7,256]{2,1,0:T(8,128)}, f32[1,256]{1,0:T(1,128)}, f32[1,256]{1,0:T(1,128)}) custom-call(bf16[1088,256]{1,0:T(8,128)(2,1)S(1)} %shard_map.163.refs_0_, bf16[1088,256]{1,0:T(8,128)(2,1)S(1)} %collective-permute-done.13.refs_1_), custom_call_target="tpu_custom_call" | custom-call | flops 1500000000 | tf_op jit(solution)/shard_map/pallas_call | solution.py:677
  (20 shorter events, 0.1 us)
Async XLA Ops:
  1.3 1.0 %copy-start.4 = (bf16[1,3,16,16,256]{4,3,2,1,0:T(8,128)(2,1)S(1)}, bf16[1,3,16,16,256]{4,3,2,1,0:T(8,128)(2,1)}, u32[]{:S(2)}) copy-start(bf16[1,3,16,16,256]{4,3,2,1,0:T(8,128)(2,1)} %param.9) | copy-start | bytes 1179652
  2.3 4.7 %copy-start.8 = (s32[3]{0:T(128)S(1)}, s32[3]{0:T(128)}, u32[]{:S(2)}) copy-start(s32[3]{0:T(128)} %param.12) | copy-start | bytes 40
  2.9 6.0 %collective-permute-start.1 = (bf16[48,256]{1,0:T(8,128)(2,1)S(1)}, bf16[48,256]{1,0:T(8,128)(2,1)S(1)}, u32[]{:S(2)}, u32[]{:S(2)}) collective-permute-start(bf16[48,256]{1,0:T(8,128)(2,1)S(1)} %get-tuple-element.55), channel_id=1, source_target_pairs={{0,16},{2,4},{4,2},{6,8},{8,6},{10,12},{12,10},{14,30},{30,14},{28... | collective-permute-start | bytes 73736 | tf_op jit(solution)/shard_map/ppermute | solution.py:536
  7.0 1.9 %collective-permute-start = (bf16[48,256]{1,0:T(8,128)(2,1)S(1)}, bf16[48,256]{1,0:T(8,128)(2,1)S(1)}, u32[]{:S(2)}, u32[]{:S(2)}) collective-permute-start(bf16[48,256]{1,0:T(8,128)(2,1)S(1)} %get-tuple-element.53.refs_3_), channel_id=1, source_target_pairs={{0,2},{2,0},{4,6},{6,4},{8,10},{10,8},{12,14},{14,12},{30,28},{28,... | collective-permute-start | bytes 73736 | tf_op jit(solution)/shard_map/ppermute | solution.py:536
  7.2 8.4 %collective-permute-start.2 = (bf16[144,256]{1,0:T(8,128)(2,1)S(1)}, bf16[144,256]{1,0:T(8,128)(2,1)S(1)}, u32[]{:S(2)}, u32[]{:S(2)}) collective-permute-start(bf16[144,256]{1,0:T(8,128)(2,1)S(1)} %get-tuple-element.56.refs_5_), channel_id=1, source_target_pairs={{0,16},{2,18},{4,20},{6,22},{8,24},{10,26},{12,28},{14,30},{30,14}... | collective-permute-start | bytes 221192 | tf_op jit(solution)/shard_map/ppermute | solution.py:536
  8.9 3.1 %copy-start.1 = (bf16[1024,256]{1,0:T(8,128)(2,1)S(1)}, bf16[1024,256]{1,0:T(8,128)(2,1)}, u32[]{:S(2)}) copy-start(bf16[1024,256]{1,0:T(8,128)(2,1)} %refs_1_.7) | copy-start | bytes 1572868
  8.9 3.1 %copy-start.2 = (bf16[1,3,16,16,256]{4,3,2,1,0:T(8,128)(2,1)S(1)}, bf16[1,3,16,16,256]{4,3,2,1,0:T(8,128)(2,1)}, u32[]{:S(2)}) copy-start(bf16[1,3,16,16,256]{4,3,2,1,0:T(8,128)(2,1)} %param.10) | copy-start | bytes 1179652
  8.9 3.1 %copy-start.3 = (f32[256]{0:T(256)S(1)}, f32[256]{0:T(256)}, u32[]{:S(2)}) copy-start(f32[256]{0:T(256)} %param.14) | copy-start | bytes 3076
  8.9 3.1 %copy-start.6 = (bf16[7,7,256]{2,1,0:T(8,128)(2,1)S(1)}, bf16[7,7,256]{2,1,0:T(8,128)(2,1)}, u32[]{:S(2)}) copy-start(bf16[7,7,256]{2,1,0:T(8,128)(2,1)} %refs_1_.9) | copy-start | bytes 75268
  9.0 3.1 %copy-start.7 = (f32[256]{0:T(256)S(1)}, f32[256]{0:T(256)}, u32[]{:S(2)}) copy-start(f32[256]{0:T(256)} %param.17) | copy-start | bytes 3076
  9.2 6.4 %collective-permute-start.3 = (bf16[48,256]{1,0:T(8,128)(2,1)S(1)}, bf16[48,256]{1,0:T(8,128)(2,1)S(1)}, u32[]{:S(2)}, u32[]{:S(2)}) collective-permute-start(bf16[48,256]{1,0:T(8,128)(2,1)S(1)} %get-tuple-element.58), channel_id=1, source_target_pairs={{0,16},{2,18},{4,20},{6,22},{8,24},{10,26},{12,28},{14,30},{30,14}... | collective-permute-start | bytes 73736 | tf_op jit(solution)/shard_map/ppermute | solution.py:536
  12.1 3.6 %copy-start = (bf16[256,1024]{1,0:T(8,128)(2,1)S(1)}, bf16[256,1024]{1,0:T(8,128)(2,1)}, u32[]{:S(2)}) copy-start(bf16[256,1024]{1,0:T(8,128)(2,1)} %refs_0_.2) | copy-start | bytes 1572868
  19.5 2.0 %collective-permute-start.4 = (bf16[1024,256]{1,0:T(8,128)(2,1)S(1)}, bf16[1024,256]{1,0:T(8,128)(2,1)S(1)}, u32[]{:S(2)}, u32[]{:S(2)}) collective-permute-start(bf16[1024,256]{1,0:T(8,128)(2,1)S(1)} %get-tuple-element.71), channel_id=1, source_target_pairs={{0,2},{2,0},{1,3},{3,1},{4,6},{6,4},{5,7},{7,5},{8,10},{10,8},{9,1... | collective-permute-start | bytes 1572872 | tf_op jit(solution)/shard_map/ppermute | solution.py:540
  21.6 6.4 %collective-permute-start.6 = (bf16[512,256]{1,0:T(8,128)(2,1)S(1)}, bf16[512,256]{1,0:T(8,128)(2,1)S(1)}, u32[]{:S(2)}, u32[]{:S(2)}) collective-permute-start(bf16[512,256]{1,0:T(8,128)(2,1)S(1)} %get-tuple-element.73.refs_3_), channel_id=1, source_target_pairs={{0,4},{1,5},{2,10},{3,11},{4,0},{5,1},{6,14},{7,15},{8,12},{9,13},... | collective-permute-start | bytes 786440 | tf_op jit(solution)/shard_map/ppermute | solution.py:560
  25.3 9.3 %collective-permute-start.5 = (bf16[192,256]{1,0:T(8,128)(2,1)S(1)}, bf16[192,256]{1,0:T(8,128)(2,1)S(1)}, u32[]{:S(2)}, u32[]{:S(2)}) collective-permute-start(bf16[192,256]{1,0:T(8,128)(2,1)S(1)} %get-tuple-element.74), channel_id=1, source_target_pairs={{0,16},{2,18},{4,20},{6,22},{8,24},{10,26},{12,28},{14,30},{30,14}... | collective-permute-start | bytes 294920 | tf_op jit(solution)/shard_map/ppermute | solution.py:536
  28.1 5.3 %collective-permute-start.7 = (bf16[256,256]{1,0:T(8,128)(2,1)S(1)}, bf16[256,256]{1,0:T(8,128)(2,1)S(1)}, u32[]{:S(2)}, u32[]{:S(2)}) collective-permute-start(bf16[256,256]{1,0:T(8,128)(2,1)S(1)} %get-tuple-element.78.refs_3_), channel_id=1, source_target_pairs={{0,1},{1,0},{2,6},{3,7},{4,5},{5,4},{6,2},{7,3},{8,9},{9,8},{10,14... | collective-permute-start | bytes 393224 | tf_op jit(solution)/shard_map/ppermute | solution.py:560
  33.4 2.7 %collective-permute-start.11 = (bf16[64,256]{1,0:T(8,128)(2,1)S(1)}, bf16[64,256]{1,0:T(8,128)(2,1)S(1)}, u32[]{:S(2)}, u32[]{:S(2)}) collective-permute-start(bf16[64,256]{1,0:T(8,128)(2,1)S(1)} %get-tuple-element.87), channel_id=1, source_target_pairs={{0,2},{2,0},{1,3},{3,1},{4,6},{6,4},{5,7},{7,5},{8,10},{10,8},{9,1... | collective-permute-start | bytes 98312 | tf_op jit(solution)/shard_map/ppermute | solution.py:540
  33.5 4.3 %collective-permute-start.10 = (bf16[128,256]{1,0:T(8,128)(2,1)S(1)}, bf16[128,256]{1,0:T(8,128)(2,1)S(1)}, u32[]{:S(2)}, u32[]{:S(2)}) collective-permute-start(bf16[128,256]{1,0:T(8,128)(2,1)S(1)} %get-tuple-element.82.refs_4_), channel_id=1, source_target_pairs={{0,8},{1,9},{2,3},{3,2},{4,12},{5,13},{6,7},{7,6},{8,0},{9,1},{10,... | collective-permute-start | bytes 196616 | tf_op jit(solution)/shard_map/ppermute | solution.py:560
  34.8 4.3 %collective-permute-start.8 = (bf16[48,256]{1,0:T(8,128)(2,1)S(1)}, bf16[48,256]{1,0:T(8,128)(2,1)S(1)}, u32[]{:S(2)}, u32[]{:S(2)}) collective-permute-start(bf16[48,256]{1,0:T(8,128)(2,1)S(1)} %get-tuple-element.84), channel_id=1, source_target_pairs={{0,2},{2,0},{4,6},{6,4},{8,10},{10,8},{12,14},{14,12},{30,28},{28,... | collective-permute-start | bytes 73736 | tf_op jit(solution)/shard_map/ppermute | solution.py:536
  34.9 4.8 %collective-permute-start.9 = (bf16[48,256]{1,0:T(8,128)(2,1)S(1)}, bf16[48,256]{1,0:T(8,128)(2,1)S(1)}, u32[]{:S(2)}, u32[]{:S(2)}) collective-permute-start(bf16[48,256]{1,0:T(8,128)(2,1)S(1)} %get-tuple-element.85), channel_id=1, source_target_pairs={{0,16},{2,4},{4,2},{6,8},{8,6},{10,12},{12,10},{14,30},{30,14},{28... | collective-permute-start | bytes 73736 | tf_op jit(solution)/shard_map/ppermute | solution.py:536
  37.9 2.9 %copy-start.5 = (bf16[1,3,16,16,256]{4,3,2,1,0:T(8,128)(2,1)S(1)}, bf16[1,3,16,16,256]{4,3,2,1,0:T(8,128)(2,1)}, u32[]{:S(2)}) copy-start(bf16[1,3,16,16,256]{4,3,2,1,0:T(8,128)(2,1)} %param.9) | copy-start | bytes 1179652
  37.9 6.7 %collective-permute-start.12 = (bf16[160,256]{1,0:T(8,128)(2,1)S(1)}, bf16[160,256]{1,0:T(8,128)(2,1)S(1)}, u32[]{:S(2)}, u32[]{:S(2)}) collective-permute-start(bf16[160,256]{1,0:T(8,128)(2,1)S(1)} %shard_map.159.refs_6_.refs_0_), channel_id=1, source_target_pairs={{0,16},{1,17},{2,18},{3,19},{4,20},{5,21},{6,22},{7,23},{8,24},{9,... | collective-permute-start | bytes 245768 | tf_op jit(solution)/shard_map/ppermute | solution.py:560
  58.1 2.0 %collective-permute-start.13 = (bf16[1088,256]{1,0:T(8,128)(2,1)S(1)}, bf16[1088,256]{1,0:T(8,128)(2,1)S(1)}, u32[]{:S(2)}, u32[]{:S(2)}) collective-permute-start(bf16[1088,256]{1,0:T(8,128)(2,1)S(1)} %shard_map.163.refs_0_), channel_id=1, source_target_pairs={{0,2},{2,0},{1,3},{3,1},{4,6},{6,4},{5,7},{7,5},{8,10},{10,8},{9,1... | collective-permute-start | bytes 1671176 | tf_op jit(solution)/shard_map/ppermute | solution.py:540

commit v12 on v11

--- a/solution.py
+++ b/solution.py
@@ -401,7 +401,7 @@
             return tuple(sums)
 
         blank = tuple(jnp.zeros((8, LANES), F32) for _ in range(KSIZE))
-        sums = lax.fori_loop(0, TILE, one_row, blank, unroll=2)
+        sums = lax.fori_loop(0, TILE, one_row, blank, unroll=8)
         for shift in range(KSIZE):
             small[pl.ds(above * KSIZE + shift, 1), :] = jnp.sum(sums[shift], axis=0, keepdims=True)
 

time: 62 us -> 60 us (0.968)
  blocking collectives: 13.4 us -> 12.1 us
  Pallas kernels: 20.9 us -> 20.2 us
    all_to_all x1, blocking collectives: 13.4 us -> 12.1 us  [shards(): came = lax.all_to_all(payload, ('near', 'dp'), 0, 0, tiled=True)]
    pallas_call x21, Pallas kernels: 20.9 us -> 20.2 us  [call(): pl.pallas_call(body, out_shape=[jax.ShapeDtypeStruct(*out) for out in out...]
  transfers between devices with their start and end apart: 14 -> 14, of which waited for: 6 -> 7; matrix products, arithmetic and copies ran while one was open for 0% -> 0% of each run, Pallas kernels for 24% -> 23%
where the time goes in v12:
time: 60 us; the launch traced here: 59.8 us
  Pallas kernels  20.2 us (34%)
  starting transfers between devices  15.7 us (26%)
  blocking collectives  12.1 us (20%)
  waiting for transfers between devices  9.14 us (15%)
  between operations  1.52 us (3%)
  local copies, waits for them, and re-layouts  1.04 us (2%)
    pallas_call x21, Pallas kernels, call(): pl.pallas_call(body, out_shape=[jax.ShapeDtypeStruct(*out) for out in out...  20.2 us
    all_to_all x1, blocking collectives, shards(): came = lax.all_to_all(payload, ('near', 'dp'), 0, 0, tiled=True)  12.1 us
    ppermute x7, starting transfers between devices, swap(): return lax.ppermute(block, TILES, pairs_of(kind))  11.6 us
    ppermute x4, waiting for transfers between devices, bit_swap(): return lax.ppermute(block, TILES + ('dp',), pairs)  5.81 us
    ppermute x4, starting transfers between devices, bit_swap(): return lax.ppermute(block, TILES + ('dp',), pairs)  3.95 us
    ppermute x3, waiting for transfers between devices, core_swap(): return lax.ppermute(block, 'core', [(0, 1), (1, 0)])  2.71 us
  transfers between devices with their start and end apart: 14, of which 7 were waited for; matrix products, arithmetic and copies ran while one was open for 0% of the time, Pallas kernels for 23%

profile of v12, /device:TPU:0, one launch (start us, length us, event | category | flops | bytes accessed | tf_op | source)
XLA Modules:
  0.0 59.8 jit_solution(8300891684377946960)
XLA Ops:
  1.3 0.0 copy-start.4
  1.3 1.0 %copy-done.4 = bf16[1,3,16,16,256]{4,3,2,1,0:T(8,128)(2,1)S(1)} copy-done((bf16[1,3,16,16,256]{4,3,2,1,0:T(8,128)(2,1)S(1)}, bf16[1,3,16,16,256]{4,3,2,1,0:T(8,128)(2,1)}, u32[]{:S(2)}) %copy-start.4) | copy-done | bytes 393240
  2.3 0.6 shard_map.144
  2.9 4.1 %collective-permute-start.1 = (bf16[48,256]{1,0:T(8,128)(2,1)S(1)}, bf16[48,256]{1,0:T(8,128)(2,1)S(1)}, u32[]{:S(2)}, u32[]{:S(2)}) collective-permute-start(bf16[48,256]{1,0:T(8,128)(2,1)S(1)} %get-tuple-element.55), channel_id=1, source_target_pairs={{0,16},{2,4},{4,2},{6,8},{8,6},{10,12},{12,10},{14,30},{30,14},{28... | collective-permute-start | bytes 73736 | tf_op jit(solution)/shard_map/ppermute | solution.py:536
  7.0 0.0 collective-permute-start
  7.0 0.3 shard_map.145
  7.2 1.7 %collective-permute-start.2 = (bf16[144,256]{1,0:T(8,128)(2,1)S(1)}, bf16[144,256]{1,0:T(8,128)(2,1)S(1)}, u32[]{:S(2)}, u32[]{:S(2)}) collective-permute-start(bf16[144,256]{1,0:T(8,128)(2,1)S(1)} %get-tuple-element.56.refs_5_), channel_id=1, source_target_pairs={{0,16},{2,18},{4,20},{6,22},{8,24},{10,26},{12,28},{14,30},{30,14}... | collective-permute-start | bytes 221192 | tf_op jit(solution)/shard_map/ppermute | solution.py:536
  8.9 0.0 collective-permute-done.1.refs_4_
  8.9 0.0 copy-start.2
  8.9 0.0 copy-start.3
  8.9 0.0 copy-start.6
  9.0 0.0 copy-start.7
  9.0 0.2 shard_map.146
  9.2 2.8 %collective-permute-start.3 = (bf16[48,256]{1,0:T(8,128)(2,1)S(1)}, bf16[48,256]{1,0:T(8,128)(2,1)S(1)}, u32[]{:S(2)}, u32[]{:S(2)}) collective-permute-start(bf16[48,256]{1,0:T(8,128)(2,1)S(1)} %get-tuple-element.58), channel_id=1, source_target_pairs={{0,16},{2,18},{4,20},{6,22},{8,24},{10,26},{12,28},{14,30},{30,14}... | collective-permute-start | bytes 73736 | tf_op jit(solution)/shard_map/ppermute | solution.py:536
  12.1 0.0 copy-start
  12.1 3.6 %shard_map.147 = (bf16[768,256]{1,0:T(8,128)(2,1)S(1)}, f32[768,256]{1,0:T(8,128)S(1)}, f32[768,128]{1,0:T(8,128)S(1)}, bf16[256,768]{1,0:T(8,128)(2,1)S(1)}, f32[768,1024]{1,0:T(8,128)S(1)}) custom-call(f32[3,8,256]{2,1,0:T(8,128)S(1)} %get-tuple-element.54.refs_1_.refs_0_.refs_8_.refs_3_, bf16[7,7,256]{2,1,0:T(8,128)(2,1)S(1)} %copy-done.6, ...), custom_call_target="tpu_custom_call" | custom-call | flops 5000000000 | tf_op jit(solution)/shard_map/pallas_call | solution.py:677
  15.7 3.8 %shard_map.148 = (f32[1024,256]{1,0:T(8,128)S(1)}, bf16[1024,256]{1,0:T(8,128)(2,1)S(1)}, bf16[768,1024]{1,0:T(8,128)(2,1)S(1)}, bf16[768,1024]{1,0:T(8,128)(2,1...) custom-call(f32[8,128]{1,0:T(8,128)S(1)} %get-tuple-element.52.refs_0_, ...), custom_call_target="tpu_custom_call" | custom-call | flops 5000000000 | tf_op jit(solution)/shard_map/pallas_call | solution.py:677
  19.5 0.1 collective-permute-start.4
  19.6 1.1 %shard_map.149 = (bf16[768,256]{1,0:T(8,128)(2,1)S(1)}, f32[768,256]{1,0:T(8,128)S(1)}, f32[8,256]{1,0:T(8,128)S(1)}, f32[8,256]{1,0:T(8,128)S(1)}) custom-call(bf16[256,1024]{1,0:T(8,128)(2,1)S(1)} %copy-done, bf16[1024,256]{1,0:T(8,128)(2,1)S(1)} %copy-done.1, f32[1,256]{1,0:T(1,128)S(1)} %bitcast.14, bf16[768,1024]{1,0:T(8,128)(2,1)S(1)} %get-tuple-element.64.refs_3_, ...), custom_call_target="tpu_custom_call" | custom-call | flops 1300000000 | tf_op jit(solution)/shard_map/pallas_call | solution.py:677
  20.7 0.8 %collective-permute-done.4.refs_1_ = bf16[1024,256]{1,0:T(8,128)(2,1)S(1)} collective-permute-done((bf16[1024,256]{1,0:T(8,128)(2,1)S(1)}, bf16[1024,256]{1,0:T(8,128)(2,1)S(1)}, u32[]{:S(2)}, u32[]{:S(2)}) %collective-permute-start.4) | collective-permute-done | bytes 524320 | tf_op jit(solution)/shard_map/ppermute | solution.py:540
  21.5 0.2 shard_map.150
  21.6 0.2 collective-permute-start.6
  21.8 1.6 %shard_map.151.refs_3_.refs_4_.refs_2_ = f32[1216,128]{1,0:T(8,128)S(1)} custom-call(f32[8,128]{1,0:T(8,128)S(1)} %get-tuple-element.52.refs_0_, bf16[7,7,256]{2,1,0:T(8,128)(2,1)S(1)} %copy-done.6, bf16[768,256]{1,0:T(8,128)(2,1)S(1)} %get-tuple-element.69.refs_2_, bf16[512,256]{1,0:T(8,128)(2,1)S(1)} %get-tuple-element.73.refs_3_), custom_call_target="tpu_custom_call" | custom-call | flops 2000000000 | tf_op jit(solution)/shard_map/pallas_call | solution.py:677
  23.4 1.9 %shard_map.152 = (f32[1216,128]{1,0:T(8,128)S(1)}, bf16[192,256]{1,0:T(8,128)(2,1)S(1)}) custom-call(f32[8,128]{1,0:T(8,128)S(1)} %get-tuple-element.52.refs_0_, bf16[7,7,256]{2,1,0:T(8,128)(2,1)S(1)} %copy-done.6, bf16[768,256]{1,0:T(8,128)(2,1)S(1)} %get-tuple-element.69.refs_2_, f32[1216,128]{1,0:T(8,128)S(1)} %shard_map.151.refs_3_.refs_4_.refs_2_, ...), custom_call_target="tpu_custom_call" | custom-call | flops 2000000000 | tf_op jit(solution)/shard_map/pallas_call | solution.py:677
  25.3 1.7 %collective-permute-start.5 = (bf16[192,256]{1,0:T(8,128)(2,1)S(1)}, bf16[192,256]{1,0:T(8,128)(2,1)S(1)}, u32[]{:S(2)}, u32[]{:S(2)}) collective-permute-start(bf16[192,256]{1,0:T(8,128)(2,1)S(1)} %get-tuple-element.74), channel_id=1, source_target_pairs={{0,16},{2,18},{4,20},{6,22},{8,24},{10,26},{12,28},{14,30},{30,14}... | collective-permute-start | bytes 294920 | tf_op jit(solution)/shard_map/ppermute | solution.py:536
  26.9 1.1 %collective-permute-done.6.refs_1_ = bf16[512,256]{1,0:T(8,128)(2,1)S(1)} collective-permute-done((bf16[512,256]{1,0:T(8,128)(2,1)S(1)}, bf16[512,256]{1,0:T(8,128)(2,1)S(1)}, u32[]{:S(2)}, u32[]{:S(2)}) %collective-permute-start.6) | collective-permute-done | bytes 262176 | tf_op jit(solution)/shard_map/ppermute | solution.py:560
  28.1 0.1 shard_map.153
  28.1 1.6 %collective-permute-start.7 = (bf16[256,256]{1,0:T(8,128)(2,1)S(1)}, bf16[256,256]{1,0:T(8,128)(2,1)S(1)}, u32[]{:S(2)}, u32[]{:S(2)}) collective-permute-start(bf16[256,256]{1,0:T(8,128)(2,1)S(1)} %get-tuple-element.78.refs_3_), channel_id=1, source_target_pairs={{0,1},{1,0},{2,6},{3,7},{4,5},{5,4},{6,2},{7,3},{8,9},{9,8},{10,14... | collective-permute-start | bytes 393224 | tf_op jit(solution)/shard_map/ppermute | solution.py:560
  29.7 1.5 %shard_map.155.refs_3_ = f32[64,128]{1,0:T(8,128)S(1)} custom-call(f32[2,1216,128]{2,1,0:T(8,128)S(1)} %get-tuple-element.57.refs_6_.refs_4_.refs_0_, f32[2,640,128]{2,1,0:T(8,128)S(1)} %get-tuple-element.80.refs_1_, bf16[768,256]{1,0:T(8,128)(2,1)S(1)} %get-tuple-element.69.refs_2_, bf16[256,256]{1,0:T(8,128)(2,1)S(1)} %get-tuple-element.78.refs_3_), custom_call_target="tpu_custom_call" | custom-call | flops 1800000000 | tf_op jit(solution)/shard_map/pallas_call | solution.py:677
  31.2 1.5 %shard_map.154.refs_2_ = f32[64,128]{1,0:T(8,128)S(1)} custom-call(f32[2,1216,128]{2,1,0:T(8,128)S(1)} %get-tuple-element.57.refs_6_.refs_4_.refs_0_, f32[2,640,128]{2,1,0:T(8,128)S(1)} %get-tuple-element.80.refs_1_, bf16[768,256]{1,0:T(8,128)(2,1)S(1)} %get-tuple-element.69.refs_2_, bf16[256,256]{1,0:T(8,128)(2,1)S(1)} %get-tuple-element.78.refs_3_), custom_call_target="tpu_custom_call" | custom-call | flops 1800000000 | tf_op jit(solution)/shard_map/pallas_call | solution.py:677
  32.7 0.1 collective-permute-start.11
  32.8 0.4 collective-permute-done.7.refs_1_
  33.2 1.1 %collective-permute-start.10 = (bf16[128,256]{1,0:T(8,128)(2,1)S(1)}, bf16[128,256]{1,0:T(8,128)(2,1)S(1)}, u32[]{:S(2)}, u32[]{:S(2)}) collective-permute-start(bf16[128,256]{1,0:T(8,128)(2,1)S(1)} %get-tuple-element.82.refs_4_), channel_id=1, source_target_pairs={{0,8},{1,9},{2,3},{3,2},{4,12},{5,13},{6,7},{7,6},{8,0},{9,1},{10,... | collective-permute-start | bytes 196616 | tf_op jit(solution)/shard_map/ppermute | solution.py:560
  34.3 0.2 shard_map.158
  34.5 0.1 collective-permute-start.8
  34.5 1.2 %collective-permute-start.9 = (bf16[48,256]{1,0:T(8,128)(2,1)S(1)}, bf16[48,256]{1,0:T(8,128)(2,1)S(1)}, u32[]{:S(2)}, u32[]{:S(2)}) collective-permute-start(bf16[48,256]{1,0:T(8,128)(2,1)S(1)} %get-tuple-element.85), channel_id=1, source_target_pairs={{0,16},{2,4},{4,2},{6,8},{8,6},{10,12},{12,10},{14,30},{30,14},{28... | collective-permute-start | bytes 73736 | tf_op jit(solution)/shard_map/ppermute | solution.py:536
  35.8 1.8 %collective-permute-done.10.refs_1_ = bf16[128,256]{1,0:T(8,128)(2,1)S(1)} collective-permute-done((bf16[128,256]{1,0:T(8,128)(2,1)S(1)}, bf16[128,256]{1,0:T(8,128)(2,1)S(1)}, u32[]{:S(2)}, u32[]{:S(2)}) %collective-permute-start.10) | collective-permute-done | bytes 65568 | tf_op jit(solution)/shard_map/ppermute | solution.py:560
  37.6 0.0 copy-start.5
  37.6 1.1 %collective-permute-start.12 = (bf16[160,256]{1,0:T(8,128)(2,1)S(1)}, bf16[160,256]{1,0:T(8,128)(2,1)S(1)}, u32[]{:S(2)}, u32[]{:S(2)}) collective-permute-start(bf16[160,256]{1,0:T(8,128)(2,1)S(1)} %shard_map.159.refs_6_.refs_0_), channel_id=1, source_target_pairs={{0,16},{1,17},{2,18},{3,19},{4,20},{5,21},{6,22},{7,23},{8,24},{9,... | collective-permute-start | bytes 245768 | tf_op jit(solution)/shard_map/ppermute | solution.py:560
  38.7 0.6 collective-permute-done.9.refs_5_
  39.3 1.2 %shard_map.160 = (bf16[768,256]{1,0:T(8,128)(2,1)}, f32[8,128]{1,0:T(8,128)S(1)}) custom-call(f32[8,128]{1,0:T(8,128)S(1)} %get-tuple-element.52.refs_0_, f32[3,8,256]{2,1,0:T(8,128)S(1)} %get-tuple-element.54.refs_1_.refs_0_.refs_8_.refs_3_, bf16[768,256]{1,0:T(8,128)(2,1)S(1)} %bitcast.11, f32[2,1024,128]{2,1,0:T(8,128)S(1)} %get-tuple-element.83.refs_4_.refs_3_, ...), custom_call_target="tpu_custom_call" | custom-call | flops 1500000000 | tf_op jit(solution)/shard_map/pallas_call | solution.py:677
  40.5 0.9 %shard_map.161 = (bf16[768,256]{1,0:T(8,128)(2,1)}, f32[8,128]{1,0:T(8,128)S(1)}) custom-call(bf16[768,256]{1,0:T(8,128)(2,1)S(1)} %bitcast.18, f32[1,256]{1,0:T(1,128)S(1)} %bitcast.20, f32[768,256]{1,0:T(8,128)S(1)} %get-tuple-element.68.refs_2_, f32[3,8,256]{2,1,0:T(8,128)S(1)} %get-tuple-element.54.refs_1_.refs_0_.refs_8_.refs_3_, ...), custom_call_target="tpu_custom_call" | custom-call | flops 1000000000 | tf_op jit(solution)/shard_map/pallas_call | solution.py:677
  41.4 2.5 %collective-permute-done.12.refs_1_ = bf16[160,256]{1,0:T(8,128)(2,1)S(1)} collective-permute-done((bf16[160,256]{1,0:T(8,128)(2,1)S(1)}, bf16[160,256]{1,0:T(8,128)(2,1)S(1)}, u32[]{:S(2)}, u32[]{:S(2)}) %collective-permute-start.12) | collective-permute-done | bytes 81952 | tf_op jit(solution)/shard_map/ppermute | solution.py:560
  43.9 12.1 %all_to_all.5.refs_0_ = bf16[8,160,256]{2,1,0:T(8,128)(2,1)S(1)} all-to-all(bf16[8,160,256]{2,1,0:T(8,128)(2,1)S(1)} %shard_map.162), channel_id=1, replica_groups=mesh['far'=2,'near'=4,'core'=2,'dp'=2] {'near','dp'}, dimensions={0} | all-to-all | bytes 1310720 | tf_op jit(solution)/shard_map/all_to_all | solution.py:855
  56.1 0.1 shard_map.163.refs_0_
  56.1 0.1 collective-permute-start.13
  56.2 1.9 %collective-permute-done.13.refs_1_ = bf16[1088,256]{1,0:T(8,128)(2,1)S(1)} collective-permute-done((bf16[1088,256]{1,0:T(8,128)(2,1)S(1)}, bf16[1088,256]{1,0:T(8,128)(2,1)S(1)}, u32[]{:S(2)}, u32[]{:S(2)}) %collective-permute-start.13) | collective-permute-done | bytes 557088 | tf_op jit(solution)/shard_map/ppermute | solution.py:540
  58.1 1.6 %shard_map.164 = (f32[256,1024]{1,0:T(8,128)}, f32[1024,256]{1,0:T(8,128)}, f32[7,7,256]{2,1,0:T(8,128)}, f32[1,256]{1,0:T(1,128)}, f32[1,256]{1,0:T(1,128)}) custom-call(bf16[1088,256]{1,0:T(8,128)(2,1)S(1)} %shard_map.163.refs_0_, bf16[1088,256]{1,0:T(8,128)(2,1)S(1)} %collective-permute-done.13.refs_1_), custom_call_target="tpu_custom_call" | custom-call | flops 1500000000 | tf_op jit(solution)/shard_map/pallas_call | solution.py:677
  (20 shorter events, 0.2 us)
Async XLA Ops:
  1.3 1.0 %copy-start.4 = (bf16[1,3,16,16,256]{4,3,2,1,0:T(8,128)(2,1)S(1)}, bf16[1,3,16,16,256]{4,3,2,1,0:T(8,128)(2,1)}, u32[]{:S(2)}) copy-start(bf16[1,3,16,16,256]{4,3,2,1,0:T(8,128)(2,1)} %param.9) | copy-start | bytes 1179652
  2.3 4.7 %copy-start.8 = (s32[3]{0:T(128)S(1)}, s32[3]{0:T(128)}, u32[]{:S(2)}) copy-start(s32[3]{0:T(128)} %param.12) | copy-start | bytes 40
  2.9 6.0 %collective-permute-start.1 = (bf16[48,256]{1,0:T(8,128)(2,1)S(1)}, bf16[48,256]{1,0:T(8,128)(2,1)S(1)}, u32[]{:S(2)}, u32[]{:S(2)}) collective-permute-start(bf16[48,256]{1,0:T(8,128)(2,1)S(1)} %get-tuple-element.55), channel_id=1, source_target_pairs={{0,16},{2,4},{4,2},{6,8},{8,6},{10,12},{12,10},{14,30},{30,14},{28... | collective-permute-start | bytes 73736 | tf_op jit(solution)/shard_map/ppermute | solution.py:536
  7.0 1.9 %collective-permute-start = (bf16[48,256]{1,0:T(8,128)(2,1)S(1)}, bf16[48,256]{1,0:T(8,128)(2,1)S(1)}, u32[]{:S(2)}, u32[]{:S(2)}) collective-permute-start(bf16[48,256]{1,0:T(8,128)(2,1)S(1)} %get-tuple-element.53.refs_3_), channel_id=1, source_target_pairs={{0,2},{2,0},{4,6},{6,4},{8,10},{10,8},{12,14},{14,12},{30,28},{28,... | collective-permute-start | bytes 73736 | tf_op jit(solution)/shard_map/ppermute | solution.py:536
  7.2 8.4 %collective-permute-start.2 = (bf16[144,256]{1,0:T(8,128)(2,1)S(1)}, bf16[144,256]{1,0:T(8,128)(2,1)S(1)}, u32[]{:S(2)}, u32[]{:S(2)}) collective-permute-start(bf16[144,256]{1,0:T(8,128)(2,1)S(1)} %get-tuple-element.56.refs_5_), channel_id=1, source_target_pairs={{0,16},{2,18},{4,20},{6,22},{8,24},{10,26},{12,28},{14,30},{30,14}... | collective-permute-start | bytes 221192 | tf_op jit(solution)/shard_map/ppermute | solution.py:536
  8.9 3.1 %copy-start.1 = (bf16[1024,256]{1,0:T(8,128)(2,1)S(1)}, bf16[1024,256]{1,0:T(8,128)(2,1)}, u32[]{:S(2)}) copy-start(bf16[1024,256]{1,0:T(8,128)(2,1)} %refs_1_.7) | copy-start | bytes 1572868
  8.9 3.1 %copy-start.2 = (bf16[1,3,16,16,256]{4,3,2,1,0:T(8,128)(2,1)S(1)}, bf16[1,3,16,16,256]{4,3,2,1,0:T(8,128)(2,1)}, u32[]{:S(2)}) copy-start(bf16[1,3,16,16,256]{4,3,2,1,0:T(8,128)(2,1)} %param.10) | copy-start | bytes 1179652
  8.9 3.1 %copy-start.3 = (f32[256]{0:T(256)S(1)}, f32[256]{0:T(256)}, u32[]{:S(2)}) copy-start(f32[256]{0:T(256)} %param.14) | copy-start | bytes 3076
  8.9 3.1 %copy-start.6 = (bf16[7,7,256]{2,1,0:T(8,128)(2,1)S(1)}, bf16[7,7,256]{2,1,0:T(8,128)(2,1)}, u32[]{:S(2)}) copy-start(bf16[7,7,256]{2,1,0:T(8,128)(2,1)} %refs_1_.9) | copy-start | bytes 75268
  9.0 3.1 %copy-start.7 = (f32[256]{0:T(256)S(1)}, f32[256]{0:T(256)}, u32[]{:S(2)}) copy-start(f32[256]{0:T(256)} %param.17) | copy-start | bytes 3076
  9.2 6.4 %collective-permute-start.3 = (bf16[48,256]{1,0:T(8,128)(2,1)S(1)}, bf16[48,256]{1,0:T(8,128)(2,1)S(1)}, u32[]{:S(2)}, u32[]{:S(2)}) collective-permute-start(bf16[48,256]{1,0:T(8,128)(2,1)S(1)} %get-tuple-element.58), channel_id=1, source_target_pairs={{0,16},{2,18},{4,20},{6,22},{8,24},{10,26},{12,28},{14,30},{30,14}... | collective-permute-start | bytes 73736 | tf_op jit(solution)/shard_map/ppermute | solution.py:536
  12.1 3.6 %copy-start = (bf16[256,1024]{1,0:T(8,128)(2,1)S(1)}, bf16[256,1024]{1,0:T(8,128)(2,1)}, u32[]{:S(2)}) copy-start(bf16[256,1024]{1,0:T(8,128)(2,1)} %refs_0_.2) | copy-start | bytes 1572868
  19.5 2.0 %collective-permute-start.4 = (bf16[1024,256]{1,0:T(8,128)(2,1)S(1)}, bf16[1024,256]{1,0:T(8,128)(2,1)S(1)}, u32[]{:S(2)}, u32[]{:S(2)}) collective-permute-start(bf16[1024,256]{1,0:T(8,128)(2,1)S(1)} %get-tuple-element.71), channel_id=1, source_target_pairs={{0,2},{2,0},{1,3},{3,1},{4,6},{6,4},{5,7},{7,5},{8,10},{10,8},{9,1... | collective-permute-start | bytes 1572872 | tf_op jit(solution)/shard_map/ppermute | solution.py:540
  21.6 6.4 %collective-permute-start.6 = (bf16[512,256]{1,0:T(8,128)(2,1)S(1)}, bf16[512,256]{1,0:T(8,128)(2,1)S(1)}, u32[]{:S(2)}, u32[]{:S(2)}) collective-permute-start(bf16[512,256]{1,0:T(8,128)(2,1)S(1)} %get-tuple-element.73.refs_3_), channel_id=1, source_target_pairs={{0,4},{1,5},{2,10},{3,11},{4,0},{5,1},{6,14},{7,15},{8,12},{9,13},... | collective-permute-start | bytes 786440 | tf_op jit(solution)/shard_map/ppermute | solution.py:560
  25.3 9.0 %collective-permute-start.5 = (bf16[192,256]{1,0:T(8,128)(2,1)S(1)}, bf16[192,256]{1,0:T(8,128)(2,1)S(1)}, u32[]{:S(2)}, u32[]{:S(2)}) collective-permute-start(bf16[192,256]{1,0:T(8,128)(2,1)S(1)} %get-tuple-element.74), channel_id=1, source_target_pairs={{0,16},{2,18},{4,20},{6,22},{8,24},{10,26},{12,28},{14,30},{30,14}... | collective-permute-start | bytes 294920 | tf_op jit(solution)/shard_map/ppermute | solution.py:536
  28.1 5.0 %collective-permute-start.7 = (bf16[256,256]{1,0:T(8,128)(2,1)S(1)}, bf16[256,256]{1,0:T(8,128)(2,1)S(1)}, u32[]{:S(2)}, u32[]{:S(2)}) collective-permute-start(bf16[256,256]{1,0:T(8,128)(2,1)S(1)} %get-tuple-element.78.refs_3_), channel_id=1, source_target_pairs={{0,1},{1,0},{2,6},{3,7},{4,5},{5,4},{6,2},{7,3},{8,9},{9,8},{10,14... | collective-permute-start | bytes 393224 | tf_op jit(solution)/shard_map/ppermute | solution.py:560
  32.7 3.0 %collective-permute-start.11 = (bf16[64,256]{1,0:T(8,128)(2,1)S(1)}, bf16[64,256]{1,0:T(8,128)(2,1)S(1)}, u32[]{:S(2)}, u32[]{:S(2)}) collective-permute-start(bf16[64,256]{1,0:T(8,128)(2,1)S(1)} %get-tuple-element.87), channel_id=1, source_target_pairs={{0,2},{2,0},{1,3},{3,1},{4,6},{6,4},{5,7},{7,5},{8,10},{10,8},{9,1... | collective-permute-start | bytes 98312 | tf_op jit(solution)/shard_map/ppermute | solution.py:540
  33.2 4.3 %collective-permute-start.10 = (bf16[128,256]{1,0:T(8,128)(2,1)S(1)}, bf16[128,256]{1,0:T(8,128)(2,1)S(1)}, u32[]{:S(2)}, u32[]{:S(2)}) collective-permute-start(bf16[128,256]{1,0:T(8,128)(2,1)S(1)} %get-tuple-element.82.refs_4_), channel_id=1, source_target_pairs={{0,8},{1,9},{2,3},{3,2},{4,12},{5,13},{6,7},{7,6},{8,0},{9,1},{10,... | collective-permute-start | bytes 196616 | tf_op jit(solution)/shard_map/ppermute | solution.py:560
  34.5 4.3 %collective-permute-start.8 = (bf16[48,256]{1,0:T(8,128)(2,1)S(1)}, bf16[48,256]{1,0:T(8,128)(2,1)S(1)}, u32[]{:S(2)}, u32[]{:S(2)}) collective-permute-start(bf16[48,256]{1,0:T(8,128)(2,1)S(1)} %get-tuple-element.84), channel_id=1, source_target_pairs={{0,2},{2,0},{4,6},{6,4},{8,10},{10,8},{12,14},{14,12},{30,28},{28,... | collective-permute-start | bytes 73736 | tf_op jit(solution)/shard_map/ppermute | solution.py:536
  34.5 4.8 %collective-permute-start.9 = (bf16[48,256]{1,0:T(8,128)(2,1)S(1)}, bf16[48,256]{1,0:T(8,128)(2,1)S(1)}, u32[]{:S(2)}, u32[]{:S(2)}) collective-permute-start(bf16[48,256]{1,0:T(8,128)(2,1)S(1)} %get-tuple-element.85), channel_id=1, source_target_pairs={{0,16},{2,4},{4,2},{6,8},{8,6},{10,12},{12,10},{14,30},{30,14},{28... | collective-permute-start | bytes 73736 | tf_op jit(solution)/shard_map/ppermute | solution.py:536
  37.6 2.9 %copy-start.5 = (bf16[1,3,16,16,256]{4,3,2,1,0:T(8,128)(2,1)S(1)}, bf16[1,3,16,16,256]{4,3,2,1,0:T(8,128)(2,1)}, u32[]{:S(2)}) copy-start(bf16[1,3,16,16,256]{4,3,2,1,0:T(8,128)(2,1)} %param.9) | copy-start | bytes 1179652
  37.6 6.3 %collective-permute-start.12 = (bf16[160,256]{1,0:T(8,128)(2,1)S(1)}, bf16[160,256]{1,0:T(8,128)(2,1)S(1)}, u32[]{:S(2)}, u32[]{:S(2)}) collective-permute-start(bf16[160,256]{1,0:T(8,128)(2,1)S(1)} %shard_map.159.refs_6_.refs_0_), channel_id=1, source_target_pairs={{0,16},{1,17},{2,18},{3,19},{4,20},{5,21},{6,22},{7,23},{8,24},{9,... | collective-permute-start | bytes 245768 | tf_op jit(solution)/shard_map/ppermute | solution.py:560
  56.1 2.0 %collective-permute-start.13 = (bf16[1088,256]{1,0:T(8,128)(2,1)S(1)}, bf16[1088,256]{1,0:T(8,128)(2,1)S(1)}, u32[]{:S(2)}, u32[]{:S(2)}) collective-permute-start(bf16[1088,256]{1,0:T(8,128)(2,1)S(1)} %shard_map.163.refs_0_), channel_id=1, source_target_pairs={{0,2},{2,0},{1,3},{3,1},{4,6},{6,4},{5,7},{7,5},{8,10},{10,8},{9,1... | collective-permute-start | bytes 1671176 | tf_op jit(solution)/shard_map/ppermute | solution.py:540

commit v13 on v12

--- a/solution.py
+++ b/solution.py
@@ -226,7 +226,7 @@
                     convolved[part, pl.ds(start, 8, stride=run), :] = sums[which][at]
         return carry
 
-    lax.fori_loop(0, rows // pair, two_rows, 0)
+    lax.fori_loop(0, rows // pair, two_rows, 0, unroll=2)
 
 
 def normalise(shape, rows, first_row, convolved, gain, normed, yhat, inverse):
@@ -247,7 +247,7 @@
                 normed[out, shape.lanes(part)] = (value * gain[:, shape.lanes(part)]).astype(BF16)
         return carry
 
-    lax.fori_loop(0, rows, one_row, 0, unroll=4)
+    lax.fori_loop(0, rows, one_row, 0, unroll=min(rows, 6))
 
 
 def early_kernel(
@@ -446,7 +446,7 @@
         one_row(step, range(KSIZE))
         return carry
 
-    lax.fori_loop(inner[0], inner[1] + 1, inner_row, 0)
+    lax.fori_loop(inner[0], inner[1] + 1, inner_row, 0, unroll=5)
     if turns:
         flip = flip_matrix(shape.pitch, owned_of(info) * TILE + 2 * LEFT - 1)
         for k in range(HALF):

time: 60 us -> 59.5 us (level)
  no operation moved by 1% of the time
where the time goes in v13:
time: 59.5 us; the launch traced here: 59.3 us
  Pallas kernels  19.7 us (33%)
  starting transfers between devices  16.1 us (27%)
  blocking collectives  12 us (20%)
  waiting for transfers between devices  8.94 us (15%)
  between operations  1.51 us (3%)
  local copies, waits for them, and re-layouts  1.04 us (2%)
    pallas_call x21, Pallas kernels, call(): pl.pallas_call(body, out_shape=[jax.ShapeDtypeStruct(*out) for out in out...  19.7 us
    all_to_all x1, blocking collectives, shards(): came = lax.all_to_all(payload, ('near', 'dp'), 0, 0, tiled=True)  12 us
    ppermute x7, starting transfers between devices, swap(): return lax.ppermute(block, TILES, pairs_of(kind))  11.6 us
    ppermute x4, waiting for transfers between devices, bit_swap(): return lax.ppermute(block, TILES + ('dp',), pairs)  5.79 us
    ppermute x4, starting transfers between devices, bit_swap(): return lax.ppermute(block, TILES + ('dp',), pairs)  4.29 us
    ppermute x3, waiting for transfers between devices, core_swap(): return lax.ppermute(block, 'core', [(0, 1), (1, 0)])  2.71 us
  transfers between devices with their start and end apart: 14, of which 7 were waited for; matrix products, arithmetic and copies ran while one was open for 0% of the time, Pallas kernels for 23%

profile of v13, /device:TPU:0, one launch (start us, length us, event | category | flops | bytes accessed | tf_op | source)
XLA Modules:
  0.0 59.3 jit_solution(5863243907468020539)
XLA Ops:
  1.3 0.0 copy-start.4
  1.3 1.0 %copy-done.4 = bf16[1,3,16,16,256]{4,3,2,1,0:T(8,128)(2,1)S(1)} copy-done((bf16[1,3,16,16,256]{4,3,2,1,0:T(8,128)(2,1)S(1)}, bf16[1,3,16,16,256]{4,3,2,1,0:T(8,128)(2,1)}, u32[]{:S(2)}) %copy-start.4) | copy-done | bytes 393240
  2.3 0.6 shard_map.144
  2.9 4.1 %collective-permute-start.1 = (bf16[48,256]{1,0:T(8,128)(2,1)S(1)}, bf16[48,256]{1,0:T(8,128)(2,1)S(1)}, u32[]{:S(2)}, u32[]{:S(2)}) collective-permute-start(bf16[48,256]{1,0:T(8,128)(2,1)S(1)} %get-tuple-element.55), channel_id=1, source_target_pairs={{0,16},{2,4},{4,2},{6,8},{8,6},{10,12},{12,10},{14,30},{30,14},{28... | collective-permute-start | bytes 73736 | tf_op jit(solution)/shard_map/ppermute | solution.py:536
  7.0 0.0 collective-permute-start
  7.0 0.3 shard_map.145
  7.2 1.7 %collective-permute-start.2 = (bf16[144,256]{1,0:T(8,128)(2,1)S(1)}, bf16[144,256]{1,0:T(8,128)(2,1)S(1)}, u32[]{:S(2)}, u32[]{:S(2)}) collective-permute-start(bf16[144,256]{1,0:T(8,128)(2,1)S(1)} %get-tuple-element.56.refs_5_), channel_id=1, source_target_pairs={{0,16},{2,18},{4,20},{6,22},{8,24},{10,26},{12,28},{14,30},{30,14}... | collective-permute-start | bytes 221192 | tf_op jit(solution)/shard_map/ppermute | solution.py:536
  8.9 0.0 copy-start.2
  8.9 0.0 copy-start.3
  8.9 0.0 copy-start.6
  9.0 0.0 copy-start.7
  9.0 0.2 shard_map.146
  9.2 2.8 %collective-permute-start.3 = (bf16[48,256]{1,0:T(8,128)(2,1)S(1)}, bf16[48,256]{1,0:T(8,128)(2,1)S(1)}, u32[]{:S(2)}, u32[]{:S(2)}) collective-permute-start(bf16[48,256]{1,0:T(8,128)(2,1)S(1)} %get-tuple-element.58), channel_id=1, source_target_pairs={{0,16},{2,18},{4,20},{6,22},{8,24},{10,26},{12,28},{14,30},{30,14}... | collective-permute-start | bytes 73736 | tf_op jit(solution)/shard_map/ppermute | solution.py:536
  12.1 0.0 copy-start
  12.1 3.4 %shard_map.147 = (bf16[768,256]{1,0:T(8,128)(2,1)S(1)}, f32[768,256]{1,0:T(8,128)S(1)}, f32[768,128]{1,0:T(8,128)S(1)}, bf16[256,768]{1,0:T(8,128)(2,1)S(1)}, f32[768,1024]{1,0:T(8,128)S(1)}) custom-call(f32[3,8,256]{2,1,0:T(8,128)S(1)} %get-tuple-element.54.refs_1_.refs_0_.refs_8_.refs_3_, bf16[7,7,256]{2,1,0:T(8,128)(2,1)S(1)} %copy-done.6, ...), custom_call_target="tpu_custom_call" | custom-call | flops 5000000000 | tf_op jit(solution)/shard_map/pallas_call | solution.py:677
  15.5 0.0 collective-permute-done.3.refs_6_
  15.5 3.6 %shard_map.148 = (f32[1024,256]{1,0:T(8,128)S(1)}, bf16[1024,256]{1,0:T(8,128)(2,1)S(1)}, bf16[768,1024]{1,0:T(8,128)(2,1)S(1)}, bf16[768,1024]{1,0:T(8,128)(2,1...) custom-call(f32[8,128]{1,0:T(8,128)S(1)} %get-tuple-element.52.refs_0_, ...), custom_call_target="tpu_custom_call" | custom-call | flops 5000000000 | tf_op jit(solution)/shard_map/pallas_call | solution.py:677
  19.1 0.1 collective-permute-start.4
  19.2 1.1 %shard_map.149 = (bf16[768,256]{1,0:T(8,128)(2,1)S(1)}, f32[768,256]{1,0:T(8,128)S(1)}, f32[8,256]{1,0:T(8,128)S(1)}, f32[8,256]{1,0:T(8,128)S(1)}) custom-call(bf16[256,1024]{1,0:T(8,128)(2,1)S(1)} %copy-done, bf16[1024,256]{1,0:T(8,128)(2,1)S(1)} %copy-done.1, f32[1,256]{1,0:T(1,128)S(1)} %bitcast.14, bf16[768,1024]{1,0:T(8,128)(2,1)S(1)} %get-tuple-element.64.refs_3_, ...), custom_call_target="tpu_custom_call" | custom-call | flops 1300000000 | tf_op jit(solution)/shard_map/pallas_call | solution.py:677
  20.3 0.8 %collective-permute-done.4.refs_1_ = bf16[1024,256]{1,0:T(8,128)(2,1)S(1)} collective-permute-done((bf16[1024,256]{1,0:T(8,128)(2,1)S(1)}, bf16[1024,256]{1,0:T(8,128)(2,1)S(1)}, u32[]{:S(2)}, u32[]{:S(2)}) %collective-permute-start.4) | collective-permute-done | bytes 524320 | tf_op jit(solution)/shard_map/ppermute | solution.py:540
  21.1 0.2 shard_map.150
  21.2 0.3 collective-permute-start.6
  21.6 1.5 %shard_map.151.refs_3_.refs_4_.refs_2_ = f32[1216,128]{1,0:T(8,128)S(1)} custom-call(f32[8,128]{1,0:T(8,128)S(1)} %get-tuple-element.52.refs_0_, bf16[7,7,256]{2,1,0:T(8,128)(2,1)S(1)} %copy-done.6, bf16[768,256]{1,0:T(8,128)(2,1)S(1)} %get-tuple-element.69.refs_2_, bf16[512,256]{1,0:T(8,128)(2,1)S(1)} %get-tuple-element.73.refs_3_), custom_call_target="tpu_custom_call" | custom-call | flops 2000000000 | tf_op jit(solution)/shard_map/pallas_call | solution.py:677
  23.1 1.8 %shard_map.152 = (f32[1216,128]{1,0:T(8,128)S(1)}, bf16[192,256]{1,0:T(8,128)(2,1)S(1)}) custom-call(f32[8,128]{1,0:T(8,128)S(1)} %get-tuple-element.52.refs_0_, bf16[7,7,256]{2,1,0:T(8,128)(2,1)S(1)} %copy-done.6, bf16[768,256]{1,0:T(8,128)(2,1)S(1)} %get-tuple-element.69.refs_2_, f32[1216,128]{1,0:T(8,128)S(1)} %shard_map.151.refs_3_.refs_4_.refs_2_, ...), custom_call_target="tpu_custom_call" | custom-call | flops 2000000000 | tf_op jit(solution)/shard_map/pallas_call | solution.py:677
  24.9 1.5 %collective-permute-start.5 = (bf16[192,256]{1,0:T(8,128)(2,1)S(1)}, bf16[192,256]{1,0:T(8,128)(2,1)S(1)}, u32[]{:S(2)}, u32[]{:S(2)}) collective-permute-start(bf16[192,256]{1,0:T(8,128)(2,1)S(1)} %get-tuple-element.74), channel_id=1, source_target_pairs={{0,16},{2,18},{4,20},{6,22},{8,24},{10,26},{12,28},{14,30},{30,14}... | collective-permute-start | bytes 294920 | tf_op jit(solution)/shard_map/ppermute | solution.py:536
  26.4 1.3 %collective-permute-done.6.refs_1_ = bf16[512,256]{1,0:T(8,128)(2,1)S(1)} collective-permute-done((bf16[512,256]{1,0:T(8,128)(2,1)S(1)}, bf16[512,256]{1,0:T(8,128)(2,1)S(1)}, u32[]{:S(2)}, u32[]{:S(2)}) %collective-permute-start.6) | collective-permute-done | bytes 262176 | tf_op jit(solution)/shard_map/ppermute | solution.py:560
  27.7 0.1 shard_map.153
  27.8 1.6 %collective-permute-start.7 = (bf16[256,256]{1,0:T(8,128)(2,1)S(1)}, bf16[256,256]{1,0:T(8,128)(2,1)S(1)}, u32[]{:S(2)}, u32[]{:S(2)}) collective-permute-start(bf16[256,256]{1,0:T(8,128)(2,1)S(1)} %get-tuple-element.78.refs_3_), channel_id=1, source_target_pairs={{0,1},{1,0},{2,6},{3,7},{4,5},{5,4},{6,2},{7,3},{8,9},{9,8},{10,14... | collective-permute-start | bytes 393224 | tf_op jit(solution)/shard_map/ppermute | solution.py:560
  29.4 1.5 %shard_map.155.refs_3_ = f32[64,128]{1,0:T(8,128)S(1)} custom-call(f32[2,1216,128]{2,1,0:T(8,128)S(1)} %get-tuple-element.57.refs_6_.refs_4_.refs_0_, f32[2,640,128]{2,1,0:T(8,128)S(1)} %get-tuple-element.80.refs_1_, bf16[768,256]{1,0:T(8,128)(2,1)S(1)} %get-tuple-element.69.refs_2_, bf16[256,256]{1,0:T(8,128)(2,1)S(1)} %get-tuple-element.78.refs_3_), custom_call_target="tpu_custom_call" | custom-call | flops 1800000000 | tf_op jit(solution)/shard_map/pallas_call | solution.py:677
  30.8 1.5 %shard_map.154.refs_2_ = f32[64,128]{1,0:T(8,128)S(1)} custom-call(f32[2,1216,128]{2,1,0:T(8,128)S(1)} %get-tuple-element.57.refs_6_.refs_4_.refs_0_, f32[2,640,128]{2,1,0:T(8,128)S(1)} %get-tuple-element.80.refs_1_, bf16[768,256]{1,0:T(8,128)(2,1)S(1)} %get-tuple-element.69.refs_2_, bf16[256,256]{1,0:T(8,128)(2,1)S(1)} %get-tuple-element.78.refs_3_), custom_call_target="tpu_custom_call" | custom-call | flops 1800000000 | tf_op jit(solution)/shard_map/pallas_call | solution.py:677
  32.3 0.1 collective-permute-start.11
  32.4 0.4 collective-permute-done.7.refs_1_
  32.8 1.1 %collective-permute-start.10 = (bf16[128,256]{1,0:T(8,128)(2,1)S(1)}, bf16[128,256]{1,0:T(8,128)(2,1)S(1)}, u32[]{:S(2)}, u32[]{:S(2)}) collective-permute-start(bf16[128,256]{1,0:T(8,128)(2,1)S(1)} %get-tuple-element.82.refs_4_), channel_id=1, source_target_pairs={{0,8},{1,9},{2,3},{3,2},{4,12},{5,13},{6,7},{7,6},{8,0},{9,1},{10,... | collective-permute-start | bytes 196616 | tf_op jit(solution)/shard_map/ppermute | solution.py:560
  33.9 0.2 shard_map.158
  34.1 0.1 collective-permute-start.8
  34.2 1.4 %collective-permute-start.9 = (bf16[48,256]{1,0:T(8,128)(2,1)S(1)}, bf16[48,256]{1,0:T(8,128)(2,1)S(1)}, u32[]{:S(2)}, u32[]{:S(2)}) collective-permute-start(bf16[48,256]{1,0:T(8,128)(2,1)S(1)} %get-tuple-element.85), channel_id=1, source_target_pairs={{0,16},{2,4},{4,2},{6,8},{8,6},{10,12},{12,10},{14,30},{30,14},{28... | collective-permute-start | bytes 73736 | tf_op jit(solution)/shard_map/ppermute | solution.py:536
  35.6 1.6 %collective-permute-done.10.refs_1_ = bf16[128,256]{1,0:T(8,128)(2,1)S(1)} collective-permute-done((bf16[128,256]{1,0:T(8,128)(2,1)S(1)}, bf16[128,256]{1,0:T(8,128)(2,1)S(1)}, u32[]{:S(2)}, u32[]{:S(2)}) %collective-permute-start.10) | collective-permute-done | bytes 65568 | tf_op jit(solution)/shard_map/ppermute | solution.py:560
  37.2 0.0 copy-start.5
  37.2 1.3 %collective-permute-start.12 = (bf16[160,256]{1,0:T(8,128)(2,1)S(1)}, bf16[160,256]{1,0:T(8,128)(2,1)S(1)}, u32[]{:S(2)}, u32[]{:S(2)}) collective-permute-start(bf16[160,256]{1,0:T(8,128)(2,1)S(1)} %shard_map.159.refs_6_.refs_0_), channel_id=1, source_target_pairs={{0,16},{1,17},{2,18},{3,19},{4,20},{5,21},{6,22},{7,23},{8,24},{9,... | collective-permute-start | bytes 245768 | tf_op jit(solution)/shard_map/ppermute | solution.py:560
  38.5 0.4 collective-permute-done.9.refs_5_
  39.0 1.2 %shard_map.160 = (bf16[768,256]{1,0:T(8,128)(2,1)}, f32[8,128]{1,0:T(8,128)S(1)}) custom-call(f32[8,128]{1,0:T(8,128)S(1)} %get-tuple-element.52.refs_0_, f32[3,8,256]{2,1,0:T(8,128)S(1)} %get-tuple-element.54.refs_1_.refs_0_.refs_8_.refs_3_, bf16[768,256]{1,0:T(8,128)(2,1)S(1)} %bitcast.11, f32[2,1024,128]{2,1,0:T(8,128)S(1)} %get-tuple-element.83.refs_4_.refs_3_, ...), custom_call_target="tpu_custom_call" | custom-call | flops 1500000000 | tf_op jit(solution)/shard_map/pallas_call | solution.py:677
  40.1 0.9 %shard_map.161 = (bf16[768,256]{1,0:T(8,128)(2,1)}, f32[8,128]{1,0:T(8,128)S(1)}) custom-call(bf16[768,256]{1,0:T(8,128)(2,1)S(1)} %bitcast.18, f32[1,256]{1,0:T(1,128)S(1)} %bitcast.20, f32[768,256]{1,0:T(8,128)S(1)} %get-tuple-element.68.refs_2_, f32[3,8,256]{2,1,0:T(8,128)S(1)} %get-tuple-element.54.refs_1_.refs_0_.refs_8_.refs_3_, ...), custom_call_target="tpu_custom_call" | custom-call | flops 1000000000 | tf_op jit(solution)/shard_map/pallas_call | solution.py:677
  41.0 2.5 %collective-permute-done.12.refs_1_ = bf16[160,256]{1,0:T(8,128)(2,1)S(1)} collective-permute-done((bf16[160,256]{1,0:T(8,128)(2,1)S(1)}, bf16[160,256]{1,0:T(8,128)(2,1)S(1)}, u32[]{:S(2)}, u32[]{:S(2)}) %collective-permute-start.12) | collective-permute-done | bytes 81952 | tf_op jit(solution)/shard_map/ppermute | solution.py:560
  43.6 12.0 %all_to_all.5.refs_0_ = bf16[8,160,256]{2,1,0:T(8,128)(2,1)S(1)} all-to-all(bf16[8,160,256]{2,1,0:T(8,128)(2,1)S(1)} %shard_map.162), channel_id=1, replica_groups=mesh['far'=2,'near'=4,'core'=2,'dp'=2] {'near','dp'}, dimensions={0} | all-to-all | bytes 1310720 | tf_op jit(solution)/shard_map/all_to_all | solution.py:855
  55.6 0.1 shard_map.163.refs_0_
  55.6 0.1 collective-permute-start.13
  55.7 1.9 %collective-permute-done.13.refs_1_ = bf16[1088,256]{1,0:T(8,128)(2,1)S(1)} collective-permute-done((bf16[1088,256]{1,0:T(8,128)(2,1)S(1)}, bf16[1088,256]{1,0:T(8,128)(2,1)S(1)}, u32[]{:S(2)}, u32[]{:S(2)}) %collective-permute-start.13) | collective-permute-done | bytes 557088 | tf_op jit(solution)/shard_map/ppermute | solution.py:540
  57.7 1.6 %shard_map.164 = (f32[256,1024]{1,0:T(8,128)}, f32[1024,256]{1,0:T(8,128)}, f32[7,7,256]{2,1,0:T(8,128)}, f32[1,256]{1,0:T(1,128)}, f32[1,256]{1,0:T(1,128)}) custom-call(bf16[1088,256]{1,0:T(8,128)(2,1)S(1)} %shard_map.163.refs_0_, bf16[1088,256]{1,0:T(8,128)(2,1)S(1)} %collective-permute-done.13.refs_1_), custom_call_target="tpu_custom_call" | custom-call | flops 1500000000 | tf_op jit(solution)/shard_map/pallas_call | solution.py:677
  (20 shorter events, 0.2 us)
Async XLA Ops:
  1.3 1.0 %copy-start.4 = (bf16[1,3,16,16,256]{4,3,2,1,0:T(8,128)(2,1)S(1)}, bf16[1,3,16,16,256]{4,3,2,1,0:T(8,128)(2,1)}, u32[]{:S(2)}) copy-start(bf16[1,3,16,16,256]{4,3,2,1,0:T(8,128)(2,1)} %param.9) | copy-start | bytes 1179652
  2.3 4.7 %copy-start.8 = (s32[3]{0:T(128)S(1)}, s32[3]{0:T(128)}, u32[]{:S(2)}) copy-start(s32[3]{0:T(128)} %param.12) | copy-start | bytes 40
  2.9 6.0 %collective-permute-start.1 = (bf16[48,256]{1,0:T(8,128)(2,1)S(1)}, bf16[48,256]{1,0:T(8,128)(2,1)S(1)}, u32[]{:S(2)}, u32[]{:S(2)}) collective-permute-start(bf16[48,256]{1,0:T(8,128)(2,1)S(1)} %get-tuple-element.55), channel_id=1, source_target_pairs={{0,16},{2,4},{4,2},{6,8},{8,6},{10,12},{12,10},{14,30},{30,14},{28... | collective-permute-start | bytes 73736 | tf_op jit(solution)/shard_map/ppermute | solution.py:536
  7.0 1.9 %collective-permute-start = (bf16[48,256]{1,0:T(8,128)(2,1)S(1)}, bf16[48,256]{1,0:T(8,128)(2,1)S(1)}, u32[]{:S(2)}, u32[]{:S(2)}) collective-permute-start(bf16[48,256]{1,0:T(8,128)(2,1)S(1)} %get-tuple-element.53.refs_3_), channel_id=1, source_target_pairs={{0,2},{2,0},{4,6},{6,4},{8,10},{10,8},{12,14},{14,12},{30,28},{28,... | collective-permute-start | bytes 73736 | tf_op jit(solution)/shard_map/ppermute | solution.py:536
  7.2 8.2 %collective-permute-start.2 = (bf16[144,256]{1,0:T(8,128)(2,1)S(1)}, bf16[144,256]{1,0:T(8,128)(2,1)S(1)}, u32[]{:S(2)}, u32[]{:S(2)}) collective-permute-start(bf16[144,256]{1,0:T(8,128)(2,1)S(1)} %get-tuple-element.56.refs_5_), channel_id=1, source_target_pairs={{0,16},{2,18},{4,20},{6,22},{8,24},{10,26},{12,28},{14,30},{30,14}... | collective-permute-start | bytes 221192 | tf_op jit(solution)/shard_map/ppermute | solution.py:536
  8.9 3.1 %copy-start.1 = (bf16[1024,256]{1,0:T(8,128)(2,1)S(1)}, bf16[1024,256]{1,0:T(8,128)(2,1)}, u32[]{:S(2)}) copy-start(bf16[1024,256]{1,0:T(8,128)(2,1)} %refs_1_.7) | copy-start | bytes 1572868
  8.9 3.1 %copy-start.2 = (bf16[1,3,16,16,256]{4,3,2,1,0:T(8,128)(2,1)S(1)}, bf16[1,3,16,16,256]{4,3,2,1,0:T(8,128)(2,1)}, u32[]{:S(2)}) copy-start(bf16[1,3,16,16,256]{4,3,2,1,0:T(8,128)(2,1)} %param.10) | copy-start | bytes 1179652
  8.9 3.1 %copy-start.3 = (f32[256]{0:T(256)S(1)}, f32[256]{0:T(256)}, u32[]{:S(2)}) copy-start(f32[256]{0:T(256)} %param.14) | copy-start | bytes 3076
  8.9 3.1 %copy-start.6 = (bf16[7,7,256]{2,1,0:T(8,128)(2,1)S(1)}, bf16[7,7,256]{2,1,0:T(8,128)(2,1)}, u32[]{:S(2)}) copy-start(bf16[7,7,256]{2,1,0:T(8,128)(2,1)} %refs_1_.9) | copy-start | bytes 75268
  9.0 3.1 %copy-start.7 = (f32[256]{0:T(256)S(1)}, f32[256]{0:T(256)}, u32[]{:S(2)}) copy-start(f32[256]{0:T(256)} %param.17) | copy-start | bytes 3076
  9.2 6.3 %collective-permute-start.3 = (bf16[48,256]{1,0:T(8,128)(2,1)S(1)}, bf16[48,256]{1,0:T(8,128)(2,1)S(1)}, u32[]{:S(2)}, u32[]{:S(2)}) collective-permute-start(bf16[48,256]{1,0:T(8,128)(2,1)S(1)} %get-tuple-element.58), channel_id=1, source_target_pairs={{0,16},{2,18},{4,20},{6,22},{8,24},{10,26},{12,28},{14,30},{30,14}... | collective-permute-start | bytes 73736 | tf_op jit(solution)/shard_map/ppermute | solution.py:536
  12.1 3.4 %copy-start = (bf16[256,1024]{1,0:T(8,128)(2,1)S(1)}, bf16[256,1024]{1,0:T(8,128)(2,1)}, u32[]{:S(2)}) copy-start(bf16[256,1024]{1,0:T(8,128)(2,1)} %refs_0_.2) | copy-start | bytes 1572868
  19.1 2.0 %collective-permute-start.4 = (bf16[1024,256]{1,0:T(8,128)(2,1)S(1)}, bf16[1024,256]{1,0:T(8,128)(2,1)S(1)}, u32[]{:S(2)}, u32[]{:S(2)}) collective-permute-start(bf16[1024,256]{1,0:T(8,128)(2,1)S(1)} %get-tuple-element.71), channel_id=1, source_target_pairs={{0,2},{2,0},{1,3},{3,1},{4,6},{6,4},{5,7},{7,5},{8,10},{10,8},{9,1... | collective-permute-start | bytes 1572872 | tf_op jit(solution)/shard_map/ppermute | solution.py:540
  21.2 6.4 %collective-permute-start.6 = (bf16[512,256]{1,0:T(8,128)(2,1)S(1)}, bf16[512,256]{1,0:T(8,128)(2,1)S(1)}, u32[]{:S(2)}, u32[]{:S(2)}) collective-permute-start(bf16[512,256]{1,0:T(8,128)(2,1)S(1)} %get-tuple-element.73.refs_3_), channel_id=1, source_target_pairs={{0,4},{1,5},{2,10},{3,11},{4,0},{5,1},{6,14},{7,15},{8,12},{9,13},... | collective-permute-start | bytes 786440 | tf_op jit(solution)/shard_map/ppermute | solution.py:560
  24.9 9.0 %collective-permute-start.5 = (bf16[192,256]{1,0:T(8,128)(2,1)S(1)}, bf16[192,256]{1,0:T(8,128)(2,1)S(1)}, u32[]{:S(2)}, u32[]{:S(2)}) collective-permute-start(bf16[192,256]{1,0:T(8,128)(2,1)S(1)} %get-tuple-element.74), channel_id=1, source_target_pairs={{0,16},{2,18},{4,20},{6,22},{8,24},{10,26},{12,28},{14,30},{30,14}... | collective-permute-start | bytes 294920 | tf_op jit(solution)/shard_map/ppermute | solution.py:536
  27.8 5.0 %collective-permute-start.7 = (bf16[256,256]{1,0:T(8,128)(2,1)S(1)}, bf16[256,256]{1,0:T(8,128)(2,1)S(1)}, u32[]{:S(2)}, u32[]{:S(2)}) collective-permute-start(bf16[256,256]{1,0:T(8,128)(2,1)S(1)} %get-tuple-element.78.refs_3_), channel_id=1, source_target_pairs={{0,1},{1,0},{2,6},{3,7},{4,5},{5,4},{6,2},{7,3},{8,9},{9,8},{10,14... | collective-permute-start | bytes 393224 | tf_op jit(solution)/shard_map/ppermute | solution.py:560
  32.3 3.2 %collective-permute-start.11 = (bf16[64,256]{1,0:T(8,128)(2,1)S(1)}, bf16[64,256]{1,0:T(8,128)(2,1)S(1)}, u32[]{:S(2)}, u32[]{:S(2)}) collective-permute-start(bf16[64,256]{1,0:T(8,128)(2,1)S(1)} %get-tuple-element.87), channel_id=1, source_target_pairs={{0,2},{2,0},{1,3},{3,1},{4,6},{6,4},{5,7},{7,5},{8,10},{10,8},{9,1... | collective-permute-start | bytes 98312 | tf_op jit(solution)/shard_map/ppermute | solution.py:540
  32.8 4.3 %collective-permute-start.10 = (bf16[128,256]{1,0:T(8,128)(2,1)S(1)}, bf16[128,256]{1,0:T(8,128)(2,1)S(1)}, u32[]{:S(2)}, u32[]{:S(2)}) collective-permute-start(bf16[128,256]{1,0:T(8,128)(2,1)S(1)} %get-tuple-element.82.refs_4_), channel_id=1, source_target_pairs={{0,8},{1,9},{2,3},{3,2},{4,12},{5,13},{6,7},{7,6},{8,0},{9,1},{10,... | collective-permute-start | bytes 196616 | tf_op jit(solution)/shard_map/ppermute | solution.py:560
  34.1 4.4 %collective-permute-start.8 = (bf16[48,256]{1,0:T(8,128)(2,1)S(1)}, bf16[48,256]{1,0:T(8,128)(2,1)S(1)}, u32[]{:S(2)}, u32[]{:S(2)}) collective-permute-start(bf16[48,256]{1,0:T(8,128)(2,1)S(1)} %get-tuple-element.84), channel_id=1, source_target_pairs={{0,2},{2,0},{4,6},{6,4},{8,10},{10,8},{12,14},{14,12},{30,28},{28,... | collective-permute-start | bytes 73736 | tf_op jit(solution)/shard_map/ppermute | solution.py:536
  34.2 4.8 %collective-permute-start.9 = (bf16[48,256]{1,0:T(8,128)(2,1)S(1)}, bf16[48,256]{1,0:T(8,128)(2,1)S(1)}, u32[]{:S(2)}, u32[]{:S(2)}) collective-permute-start(bf16[48,256]{1,0:T(8,128)(2,1)S(1)} %get-tuple-element.85), channel_id=1, source_target_pairs={{0,16},{2,4},{4,2},{6,8},{8,6},{10,12},{12,10},{14,30},{30,14},{28... | collective-permute-start | bytes 73736 | tf_op jit(solution)/shard_map/ppermute | solution.py:536
  37.2 2.9 %copy-start.5 = (bf16[1,3,16,16,256]{4,3,2,1,0:T(8,128)(2,1)S(1)}, bf16[1,3,16,16,256]{4,3,2,1,0:T(8,128)(2,1)}, u32[]{:S(2)}) copy-start(bf16[1,3,16,16,256]{4,3,2,1,0:T(8,128)(2,1)} %param.9) | copy-start | bytes 1179652
  37.2 6.3 %collective-permute-start.12 = (bf16[160,256]{1,0:T(8,128)(2,1)S(1)}, bf16[160,256]{1,0:T(8,128)(2,1)S(1)}, u32[]{:S(2)}, u32[]{:S(2)}) collective-permute-start(bf16[160,256]{1,0:T(8,128)(2,1)S(1)} %shard_map.159.refs_6_.refs_0_), channel_id=1, source_target_pairs={{0,16},{1,17},{2,18},{3,19},{4,20},{5,21},{6,22},{7,23},{8,24},{9,... | collective-permute-start | bytes 245768 | tf_op jit(solution)/shard_map/ppermute | solution.py:560
  55.6 2.0 %collective-permute-start.13 = (bf16[1088,256]{1,0:T(8,128)(2,1)S(1)}, bf16[1088,256]{1,0:T(8,128)(2,1)S(1)}, u32[]{:S(2)}, u32[]{:S(2)}) collective-permute-start(bf16[1088,256]{1,0:T(8,128)(2,1)S(1)} %shard_map.163.refs_0_), channel_id=1, source_target_pairs={{0,2},{2,0},{1,3},{3,1},{4,6},{6,4},{5,7},{7,5},{8,10},{10,8},{9,1... | collective-permute-start | bytes 1671176 | tf_op jit(solution)/shard_map/ppermute | solution.py:540
